TPU v7x, 32 devices: a whole 2x2x4 slice. The times are simulated.
32 devices in a mesh: lvl: 4 (over z), col: 8 (over y, x, core).
Axes of the slice: x: 2, y: 2, z: 4, core: 2. Of those that a mesh axis runs over, the one named last changes fastest.
Arguments:
- rhs: float32 [4, 1536, 128], P('lvl', 'col'), may hold values from -6 to 6
- panel: bfloat16 [4, 2, 1536, 1536], P('lvl', None, 'col'), may hold values from -0.078125 to 0.078125
- inverse_t: bfloat16 [4, 1536, 1536], P('lvl', 'col'), as said below
- pattern: int32 [4, 2, 12, 12], P('lvl'), may hold values 0 or 1
Outputs:
- sample: float32 [4, 1536, 128], P('lvl', 'col')
- solution: float32 [4, 1536, 128], P('lvl', 'col')
Inputs may be any that keep to these rules, and one draw needn't show every extreme that they name: `pattern`: 1 marks a 128 x 128 tile of a panel slot that is structurally nonzero. Each inverse_t[s] is upper triangular with a positive diagonal.
All inputs are finite; a program needn't handle non-finite values.
Results may differ from a plain program's by a relative error of at most 0.035.
Values may be sent and summed in bfloat16 or wider, within the bound.
No kernel may reach another device: no remote copies, remote signals or barrier semaphores. Data moves between devices by JAX's collectives and lax.ppermute only.
A program may use at most 64 MiB of HBM per device.

v0:
```python
import jax
import jax.numpy as jnp
from jax import lax
from jax.sharding import PartitionSpec as P


def as_sent(x):

    def short(part):
        return part.astype(jnp.bfloat16) if part.dtype == jnp.float32 else part

    return jax.tree.map(short, x)


def level_rank(device_pos, levels):
    running = jnp.zeros((), jnp.int32)
    for exponent in range(1, levels + 1):
        running = running + ((device_pos + 1) % 2**exponent == 0).astype(jnp.int32)
    return running


def expand_pattern(pattern_own, row_start, row_count, full_width):
    tile_count = pattern_own.shape[1]
    tile_size = full_width // tile_count
    row_ids = row_start + lax.iota(jnp.int32, row_count)
    row_pick = (row_ids[:, None] // tile_size == lax.iota(jnp.int32, tile_count)[None, :]).astype(
        jnp.bfloat16
    )
    col_pick = (
        lax.iota(jnp.int32, full_width)[None, :] // tile_size
        == lax.iota(jnp.int32, tile_count)[:, None]
    ).astype(jnp.bfloat16)
    row_mask = jnp.einsum(
        "rb,kbc->krc",
        row_pick,
        pattern_own.astype(jnp.bfloat16),
        preferred_element_type=jnp.float32,
    ).astype(jnp.bfloat16)
    return jnp.einsum("krc,cn->krn", row_mask, col_pick, preferred_element_type=jnp.float32).astype(
        jnp.bfloat16
    )


def pick_member(everyone, member_pos, member_total):
    safe_pos = jnp.clip(member_pos, 0, member_total - 1)
    picked = lax.dynamic_index_in_dim(everyone, safe_pos, 0, keepdims=False)
    inside = jnp.logical_and(member_pos >= 0, member_pos < member_total)
    return jnp.where(inside, picked, jnp.zeros_like(picked))


def on_device(rhs, panel, inverse_t, pattern):
    member_total = lax.axis_size("lvl")
    levels = member_total.bit_length() - 1
    device_pos = lax.axis_index("lvl")
    column_pos = lax.axis_index("col")
    row_count = rhs.shape[1]
    rhs_count = rhs.shape[2]
    full_width = inverse_t.shape[2]
    height = level_rank(device_pos, levels)
    right_side = rhs[0]
    inverse_own = inverse_t[0]
    factor = panel[0] * expand_pattern(pattern[0], column_pos * row_count, row_count, full_width)
    sample = jnp.zeros((row_count, rhs_count), jnp.float32)
    upward = jnp.zeros((levels + 1, row_count, rhs_count), jnp.float32)
    for section_num in range(levels + 1):
        if section_num == 0:
            gathered = upward
        else:
            reach_dist = 2 ** (section_num - 1)
            everyone = lax.all_gather(as_sent(upward[None]), "lvl", axis=0, tiled=True)
            from_left = pick_member(everyone, device_pos - reach_dist, member_total)
            from_right = pick_member(everyone, device_pos + reach_dist, member_total)
            gathered = from_left + from_right
        active = height == section_num
        residual = (right_side - gathered[0]).astype(jnp.bfloat16)
        partial_sum = jnp.einsum(
            "ri,rn->in", inverse_own, residual, preferred_element_type=jnp.float32
        )
        solved_all = lax.psum(partial_sum.astype(jnp.bfloat16), "col").astype(jnp.float32)
        own_rows = lax.dynamic_slice_in_dim(solved_all, column_pos * row_count, row_count, 0)
        solved_half = solved_all.astype(jnp.bfloat16)
        sample = jnp.where(active, own_rows, sample)
        remain = levels - section_num
        if remain > 0:
            pushed = jnp.einsum(
                "krn,nm->krm", factor[:remain], solved_half, preferred_element_type=jnp.float32
            )
            upward = jnp.where(active, pushed + gathered[1 : remain + 1], 0.0)
    answer = jnp.zeros((row_count, rhs_count), jnp.float32)
    ancestry = jnp.zeros((levels, row_count, rhs_count), jnp.bfloat16)
    downward = ancestry
    for section_num in range(levels, -1, -1):
        remain = levels - section_num
        active = height == section_num
        if remain > 0:
            reach_dist = 2**section_num
            everyone = lax.all_gather(downward[None], "lvl", axis=0, tiled=True)
            parent_up = device_pos // (2 * reach_dist) % 2 == 0
            parent_pos = jnp.where(parent_up, device_pos + reach_dist, device_pos - reach_dist)
            received = pick_member(everyone, parent_pos, member_total)
            ancestry = ancestry.at[:remain].set(jnp.where(active, received, ancestry[:remain]))
            partial_adj = jnp.einsum(
                "krn,krm->nm",
                factor[:remain],
                ancestry[:remain],
                preferred_element_type=jnp.float32,
            )
            adjoint = lax.psum_scatter(
                partial_adj.astype(jnp.bfloat16), "col", scatter_dimension=0, tiled=True
            ).astype(jnp.float32)
            back_full = sample - adjoint
        else:
            back_full = sample
        back_whole = lax.all_gather(back_full.astype(jnp.bfloat16), "col", axis=0, tiled=True)
        solved = jnp.dot(inverse_own, back_whole, preferred_element_type=jnp.float32)
        answer = jnp.where(active, solved, answer)
        solved_half = solved.astype(jnp.bfloat16)
        if section_num > 0:
            downward = jnp.concatenate(
                [solved_half[None], ancestry[: levels - section_num]], axis=0
            )
    return (sample[None], answer[None])


def solution(mesh):
    in_specs = (
        P("lvl", "col", None),
        P("lvl", None, "col", None),
        P("lvl", "col", None),
        P("lvl", None, None, None),
    )
    out_specs = (P("lvl", "col", None), P("lvl", "col", None))
    return jax.shard_map(
        on_device, mesh=mesh, in_specs=in_specs, out_specs=out_specs, check_vma=False
    )
```

profile of v0, /device:TPU:0, one launch (start us, length us, event | category | flops | bytes accessed | tf_op | source)
XLA Modules:
  0.0 348.2 jit_solution(807737058820212639)
XLA Ops:
  7.2 0.0 copy-start
  7.2 0.0 copy-start.3
  7.2 0.0 copy-start.1
  7.2 0.0 all-reduce.5.cloned.1.call-start
  7.2 1.0 copy-done
  8.2 2.1 convolution_convert_fusion.4
  10.3 0.0 all-reduce.5.cloned.1.call-update
  10.3 0.0 all-reduce.7.cloned.1.call-start
  10.5 0.0 copy-done.3
  10.5 0.0 copy-done.1
  10.5 0.8 fusion
  11.3 0.0 copy-start.2
  11.3 56.7 %all-reduce.5.cloned.1.call-done = bf16[1536,128]{1,0:T(8,128)(2,1)} async-done(((bf16[1536,128]{1,0:T(8,128)(2,1)}), bf16[1536,128]{1,0:T(8,128)(2,1)}) %all-reduce.5.cloned.1.call-update) | async-done | bytes 393232 | tf_op jit(solution)/shard_map/psum | solution.py:79
  68.0 1.5 fusion.4
  69.4 14.4 %all-gather = bf16[8,192,128]{2,1,0:T(8,128)(2,1)S(1)} all-gather(bf16[2,192,128]{2,1,0:T(8,128)(2,1)S(1)} %fusion.4), channel_id=2, replica_groups=mesh['lvl'=4,'col'=8] {'lvl'}, dimensions={0}, use_global_device_ids=true | all-gather | bytes 491520 | tf_op jit(solution)/shard_map/all_gather | solution.py:70
  83.9 0.0 copy-done.2
  83.9 1.2 fusion.2
  85.1 0.0 all-reduce.7.cloned.1.call-update
  85.1 0.0 all-reduce.9.cloned.1.call-start
  85.2 53.9 %all-reduce.7.cloned.1.call-done = bf16[1536,128]{1,0:T(8,128)(2,1)} async-done(((bf16[1536,128]{1,0:T(8,128)(2,1)}), bf16[1536,128]{1,0:T(8,128)(2,1)}) %all-reduce.7.cloned.1.call-update) | async-done | bytes 393232 | tf_op jit(solution)/shard_map/psum | solution.py:79
  139.1 1.3 fusion.8
  140.4 13.7 %all-gather.1 = bf16[4,192,128]{2,1,0:T(8,128)(2,1)S(1)} all-gather(bf16[1,192,128]{2,1,0:T(8,128)(2,1)S(1)} %fusion.8), channel_id=3, replica_groups=mesh['lvl'=4,'col'=8] {'lvl'}, dimensions={0}, use_global_device_ids=true | all-gather | bytes 245760 | tf_op jit(solution)/shard_map/all_gather | solution.py:70
  154.1 1.2 fusion.3
  155.3 0.0 all-reduce.9.cloned.1.call-update
  155.3 0.0 reduce-scatter.3.cloned.1.call-start
  155.4 53.6 %all-reduce.9.cloned.1.call-done = bf16[1536,128]{1,0:T(8,128)(2,1)} async-done(((bf16[1536,128]{1,0:T(8,128)(2,1)}), bf16[1536,128]{1,0:T(8,128)(2,1)}) %all-reduce.9.cloned.1.call-update) | async-done | bytes 393232 | tf_op jit(solution)/shard_map/psum | solution.py:79
  209.0 0.9 fusion.63
  209.8 8.9 %all_gather.23 = bf16[1536,128]{1,0:T(8,128)(2,1)S(1)} all-gather(bf16[192,128]{1,0:T(8,128)(2,1)S(1)} %fusion.63), channel_id=1, replica_groups=mesh['lvl'=4,'col'=8] {'col'}, dimensions={0}, use_global_device_ids=true | all-gather | bytes 442368 | tf_op jit(solution)/shard_map/all_gather | solution.py:114
  218.7 0.3 fusion.10
  219.0 13.7 %all-gather.2 = bf16[768,128]{1,0:T(8,128)(2,1)S(1)} all-gather(bf16[192,128]{1,0:T(8,128)(2,1)S(1)} %convert_bitcast_fusion.1), channel_id=4, replica_groups=mesh['lvl'=4,'col'=8] {'lvl'}, dimensions={0}, use_global_device_ids=true | all-gather | bytes 245760 | tf_op jit(solution)/shard_map/all_gather | solution.py:97
  232.8 1.2 convolution_convert_fusion.1
  233.9 0.0 reduce-scatter.3.cloned.1.call-update
  234.0 0.0 reduce-scatter.5.cloned.1.call-start
  234.1 34.1 %reduce-scatter.3.cloned.1.call-done = bf16[192,128]{1,0:T(8,128)(2,1)} async-done(((bf16[1536,128]{1,0:T(8,128)(2,1)}), bf16[192,128]{1,0:T(8,128)(2,1)}) %reduce-scatter.3.cloned.1.call-update) | async-done | bytes 49168 | tf_op jit(solution)/shard_map/reduce_scatter | solution.py:108
  268.2 0.9 subtract_convert_fusion.1
  269.1 9.5 %all_gather.25 = bf16[1536,128]{1,0:T(8,128)(2,1)S(1)} all-gather(bf16[192,128]{1,0:T(8,128)(2,1)S(1)} %subtract_convert_fusion.1), channel_id=1, replica_groups=mesh['lvl'=4,'col'=8] {'col'}, dimensions={0}, use_global_device_ids=true | all-gather | bytes 442368 | tf_op jit(solution)/shard_map/all_gather | solution.py:114
  278.7 0.3 fusion.12
  279.0 14.7 %all-gather.3 = bf16[8,192,128]{2,1,0:T(8,128)(2,1)S(1)} all-gather(bf16[2,192,128]{2,1,0:T(8,128)(2,1)S(1)} %pad_maximum_fusion), channel_id=5, replica_groups=mesh['lvl'=4,'col'=8] {'lvl'}, dimensions={0}, use_global_device_ids=true | all-gather | bytes 491520 | tf_op jit(solution)/shard_map/all_gather | solution.py:97
  293.7 1.3 fusion.1
  295.0 0.0 reduce-scatter.5.cloned.1.call-update
  295.0 34.7 %reduce-scatter.5.cloned.1.call-done = bf16[192,128]{1,0:T(8,128)(2,1)} async-done(((bf16[1536,128]{1,0:T(8,128)(2,1)}), bf16[192,128]{1,0:T(8,128)(2,1)}) %reduce-scatter.5.cloned.1.call-update) | async-done | bytes 49168 | tf_op jit(solution)/shard_map/reduce_scatter | solution.py:108
  329.7 1.5 subtract_convert_fusion
  331.2 9.5 %all_gather.27 = bf16[1536,128]{1,0:T(8,128)(2,1)S(1)} all-gather(bf16[192,128]{1,0:T(8,128)(2,1)S(1)} %get-tuple-element.34), channel_id=1, replica_groups=mesh['lvl'=4,'col'=8] {'col'}, dimensions={0}, use_global_device_ids=true | all-gather | bytes 442368 | tf_op jit(solution)/shard_map/all_gather | solution.py:114
  340.7 0.9 fusion.5
  (8 shorter events, 0.1 us)
Async XLA Ops:
  7.2 1.1 copy-start
  7.2 3.3 copy-start.3
  7.2 3.3 copy-start.1
  7.2 60.8 %all-reduce.5.cloned.1.call-start = ((), (), s32[]{:S(2)}) async-start(), calls=%async_computation.2 | async-start | bytes 786432 | tf_op jit(solution)/shard_map/psum | solution.py:79
  10.3 128.8 %all-reduce.7.cloned.1.call-start = ((), (), s32[]{:S(2)}) async-start(), calls=%async_computation.3 | async-start | bytes 786432 | tf_op jit(solution)/shard_map/psum | solution.py:79
  11.3 72.6 %copy-start.2 = (f32[1,192,128]{2,1,0:T(8,128)S(1)}, f32[1,192,128]{2,1,0:T(8,128)}, u32[]{:S(2)}) copy-start(f32[1,192,128]{2,1,0:T(8,128)} %param.10) | copy-start | bytes 294916
  85.1 123.9 %all-reduce.9.cloned.1.call-start = ((), (), s32[]{:S(2)}) async-start(), calls=%async_computation.4 | async-start | bytes 786432 | tf_op jit(solution)/shard_map/psum | solution.py:79
  155.3 112.9 %reduce-scatter.3.cloned.1.call-start = ((), (), s32[]{:S(2)}) async-start(), calls=%async_computation.5 | async-start | bytes 442368 | tf_op jit(solution)/shard_map/reduce_scatter | solution.py:108
  234.0 95.7 %reduce-scatter.5.cloned.1.call-start = ((), (), s32[]{:S(2)}) async-start(), calls=%async_computation.6 | async-start | bytes 442368 | tf_op jit(solution)/shard_map/reduce_scatter | solution.py:108
Sparse Core Ops, SparseCore 0:
  11.1 56.8 all-reduce.4
  85.2 53.8 all-reduce.6
  155.4 53.4 all-reduce.8
  234.1 34.0 reduce-scatter.2
  295.1 34.4 reduce-scatter.4
where the time goes:
time: 349 us; the launch traced here: 348 us
  waiting for transfers between devices  233 us (67%)
  blocking collectives  84.4 us (24%)
  between operations  14.1 us (4%)
  matrix products  12 us (3%)
    psum x3, waiting for transfers between devices, on_device(): lax.psum(partial_sum.astype(jnp.bfloat16), 'col').astype(jnp.float32)  164 us
    reduce_scatter x2, waiting for transfers between devices, on_device(): lax.psum_scatter(partial_adj.astype(jnp.bfloat16), 'col', scatter_dimensi...  68.8 us
    all_gather x2, blocking collectives, on_device(): everyone = lax.all_gather(downward[None], 'lvl', axis=0, tiled=True)  28.5 us
    all_gather x2, blocking collectives, on_device(): everyone = lax.all_gather(as_sent(upward[None]), 'lvl', axis=0, tiled=True)  28.1 us
    all_gather x3, blocking collectives, on_device(): lax.all_gather(back_full.astype(jnp.bfloat16), 'col', axis=0, tiled=True)  27.9 us
  transfers between devices with their start and end apart: 5, of which 5 were waited for; matrix products, arithmetic and copies ran while one was open for 0% of the time, Pallas kernels for 0%

commit v1 on v0

v1 whole, which is shorter than its diff:
```python
import jax
import jax.numpy as jnp
from jax import lax
from jax.sharding import PartitionSpec as P

F32 = jnp.float32
BF16 = jnp.bfloat16


def trailing_ones(node):
    ones = 0
    while node % 2 == 1:
        ones += 1
        node //= 2
    return ones


def level_rank(device_pos, levels):
    running = jnp.zeros((), jnp.int32)
    for exponent in range(1, levels + 1):
        running = running + ((device_pos + 1) % 2**exponent == 0).astype(jnp.int32)
    return running


def child_pairs(section, members):
    reach = 2 ** (section - 1)
    parents = [node for node in range(members - 1) if trailing_ones(node) == section]
    left = [(node - reach, node) for node in parents]
    right = [(node + reach, node) for node in parents]
    return left, right


def expand_pattern(pattern_own, row_start, row_count, full_width):
    tile_count = pattern_own.shape[1]
    tile_size = full_width // tile_count
    row_ids = row_start + lax.iota(jnp.int32, row_count)
    row_pick = (row_ids[:, None] // tile_size == lax.iota(jnp.int32, tile_count)[None, :]).astype(BF16)
    col_pick = (
        lax.iota(jnp.int32, full_width)[None, :] // tile_size == lax.iota(jnp.int32, tile_count)[:, None]
    ).astype(BF16)
    row_mask = jnp.einsum("rb,kbc->krc", row_pick, pattern_own.astype(BF16), preferred_element_type=F32)
    return jnp.einsum("krc,cn->krn", row_mask.astype(BF16), col_pick, preferred_element_type=F32).astype(BF16)


def on_device(rhs, panel, inverse_t, pattern):
    members = lax.axis_size("lvl")
    cols = lax.axis_size("col")
    levels = members.bit_length() - 1
    root, heir = members - 1, members // 2 - 1
    lvl_pos = lax.axis_index("lvl")
    col_pos = lax.axis_index("col")
    core = col_pos % 2
    row_count, rhs_count = rhs.shape[1:]
    half = rhs_count // 2
    full_width = inverse_t.shape[2]
    height = level_rank(lvl_pos, levels)

    def swap(x, offset):
        return lax.ppermute(x, "col", [(i, i ^ offset) for i in range(cols)])

    def along(x, pairs):
        return lax.ppermute(x, "lvl", pairs)

    def col_sum(partial):
        terms = partial.astype(BF16)
        low, high = terms[:half], terms[half:]
        keep = jnp.where(core == 0, low, high)
        give = jnp.where(core == 0, high, low)
        chip = (keep.astype(F32) + swap(give, 1).astype(F32)).astype(BF16)
        total = chip.astype(F32)
        for offset in range(2, cols, 2):
            total = total + swap(chip, offset).astype(F32)
        own = total.astype(BF16)
        other = swap(own, 1)
        return jnp.concatenate([jnp.where(core == 0, own, other), jnp.where(core == 0, other, own)], axis=0)

    def own_rows(whole):
        return lax.dynamic_slice_in_dim(whole, col_pos * row_count, row_count, 1).T.astype(F32)

    inverse_own = inverse_t[0]
    right_side = rhs[0]
    root_inverse = along(inverse_own, [(root, heir)])
    root_rhs = along(right_side, [(root, heir)])
    factor = panel[0] * expand_pattern(pattern[0], col_pos * row_count, row_count, full_width)

    def down_solve(inverse, residual):
        return col_sum(jnp.einsum("ri,rn->ni", inverse, residual.astype(BF16), preferred_element_type=F32))

    def up_solve(inverse, back):
        return jnp.einsum("ri,ni->rn", inverse, back, preferred_element_type=F32)

    samples = [None] * levels
    gathered = None
    for section in range(levels):
        if section > 0:
            left, right = child_pairs(section, members)
            sent = pushed.astype(BF16)
            gathered = along(sent, left).astype(F32) + along(sent, right).astype(F32)
        residual = right_side if gathered is None else right_side - gathered[0]
        samples[section] = down_solve(inverse_own, residual)
        pushed = jnp.einsum("krn,mn->krm", factor[: levels - section], samples[section], preferred_element_type=F32)
        if gathered is not None:
            pushed = pushed + gathered[1:]
    root_sample = down_solve(root_inverse, root_rhs - pushed[0])
    root_answer = up_solve(root_inverse, root_sample)
    sample = own_rows(samples[0])
    for section in range(1, levels):
        sample = jnp.where(height == section, own_rows(samples[section]), sample)

    ancestry = root_answer.astype(BF16)[None]
    answer = None
    for section in range(levels - 1, -1, -1):
        if section < levels - 1:
            left, right = child_pairs(section + 1, members)
            sent = jnp.concatenate([solved.astype(BF16)[None], ancestry], axis=0)
            ancestry = along(sent, [(b, a) for a, b in left]) + along(sent, [(b, a) for a, b in right])
        adjoint = col_sum(jnp.einsum("krn,krm->mn", factor[: levels - section], ancestry, preferred_element_type=F32))
        back = (samples[section].astype(F32) - adjoint.astype(F32)).astype(BF16)
        solved = up_solve(inverse_own, back)
        answer = solved if answer is None else jnp.where(height == section, solved, answer)
    root_out = along(jnp.stack([own_rows(root_sample), root_answer]), [(heir, root)])
    at_root = lvl_pos == root
    sample = jnp.where(at_root, root_out[0], sample)
    answer = jnp.where(at_root, root_out[1], answer)
    return (sample[None], answer[None])


def solution(mesh):
    in_specs = (
        P("lvl", "col", None),
        P("lvl", None, "col", None),
        P("lvl", "col", None),
        P("lvl", None, None, None),
    )
    out_specs = (P("lvl", "col", None), P("lvl", "col", None))
    return jax.shard_map(
        on_device, mesh=mesh, in_specs=in_specs, out_specs=out_specs, check_vma=False
    )
```

time: 349 us -> 171 us (0.49)
  waiting for transfers between devices: 233 us -> 124 us
  blocking collectives: 84.4 us -> 0 us
  starting transfers between devices: 0.21 us -> 29.1 us
  between operations: 14.1 us -> 1.14 us
    psum x3 -> x0, waiting for transfers between devices: 164 us -> none  [on_device(): lax.psum(partial_sum.astype(jnp.bfloat16), 'col').astype(jnp.float32)]
    ppermute x0 -> x32, waiting for transfers between devices: none -> 124 us  [the longest x25 97.2 us: swap(): return lax.ppermute(x, 'col', [(i, i ^ offset) for i in range(cols)])]
    all_gather x7 -> x0, blocking collectives: 84.4 us -> none  [the longest x2 28.5 us: on_device(): everyone = lax.all_gather(downward[None], 'lvl', axis=0, tiled=True)]
    reduce_scatter x2 -> x0, waiting for transfers between devices: 68.8 us -> none  [on_device(): lax.psum_scatter(partial_adj.astype(jnp.bfloat16), 'col', scatter_dimensi...]
    ppermute x0 -> x32, starting transfers between devices: none -> 29.1 us  [the longest x25 20.2 us: swap(): return lax.ppermute(x, 'col', [(i, i ^ offset) for i in range(cols)])]
    dot_general x11 -> x10, matrix products: 12 us -> 9.83 us  [the longest x3 3.9 us: down_solve(): jnp.einsum('ri,rn->ni', inverse, residual.astype(BF16), preferred_element...]
  transfers between devices with their start and end apart: 5 -> 32, of which waited for: 5 -> 22; matrix products, arithmetic and copies ran while one was open for 0% -> 2% of each run, Pallas kernels for 0% -> 0%
where the time goes in v1:
time: 171 us
  waiting for transfers between devices  124 us (73%)
  starting transfers between devices  29.1 us (17%)
  matrix products  9.83 us (6%)
  other arithmetic  5.28 us (3%)
    ppermute x25, waiting for transfers between devices, swap(): return lax.ppermute(x, 'col', [(i, i ^ offset) for i in range(cols)])  97.2 us
    ppermute x7, waiting for transfers between devices, along(): return lax.ppermute(x, 'lvl', pairs)  26.4 us
    ppermute x25, starting transfers between devices, swap(): return lax.ppermute(x, 'col', [(i, i ^ offset) for i in range(cols)])  20.2 us
    ppermute x7, starting transfers between devices, along(): return lax.ppermute(x, 'lvl', pairs)  8.9 us
    dot_general x3, matrix products, down_solve(): jnp.einsum('ri,rn->ni', inverse, residual.astype(BF16), preferred_element...  3.9 us
  transfers between devices with their start and end apart: 32, of which 22 were waited for; matrix products, arithmetic and copies ran while one was open for 2% of the time, Pallas kernels for 0%

profile of v1, /device:TPU:0, one launch (start us, length us, event | category | flops | bytes accessed | tf_op | source)
XLA Modules:
  0.0 170.5 jit_solution(16180201663209595591)
XLA Ops:
  0.6 1.6 convolution_convert_fusion.4
  2.4 0.5 collective-permute-start.1
  3.0 1.3 collective-permute-done.1
  4.3 0.2 add_convert_fusion.9
  4.5 3.9 %collective-permute-start.4 = (bf16[64,1536]{0,1:T(8,128)(2,1)S(1)}, bf16[64,1536]{0,1:T(8,128)(2,1)S(1)}, u32[]{:S(2)}, u32[]{:S(2)}) collective-permute-start(bf16[64,1536]{0,1:T(8,128)(2,1)S(1)} %add_convert_fusion.9), channel_id=1, source_target_pairs={{0,6},{1,7},{2,4},{3,5},{4,2},{5,3},{6,0},{7,1},{8,14},{9,15},{10,... | collective-permute-start | bytes 589832 | tf_op jit(solution)/shard_map/ppermute | solution.py:59
  8.4 0.5 collective-permute-start.3
  9.1 9.3 %collective-permute-done.4 = bf16[64,1536]{0,1:T(8,128)(2,1)S(1)} collective-permute-done((bf16[64,1536]{0,1:T(8,128)(2,1)S(1)}, bf16[64,1536]{0,1:T(8,128)(2,1)S(1)}, u32[]{:S(2)}, u32[]{:S(2)}) %collective-permute-start.4) | collective-permute-done | bytes 196640 | tf_op jit(solution)/shard_map/ppermute | solution.py:59
  18.3 7.9 %collective-permute-done.3 = bf16[64,1536]{0,1:T(8,128)(2,1)S(1)} collective-permute-done((bf16[64,1536]{0,1:T(8,128)(2,1)S(1)}, bf16[64,1536]{0,1:T(8,128)(2,1)S(1)}, u32[]{:S(2)}, u32[]{:S(2)}) %collective-permute-start.3) | collective-permute-done | bytes 196640 | tf_op jit(solution)/shard_map/ppermute | solution.py:59
  26.2 0.3 collective-permute-done.2
  26.5 0.2 add_convert_fusion.8
  26.8 2.0 %fusion = bf16[2,192,1536]{2,1,0:T(8,128)(2,1)S(1)} fusion(bf16[1,2,192,1536]{3,2,1,0:T(8,128)(2,1)} %param.5, s32[1536]{0:T(1024)S(1)} %add_select_fusion, s32[192]{0:T(256)S(1)} %and_select_fusion, bf16[2,12,12]{2,0,1:T(2,128)(2,1)S(1)} %convert_bitcast_fusion.2), kind=kOutput, calls=%fused_computation.1 | convolution fusion | flops 17240832 | bytes 2366784 | tf_op jit(solution)/shard_map/krc,cn->krn/dot_general | solution.py:42
  29.0 0.6 convolution_convert_fusion.5
  29.5 0.7 collective-permute-start.7
  30.2 4.1 %collective-permute-start.6 = (bf16[2,192,128]{2,1,0:T(8,128)(2,1)S(1)}, bf16[2,192,128]{2,1,0:T(8,128)(2,1)S(1)}, u32[]{:S(2)}, u32[]{:S(2)}) collective-permute-start(bf16[2,192,128]{2,1,0:T(8,128)(2,1)S(1)} %convolution_convert_fusion.5), channel_id=1, source_target_pairs={{0,8},{1,9},{2,10},{3,11},{4,12},{5,13},{6,14},{7,15}} | collective-permute-start | bytes 294920 | tf_op jit(solution)/shard_map/ppermute | solution.py:62
  34.3 2.7 %collective-permute-done.6 = bf16[2,192,128]{2,1,0:T(8,128)(2,1)S(1)} collective-permute-done((bf16[2,192,128]{2,1,0:T(8,128)(2,1)S(1)}, bf16[2,192,128]{2,1,0:T(8,128)(2,1)S(1)}, u32[]{:S(2)}, u32[]{:S(2)}) %collective-permute-start.6) | collective-permute-done | bytes 98336 | tf_op jit(solution)/shard_map/ppermute | solution.py:62
  37.1 0.5 convolution_convert_fusion.3
  37.8 1.7 %collective-permute-done.8 = bf16[64,1536]{0,1:T(8,128)(2,1)S(1)} collective-permute-done((bf16[64,1536]{0,1:T(8,128)(2,1)S(1)}, bf16[64,1536]{0,1:T(8,128)(2,1)S(1)}, u32[]{:S(2)}, u32[]{:S(2)}) %collective-permute-start.8) | collective-permute-done | bytes 196640 | tf_op jit(solution)/shard_map/ppermute | solution.py:59
  39.5 0.2 add_convert_fusion.7
  39.7 1.7 %collective-permute-start.11 = (bf16[64,1536]{0,1:T(8,128)(2,1)S(1)}, bf16[64,1536]{0,1:T(8,128)(2,1)S(1)}, u32[]{:S(2)}, u32[]{:S(2)}) collective-permute-start(bf16[64,1536]{0,1:T(8,128)(2,1)S(1)} %add_convert_fusion.7), channel_id=1, source_target_pairs={{0,6},{1,7},{2,4},{3,5},{4,2},{5,3},{6,0},{7,1},{8,14},{9,15},{10,... | collective-permute-start | bytes 589832 | tf_op jit(solution)/shard_map/ppermute | solution.py:59
  41.4 1.3 collective-permute-start.10
  42.8 0.5 collective-permute-start.9
  43.3 9.4 %collective-permute-done.11 = bf16[64,1536]{0,1:T(8,128)(2,1)S(1)} collective-permute-done((bf16[64,1536]{0,1:T(8,128)(2,1)S(1)}, bf16[64,1536]{0,1:T(8,128)(2,1)S(1)}, u32[]{:S(2)}, u32[]{:S(2)}) %collective-permute-start.11) | collective-permute-done | bytes 196640 | tf_op jit(solution)/shard_map/ppermute | solution.py:59
  52.7 7.6 %collective-permute-done.10 = bf16[64,1536]{0,1:T(8,128)(2,1)S(1)} collective-permute-done((bf16[64,1536]{0,1:T(8,128)(2,1)S(1)}, bf16[64,1536]{0,1:T(8,128)(2,1)S(1)}, u32[]{:S(2)}, u32[]{:S(2)}) %collective-permute-start.10) | collective-permute-done | bytes 196640 | tf_op jit(solution)/shard_map/ppermute | solution.py:59
  60.6 0.7 collective-permute-start.13
  61.3 0.7 collective-permute-start
  62.0 0.3 collective-permute-done.12
  62.4 0.6 copy-done.10
  63.2 1.9 %convolution_convert_fusion.2 = bf16[128,1536]{0,1:T(8,128)(2,1)S(1)} fusion(bf16[192,1536]{1,0:T(8,128)(2,1)} %copy-done.7, f32[192,128]{1,0:T(8,128)} %copy-done.10, bf16[2,192,1536]{2,1,0:T(8,128)(2,1)S(1)} %fusion, f32[2,192,128]{2,1,0:T(8,128)S(1)} %convert_add_fusion, bf16[64,1536]{0,1:T(8,128)(2,1)S(1)} %get-tuple-element.11, ...), kind=kOutput, calls=%fused_computation.5 | convolution fusion | flops 152051712 | bytes 2555904 | tf_op jit(solution)/shard_map/ri,rn->ni/dot_general | solution.py:87
  65.3 0.2 collective-permute-start.14
  65.5 1.6 collective-permute-done.14
  67.1 0.2 add_convert_fusion.5
  67.3 1.7 %collective-permute-start.17 = (bf16[64,1536]{0,1:T(8,128)(2,1)S(1)}, bf16[64,1536]{0,1:T(8,128)(2,1)S(1)}, u32[]{:S(2)}, u32[]{:S(2)}) collective-permute-start(bf16[64,1536]{0,1:T(8,128)(2,1)S(1)} %add_convert_fusion.5), channel_id=1, source_target_pairs={{0,6},{1,7},{2,4},{3,5},{4,2},{5,3},{6,0},{7,1},{8,14},{9,15},{10,... | collective-permute-start | bytes 589832 | tf_op jit(solution)/shard_map/ppermute | solution.py:59
  69.0 1.3 collective-permute-start.16
  70.3 0.5 collective-permute-start.15
  70.8 9.4 %collective-permute-done.17 = bf16[64,1536]{0,1:T(8,128)(2,1)S(1)} collective-permute-done((bf16[64,1536]{0,1:T(8,128)(2,1)S(1)}, bf16[64,1536]{0,1:T(8,128)(2,1)S(1)}, u32[]{:S(2)}, u32[]{:S(2)}) %collective-permute-start.17) | collective-permute-done | bytes 196640 | tf_op jit(solution)/shard_map/ppermute | solution.py:59
  80.3 7.6 %collective-permute-done.16 = bf16[64,1536]{0,1:T(8,128)(2,1)S(1)} collective-permute-done((bf16[64,1536]{0,1:T(8,128)(2,1)S(1)}, bf16[64,1536]{0,1:T(8,128)(2,1)S(1)}, u32[]{:S(2)}, u32[]{:S(2)}) %collective-permute-start.16) | collective-permute-done | bytes 196640 | tf_op jit(solution)/shard_map/ppermute | solution.py:59
  88.2 1.7 %collective-permute-done.18 = bf16[64,1536]{0,1:T(8,128)(2,1)S(1)} collective-permute-done((bf16[64,1536]{0,1:T(8,128)(2,1)S(1)}, bf16[64,1536]{0,1:T(8,128)(2,1)S(1)}, u32[]{:S(2)}, u32[]{:S(2)}) %collective-permute-start.18) | collective-permute-done | bytes 196640 | tf_op jit(solution)/shard_map/ppermute | solution.py:59
  90.0 0.7 copy-done.5
  90.7 0.4 fusion.9
  91.1 0.5 convolution_convert_fusion.1
  92.0 1.6 collective-permute-done.20
  93.6 0.2 add_convert_fusion.3
  93.8 1.7 collective-permute-start.23
  95.5 1.3 collective-permute-start.22
  96.8 0.5 collective-permute-start.21
  97.3 9.4 %collective-permute-done.23 = bf16[64,1536]{0,1:T(8,128)(2,1)S(1)} collective-permute-done((bf16[64,1536]{0,1:T(8,128)(2,1)S(1)}, bf16[64,1536]{0,1:T(8,128)(2,1)S(1)}, u32[]{:S(2)}, u32[]{:S(2)}) %collective-permute-start.23) | collective-permute-done | bytes 196640 | tf_op jit(solution)/shard_map/ppermute | solution.py:59
  106.8 7.6 %collective-permute-done.22 = bf16[64,1536]{0,1:T(8,128)(2,1)S(1)} collective-permute-done((bf16[64,1536]{0,1:T(8,128)(2,1)S(1)}, bf16[64,1536]{0,1:T(8,128)(2,1)S(1)}, u32[]{:S(2)}, u32[]{:S(2)}) %collective-permute-start.22) | collective-permute-done | bytes 196640 | tf_op jit(solution)/shard_map/ppermute | solution.py:59
  114.6 1.7 collective-permute-done.24
  116.4 0.6 fusion.8
  117.1 1.3 collective-permute-start.25
  118.4 0.7 collective-permute-start.26
  119.0 23.7 %collective-permute-done.25 = bf16[2,192,128]{2,1,0:T(8,128)(2,1)S(1)} collective-permute-done((bf16[2,192,128]{2,1,0:T(8,128)(2,1)S(1)}, bf16[2,192,128]{2,1,0:T(8,128)(2,1)S(1)}, u32[]{:S(2)}, u32[]{:S(2)}) %collective-permute-start.25) | collective-permute-done | bytes 98336 | tf_op jit(solution)/shard_map/ppermute | solution.py:62
  142.7 0.6 fusion.1
  143.6 1.8 %collective-permute-done.27 = bf16[64,1536]{0,1:T(8,128)(2,1)} collective-permute-done((bf16[64,1536]{0,1:T(8,128)(2,1)S(1)}, bf16[64,1536]{0,1:T(8,128)(2,1)}, u32[]{:S(2)}, u32[]{:S(2)}) %collective-permute-start.27) | collective-permute-done | bytes 196640 | tf_op jit(solution)/shard_map/ppermute | solution.py:59
  145.4 1.2 add_convert_fusion.1
  146.7 1.7 collective-permute-start.30
  148.4 1.3 collective-permute-start.29
  149.7 0.5 collective-permute-start.28
  150.4 0.8 collective-permute-start.19
  151.2 8.5 %collective-permute-done.30 = bf16[64,1536]{0,1:T(8,128)(2,1)S(1)} collective-permute-done((bf16[64,1536]{0,1:T(8,128)(2,1)S(1)}, bf16[64,1536]{0,1:T(8,128)(2,1)S(1)}, u32[]{:S(2)}, u32[]{:S(2)}) %collective-permute-start.30) | collective-permute-done | bytes 196640 | tf_op jit(solution)/shard_map/ppermute | solution.py:59
  159.6 7.6 %collective-permute-done.29 = bf16[64,1536]{0,1:T(8,128)(2,1)S(1)} collective-permute-done((bf16[64,1536]{0,1:T(8,128)(2,1)S(1)}, bf16[64,1536]{0,1:T(8,128)(2,1)S(1)}, u32[]{:S(2)}, u32[]{:S(2)}) %collective-permute-start.29) | collective-permute-done | bytes 196640 | tf_op jit(solution)/shard_map/ppermute | solution.py:59
  167.5 0.8 fusion.23
  168.3 0.9 collective-permute-done.31
  169.3 1.3 fusion.21
  (64 shorter events, 3.3 us)
Async XLA Ops:
  2.2 6.8 %copy-start.11 = (s32[1,2,12,12]{3,1,2,0:T(2,128)S(1)}, s32[1,2,12,12]{3,1,2,0:T(2,128)}, u32[]{:S(2)}) copy-start(s32[1,2,12,12]{3,1,2,0:T(2,128)} %param.7) | copy-start | bytes 3460
  2.4 1.9 %collective-permute-start.1 = (bf16[64,1536]{0,1:T(8,128)(2,1)S(1)}, bf16[64,1536]{0,1:T(8,128)(2,1)S(1)}, u32[]{:S(2)}, u32[]{:S(2)}) collective-permute-start(bf16[64,1536]{0,1:T(8,128)(2,1)S(1)} %broadcast_select_fusion.14), channel_id=1, source_target_pairs={{0,1},{1,0},{2,3},{3,2},{4,5},{5,4},{6,7},{7,6},{8,9},{9,8},{10,11... | collective-permute-start | bytes 589832 | tf_op jit(solution)/shard_map/ppermute | solution.py:59
  4.5 13.8 %collective-permute-start.4 = (bf16[64,1536]{0,1:T(8,128)(2,1)S(1)}, bf16[64,1536]{0,1:T(8,128)(2,1)S(1)}, u32[]{:S(2)}, u32[]{:S(2)}) collective-permute-start(bf16[64,1536]{0,1:T(8,128)(2,1)S(1)} %add_convert_fusion.9), channel_id=1, source_target_pairs={{0,6},{1,7},{2,4},{3,5},{4,2},{5,3},{6,0},{7,1},{8,14},{9,15},{10,... | collective-permute-start | bytes 589832 | tf_op jit(solution)/shard_map/ppermute | solution.py:59
  8.4 17.8 %collective-permute-start.3 = (bf16[64,1536]{0,1:T(8,128)(2,1)S(1)}, bf16[64,1536]{0,1:T(8,128)(2,1)S(1)}, u32[]{:S(2)}, u32[]{:S(2)}) collective-permute-start(bf16[64,1536]{0,1:T(8,128)(2,1)S(1)} %add_convert_fusion.9), channel_id=1, source_target_pairs={{0,4},{1,5},{2,6},{3,7},{4,0},{5,1},{6,2},{7,3},{8,12},{9,13},{10,... | collective-permute-start | bytes 589832 | tf_op jit(solution)/shard_map/ppermute | solution.py:59
  8.9 17.6 %collective-permute-start.2 = (bf16[64,1536]{0,1:T(8,128)(2,1)S(1)}, bf16[64,1536]{0,1:T(8,128)(2,1)S(1)}, u32[]{:S(2)}, u32[]{:S(2)}) collective-permute-start(bf16[64,1536]{0,1:T(8,128)(2,1)S(1)} %add_convert_fusion.9), channel_id=1, source_target_pairs={{0,2},{1,3},{2,0},{3,1},{4,6},{5,7},{6,4},{7,5},{8,10},{9,11},{10,... | collective-permute-start | bytes 589832 | tf_op jit(solution)/shard_map/ppermute | solution.py:59
  26.7 2.1 %collective-permute-start.5 = (bf16[64,1536]{0,1:T(8,128)(2,1)S(1)}, bf16[64,1536]{0,1:T(8,128)(2,1)S(1)}, u32[]{:S(2)}, u32[]{:S(2)}) collective-permute-start(bf16[64,1536]{0,1:T(8,128)(2,1)S(1)} %add_convert_fusion.8), channel_id=1, source_target_pairs={{0,1},{1,0},{2,3},{3,2},{4,5},{5,4},{6,7},{7,6},{8,9},{9,8},{10,11... | collective-permute-start | bytes 589832 | tf_op jit(solution)/shard_map/ppermute | solution.py:59
  28.9 8.1 %copy-start.1 = (bf16[64,1536]{0,1:T(8,128)(2,1)}, bf16[64,1536]{0,1:T(8,128)(2,1)S(1)}, u32[]{:S(2)}) copy-start(bf16[64,1536]{0,1:T(8,128)(2,1)S(1)} %get-tuple-element.13) | copy-start | bytes 589828
  28.9 8.1 %copy-start = (bf16[1,192,1536]{2,1,0:T(8,128)(2,1)S(1)}, bf16[1,192,1536]{2,1,0:T(8,128)(2,1)}, u32[]{:S(2)}) copy-start(bf16[1,192,1536]{2,1,0:T(8,128)(2,1)} %param.6) | copy-start | bytes 1769476
  29.0 8.1 %copy-start.9 = (f32[1,192,128]{2,1,0:T(8,128)S(1)}, f32[1,192,128]{2,1,0:T(8,128)}, u32[]{:S(2)}) copy-start(f32[1,192,128]{2,1,0:T(8,128)} %param.4) | copy-start | bytes 294916
  29.5 4.8 %collective-permute-start.7 = (bf16[2,192,128]{2,1,0:T(8,128)(2,1)S(1)}, bf16[2,192,128]{2,1,0:T(8,128)(2,1)S(1)}, u32[]{:S(2)}, u32[]{:S(2)}) collective-permute-start(bf16[2,192,128]{2,1,0:T(8,128)(2,1)S(1)} %convolution_convert_fusion.5), channel_id=1, source_target_pairs={{16,8},{17,9},{18,10},{19,11},{20,12},{21,13},{22,14},{23,15}} | collective-permute-start | bytes 294920 | tf_op jit(solution)/shard_map/ppermute | solution.py:62
  30.2 6.8 %collective-permute-start.6 = (bf16[2,192,128]{2,1,0:T(8,128)(2,1)S(1)}, bf16[2,192,128]{2,1,0:T(8,128)(2,1)S(1)}, u32[]{:S(2)}, u32[]{:S(2)}) collective-permute-start(bf16[2,192,128]{2,1,0:T(8,128)(2,1)S(1)} %convolution_convert_fusion.5), channel_id=1, source_target_pairs={{0,8},{1,9},{2,10},{3,11},{4,12},{5,13},{6,14},{7,15}} | collective-permute-start | bytes 294920 | tf_op jit(solution)/shard_map/ppermute | solution.py:62
  37.7 1.8 %collective-permute-start.8 = (bf16[64,1536]{0,1:T(8,128)(2,1)S(1)}, bf16[64,1536]{0,1:T(8,128)(2,1)S(1)}, u32[]{:S(2)}, u32[]{:S(2)}) collective-permute-start(bf16[64,1536]{0,1:T(8,128)(2,1)S(1)} %broadcast_select_fusion.11), channel_id=1, source_target_pairs={{0,1},{1,0},{2,3},{3,2},{4,5},{5,4},{6,7},{7,6},{8,9},{9,8},{10,11... | collective-permute-start | bytes 589832 | tf_op jit(solution)/shard_map/ppermute | solution.py:59
  39.7 13.0 %collective-permute-start.11 = (bf16[64,1536]{0,1:T(8,128)(2,1)S(1)}, bf16[64,1536]{0,1:T(8,128)(2,1)S(1)}, u32[]{:S(2)}, u32[]{:S(2)}) collective-permute-start(bf16[64,1536]{0,1:T(8,128)(2,1)S(1)} %add_convert_fusion.7), channel_id=1, source_target_pairs={{0,6},{1,7},{2,4},{3,5},{4,2},{5,3},{6,0},{7,1},{8,14},{9,15},{10,... | collective-permute-start | bytes 589832 | tf_op jit(solution)/shard_map/ppermute | solution.py:59
  41.4 18.8 %collective-permute-start.10 = (bf16[64,1536]{0,1:T(8,128)(2,1)S(1)}, bf16[64,1536]{0,1:T(8,128)(2,1)S(1)}, u32[]{:S(2)}, u32[]{:S(2)}) collective-permute-start(bf16[64,1536]{0,1:T(8,128)(2,1)S(1)} %add_convert_fusion.7), channel_id=1, source_target_pairs={{0,4},{1,5},{2,6},{3,7},{4,0},{5,1},{6,2},{7,3},{8,12},{9,13},{10,... | collective-permute-start | bytes 589832 | tf_op jit(solution)/shard_map/ppermute | solution.py:59
  42.8 17.5 %collective-permute-start.9 = (bf16[64,1536]{0,1:T(8,128)(2,1)S(1)}, bf16[64,1536]{0,1:T(8,128)(2,1)S(1)}, u32[]{:S(2)}, u32[]{:S(2)}) collective-permute-start(bf16[64,1536]{0,1:T(8,128)(2,1)S(1)} %add_convert_fusion.7), channel_id=1, source_target_pairs={{0,2},{1,3},{2,0},{3,1},{4,6},{5,7},{6,4},{7,5},{8,10},{9,11},{10,... | collective-permute-start | bytes 589832 | tf_op jit(solution)/shard_map/ppermute | solution.py:59
  60.5 1.8 %collective-permute-start.12 = (bf16[64,1536]{0,1:T(8,128)(2,1)S(1)}, bf16[64,1536]{0,1:T(8,128)(2,1)S(1)}, u32[]{:S(2)}, u32[]{:S(2)}) collective-permute-start(bf16[64,1536]{0,1:T(8,128)(2,1)S(1)} %add_convert_fusion.6), channel_id=1, source_target_pairs={{0,1},{1,0},{2,3},{3,2},{4,5},{5,4},{6,7},{7,6},{8,9},{9,8},{10,11... | collective-permute-start | bytes 589832 | tf_op jit(solution)/shard_map/ppermute | solution.py:59
  60.6 1.8 %collective-permute-start.13 = (bf16[192,1536]{1,0:T(8,128)(2,1)S(1)}, bf16[192,1536]{1,0:T(8,128)(2,1)S(1)}, u32[]{:S(2)}, u32[]{:S(2)}) collective-permute-start(bf16[192,1536]{1,0:T(8,128)(2,1)S(1)} %bitcast.115), channel_id=1, source_target_pairs={{24,8},{25,9},{26,10},{27,11},{28,12},{29,13},{30,14},{31,15}} | collective-permute-start | bytes 1769480 | tf_op jit(solution)/shard_map/ppermute | solution.py:62
  61.3 1.1 collective-permute-start
  62.4 0.6 copy-start.10
  62.4 0.8 copy-start.7
  65.3 1.8 %collective-permute-start.14 = (bf16[64,1536]{0,1:T(8,128)(2,1)S(1)}, bf16[64,1536]{0,1:T(8,128)(2,1)S(1)}, u32[]{:S(2)}, u32[]{:S(2)}) collective-permute-start(bf16[64,1536]{0,1:T(8,128)(2,1)S(1)} %broadcast_select_fusion.8), channel_id=1, source_target_pairs={{0,1},{1,0},{2,3},{3,2},{4,5},{5,4},{6,7},{7,6},{8,9},{9,8},{10,11... | collective-permute-start | bytes 589832 | tf_op jit(solution)/shard_map/ppermute | solution.py:59
  67.3 13.0 %collective-permute-start.17 = (bf16[64,1536]{0,1:T(8,128)(2,1)S(1)}, bf16[64,1536]{0,1:T(8,128)(2,1)S(1)}, u32[]{:S(2)}, u32[]{:S(2)}) collective-permute-start(bf16[64,1536]{0,1:T(8,128)(2,1)S(1)} %add_convert_fusion.5), channel_id=1, source_target_pairs={{0,6},{1,7},{2,4},{3,5},{4,2},{5,3},{6,0},{7,1},{8,14},{9,15},{10,... | collective-permute-start | bytes 589832 | tf_op jit(solution)/shard_map/ppermute | solution.py:59
  69.0 18.9 %collective-permute-start.16 = (bf16[64,1536]{0,1:T(8,128)(2,1)S(1)}, bf16[64,1536]{0,1:T(8,128)(2,1)S(1)}, u32[]{:S(2)}, u32[]{:S(2)}) collective-permute-start(bf16[64,1536]{0,1:T(8,128)(2,1)S(1)} %add_convert_fusion.5), channel_id=1, source_target_pairs={{0,4},{1,5},{2,6},{3,7},{4,0},{5,1},{6,2},{7,3},{8,12},{9,13},{10,... | collective-permute-start | bytes 589832 | tf_op jit(solution)/shard_map/ppermute | solution.py:59
  70.3 17.6 %collective-permute-start.15 = (bf16[64,1536]{0,1:T(8,128)(2,1)S(1)}, bf16[64,1536]{0,1:T(8,128)(2,1)S(1)}, u32[]{:S(2)}, u32[]{:S(2)}) collective-permute-start(bf16[64,1536]{0,1:T(8,128)(2,1)S(1)} %add_convert_fusion.5), channel_id=1, source_target_pairs={{0,2},{1,3},{2,0},{3,1},{4,6},{5,7},{6,4},{7,5},{8,10},{9,11},{10,... | collective-permute-start | bytes 589832 | tf_op jit(solution)/shard_map/ppermute | solution.py:59
  88.1 2.6 %copy-start.8 = (bf16[192,1536]{1,0:T(8,128)(2,1)S(1)}, bf16[192,1536]{1,0:T(8,128)(2,1)}, u32[]{:S(2)}) copy-start(bf16[192,1536]{1,0:T(8,128)(2,1)} %copy-done.7) | copy-start | bytes 1769476
  88.1 1.8 %collective-permute-start.18 = (bf16[64,1536]{0,1:T(8,128)(2,1)S(1)}, bf16[64,1536]{0,1:T(8,128)(2,1)S(1)}, u32[]{:S(2)}, u32[]{:S(2)}) collective-permute-start(bf16[64,1536]{0,1:T(8,128)(2,1)S(1)} %add_convert_fusion.4), channel_id=1, source_target_pairs={{0,1},{1,0},{2,3},{3,2},{4,5},{5,4},{6,7},{7,6},{8,9},{9,8},{10,11... | collective-permute-start | bytes 589832 | tf_op jit(solution)/shard_map/ppermute | solution.py:59
  90.0 0.7 copy-start.5
  90.0 1.6 copy-start.3
  91.8 1.8 %collective-permute-start.20 = (bf16[64,1536]{0,1:T(8,128)(2,1)S(1)}, bf16[64,1536]{0,1:T(8,128)(2,1)S(1)}, u32[]{:S(2)}, u32[]{:S(2)}) collective-permute-start(bf16[64,1536]{0,1:T(8,128)(2,1)S(1)} %broadcast_select_fusion.5), channel_id=1, source_target_pairs={{0,1},{1,0},{2,3},{3,2},{4,5},{5,4},{6,7},{7,6},{8,9},{9,8},{10,11... | collective-permute-start | bytes 589832 | tf_op jit(solution)/shard_map/ppermute | solution.py:59
  93.8 13.0 %collective-permute-start.23 = (bf16[64,1536]{0,1:T(8,128)(2,1)S(1)}, bf16[64,1536]{0,1:T(8,128)(2,1)S(1)}, u32[]{:S(2)}, u32[]{:S(2)}) collective-permute-start(bf16[64,1536]{0,1:T(8,128)(2,1)S(1)} %add_convert_fusion.3), channel_id=1, source_target_pairs={{0,6},{1,7},{2,4},{3,5},{4,2},{5,3},{6,0},{7,1},{8,14},{9,15},{10,... | collective-permute-start | bytes 589832 | tf_op jit(solution)/shard_map/ppermute | solution.py:59
  95.5 18.8 %collective-permute-start.22 = (bf16[64,1536]{0,1:T(8,128)(2,1)S(1)}, bf16[64,1536]{0,1:T(8,128)(2,1)S(1)}, u32[]{:S(2)}, u32[]{:S(2)}) collective-permute-start(bf16[64,1536]{0,1:T(8,128)(2,1)S(1)} %add_convert_fusion.3), channel_id=1, source_target_pairs={{0,4},{1,5},{2,6},{3,7},{4,0},{5,1},{6,2},{7,3},{8,12},{9,13},{10,... | collective-permute-start | bytes 589832 | tf_op jit(solution)/shard_map/ppermute | solution.py:59
  96.8 17.5 %collective-permute-start.21 = (bf16[64,1536]{0,1:T(8,128)(2,1)S(1)}, bf16[64,1536]{0,1:T(8,128)(2,1)S(1)}, u32[]{:S(2)}, u32[]{:S(2)}) collective-permute-start(bf16[64,1536]{0,1:T(8,128)(2,1)S(1)} %add_convert_fusion.3), channel_id=1, source_target_pairs={{0,2},{1,3},{2,0},{3,1},{4,6},{5,7},{6,4},{7,5},{8,10},{9,11},{10,... | collective-permute-start | bytes 589832 | tf_op jit(solution)/shard_map/ppermute | solution.py:59
  114.6 1.8 %collective-permute-start.24 = (bf16[64,1536]{0,1:T(8,128)(2,1)S(1)}, bf16[64,1536]{0,1:T(8,128)(2,1)S(1)}, u32[]{:S(2)}, u32[]{:S(2)}) collective-permute-start(bf16[64,1536]{0,1:T(8,128)(2,1)S(1)} %add_convert_fusion.2), channel_id=1, source_target_pairs={{0,1},{1,0},{2,3},{3,2},{4,5},{5,4},{6,7},{7,6},{8,9},{9,8},{10,11... | collective-permute-start | bytes 589832 | tf_op jit(solution)/shard_map/ppermute | solution.py:59
  117.1 25.7 %collective-permute-start.25 = (bf16[2,192,128]{2,1,0:T(8,128)(2,1)S(1)}, bf16[2,192,128]{2,1,0:T(8,128)(2,1)S(1)}, u32[]{:S(2)}, u32[]{:S(2)}) collective-permute-start(bf16[2,192,128]{2,1,0:T(8,128)(2,1)S(1)} %pad_maximum_fusion.3), channel_id=1, source_target_pairs={{8,0},{9,1},{10,2},{11,3},{12,4},{13,5},{14,6},{15,7}} | collective-permute-start | bytes 294920 | tf_op jit(solution)/shard_map/ppermute | solution.py:62
  118.4 24.4 %collective-permute-start.26 = (bf16[2,192,128]{2,1,0:T(8,128)(2,1)S(1)}, bf16[2,192,128]{2,1,0:T(8,128)(2,1)S(1)}, u32[]{:S(2)}, u32[]{:S(2)}) collective-permute-start(bf16[2,192,128]{2,1,0:T(8,128)(2,1)S(1)} %pad_maximum_fusion.3), channel_id=1, source_target_pairs={{8,16},{9,17},{10,18},{11,19},{12,20},{13,21},{14,22},{15,23}} | collective-permute-start | bytes 294920 | tf_op jit(solution)/shard_map/ppermute | solution.py:62
  143.3 6.9 %copy-start.4 = (bf16[64,1536]{0,1:T(8,128)(2,1)S(1)}, bf16[64,1536]{0,1:T(8,128)(2,1)}, u32[]{:S(2)}) copy-start(bf16[64,1536]{0,1:T(8,128)(2,1)} %copy-done.3) | copy-start | bytes 589828
  143.3 6.9 %copy-start.6 = (bf16[64,1536]{0,1:T(8,128)(2,1)S(1)}, bf16[64,1536]{0,1:T(8,128)(2,1)}, u32[]{:S(2)}) copy-start(bf16[64,1536]{0,1:T(8,128)(2,1)} %copy-done.5) | copy-start | bytes 589828
  143.5 1.9 %collective-permute-start.27 = (bf16[64,1536]{0,1:T(8,128)(2,1)S(1)}, bf16[64,1536]{0,1:T(8,128)(2,1)}, u32[]{:S(2)}, u32[]{:S(2)}) collective-permute-start(bf16[64,1536]{0,1:T(8,128)(2,1)S(1)} %broadcast_select_fusion.2), channel_id=1, source_target_pairs={{0,1},{1,0},{2,3},{3,2},{4,5},{5,4},{6,7},{7,6},{8,9},{9,8},{10,11... | collective-permute-start | bytes 589832 | tf_op jit(solution)/shard_map/ppermute | solution.py:59
  146.7 13.0 %collective-permute-start.30 = (bf16[64,1536]{0,1:T(8,128)(2,1)S(1)}, bf16[64,1536]{0,1:T(8,128)(2,1)S(1)}, u32[]{:S(2)}, u32[]{:S(2)}) collective-permute-start(bf16[64,1536]{0,1:T(8,128)(2,1)S(1)} %add_convert_fusion.1), channel_id=1, source_target_pairs={{0,6},{1,7},{2,4},{3,5},{4,2},{5,3},{6,0},{7,1},{8,14},{9,15},{10,... | collective-permute-start | bytes 589832 | tf_op jit(solution)/shard_map/ppermute | solution.py:59
  148.4 18.9 %collective-permute-start.29 = (bf16[64,1536]{0,1:T(8,128)(2,1)S(1)}, bf16[64,1536]{0,1:T(8,128)(2,1)S(1)}, u32[]{:S(2)}, u32[]{:S(2)}) collective-permute-start(bf16[64,1536]{0,1:T(8,128)(2,1)S(1)} %add_convert_fusion.1), channel_id=1, source_target_pairs={{0,4},{1,5},{2,6},{3,7},{4,0},{5,1},{6,2},{7,3},{8,12},{9,13},{10,... | collective-permute-start | bytes 589832 | tf_op jit(solution)/shard_map/ppermute | solution.py:59
  149.7 17.5 %collective-permute-start.28 = (bf16[64,1536]{0,1:T(8,128)(2,1)S(1)}, bf16[64,1536]{0,1:T(8,128)(2,1)S(1)}, u32[]{:S(2)}, u32[]{:S(2)}) collective-permute-start(bf16[64,1536]{0,1:T(8,128)(2,1)S(1)} %add_convert_fusion.1), channel_id=1, source_target_pairs={{0,2},{1,3},{2,0},{3,1},{4,6},{5,7},{6,4},{7,5},{8,10},{9,11},{10,... | collective-permute-start | bytes 589832 | tf_op jit(solution)/shard_map/ppermute | solution.py:59
  150.3 17.2 %copy-start.2 = (bf16[64,1536]{0,1:T(8,128)(2,1)S(1)}, bf16[64,1536]{0,1:T(8,128)(2,1)}, u32[]{:S(2)}) copy-start(bf16[64,1536]{0,1:T(8,128)(2,1)} %copy-done.1) | copy-start | bytes 589828
  150.4 17.2 %collective-permute-start.19 = (f32[2,192,128]{2,1,0:T(8,128)S(1)}, f32[2,192,128]{2,1,0:T(8,128)S(1)}, u32[]{:S(2)}, u32[]{:S(2)}) collective-permute-start(f32[2,192,128]{2,1,0:T(8,128)S(1)} %pad_maximum_fusion.2), channel_id=1, source_target_pairs={{8,24},{9,25},{10,26},{11,27},{12,28},{13,29},{14,30},{15,31}} | collective-permute-start | bytes 589832 | tf_op jit(solution)/shard_map/ppermute | solution.py:62
  167.4 1.8 %collective-permute-start.31 = (bf16[64,1536]{0,1:T(8,128)(2,1)S(1)}, bf16[64,1536]{0,1:T(8,128)(2,1)S(1)}, u32[]{:S(2)}, u32[]{:S(2)}) collective-permute-start(bf16[64,1536]{0,1:T(8,128)(2,1)S(1)} %add_convert_fusion), channel_id=1, source_target_pairs={{0,1},{1,0},{2,3},{3,2},{4,5},{5,4},{6,7},{7,6},{8,9},{9,8},{10,11... | collective-permute-start | bytes 589832 | tf_op jit(solution)/shard_map/ppermute | solution.py:59

commit v2 on v1

v2 whole, which is shorter than its diff:
```python
import jax
import jax.numpy as jnp
from jax import lax
from jax.sharding import PartitionSpec as P

F32 = jnp.float32
BF16 = jnp.bfloat16


def trailing_ones(node):
    ones = 0
    while node % 2 == 1:
        ones += 1
        node //= 2
    return ones


def child_links(section, members):
    reach = 2 ** (section - 1)
    parents = [node for node in range(members - 1) if trailing_ones(node) == section]
    return [(node - reach, node) for node in parents], [(node + reach, node) for node in parents]


def expand_pattern(pattern_own, row_start, row_count, full_width):
    tile_count = pattern_own.shape[1]
    tile_size = full_width // tile_count
    row_ids = row_start + lax.iota(jnp.int32, row_count)
    row_pick = (row_ids[:, None] // tile_size == lax.iota(jnp.int32, tile_count)[None, :]).astype(BF16)
    col_pick = (
        lax.iota(jnp.int32, full_width)[None, :] // tile_size == lax.iota(jnp.int32, tile_count)[:, None]
    ).astype(BF16)
    row_mask = jnp.einsum("rb,kbc->krc", row_pick, pattern_own.astype(BF16), preferred_element_type=F32)
    return jnp.einsum("krc,cn->krn", row_mask.astype(BF16), col_pick, preferred_element_type=F32).astype(BF16)


def xor_order(blocks, mask, axis=0):
    count = blocks.shape[axis]
    step = 1
    while step < count:
        flipped = jnp.stack(
            [lax.index_in_dim(blocks, b ^ step, axis, keepdims=False) for b in range(count)], axis=axis
        )
        blocks = jnp.where((mask // step) % 2 == 1, flipped, blocks)
        step *= 2
    return blocks


def on_device(rhs, panel, inverse_t, pattern):
    members = lax.axis_size("lvl")
    cols = lax.axis_size("col")
    levels = members.bit_length() - 1
    root, heir = members - 1, members // 2 - 1
    chips = cols // 2
    lanes = 1 << ((chips.bit_length() - 1) // 2)
    lvl_pos = lax.axis_index("lvl")
    col_pos = lax.axis_index("col")
    core, lane, row = col_pos % 2, col_pos // 2 % lanes, col_pos // (2 * lanes)
    row_count, rhs_count = rhs.shape[1:]
    full_width = inverse_t.shape[2]
    group = rhs_count // (2 * lanes)
    blocks = 2 * lanes
    own_group = core * lanes + lane
    levels_of = [trailing_ones(node) for node in range(members)]
    leaves = [node for node in range(members) if levels_of[node] == 0]
    inner = [node for node in range(members - 1) if levels_of[node] > 0]

    def across(x, offset, planes):
        pairs = [(p * cols + c, p * cols + (c ^ offset)) for p in planes for c in range(cols)]
        return lax.ppermute(x, ("lvl", "col"), pairs)

    def along(x, links, offset=0):
        pairs = [(a * cols + c, b * cols + (c ^ offset)) for a, b in links for c in range(cols)]
        return lax.ppermute(x, ("lvl", "col"), pairs)

    def down(links):
        return [(b, a) for a, b in links]

    def chip_sum(mine):
        total = mine.astype(F32)
        for chip in range(1, chips):
            got = across(mine, 2 * chip, leaves)
            turned = jnp.stack([got[i ^ (chip % lanes)] for i in range(lanes)])
            total = total + turned.astype(F32)
        return total

    def row_sum(partial, planes):
        terms = partial.astype(BF16)
        total = terms.astype(F32)
        for offset in range(2 * lanes, cols, 2 * lanes):
            total = total + across(terms, offset, planes).astype(F32)
        return total

    def spread_rows(matrix, planes):
        lane_parts = [matrix] + [across(matrix, 2 * i, planes) for i in range(1, lanes)]
        return jnp.stack([part for own in lane_parts for part in (own, across(own, 1, planes))])

    def turn_blocks(parts, planes):
        got = [parts[..., 0, :, :]] + [across(parts[..., b, :, :], b, planes) for b in range(1, blocks)]
        return jnp.stack(got, axis=-3)

    def to_blocks(vector):
        by_group = xor_order(vector.T.reshape(blocks, group, row_count), own_group)
        return by_group.reshape(2, lanes, group, row_count).swapaxes(0, 1).reshape(blocks, group, row_count)

    def from_blocks(parts):
        by_group = parts.reshape(lanes, 2, group, row_count).swapaxes(0, 1).reshape(blocks, group, row_count)
        return xor_order(by_group, own_group).reshape(rhs_count, row_count).T

    inverse_own = inverse_t[0]
    factor = panel[0] * expand_pattern(pattern[0], col_pos * row_count, row_count, full_width)

    first = xor_order(rhs[0].T.reshape(blocks, group, row_count), own_group).astype(BF16)
    partial = jnp.einsum("bnr,ri->bni", first, inverse_own, preferred_element_type=F32).astype(BF16)
    got = across(partial[lanes:], 1, leaves)
    chip_part = (partial[:lanes].astype(F32) + got.astype(F32)).astype(BF16)
    leaf_half = chip_sum(chip_part).astype(BF16)
    factor_pair = jnp.stack([factor, across(factor, 1, leaves)], axis=1)
    pushed = jnp.einsum("lni,kjri->kjlnr", leaf_half, factor_pair, preferred_element_type=F32).astype(BF16)

    root_inverse = along(inverse_own, [(root, heir)])
    root_rhs = along(rhs[0], [(root, heir)])
    inner_inverse = spread_rows(inverse_own, inner)
    inner_factor = jnp.stack([spread_rows(factor[k], inner) for k in range(levels - 1)])
    root_spread = spread_rows(root_inverse, [heir])
    inner_rhs = turn_blocks(jnp.stack([to_blocks(rhs[0]), to_blocks(root_rhs)]), inner)

    samples = {}
    for section in range(1, levels):
        left, right = child_links(section, members)
        nodes = [node for node in inner if levels_of[node] == section]
        if section == 1:
            parts = [
                along(pushed[:, :, i], left, 2 * i).astype(F32) + along(pushed[:, :, i], right, 2 * i).astype(F32)
                for i in range(lanes)
            ]
            gathered = jnp.stack(parts, axis=1).reshape(levels, blocks, group, row_count)
        else:
            sent = pushed.astype(BF16)
            gathered = along(sent, left).astype(F32) + along(sent, right).astype(F32)
        residual = (inner_rhs[0] - gathered[0]).astype(BF16)
        samples[section] = row_sum(
            jnp.einsum("bnr,bri->ni", residual, inner_inverse, preferred_element_type=F32), nodes
        )
        pushed = gathered[1:] + jnp.einsum(
            "ni,kbri->kbnr", samples[section].astype(BF16), inner_factor[: levels - section], preferred_element_type=F32
        )
    residual = (inner_rhs[1] - pushed[0]).astype(BF16)
    root_sample = row_sum(jnp.einsum("bnr,bri->ni", residual, root_spread, preferred_element_type=F32), [heir])
    root_answer = jnp.einsum("ni,bri->bnr", root_sample.astype(BF16), root_spread, preferred_element_type=F32)

    answers = {}
    ancestry = root_answer.astype(BF16)[None]
    for section in range(levels - 1, 0, -1):
        nodes = [node for node in inner if levels_of[node] == section]
        if section < levels - 1:
            left, right = child_links(section + 1, members)
            ancestry = along(sent, down(left)) + along(sent, down(right))
        adjoint = row_sum(
            jnp.einsum("kbnr,kbri->ni", ancestry, inner_factor[: levels - section], preferred_element_type=F32), nodes
        )
        back = (samples[section] - adjoint).astype(BF16)
        answers[section] = jnp.einsum("ni,bri->bnr", back, inner_inverse, preferred_element_type=F32)
        sent = jnp.concatenate([answers[section].astype(BF16)[None], ancestry], axis=0)

    left, right = child_links(1, members)
    sent = sent.reshape(levels, lanes, 2, group, row_count)
    ancestry = jnp.stack(
        [along(sent[:, i], down(left), 2 * i) + along(sent[:, i], down(right), 2 * i) for i in range(lanes)], axis=2
    )
    partial = jnp.einsum("kjlnr,kjri->lni", ancestry, factor_pair, preferred_element_type=F32).astype(BF16)
    back = (leaf_half.astype(F32) - chip_sum(partial)).astype(BF16)

    def whole(half):
        both = jnp.concatenate([half, across(half, 1, leaves)], axis=0)
        return xor_order(both, own_group).reshape(rhs_count, full_width)

    leaf_answer = jnp.einsum("ri,ni->rn", inverse_own, whole(back), preferred_element_type=F32)
    leaf_sample = lax.dynamic_slice_in_dim(whole(leaf_half), col_pos * row_count, row_count, 1).T.astype(F32)

    def own_blocks(vector):
        here = lax.dynamic_slice_in_dim(vector, row * blocks * row_count, blocks * row_count, 1)
        return xor_order(here.reshape(group, blocks, row_count).swapaxes(0, 1), lane * 2 + core)

    height = jnp.asarray(levels_of)[lvl_pos]
    inner_sample, inner_answer = samples[1], answers[1]
    for section in range(2, levels):
        inner_sample = jnp.where(height == section, samples[section], inner_sample)
        inner_answer = jnp.where(height == section, answers[section], inner_answer)
    parts = turn_blocks(
        jnp.stack([own_blocks(inner_sample), inner_answer, own_blocks(root_sample), root_answer]), inner
    )
    results = jnp.stack([from_blocks(parts[n]) for n in range(4)])
    root_results = along(results[2:], [(heir, root)])
    at_leaf, at_root = height == 0, lvl_pos == root
    sample = jnp.where(at_leaf, leaf_sample, jnp.where(at_root, root_results[0], results[0]))
    answer = jnp.where(at_leaf, leaf_answer, jnp.where(at_root, root_results[1], results[1]))
    return (sample[None], answer[None])


def solution(mesh):
    in_specs = (
        P("lvl", "col", None),
        P("lvl", None, "col", None),
        P("lvl", "col", None),
        P("lvl", None, None, None),
    )
    out_specs = (P("lvl", "col", None), P("lvl", "col", None))
    return jax.shard_map(
        on_device, mesh=mesh, in_specs=in_specs, out_specs=out_specs, check_vma=False
    )
```

time: 171 us -> 137 us (0.80)
  waiting for transfers between devices: 124 us -> 39.9 us
  starting transfers between devices: 29.1 us -> 60.9 us
  matrix products: 9.83 us -> 18.5 us
  local copies, waits for them, and re-layouts: 1.59 us -> 7.66 us
  between operations: 1.14 us -> 2.86 us
    ppermute x32 -> x39, waiting for transfers between devices: 124 us -> 39.9 us  [the longest x11 26.1 us: along(): return lax.ppermute(x, ('lvl', 'col'), pairs)]
    ppermute x32 -> x39, starting transfers between devices: 29.1 us -> 60.9 us  [the longest x28 47.8 us: across(): return lax.ppermute(x, ('lvl', 'col'), pairs)]
    dot_general x9, matrix products: 7.8 us -> 16.6 us  [the longest x1 3.54 us: on_device(): jnp.einsum('bnr,bri->ni', residual, root_spread, preferred_element_type=F32)]
    convert_element_type x10 -> x5, other arithmetic: 3.2 us -> 0.32 us  [the longest x1 0.13 us: on_device(): back = (leaf_half.astype(F32) - chip_sum(partial)).astype(BF16)]
    slice x0 -> x37, local copies, waits for them, and re-layouts: none -> 1.95 us  [the longest x30 1.76 us: xor_order(): lax.index_in_dim(blocks, b ^ step, axis, keepdims=False)]
    another operation x2 -> x24, other arithmetic: 0.11 us -> 2.02 us  [the longest x2 0.89 us: turn_blocks(): return jnp.stack(got, axis=-3)]
  transfers between devices with their start and end apart: 32 -> 39, of which waited for: 22 -> 9; matrix products, arithmetic and copies ran while one was open for 2% -> 15% of each run, Pallas kernels for 0% -> 0%
where the time goes in v2:
time: 137 us; the launch traced here: 136 us
  starting transfers between devices  60.9 us (44%)
  waiting for transfers between devices  39.9 us (29%)
  matrix products  18.5 us (14%)
  local copies, waits for them, and re-layouts  7.66 us (6%)
  other arithmetic  5.82 us (4%)
  between operations  2.86 us (2%)
    ppermute x28, starting transfers between devices, across(): return lax.ppermute(x, ('lvl', 'col'), pairs)  47.8 us
    ppermute x11, waiting for transfers between devices, along(): return lax.ppermute(x, ('lvl', 'col'), pairs)  26.1 us
    ppermute x28, waiting for transfers between devices, across(): return lax.ppermute(x, ('lvl', 'col'), pairs)  13.8 us
    ppermute x11, starting transfers between devices, along(): return lax.ppermute(x, ('lvl', 'col'), pairs)  13.2 us
    dot_general x1, matrix products, on_device(): jnp.einsum('bnr,bri->ni', residual, root_spread, preferred_element_type=F32)  3.54 us
  transfers between devices with their start and end apart: 39, of which 9 were waited for; matrix products, arithmetic and copies ran while one was open for 15% of the time, Pallas kernels for 0%

profile of v2, /device:TPU:0, one launch (start us, length us, event | category | flops | bytes accessed | tf_op | source)
XLA Modules:
  0.0 135.7 jit_solution(2328101432365888436)
XLA Ops:
  0.6 0.7 collective-permute-start.5
  1.3 0.7 convert_bitcast_fusion
  2.1 2.0 %fusion = bf16[2,192,1536]{2,1,0:T(8,128)(2,1)S(1)} fusion(bf16[1,2,192,1536]{3,2,1,0:T(8,128)(2,1)} %param.6, s32[1536]{0:T(1024)S(1)} %add_select_fusion, bf16[2,12,12]{2,0,1:T(2,128)(2,1)S(1)} %convert_bitcast_fusion, s32[192]{0:T(256)S(1)} %and_select_fusion), kind=kOutput, calls=%fused_computation.1 | convolution fusion | flops 17240832 | bytes 2366784 | tf_op jit(solution)/shard_map/krc,cn->krn/dot_general | solution.py:33
  4.0 2.4 %collective-permute-start.9 = (bf16[2,192,1536]{2,1,0:T(8,128)(2,1)S(1)}, bf16[2,192,1536]{2,1,0:T(8,128)(2,1)}, u32[]{:S(2)}, u32[]{:S(2)}) collective-permute-start(bf16[2,192,1536]{2,1,0:T(8,128)(2,1)S(1)} %fusion), channel_id=1, source_target_pairs={{0,1},{1,0},{2,3},{3,2},{4,5},{5,4},{6,7},{7,6},{16,17},{17,16},{1... | collective-permute-start | bytes 3538952 | tf_op jit(solution)/shard_map/ppermute | solution.py:69
  9.0 2.0 %collective-permute-start = (bf16[2,32,1536]{2,1,0:T(8,128)(2,1)S(1)}, bf16[2,32,1536]{2,1,0:T(8,128)(2,1)S(1)}, u32[]{:S(2)}, u32[]{:S(2)}) collective-permute-start(bf16[2,32,1536]{2,1,0:T(8,128)(2,1)S(1)} %slice.474), channel_id=1, source_target_pairs={{0,1},{1,0},{2,3},{3,2},{4,5},{5,4},{6,7},{7,6},{16,17},{17,16},{1... | collective-permute-start | bytes 589832 | tf_op jit(solution)/shard_map/ppermute | solution.py:69
  11.1 0.7 fusion.60
  12.4 0.7 collective-permute-start.7
  13.1 1.3 collective-permute-start.8
  14.4 5.8 %collective-permute-start.3 = (bf16[2,32,1536]{2,1,0:T(8,128)(2,1)S(1)}, bf16[2,32,1536]{2,1,0:T(8,128)(2,1)S(1)}, u32[]{:S(2)}, u32[]{:S(2)}) collective-permute-start(bf16[2,32,1536]{2,1,0:T(8,128)(2,1)S(1)} %add_convert_fusion.1), channel_id=1, source_target_pairs={{0,6},{1,7},{2,4},{3,5},{4,2},{5,3},{6,0},{7,1},{16,22},{17,23},{1... | collective-permute-start | bytes 589832 | tf_op jit(solution)/shard_map/ppermute | solution.py:69
  21.7 0.7 collective-permute-start.15
  22.4 0.7 collective-permute-start.14
  23.1 1.5 %collective-permute-start.18 = (bf16[192,1536]{1,0:T(8,128)(2,1)S(1)}, bf16[192,1536]{1,0:T(8,128)(2,1)}, u32[]{:S(2)}, u32[]{:S(2)}) collective-permute-start(bf16[192,1536]{1,0:T(8,128)(2,1)S(1)} %bitcast.326), channel_id=1, source_target_pairs={{24,8},{25,9},{26,10},{27,11},{28,12},{29,13},{30,14},{31,15}} | collective-permute-start | bytes 1769480 | tf_op jit(solution)/shard_map/ppermute | solution.py:73
  24.6 0.9 pad_maximum_fusion.14
  25.5 3.4 %collective-permute-start.1 = (bf16[2,32,1536]{2,1,0:T(8,128)(2,1)S(1)}, bf16[2,32,1536]{2,1,0:T(8,128)(2,1)S(1)}, u32[]{:S(2)}, u32[]{:S(2)}) collective-permute-start(bf16[2,32,1536]{2,1,0:T(8,128)(2,1)S(1)} %add_convert_fusion.1), channel_id=1, source_target_pairs={{0,2},{1,3},{2,0},{3,1},{4,6},{5,7},{6,4},{7,5},{16,18},{17,19},{1... | collective-permute-start | bytes 589832 | tf_op jit(solution)/shard_map/ppermute | solution.py:69
  28.9 5.0 %collective-permute-done.1 = bf16[2,32,1536]{2,1,0:T(8,128)(2,1)S(1)} collective-permute-done((bf16[2,32,1536]{2,1,0:T(8,128)(2,1)S(1)}, bf16[2,32,1536]{2,1,0:T(8,128)(2,1)S(1)}, u32[]{:S(2)}, u32[]{:S(2)}) %collective-permute-start.1) | collective-permute-done | bytes 196640 | tf_op jit(solution)/shard_map/ppermute | solution.py:69
  33.9 2.8 %collective-permute-start.2 = (bf16[2,32,1536]{2,1,0:T(8,128)(2,1)S(1)}, bf16[2,32,1536]{2,1,0:T(8,128)(2,1)S(1)}, u32[]{:S(2)}, u32[]{:S(2)}) collective-permute-start(bf16[2,32,1536]{2,1,0:T(8,128)(2,1)S(1)} %add_convert_fusion.1), channel_id=1, source_target_pairs={{0,4},{1,5},{2,6},{3,7},{4,0},{5,1},{6,2},{7,3},{16,20},{17,21},{1... | collective-permute-start | bytes 589832 | tf_op jit(solution)/shard_map/ppermute | solution.py:69
  36.8 4.7 %collective-permute-done.2 = bf16[2,32,1536]{2,1,0:T(8,128)(2,1)S(1)} collective-permute-done((bf16[2,32,1536]{2,1,0:T(8,128)(2,1)S(1)}, bf16[2,32,1536]{2,1,0:T(8,128)(2,1)S(1)}, u32[]{:S(2)}, u32[]{:S(2)}) %collective-permute-start.2) | collective-permute-done | bytes 196640 | tf_op jit(solution)/shard_map/ppermute | solution.py:69
  41.6 1.9 %collective-permute-start.4 = (bf16[2,32,1536]{2,1,0:T(8,128)(2,1)S(1)}, bf16[2,32,1536]{2,1,0:T(8,128)(2,1)S(1)}, u32[]{:S(2)}, u32[]{:S(2)}) collective-permute-start(bf16[2,32,1536]{2,1,0:T(8,128)(2,1)S(1)} %add_convert_fusion), channel_id=1, source_target_pairs={{0,1},{1,0},{2,3},{3,2},{4,5},{5,4},{6,7},{7,6},{16,17},{17,16},{1... | collective-permute-start | bytes 589832 | tf_op jit(solution)/shard_map/ppermute | solution.py:69
  43.6 1.4 %collective-permute-done.4 = bf16[2,32,1536]{2,1,0:T(8,128)(2,1)S(1)} collective-permute-done((bf16[2,32,1536]{2,1,0:T(8,128)(2,1)S(1)}, bf16[2,32,1536]{2,1,0:T(8,128)(2,1)S(1)}, u32[]{:S(2)}, u32[]{:S(2)}) %collective-permute-start.4) | collective-permute-done | bytes 196640 | tf_op jit(solution)/shard_map/ppermute | solution.py:69
  45.1 2.1 %fusion.18 = bf16[2,2,2,32,192]{4,3,2,1,0:T(8,128)(2,1)S(1)} fusion(bf16[2,32,1536]{2,1,0:T(8,128)(2,1)S(1)} %add_convert_fusion, bf16[2,1,192,1536]{3,2,0,1:T(8,128)(2,1)} %bitcast.48, bf16[2,1,192,1536]{3,2,0,1:T(8,128)(2,1)S(1)} %bitcast.320), kind=kOutput, calls=%fused_computation.21 | convolution fusion | flops 152223744 | bytes 2654208 | tf_op jit(solution)/shard_map/lni,kjri->kjlnr/dot_general | solution.py:118
  47.2 1.3 collective-permute-start.12
  48.5 0.7 collective-permute-start.13
  49.3 1.5 %collective-permute-start.23 = (bf16[192,1536]{1,0:T(8,128)(2,1)S(1)}, bf16[192,1536]{1,0:T(8,128)(2,1)}, u32[]{:S(2)}, u32[]{:S(2)}) collective-permute-start(bf16[192,1536]{1,0:T(8,128)(2,1)S(1)} %get-tuple-element.3), channel_id=1, source_target_pairs={{8,10},{9,11},{10,8},{11,9},{12,14},{13,15},{14,12},{15,13}} | collective-permute-start | bytes 1769480 | tf_op jit(solution)/shard_map/ppermute | solution.py:69
  50.8 0.7 collective-permute-start.16
  51.5 3.8 %collective-permute-start.10 = (bf16[2,2,32,192]{3,2,1,0:T(8,128)(2,1)S(1)}, bf16[2,2,32,192]{3,2,1,0:T(8,128)(2,1)S(1)}, u32[]{:S(2)}, u32[]{:S(2)}) collective-permute-start(bf16[2,2,32,192]{3,2,1,0:T(8,128)(2,1)S(1)} %get-tuple-element.88), channel_id=1, source_target_pairs={{0,8},{1,9},{2,10},{3,11},{4,12},{5,13},{6,14},{7,15}} | collective-permute-start | bytes 147464 | tf_op jit(solution)/shard_map/ppermute | solution.py:73
  55.3 0.7 collective-permute-start.11
  56.0 1.2 collective-permute-done.10
  57.2 1.5 %collective-permute-start.22 = (bf16[192,1536]{1,0:T(8,128)(2,1)S(1)}, bf16[192,1536]{1,0:T(8,128)(2,1)}, u32[]{:S(2)}, u32[]{:S(2)}) collective-permute-start(bf16[192,1536]{1,0:T(8,128)(2,1)S(1)} %get-tuple-element.3), channel_id=1, source_target_pairs={{8,9},{9,8},{10,11},{11,10},{12,13},{13,12},{14,15},{15,14}} | collective-permute-start | bytes 1769480 | tf_op jit(solution)/shard_map/ppermute | solution.py:69
  58.6 1.5 %collective-permute-start.20 = (bf16[192,1536]{1,0:T(8,128)(2,1)}, bf16[192,1536]{1,0:T(8,128)(2,1)}, u32[]{:S(2)}, u32[]{:S(2)}) collective-permute-start(bf16[192,1536]{1,0:T(8,128)(2,1)} %collective-permute-done.18), channel_id=1, source_target_pairs={{8,10},{9,11},{10,8},{11,9},{12,14},{13,15},{14,12},{15,13}} | collective-permute-start | bytes 1769480 | tf_op jit(solution)/shard_map/ppermute | solution.py:69
  60.1 0.7 fusion.30
  60.9 1.5 %collective-permute-start.19 = (bf16[192,1536]{1,0:T(8,128)(2,1)}, bf16[192,1536]{1,0:T(8,128)(2,1)}, u32[]{:S(2)}, u32[]{:S(2)}) collective-permute-start(bf16[192,1536]{1,0:T(8,128)(2,1)} %collective-permute-done.18), channel_id=1, source_target_pairs={{8,9},{9,8},{10,11},{11,10},{12,13},{13,12},{14,15},{15,14}} | collective-permute-start | bytes 1769480 | tf_op jit(solution)/shard_map/ppermute | solution.py:69
  62.3 1.5 %collective-permute-start.24 = (bf16[192,1536]{1,0:T(8,128)(2,1)}, bf16[192,1536]{1,0:T(8,128)(2,1)}, u32[]{:S(2)}, u32[]{:S(2)}) collective-permute-start(bf16[192,1536]{1,0:T(8,128)(2,1)} %collective-permute-done.23), channel_id=1, source_target_pairs={{8,9},{9,8},{10,11},{11,10},{12,13},{13,12},{14,15},{15,14}} | collective-permute-start | bytes 1769480 | tf_op jit(solution)/shard_map/ppermute | solution.py:69
  63.8 1.2 fusion.11
  65.0 1.4 %collective-permute-start.17 = (bf16[32,1536]{1,0:T(8,128)(2,1)}, bf16[32,1536]{1,0:T(8,128)(2,1)}, u32[]{:S(2)}, u32[]{:S(2)}) collective-permute-start(bf16[32,1536]{1,0:T(8,128)(2,1)} %fusion.11), channel_id=1, source_target_pairs={{8,12},{9,13},{10,14},{11,15},{12,8},{13,9},{14,10},{15,11}} | collective-permute-start | bytes 294920 | tf_op jit(solution)/shard_map/ppermute | solution.py:69
  66.6 0.7 copy.151
  67.3 1.5 %collective-permute-start.21 = (bf16[192,1536]{1,0:T(8,128)(2,1)}, bf16[192,1536]{1,0:T(8,128)(2,1)}, u32[]{:S(2)}, u32[]{:S(2)}) collective-permute-start(bf16[192,1536]{1,0:T(8,128)(2,1)} %collective-permute-done.20), channel_id=1, source_target_pairs={{8,9},{9,8},{10,11},{11,10},{12,13},{13,12},{14,15},{15,14}} | collective-permute-start | bytes 1769480 | tf_op jit(solution)/shard_map/ppermute | solution.py:69
  68.8 1.0 convert_add_fusion.1
  69.8 0.7 constant_dynamic-slice_fusion.1
  70.4 1.0 reshape.200
  72.4 3.5 %fusion.12 = bf16[32,1536]{1,0:T(8,128)(2,1)S(1)} fusion(f32[1,4,32,192]{3,2,1,0:T(8,128)} %bitcast.364, bf16[1,192,1536]{2,1,0:T(8,128)(2,1)} %bitcast.72, bf16[1,192,1536]{2,1,0:T(8,128)(2,1)} %bitcast.71, bf16[1,192,1536]{2,1,0:T(8,128)(2,1)} %bitcast.70, bf16[1,192,1536]{2,1,0:T(8,128)(2,1)S(1)} %get-tuple-element.2, ...), kind=kOutput, calls=%fused_computation.17 | convolution fusion | flops 158392320 | bytes 5242880 | tf_op jit(solution)/shard_map/bnr,bri->ni/dot_general | solution.py:148
  75.9 0.7 collective-permute-start.25
  76.7 2.4 %bitcast_convert_fusion.1 = (bf16[4,32,192]{2,1,0:T(8,128)(2,1)S(1)}, f32[4,192,32]{1,2,0:T(8,128)S(1)}) fusion(bf16[32,1536]{1,0:T(8,128)(2,1)S(1)} %collective-permute-done.25, bf16[32,1536]{1,0:T(8,128)(2,1)S(1)} %fusion.12, bf16[1,192,1536]{2,1,0:T(8,128)(2,1)} %bitcast.67, bf16[1,192,1536]{2,1,0:T(8,128)(2,1)} %bitcast.66, ...), kind=kOutput, calls=%fused_computation.90 | convolution fusion | flops 79257600 | bytes 2703360 | tf_op jit(solution)/shard_map/ni,bri->bnr/dot_general | solution.py:149
  79.1 2.0 %fusion.13 = bf16[32,1536]{1,0:T(8,128)(2,1)S(1)} fusion(bf16[4,32,192]{2,1,0:T(8,128)(2,1)S(1)} %get-tuple-element.102, bf16[1,192,1536]{2,1,0:T(8,128)(2,1)} %bitcast.72, bf16[1,192,1536]{2,1,0:T(8,128)(2,1)} %bitcast.71, bf16[1,192,1536]{2,1,0:T(8,128)(2,1)} %bitcast.70, bf16[1,192,1536]{2,1,0:T(8,128)(2,1)S(1)} %get-tuple-element.2), kind=kOutput, calls=%fused_computation.18 | convolution fusion | flops 79085568 | bytes 2506752 | tf_op jit(solution)/shard_map/kbnr,kbri->ni/dot_general | solution.py:159
  81.1 0.7 collective-permute-start.26
  82.2 2.3 %bitcast_convert_fusion = (bf16[4,32,192]{2,1,0:T(8,128)(2,1)S(1)}, f32[4,192,32]{1,2,0:T(8,128)S(1)}) fusion(bf16[32,1536]{1,0:T(8,128)(2,1)S(1)} %collective-permute-done.26, bf16[32,1536]{1,0:T(8,128)(2,1)S(1)} %fusion.13, bf16[32,1536]{1,0:T(8,128)(2,1)} %collective-permute-done.17, bf16[32,1536]{1,0:T(8,128)(2,1)} %fusion.11, ...), kind=kOutput, calls=%fused_computation.89 | convolution fusion | flops 79454208 | bytes 2899968 | tf_op jit(solution)/shard_map/ni,bri->bnr/dot_general | solution.py:162
  84.5 1.3 collective-permute-start.31
  85.8 0.7 collective-permute-start.32
  86.4 1.3 collective-permute-start.33
  87.7 0.7 collective-permute-start.34
  88.5 0.7 collective-permute-start.27
  89.2 23.4 %collective-permute-done.31 = bf16[2,2,32,192]{3,2,0,1:T(8,128)(2,1)S(1)} collective-permute-done((bf16[2,2,32,192]{3,2,0,1:T(8,128)(2,1)S(1)}, bf16[2,2,32,192]{3,2,0,1:T(8,128)(2,1)S(1)}, u32[]{:S(2)}, u32[]{:S(2)}) %collective-permute-start.31) | collective-permute-done | bytes 49184 | tf_op jit(solution)/shard_map/ppermute | solution.py:73
  112.5 0.7 collective-permute-start.28
  113.2 0.7 collective-permute-start.29
  113.9 1.5 %collective-permute-done.33 = bf16[2,2,32,192]{3,2,0,1:T(8,128)(2,1)S(1)} collective-permute-done((bf16[2,2,32,192]{3,2,0,1:T(8,128)(2,1)S(1)}, bf16[2,2,32,192]{3,2,0,1:T(8,128)(2,1)S(1)}, u32[]{:S(2)}, u32[]{:S(2)}) %collective-permute-start.33) | collective-permute-done | bytes 49184 | tf_op jit(solution)/shard_map/ppermute | solution.py:73
  115.4 1.9 %fusion.8 = bf16[2,32,1536]{2,1,0:T(8,128)(2,1)S(1)} fusion(bf16[2,1,192,1536]{3,2,0,1:T(8,128)(2,1)} %bitcast.48, bf16[2,1,192,1536]{3,2,0,1:T(8,128)(2,1)S(1)} %bitcast.321, bf16[2,2,1,32,192]{4,3,0,2,1:T(8,128)(2,1)S(1)} %add_bitcast_fusion.2, bf16[2,2,1,32,192]{4,3,0,2,1:T(8,128)(2,1)S(1)} %add_bitcast_fusion.3), kind=kOutput, calls=%fused_computation.12 | convolution fusion | flops 152322048 | bytes 2654208 | tf_op jit(solution)/shard_map/kjlnr,kjri->lni/dot_general | solution.py:170
  117.3 3.8 %collective-permute-start.37 = (bf16[2,32,1536]{2,1,0:T(8,128)(2,1)S(1)}, bf16[2,32,1536]{2,1,0:T(8,128)(2,1)S(1)}, u32[]{:S(2)}, u32[]{:S(2)}) collective-permute-start(bf16[2,32,1536]{2,1,0:T(8,128)(2,1)S(1)} %fusion.8), channel_id=1, source_target_pairs={{0,6},{1,7},{2,4},{3,5},{4,2},{5,3},{6,0},{7,1},{16,22},{17,23},{1... | collective-permute-start | bytes 589832 | tf_op jit(solution)/shard_map/ppermute | solution.py:69
  121.0 2.4 %collective-permute-start.35 = (bf16[2,32,1536]{2,1,0:T(8,128)(2,1)S(1)}, bf16[2,32,1536]{2,1,0:T(8,128)(2,1)S(1)}, u32[]{:S(2)}, u32[]{:S(2)}) collective-permute-start(bf16[2,32,1536]{2,1,0:T(8,128)(2,1)S(1)} %fusion.8), channel_id=1, source_target_pairs={{0,2},{1,3},{2,0},{3,1},{4,6},{5,7},{6,4},{7,5},{16,18},{17,19},{1... | collective-permute-start | bytes 589832 | tf_op jit(solution)/shard_map/ppermute | solution.py:69
  123.5 3.0 %collective-permute-start.36 = (bf16[2,32,1536]{2,1,0:T(8,128)(2,1)S(1)}, bf16[2,32,1536]{2,1,0:T(8,128)(2,1)S(1)}, u32[]{:S(2)}, u32[]{:S(2)}) collective-permute-start(bf16[2,32,1536]{2,1,0:T(8,128)(2,1)S(1)} %fusion.8), channel_id=1, source_target_pairs={{0,4},{1,5},{2,6},{3,7},{4,0},{5,1},{6,2},{7,3},{16,20},{17,21},{1... | collective-permute-start | bytes 589832 | tf_op jit(solution)/shard_map/ppermute | solution.py:69
  127.9 0.7 collective-permute-start.30
  129.4 1.6 %collective-permute-done.36 = bf16[2,32,1536]{2,1,0:T(8,128)(2,1)S(1)} collective-permute-done((bf16[2,32,1536]{2,1,0:T(8,128)(2,1)S(1)}, bf16[2,32,1536]{2,1,0:T(8,128)(2,1)S(1)}, u32[]{:S(2)}, u32[]{:S(2)}) %collective-permute-start.36) | collective-permute-done | bytes 196640 | tf_op jit(solution)/shard_map/ppermute | solution.py:69
  131.2 1.9 %collective-permute-start.38 = (bf16[2,32,1536]{2,1,0:T(8,128)(2,1)S(1)}, bf16[2,32,1536]{2,1,0:T(8,128)(2,1)S(1)}, u32[]{:S(2)}, u32[]{:S(2)}) collective-permute-start(bf16[2,32,1536]{2,1,0:T(8,128)(2,1)S(1)} %subtract_convert_fusion), channel_id=1, source_target_pairs={{0,1},{1,0},{2,3},{3,2},{4,5},{5,4},{6,7},{7,6},{16,17},{17,16},{1... | collective-permute-start | bytes 589832 | tf_op jit(solution)/shard_map/ppermute | solution.py:69
  133.2 0.7 fusion.46
  133.8 0.7 collective-permute-done.38
  134.7 1.0 fusion.43
  (178 shorter events, 7.9 us)
Async XLA Ops:
  0.6 6.4 %collective-permute-start.5 = (f32[192,128]{1,0:T(8,128)}, f32[192,128]{1,0:T(8,128)S(1)}, u32[]{:S(2)}, u32[]{:S(2)}) collective-permute-start(f32[192,128]{1,0:T(8,128)} %bitcast.317), channel_id=1, source_target_pairs={{24,8},{25,9},{26,10},{27,11},{28,12},{29,13},{30,14},{31,15}} | collective-permute-start | bytes 294920 | tf_op jit(solution)/shard_map/ppermute | solution.py:73
  2.1 4.4 %copy-start = (f32[1,192,128]{2,1,0:T(8,128)S(1)}, f32[1,192,128]{2,1,0:T(8,128)}, u32[]{:S(2)}) copy-start(f32[1,192,128]{2,1,0:T(8,128)} %param.5) | copy-start | bytes 294916
  4.0 41.0 %collective-permute-start.9 = (bf16[2,192,1536]{2,1,0:T(8,128)(2,1)S(1)}, bf16[2,192,1536]{2,1,0:T(8,128)(2,1)}, u32[]{:S(2)}, u32[]{:S(2)}) collective-permute-start(bf16[2,192,1536]{2,1,0:T(8,128)(2,1)S(1)} %fusion), channel_id=1, source_target_pairs={{0,1},{1,0},{2,3},{3,2},{4,5},{5,4},{6,7},{7,6},{16,17},{17,16},{1... | collective-permute-start | bytes 3538952 | tf_op jit(solution)/shard_map/ppermute | solution.py:69
  7.6 1.1 copy-start.1
  9.0 5.4 %collective-permute-start = (bf16[2,32,1536]{2,1,0:T(8,128)(2,1)S(1)}, bf16[2,32,1536]{2,1,0:T(8,128)(2,1)S(1)}, u32[]{:S(2)}, u32[]{:S(2)}) collective-permute-start(bf16[2,32,1536]{2,1,0:T(8,128)(2,1)S(1)} %slice.474), channel_id=1, source_target_pairs={{0,1},{1,0},{2,3},{3,2},{4,5},{5,4},{6,7},{7,6},{16,17},{17,16},{1... | collective-permute-start | bytes 589832 | tf_op jit(solution)/shard_map/ppermute | solution.py:69
  11.8 9.9 %collective-permute-start.6 = (f32[2,32,192]{2,1,0:T(8,128)}, f32[2,32,192]{2,1,0:T(8,128)S(1)}, u32[]{:S(2)}, u32[]{:S(2)}) collective-permute-start(f32[2,32,192]{2,1,0:T(8,128)} %get-tuple-element.19), channel_id=1, source_target_pairs={{8,9},{9,8},{10,11},{11,10},{12,13},{13,12},{14,15},{15,14}} | collective-permute-start | bytes 147464 | tf_op jit(solution)/shard_map/ppermute | solution.py:69
  12.4 10.0 %collective-permute-start.7 = (f32[2,32,192]{2,1,0:T(8,128)}, f32[2,32,192]{2,1,0:T(8,128)S(1)}, u32[]{:S(2)}, u32[]{:S(2)}) collective-permute-start(f32[2,32,192]{2,1,0:T(8,128)} %get-tuple-element.21), channel_id=1, source_target_pairs={{8,10},{9,11},{10,8},{11,9},{12,14},{13,15},{14,12},{15,13}} | collective-permute-start | bytes 147464 | tf_op jit(solution)/shard_map/ppermute | solution.py:69
  13.1 7.3 %copy-start.18 = (s32[4]{0:T(128)S(1)}, s32[4]{0:T(128)}, u32[]{:S(2)}) copy-start(s32[4]{0:T(128)} %constant.201.clone) | copy-start | bytes 52
  13.1 10.0 %collective-permute-start.8 = (f32[2,32,192]{2,1,0:T(8,128)}, f32[2,32,192]{2,1,0:T(8,128)}, u32[]{:S(2)}, u32[]{:S(2)}) collective-permute-start(f32[2,32,192]{2,1,0:T(8,128)} %get-tuple-element.20), channel_id=1, source_target_pairs={{8,11},{9,10},{10,9},{11,8},{12,15},{13,14},{14,13},{15,12}} | collective-permute-start | bytes 147464 | tf_op jit(solution)/shard_map/ppermute | solution.py:69
  14.4 11.1 %collective-permute-start.3 = (bf16[2,32,1536]{2,1,0:T(8,128)(2,1)S(1)}, bf16[2,32,1536]{2,1,0:T(8,128)(2,1)S(1)}, u32[]{:S(2)}, u32[]{:S(2)}) collective-permute-start(bf16[2,32,1536]{2,1,0:T(8,128)(2,1)S(1)} %add_convert_fusion.1), channel_id=1, source_target_pairs={{0,6},{1,7},{2,4},{3,5},{4,2},{5,3},{6,0},{7,1},{16,22},{17,23},{1... | collective-permute-start | bytes 589832 | tf_op jit(solution)/shard_map/ppermute | solution.py:69
  21.7 27.6 %collective-permute-start.15 = (bf16[192,1536]{1,0:T(8,128)(2,1)S(1)}, bf16[192,1536]{1,0:T(8,128)(2,1)S(1)}, u32[]{:S(2)}, u32[]{:S(2)}) collective-permute-start(bf16[192,1536]{1,0:T(8,128)(2,1)S(1)} %bitcast.324), channel_id=1, source_target_pairs={{8,10},{9,11},{10,8},{11,9},{12,14},{13,15},{14,12},{15,13}} | collective-permute-start | bytes 1769480 | tf_op jit(solution)/shard_map/ppermute | solution.py:69
  22.4 38.4 %collective-permute-start.14 = (bf16[192,1536]{1,0:T(8,128)(2,1)S(1)}, bf16[192,1536]{1,0:T(8,128)(2,1)S(1)}, u32[]{:S(2)}, u32[]{:S(2)}) collective-permute-start(bf16[192,1536]{1,0:T(8,128)(2,1)S(1)} %bitcast.325), channel_id=1, source_target_pairs={{8,9},{9,8},{10,11},{11,10},{12,13},{13,12},{14,15},{15,14}} | collective-permute-start | bytes 1769480 | tf_op jit(solution)/shard_map/ppermute | solution.py:69
  23.1 27.6 %collective-permute-start.18 = (bf16[192,1536]{1,0:T(8,128)(2,1)S(1)}, bf16[192,1536]{1,0:T(8,128)(2,1)}, u32[]{:S(2)}, u32[]{:S(2)}) collective-permute-start(bf16[192,1536]{1,0:T(8,128)(2,1)S(1)} %bitcast.326), channel_id=1, source_target_pairs={{24,8},{25,9},{26,10},{27,11},{28,12},{29,13},{30,14},{31,15}} | collective-permute-start | bytes 1769480 | tf_op jit(solution)/shard_map/ppermute | solution.py:73
  25.5 35.3 %copy-start.2 = (f32[2,4,32,192]{3,2,1,0:T(8,128)}, f32[2,4,32,192]{3,2,1,0:T(8,128)S(1)}, u32[]{:S(2)}) copy-start(f32[2,4,32,192]{3,2,1,0:T(8,128)S(1)} %pad_maximum_fusion.14) | copy-start | bytes 589828
  25.5 8.4 %collective-permute-start.1 = (bf16[2,32,1536]{2,1,0:T(8,128)(2,1)S(1)}, bf16[2,32,1536]{2,1,0:T(8,128)(2,1)S(1)}, u32[]{:S(2)}, u32[]{:S(2)}) collective-permute-start(bf16[2,32,1536]{2,1,0:T(8,128)(2,1)S(1)} %add_convert_fusion.1), channel_id=1, source_target_pairs={{0,2},{1,3},{2,0},{3,1},{4,6},{5,7},{6,4},{7,5},{16,18},{17,19},{1... | collective-permute-start | bytes 589832 | tf_op jit(solution)/shard_map/ppermute | solution.py:69
  33.9 7.6 %collective-permute-start.2 = (bf16[2,32,1536]{2,1,0:T(8,128)(2,1)S(1)}, bf16[2,32,1536]{2,1,0:T(8,128)(2,1)S(1)}, u32[]{:S(2)}, u32[]{:S(2)}) collective-permute-start(bf16[2,32,1536]{2,1,0:T(8,128)(2,1)S(1)} %add_convert_fusion.1), channel_id=1, source_target_pairs={{0,4},{1,5},{2,6},{3,7},{4,0},{5,1},{6,2},{7,3},{16,20},{17,21},{1... | collective-permute-start | bytes 589832 | tf_op jit(solution)/shard_map/ppermute | solution.py:69
  41.6 3.3 %collective-permute-start.4 = (bf16[2,32,1536]{2,1,0:T(8,128)(2,1)S(1)}, bf16[2,32,1536]{2,1,0:T(8,128)(2,1)S(1)}, u32[]{:S(2)}, u32[]{:S(2)}) collective-permute-start(bf16[2,32,1536]{2,1,0:T(8,128)(2,1)S(1)} %add_convert_fusion), channel_id=1, source_target_pairs={{0,1},{1,0},{2,3},{3,2},{4,5},{5,4},{6,7},{7,6},{16,17},{17,16},{1... | collective-permute-start | bytes 589832 | tf_op jit(solution)/shard_map/ppermute | solution.py:69
  47.2 4.2 %collective-permute-start.12 = (bf16[2,2,32,192]{3,2,1,0:T(8,128)(2,1)S(1)}, bf16[2,2,32,192]{3,2,1,0:T(8,128)(2,1)S(1)}, u32[]{:S(2)}, u32[]{:S(2)}) collective-permute-start(bf16[2,2,32,192]{3,2,1,0:T(8,128)(2,1)S(1)} %get-tuple-element.89), channel_id=1, source_target_pairs={{0,10},{1,11},{2,8},{3,9},{4,14},{5,15},{6,12},{7,13}} | collective-permute-start | bytes 147464 | tf_op jit(solution)/shard_map/ppermute | solution.py:73
  48.5 6.8 %collective-permute-start.13 = (bf16[2,2,32,192]{3,2,1,0:T(8,128)(2,1)S(1)}, bf16[2,2,32,192]{3,2,1,0:T(8,128)(2,1)S(1)}, u32[]{:S(2)}, u32[]{:S(2)}) collective-permute-start(bf16[2,2,32,192]{3,2,1,0:T(8,128)(2,1)S(1)} %get-tuple-element.89), channel_id=1, source_target_pairs={{16,10},{17,11},{18,8},{19,9},{20,14},{21,15},{22,12},{23,13}} | collective-permute-start | bytes 147464 | tf_op jit(solution)/shard_map/ppermute | solution.py:73
  49.3 15.7 %copy-start.15 = (bf16[192,1536]{1,0:T(8,128)(2,1)}, bf16[192,1536]{1,0:T(8,128)(2,1)S(1)}, u32[]{:S(2)}) copy-start(bf16[192,1536]{1,0:T(8,128)(2,1)S(1)} %collective-permute-done.15) | copy-start | bytes 1769476
  49.3 13.0 %collective-permute-start.23 = (bf16[192,1536]{1,0:T(8,128)(2,1)S(1)}, bf16[192,1536]{1,0:T(8,128)(2,1)}, u32[]{:S(2)}, u32[]{:S(2)}) collective-permute-start(bf16[192,1536]{1,0:T(8,128)(2,1)S(1)} %get-tuple-element.3), channel_id=1, source_target_pairs={{8,10},{9,11},{10,8},{11,9},{12,14},{13,15},{14,12},{15,13}} | collective-permute-start | bytes 1769480 | tf_op jit(solution)/shard_map/ppermute | solution.py:69
  50.8 13.0 %collective-permute-start.16 = (bf16[192,1536]{1,0:T(8,128)(2,1)S(1)}, bf16[192,1536]{1,0:T(8,128)(2,1)S(1)}, u32[]{:S(2)}, u32[]{:S(2)}) collective-permute-start(bf16[192,1536]{1,0:T(8,128)(2,1)S(1)} %collective-permute-done.15), channel_id=1, source_target_pairs={{8,9},{9,8},{10,11},{11,10},{12,13},{13,12},{14,15},{15,14}} | collective-permute-start | bytes 1769480 | tf_op jit(solution)/shard_map/ppermute | solution.py:69
  51.5 5.7 %collective-permute-start.10 = (bf16[2,2,32,192]{3,2,1,0:T(8,128)(2,1)S(1)}, bf16[2,2,32,192]{3,2,1,0:T(8,128)(2,1)S(1)}, u32[]{:S(2)}, u32[]{:S(2)}) collective-permute-start(bf16[2,2,32,192]{3,2,1,0:T(8,128)(2,1)S(1)} %get-tuple-element.88), channel_id=1, source_target_pairs={{0,8},{1,9},{2,10},{3,11},{4,12},{5,13},{6,14},{7,15}} | collective-permute-start | bytes 147464 | tf_op jit(solution)/shard_map/ppermute | solution.py:73
  55.3 3.3 %collective-permute-start.11 = (bf16[2,2,32,192]{3,2,1,0:T(8,128)(2,1)S(1)}, bf16[2,2,32,192]{3,2,1,0:T(8,128)(2,1)S(1)}, u32[]{:S(2)}, u32[]{:S(2)}) collective-permute-start(bf16[2,2,32,192]{3,2,1,0:T(8,128)(2,1)S(1)} %get-tuple-element.88), channel_id=1, source_target_pairs={{16,8},{17,9},{18,10},{19,11},{20,12},{21,13},{22,14},{23,15}} | collective-permute-start | bytes 147464 | tf_op jit(solution)/shard_map/ppermute | solution.py:73
  57.2 15.1 %collective-permute-start.22 = (bf16[192,1536]{1,0:T(8,128)(2,1)S(1)}, bf16[192,1536]{1,0:T(8,128)(2,1)}, u32[]{:S(2)}, u32[]{:S(2)}) collective-permute-start(bf16[192,1536]{1,0:T(8,128)(2,1)S(1)} %get-tuple-element.3), channel_id=1, source_target_pairs={{8,9},{9,8},{10,11},{11,10},{12,13},{13,12},{14,15},{15,14}} | collective-permute-start | bytes 1769480 | tf_op jit(solution)/shard_map/ppermute | solution.py:69
  58.6 8.6 %collective-permute-start.20 = (bf16[192,1536]{1,0:T(8,128)(2,1)}, bf16[192,1536]{1,0:T(8,128)(2,1)}, u32[]{:S(2)}, u32[]{:S(2)}) collective-permute-start(bf16[192,1536]{1,0:T(8,128)(2,1)} %collective-permute-done.18), channel_id=1, source_target_pairs={{8,10},{9,11},{10,8},{11,9},{12,14},{13,15},{14,12},{15,13}} | collective-permute-start | bytes 1769480 | tf_op jit(solution)/shard_map/ppermute | solution.py:69
  60.8 4.2 %copy-start.16 = (bf16[192,1536]{1,0:T(8,128)(2,1)}, bf16[192,1536]{1,0:T(8,128)(2,1)S(1)}, u32[]{:S(2)}) copy-start(bf16[192,1536]{1,0:T(8,128)(2,1)S(1)} %collective-permute-done.14) | copy-start | bytes 1769476
  60.9 11.4 %collective-permute-start.19 = (bf16[192,1536]{1,0:T(8,128)(2,1)}, bf16[192,1536]{1,0:T(8,128)(2,1)}, u32[]{:S(2)}, u32[]{:S(2)}) collective-permute-start(bf16[192,1536]{1,0:T(8,128)(2,1)} %collective-permute-done.18), channel_id=1, source_target_pairs={{8,9},{9,8},{10,11},{11,10},{12,13},{13,12},{14,15},{15,14}} | collective-permute-start | bytes 1769480 | tf_op jit(solution)/shard_map/ppermute | solution.py:69
  62.3 9.9 %collective-permute-start.24 = (bf16[192,1536]{1,0:T(8,128)(2,1)}, bf16[192,1536]{1,0:T(8,128)(2,1)}, u32[]{:S(2)}, u32[]{:S(2)}) collective-permute-start(bf16[192,1536]{1,0:T(8,128)(2,1)} %collective-permute-done.23), channel_id=1, source_target_pairs={{8,9},{9,8},{10,11},{11,10},{12,13},{13,12},{14,15},{15,14}} | collective-permute-start | bytes 1769480 | tf_op jit(solution)/shard_map/ppermute | solution.py:69
  63.8 1.2 copy-start.17
  65.0 7.3 %copy-start.3 = (f32[2,4,32,192]{3,2,1,0:T(8,128)S(1)}, f32[2,4,32,192]{3,2,1,0:T(8,128)}, u32[]{:S(2)}) copy-start(f32[2,4,32,192]{3,2,1,0:T(8,128)} %copy-done.2) | copy-start | bytes 589828
  65.0 3.8 %collective-permute-start.17 = (bf16[32,1536]{1,0:T(8,128)(2,1)}, bf16[32,1536]{1,0:T(8,128)(2,1)}, u32[]{:S(2)}, u32[]{:S(2)}) collective-permute-start(bf16[32,1536]{1,0:T(8,128)(2,1)} %fusion.11), channel_id=1, source_target_pairs={{8,12},{9,13},{10,14},{11,15},{12,8},{13,9},{14,10},{15,11}} | collective-permute-start | bytes 294920 | tf_op jit(solution)/shard_map/ppermute | solution.py:69
  67.3 5.0 %collective-permute-start.21 = (bf16[192,1536]{1,0:T(8,128)(2,1)}, bf16[192,1536]{1,0:T(8,128)(2,1)}, u32[]{:S(2)}, u32[]{:S(2)}) collective-permute-start(bf16[192,1536]{1,0:T(8,128)(2,1)} %collective-permute-done.20), channel_id=1, source_target_pairs={{8,9},{9,8},{10,11},{11,10},{12,13},{13,12},{14,15},{15,14}} | collective-permute-start | bytes 1769480 | tf_op jit(solution)/shard_map/ppermute | solution.py:69
  71.5 0.7 copy-start.4
  71.5 0.8 copy-start.6
  71.5 0.8 copy-start.8
  71.5 0.8 copy-start.10
  72.3 4.3 %copy-start.5 = (f32[1,32,192]{2,1,0:T(8,128)S(1)}, f32[1,32,192]{2,1,0:T(8,128)}, u32[]{:S(2)}) copy-start(f32[1,32,192]{2,1,0:T(8,128)} %copy-done.4) | copy-start | bytes 73732
  72.3 4.3 %copy-start.7 = (f32[1,32,192]{2,1,0:T(8,128)S(1)}, f32[1,32,192]{2,1,0:T(8,128)}, u32[]{:S(2)}) copy-start(f32[1,32,192]{2,1,0:T(8,128)} %copy-done.6) | copy-start | bytes 73732
  72.3 4.3 %copy-start.9 = (f32[1,32,192]{2,1,0:T(8,128)S(1)}, f32[1,32,192]{2,1,0:T(8,128)}, u32[]{:S(2)}) copy-start(f32[1,32,192]{2,1,0:T(8,128)} %copy-done.8) | copy-start | bytes 73732
  72.4 4.3 %copy-start.11 = (f32[1,32,192]{2,1,0:T(8,128)S(1)}, f32[1,32,192]{2,1,0:T(8,128)}, u32[]{:S(2)}) copy-start(f32[1,32,192]{2,1,0:T(8,128)} %copy-done.10) | copy-start | bytes 73732
  72.4 4.3 %copy-start.12 = (f32[2,32,192]{2,1,0:T(8,128)S(1)}, f32[2,32,192]{2,1,0:T(8,128)}, u32[]{:S(2)}) copy-start(f32[2,32,192]{2,1,0:T(8,128)} %get-tuple-element.72) | copy-start | bytes 147460
  72.4 4.3 %copy-start.13 = (f32[2,32,192]{2,1,0:T(8,128)S(1)}, f32[2,32,192]{2,1,0:T(8,128)}, u32[]{:S(2)}) copy-start(f32[2,32,192]{2,1,0:T(8,128)} %get-tuple-element.73) | copy-start | bytes 147460
  75.9 0.8 collective-permute-start.25
  81.1 1.0 collective-permute-start.26
  84.5 28.1 %collective-permute-start.31 = (bf16[2,2,32,192]{3,2,0,1:T(8,128)(2,1)S(1)}, bf16[2,2,32,192]{3,2,0,1:T(8,128)(2,1)S(1)}, u32[]{:S(2)}, u32[]{:S(2)}) collective-permute-start(bf16[2,2,32,192]{3,2,0,1:T(8,128)(2,1)S(1)} %get-tuple-element.38), channel_id=1, source_target_pairs={{8,0},{9,1},{10,2},{11,3},{12,4},{13,5},{14,6},{15,7}} | collective-permute-start | bytes 147464 | tf_op jit(solution)/shard_map/ppermute | solution.py:73
  85.8 27.4 %collective-permute-start.32 = (bf16[2,2,32,192]{3,2,0,1:T(8,128)(2,1)S(1)}, bf16[2,2,32,192]{3,2,0,1:T(8,128)(2,1)S(1)}, u32[]{:S(2)}, u32[]{:S(2)}) collective-permute-start(bf16[2,2,32,192]{3,2,0,1:T(8,128)(2,1)S(1)} %get-tuple-element.38), channel_id=1, source_target_pairs={{8,16},{9,17},{10,18},{11,19},{12,20},{13,21},{14,22},{15,23}} | collective-permute-start | bytes 147464 | tf_op jit(solution)/shard_map/ppermute | solution.py:73
  86.4 29.0 %collective-permute-start.33 = (bf16[2,2,32,192]{3,2,0,1:T(8,128)(2,1)S(1)}, bf16[2,2,32,192]{3,2,0,1:T(8,128)(2,1)S(1)}, u32[]{:S(2)}, u32[]{:S(2)}) collective-permute-start(bf16[2,2,32,192]{3,2,0,1:T(8,128)(2,1)S(1)} %get-tuple-element.39), channel_id=1, source_target_pairs={{8,2},{9,3},{10,0},{11,1},{12,6},{13,7},{14,4},{15,5}} | collective-permute-start | bytes 147464 | tf_op jit(solution)/shard_map/ppermute | solution.py:73
  87.7 27.7 %collective-permute-start.34 = (bf16[2,2,32,192]{3,2,0,1:T(8,128)(2,1)S(1)}, bf16[2,2,32,192]{3,2,0,1:T(8,128)(2,1)S(1)}, u32[]{:S(2)}, u32[]{:S(2)}) collective-permute-start(bf16[2,2,32,192]{3,2,0,1:T(8,128)(2,1)S(1)} %get-tuple-element.39), channel_id=1, source_target_pairs={{8,18},{9,19},{10,16},{11,17},{12,22},{13,23},{14,20},{15,21}} | collective-permute-start | bytes 147464 | tf_op jit(solution)/shard_map/ppermute | solution.py:73
  88.5 35.0 %collective-permute-start.27 = (f32[4,32,192]{2,1,0:T(8,128)S(1)}, f32[4,32,192]{2,1,0:T(8,128)S(1)}, u32[]{:S(2)}, u32[]{:S(2)}) collective-permute-start(f32[4,32,192]{2,1,0:T(8,128)S(1)} %get-tuple-element.9), channel_id=1, source_target_pairs={{8,9},{9,8},{10,11},{11,10},{12,13},{13,12},{14,15},{15,14}} | collective-permute-start | bytes 294920 | tf_op jit(solution)/shard_map/ppermute | solution.py:69
  112.5 14.0 %collective-permute-start.28 = (f32[4,32,192]{2,1,0:T(8,128)S(1)}, f32[4,32,192]{2,1,0:T(8,128)S(1)}, u32[]{:S(2)}, u32[]{:S(2)}) collective-permute-start(f32[4,32,192]{2,1,0:T(8,128)S(1)} %get-tuple-element.11), channel_id=1, source_target_pairs={{8,10},{9,11},{10,8},{11,9},{12,14},{13,15},{14,12},{15,13}} | collective-permute-start | bytes 294920 | tf_op jit(solution)/shard_map/ppermute | solution.py:69
  113.2 13.3 %collective-permute-start.29 = (f32[4,32,192]{2,1,0:T(8,128)S(1)}, f32[4,32,192]{2,1,0:T(8,128)S(1)}, u32[]{:S(2)}, u32[]{:S(2)}) collective-permute-start(f32[4,32,192]{2,1,0:T(8,128)S(1)} %get-tuple-element.10), channel_id=1, source_target_pairs={{8,11},{9,10},{10,9},{11,8},{12,15},{13,14},{14,13},{15,12}} | collective-permute-start | bytes 294920 | tf_op jit(solution)/shard_map/ppermute | solution.py:69
  117.3 11.8 %collective-permute-start.37 = (bf16[2,32,1536]{2,1,0:T(8,128)(2,1)S(1)}, bf16[2,32,1536]{2,1,0:T(8,128)(2,1)S(1)}, u32[]{:S(2)}, u32[]{:S(2)}) collective-permute-start(bf16[2,32,1536]{2,1,0:T(8,128)(2,1)S(1)} %fusion.8), channel_id=1, source_target_pairs={{0,6},{1,7},{2,4},{3,5},{4,2},{5,3},{6,0},{7,1},{16,22},{17,23},{1... | collective-permute-start | bytes 589832 | tf_op jit(solution)/shard_map/ppermute | solution.py:69
  121.0 8.4 %collective-permute-start.35 = (bf16[2,32,1536]{2,1,0:T(8,128)(2,1)S(1)}, bf16[2,32,1536]{2,1,0:T(8,128)(2,1)S(1)}, u32[]{:S(2)}, u32[]{:S(2)}) collective-permute-start(bf16[2,32,1536]{2,1,0:T(8,128)(2,1)S(1)} %fusion.8), channel_id=1, source_target_pairs={{0,2},{1,3},{2,0},{3,1},{4,6},{5,7},{6,4},{7,5},{16,18},{17,19},{1... | collective-permute-start | bytes 589832 | tf_op jit(solution)/shard_map/ppermute | solution.py:69
  123.5 7.6 %collective-permute-start.36 = (bf16[2,32,1536]{2,1,0:T(8,128)(2,1)S(1)}, bf16[2,32,1536]{2,1,0:T(8,128)(2,1)S(1)}, u32[]{:S(2)}, u32[]{:S(2)}) collective-permute-start(bf16[2,32,1536]{2,1,0:T(8,128)(2,1)S(1)} %fusion.8), channel_id=1, source_target_pairs={{0,4},{1,5},{2,6},{3,7},{4,0},{5,1},{6,2},{7,3},{16,20},{17,21},{1... | collective-permute-start | bytes 589832 | tf_op jit(solution)/shard_map/ppermute | solution.py:69
  127.9 5.2 %collective-permute-start.30 = (f32[2,192,128]{2,1,0:T(8,128)S(1)}, f32[2,192,128]{2,1,0:T(8,128)S(1)}, u32[]{:S(2)}, u32[]{:S(2)}) collective-permute-start(f32[2,192,128]{2,1,0:T(8,128)S(1)} %pad_maximum_fusion.15), channel_id=1, source_target_pairs={{8,24},{9,25},{10,26},{11,27},{12,28},{13,29},{14,30},{15,31}} | collective-permute-start | bytes 589832 | tf_op jit(solution)/shard_map/ppermute | solution.py:73
  129.0 4.2 %copy-start.14 = (bf16[128,192]{0,1:T(8,128)(2,1)S(1)}, bf16[128,192]{0,1:T(8,128)(2,1)}, u32[]{:S(2)}) copy-start(bf16[128,192]{0,1:T(8,128)(2,1)} %copy.151) | copy-start | bytes 147460
  131.2 3.3 %collective-permute-start.38 = (bf16[2,32,1536]{2,1,0:T(8,128)(2,1)S(1)}, bf16[2,32,1536]{2,1,0:T(8,128)(2,1)S(1)}, u32[]{:S(2)}, u32[]{:S(2)}) collective-permute-start(bf16[2,32,1536]{2,1,0:T(8,128)(2,1)S(1)} %subtract_convert_fusion), channel_id=1, source_target_pairs={{0,1},{1,0},{2,3},{3,2},{4,5},{5,4},{6,7},{7,6},{16,17},{17,16},{1... | collective-permute-start | bytes 589832 | tf_op jit(solution)/shard_map/ppermute | solution.py:69

commit v3 on v1

v3 whole, which is shorter than its diff:
```python
import jax
import jax.numpy as jnp
from jax import lax
from jax.experimental import pallas as pl
from jax.experimental.pallas import tpu as pltpu
from jax.sharding import PartitionSpec as P

F32 = jnp.float32
BF16 = jnp.bfloat16


def trailing_ones(node):
    ones = 0
    while node % 2 == 1:
        ones += 1
        node //= 2
    return ones


def child_links(section, members):
    reach = 2 ** (section - 1)
    parents = [node for node in range(members) if trailing_ones(node) == section]
    links = [[(node - reach, node) for node in parents], [(node + reach, node) for node in parents]]
    return [[(a, b) for a, b in side if a < members] for side in links if any(a < members for a, b in side)]


def mm(a, b):
    return jnp.dot(a, b, preferred_element_type=F32)


def mmt(a, b):
    return lax.dot_general(a, b, (((1,), (1,)), ((), ())), preferred_element_type=F32)


class Columns:
    def __init__(self, array, start, count):
        self.array, self.start, self.count = array, start, count


def call(body, outs, args, scratch=()):
    single = isinstance(outs, tuple)
    shapes = [outs] if single else outs
    specs, arrays, buffers, copies = [], [], [], []
    for n, arg in enumerate(args):
        if isinstance(arg, Columns):
            rows = arg.array.shape[0]
            pieces = 2 if rows % 32 == 0 else 1
            copies.append((n, arg, rows // pieces, pieces))
            buffers += [pltpu.VMEM((rows, arg.count), arg.array.dtype), pltpu.SemaphoreType.DMA((pieces,))]
            specs.append(pl.BlockSpec(memory_space=pl.ANY))
            arrays.append(arg.array)
        else:
            specs.append(pl.BlockSpec(memory_space=pltpu.VMEM))
            arrays.append(arg)

    def kernel(*refs):
        inputs = list(refs[: len(args)])
        results = refs[len(args) : len(args) + len(shapes)]
        held = refs[len(args) + len(shapes) :]
        started = []
        for m, (n, arg, rows, pieces) in enumerate(copies):
            source, buffer, sems = inputs[n], held[2 * m], held[2 * m + 1]
            for p in range(pieces):
                span = pl.ds(p * rows, rows)
                started.append(
                    pltpu.make_async_copy(
                        source.at[span, pl.ds(arg.start, arg.count)], buffer.at[span], sems.at[p]
                    )
                )
            inputs[n] = buffer
        for copy in started:
            copy.start()

        def ready():
            for copy in started:
                copy.wait()

        body(ready, inputs, results, *held[2 * len(copies) :])

    moved = sum(a.size * a.dtype.itemsize for a in arrays)
    result = pl.pallas_call(
        kernel,
        out_shape=[jax.ShapeDtypeStruct(shape, dtype) for shape, dtype in shapes],
        in_specs=specs,
        out_specs=[pl.BlockSpec(memory_space=pltpu.VMEM) for _ in shapes],
        scratch_shapes=buffers + list(scratch),
        compiler_params=pltpu.CompilerParams(vmem_limit_bytes=24 << 20),
        cost_estimate=pl.CostEstimate(flops=1 << 28, bytes_accessed=moved, transcendentals=0),
    )(*arrays)
    return result[0] if single else result


def on_device(rhs, panel, inverse_t, pattern):
    members = lax.axis_size("lvl")
    cols = lax.axis_size("col")
    levels = members.bit_length() - 1
    last = levels - 1
    chips = cols // 2
    lanes = 1 << ((chips.bit_length() - 1) // 2)
    row_count, rhs_count = rhs.shape[1:]
    width = inverse_t.shape[2]
    blocks = 2 * lanes
    group = rhs_count // blocks
    half = rhs_count // 2
    levels_of = [trailing_ones(node) for node in range(members)]
    nodes_at = [[node for node in range(members) if levels_of[node] == s] for s in range(levels + 1)]
    leaves = nodes_at[0]
    inner = [node for node in range(members) if levels_of[node] > 0]

    def place():
        at = lax.axis_index("col")
        core, lane = at % 2, at // 2 % lanes
        return at // blocks, lane, core, core * lanes + lane

    def height():
        at, rank = lax.axis_index("lvl"), 0
        for s in range(1, levels + 1):
            rank = rank + ((at + 1) % 2**s == 0).astype(jnp.int32)
        return rank

    def across(x, offset, planes):
        pairs = [(p * cols + c, p * cols + (c ^ offset)) for p in planes for c in range(cols)]
        return lax.ppermute(x, ("lvl", "col"), pairs)

    def along(x, links, offset=0):
        pairs = [(a * cols + c, b * cols + (c ^ offset)) for a, b in links for c in range(cols)]
        return lax.ppermute(x, ("lvl", "col"), pairs)

    def down(links):
        return [(b, a) for a, b in links]

    def after(x, *earlier):
        return lax.optimization_barrier((x, *earlier))[0]

    def over_chips(mine):
        return [mine] + [across(mine, 2 * chip, leaves) for chip in range(1, chips)]

    def over_rows(mine, planes):
        return [mine] + [across(mine, offset, planes) for offset in range(2 * lanes, cols, 2 * lanes)]

    def chip_total(refs):
        parts = []
        for i in range(lanes):
            total = refs[0][i * group : (i + 1) * group, :].astype(F32)
            for chip in range(1, chips):
                k = i ^ (chip % lanes)
                total = total + refs[chip][k * group : (k + 1) * group, :].astype(F32)
            parts.append(total)
        return jnp.concatenate(parts, axis=0)

    def row_total(refs):
        total = refs[0][...].astype(F32)
        for ref in refs[1:]:
            total = total + ref[...].astype(F32)
        return total

    def total_of(parts):
        total = parts[0]
        for part in parts[1:]:
            total = total + part
        return total

    def groups(b):
        return pl.ds(pl.multiple_of((b ^ place()[3]) * group, group), group)

    inverse_own = Columns(inverse_t[0], 0, width)
    chip_rows = len(range(0, cols, 2 * lanes))

    def leaf_first(ready, ins, outs, turned, ordered):
        turned[...] = ins[0][...].T
        for b in range(blocks):
            ordered[b * group : (b + 1) * group, :] = turned[groups(b), :]
        terms = ordered[...].astype(BF16)
        ready()
        outs[0][...] = mm(terms[:half], ins[1][...]).astype(BF16)
        outs[1][...] = mm(terms[half:], ins[1][...]).astype(BF16)

    keep, give = call(
        leaf_first,
        [((half, width), BF16)] * 2,
        [rhs[0], inverse_own],
        [pltpu.VMEM((rhs_count, row_count), F32)] * 2,
    )
    got = across(give, 1, leaves)

    tiles = pattern.shape[-1]
    tile = width // tiles
    full = levels * width + 2 * rhs_count

    def build(ready, ins, outs):
        (rhs_ref, pattern_ref, inv_ref, *panels), (out,) = ins, outs
        first_row = lax.axis_index("col") * row_count
        row_ids = lax.broadcasted_iota(jnp.int32, (row_count, tiles), 0) + first_row
        row_tile = lax.broadcasted_iota(jnp.int32, (row_count, tiles), 1)
        row_pick = ((row_ids >= row_tile * tile) & (row_ids < (row_tile + 1) * tile)).astype(F32).astype(BF16)
        col_ids = lax.broadcasted_iota(jnp.int32, (tiles, width), 1)
        col_tile = lax.broadcasted_iota(jnp.int32, (tiles, width), 0)
        col_pick = ((col_ids >= col_tile * tile) & (col_ids < (col_tile + 1) * tile)).astype(F32).astype(BF16)
        high = rhs_ref[...].astype(BF16)
        out[:, levels * width : levels * width + rhs_count] = high
        out[:, levels * width + rhs_count :] = (rhs_ref[...] - high.astype(F32)).astype(BF16)
        masks = []
        for k in range(levels):
            kept = mm(row_pick, pattern_ref[0, k].astype(F32).astype(BF16)).astype(BF16)
            masks.append(mm(kept, col_pick).astype(BF16))
        ready()
        for k in range(levels):
            block = panels[k][...] * masks[k]
            if k == last:
                block = jnp.where(height() == 0, block, inv_ref[...])
            out[:, k * width : (k + 1) * width] = block

    slots = [Columns(panel[0, k], 0, width) for k in range(levels)]
    rows_own = call(
        build, ((row_count, full), BF16), [after(rhs[0], give), pattern, inverse_own, *slots]
    )
    rows_own = after(rows_own, got)
    rows_far = across(rows_own, 1, range(members))
    rows_lanes = [across(rows_own, 2 * i, inner) for i in range(1, lanes)]
    chip_part = (keep.astype(F32) + got.astype(F32)).astype(BF16)
    terms = over_chips(chip_part)

    def factors(array, k, count=1):
        return Columns(array, k * width, count * width)

    def inverses(array):
        return Columns(array, last * width, width)

    def leaf_push(ready, ins, outs):
        solved = chip_total(ins[:chips]).astype(BF16)
        outs[0][...] = solved
        ready()
        for k in range(levels):
            for j in range(2):
                product = mmt(solved, ins[chips + j][:, k * width : (k + 1) * width]).astype(BF16)
                for i in range(lanes):
                    outs[1 + i][k, j] = product[i * group : (i + 1) * group]

    message = ((levels, 2, group, row_count), BF16)
    vector = ((blocks, group, row_count), F32)
    term = ((group, width), BF16)
    leaf_pair = [factors(rows_own, 0, levels), factors(rows_far, 0, levels)]
    leaf_half, *pushed = call(leaf_push, [((half, width), BF16)] + [message] * lanes, [*terms, *leaf_pair])
    sides = child_links(1, members)
    arrived = [along(pushed[i], links, 2 * i) for i in range(lanes) for links in sides]

    inner_rows = [rows_own, rows_far]
    for near in rows_lanes:
        inner_rows += [near, across(after(near, *arrived), 1, inner)]

    samples = {}
    for section in range(1, levels + 1):
        remain = levels - section
        count = len(arrived)

        def inner_first(ready, ins, outs):
            came, rows_of = ins[:count], ins[count:]

            def total(k, b):
                if section == 1:
                    pair = came[b // 2 * 2 : b // 2 * 2 + 2]
                    return pair[0][k, b % 2].astype(F32) + pair[1][k, b % 2].astype(F32)
                return total_of([ref[k, b].astype(F32) for ref in came])

            for k in range(remain):
                for b in range(blocks):
                    outs[1][k, b] = total(k + 1, b)
            own = lax.broadcasted_iota(jnp.int32, (group, rhs_count), 0) + place()[3] * group
            pick = (lax.broadcasted_iota(jnp.int32, (group, rhs_count), 1) == own).astype(F32).astype(BF16)
            ready()
            parts = []
            for b in range(blocks):
                both = rows_of[b][:, width:]
                side = mmt(pick, both[:, :rhs_count]) + mmt(pick, both[:, rhs_count:])
                parts.append(mm((side - total(0, b)).astype(BF16), rows_of[b][:, :width]))
            outs[0][...] = total_of(parts).astype(BF16)

        outs = [term] + ([((remain, blocks, group, row_count), F32)] if remain else [])
        own_term, *rest = call(
            inner_first,
            outs,
            [*arrived, *[Columns(rows, last * width, width + 2 * rhs_count) for rows in inner_rows]],
        )
        terms = over_rows(own_term, nodes_at[section])
        if section == 1:
            leaf_far = across(after(leaf_half, own_term), 1, leaves)
        if remain:

            def inner_push(ready, ins, outs):
                solved = row_total(ins[:chip_rows])
                more, rows_of = ins[chip_rows], ins[chip_rows + 1 :]
                outs[0][...] = solved
                short = solved.astype(BF16)
                ready()
                for k in range(remain):
                    for b in range(blocks):
                        product = mmt(short, rows_of[b][:, k * width : (k + 1) * width])
                        outs[1][k, b] = (more[k, b] + product).astype(BF16)

            samples[section], sent = call(
                inner_push,
                [((group, width), F32), ((remain, blocks, group, row_count), BF16)],
                [*terms, *rest, *[factors(rows, 0, remain) for rows in inner_rows]],
            )
            arrived = [along(sent, links) for links in child_links(section + 1, members)]

    def root_back(ready, ins, outs):
        solved = row_total(ins[:chip_rows])
        outs[0][...] = solved
        short = solved.astype(BF16)
        ready()
        for b in range(blocks):
            answer = mmt(short, ins[chip_rows + b][...])
            outs[1][b] = answer
            outs[2][0, b] = answer.astype(BF16)

    samples[levels], answer, sent = call(
        root_back,
        [((group, width), F32), vector, ((1, blocks, group, row_count), BF16)],
        [*terms, *[inverses(rows) for rows in inner_rows]],
    )

    def split_rows(ready, ins, outs):
        rank = height()
        solved = ins[0][...]
        for s in range(2, levels + 1):
            solved = jnp.where(rank == s, ins[s - 1][...], solved)
        high = solved.astype(BF16)
        stacked = jnp.concatenate([high, (solved - high.astype(F32)).astype(BF16)], axis=0)
        row, lane, core, _ = place()
        for b in range(blocks):
            start = (row * blocks + (b ^ (lane * 2 + core))) * row_count
            at = lax.broadcasted_iota(jnp.int32, (row_count, width), 0) + start
            pick = (lax.broadcasted_iota(jnp.int32, (row_count, width), 1) == at).astype(F32).astype(BF16)
            both = mmt(stacked, pick)
            outs[0][b] = both[:group] + both[group:]

    for section in range(levels - 1, 0, -1):
        remain = levels - section
        ancestry = total_of([along(sent, down(links)) for links in child_links(section + 1, members)])

        def adjoint_first(ready, ins, outs):
            ready()
            parts = []
            for b in range(blocks):
                for k in range(remain):
                    parts.append(mm(ins[0][k, b], ins[1 + b][:, k * width : (k + 1) * width]))
            outs[0][...] = total_of(parts).astype(BF16)

        own_term = call(adjoint_first, term, [ancestry, *[factors(rows, 0, remain) for rows in inner_rows]])
        terms = over_rows(own_term, nodes_at[section])
        if section == 1:
            order = [after(samples[s], own_term) for s in range(1, levels + 1)]
            sample_rows = call(split_rows, vector, order)

        def inner_back(ready, ins, outs):
            came, ins = ins[:chip_rows], ins[chip_rows:]
            (solved, anc, higher), rows_of = ins[:3], ins[3 : 3 + blocks]
            back = (solved[...] - row_total(came)).astype(BF16)
            rank = height()
            ready()
            for b in range(blocks):
                mine = mmt(back, rows_of[b][...])
                if section > 1:
                    outs[0][b] = jnp.where(rank == section, mine, higher[b])
                    outs[1][0, b] = mine.astype(BF16)
                    for k in range(remain):
                        outs[1][k + 1, b] = anc[k, b]
                else:
                    outs[b // 2][0, b % 2] = mine.astype(BF16)
                    for k in range(remain):
                        outs[b // 2][k + 1, b % 2] = anc[k, b]
                    outs[lanes + b][0] = ins[-1][b]
                    outs[lanes + b][1] = jnp.where(rank == 1, mine, higher[b])

        args = [*terms, samples[section], ancestry, answer, *[inverses(rows) for rows in inner_rows]]
        if section > 1:
            answer, sent = call(
                inner_back, [vector, ((remain + 1, blocks, group, row_count), BF16)], args
            )
        else:
            outs = [message] * lanes + [((2, group, row_count), F32)] * blocks
            results = call(inner_back, outs, [*args, sample_rows])
            sent, results = results[:lanes], results[lanes:]

    arrived = [along(sent[i], down(links), 2 * i) for i in range(lanes) for links in sides]

    def leaf_adjoint(ready, ins, outs):
        came, pair = ins[:-2], ins[-2:]
        ready()
        parts = []
        for k in range(levels):
            for j in range(2):
                anc = [came[2 * i][k, j] + came[2 * i + 1][k, j] for i in range(lanes)]
                parts.append(mm(jnp.concatenate(anc, axis=0), pair[j][:, k * width : (k + 1) * width]))
        outs[0][...] = total_of(parts).astype(BF16)

    own_term = call(leaf_adjoint, ((half, width), BF16), [*arrived, *leaf_pair])
    terms = over_chips(own_term)

    def in_order(near, far, whole):
        for b in range(blocks):
            source = near if b < lanes else far
            whole[groups(b), :] = source[b % lanes * group : (b % lanes + 1) * group, :]

    def leaf_rows(ready, ins, outs, whole):
        in_order(ins[0], ins[1], whole)
        at = lax.broadcasted_iota(jnp.int32, (row_count, width), 0) + lax.axis_index("col") * row_count
        pick = (lax.broadcasted_iota(jnp.int32, (row_count, width), 1) == at).astype(F32).astype(BF16)
        outs[0][...] = mmt(pick, whole[...])

    whole_half = [pltpu.VMEM((rhs_count, width), BF16)]
    leaf_sample = call(leaf_rows, ((row_count, rhs_count), F32), [leaf_half, leaf_far], whole_half)

    parts = [results[0]] + [across(results[b], b, inner) for b in range(1, blocks)]

    def join_groups(ready, ins, outs, whole):
        for n in range(2):
            for b in range(blocks):
                whole[groups(b % 2 * lanes + b // 2), :] = ins[b][n]
            outs[n][...] = whole[...].T

    shape = ((row_count, rhs_count), F32)
    inner_sample, inner_answer = call(
        join_groups, [shape] * 2, parts, [pltpu.VMEM((rhs_count, row_count), F32)]
    )

    def leaf_back(ready, ins, outs):
        outs[0][...] = (ins[chips][...].astype(F32) - chip_total(ins[:chips])).astype(BF16)

    terms[0] = after(terms[0], inner_sample, inner_answer, leaf_sample)
    back = call(leaf_back, ((half, width), BF16), [*terms, leaf_half])
    back_far = across(back, 1, leaves)

    def leaf_last(ready, ins, outs, whole):
        in_order(ins[0], ins[1], whole)
        is_leaf = height() == 0
        outs[0][...] = jnp.where(is_leaf, ins[2][...], ins[3][...])
        ready()
        outs[1][...] = jnp.where(is_leaf, mmt(ins[5][...], whole[...]), ins[4][...])

    sample, answer = call(
        leaf_last,
        [shape] * 2,
        [back, back_far, leaf_sample, inner_sample, inner_answer, inverse_own],
        whole_half,
    )
    return (sample[None], answer[None])


def solution(mesh):
    in_specs = (
        P("lvl", "col", None),
        P("lvl", None, "col", None),
        P("lvl", "col", None),
        P("lvl", None, None, None),
    )
    out_specs = (P("lvl", "col", None), P("lvl", "col", None))
    return jax.shard_map(
        on_device, mesh=mesh, in_specs=in_specs, out_specs=out_specs, check_vma=False
    )
```

time: 171 us -> 115 us (0.67)
  waiting for transfers between devices: 124 us -> 55.2 us
  Pallas kernels: 0 us -> 14.1 us
  starting transfers between devices: 29.1 us -> 40.3 us
  matrix products: 9.83 us -> 0 us
  other arithmetic: 5.28 us -> 0.05 us
    ppermute x32 -> x28, waiting for transfers between devices: 124 us -> 55.2 us  [the longest x10 46.1 us: along(): return lax.ppermute(x, ('lvl', 'col'), pairs)]
    pallas_call x0 -> x15, Pallas kernels: none -> 14.1 us  [call(): pl.pallas_call(kernel, out_shape=[jax.ShapeDtypeStruct(shape, dtype) for...]
    ppermute x32 -> x28, starting transfers between devices: 29.1 us -> 40.3 us  [the longest x18 31.2 us: across(): return lax.ppermute(x, ('lvl', 'col'), pairs)]
    dot_general x10 -> x0, matrix products: 9.83 us -> none  [the longest x3 3.9 us: down_solve(): jnp.einsum('ri,rn->ni', inverse, residual.astype(BF16), preferred_element...]
    convert_element_type x11 -> x1, other arithmetic: 3.21 us -> 0.05 us  [on_device(): chip_part = (keep.astype(F32) + got.astype(F32)).astype(BF16)]
  transfers between devices with their start and end apart: 32 -> 28, of which waited for: 22 -> 9; matrix products, arithmetic and copies ran while one was open for 2% -> 1% of each run, Pallas kernels for 0% -> 5%
where the time goes in v3:
time: 115 us; the launch traced here: 114 us
  waiting for transfers between devices  55.2 us (48%)
  starting transfers between devices  40.3 us (35%)
  Pallas kernels  14.1 us (12%)
  local copies, waits for them, and re-layouts  3.29 us (3%)
    ppermute x10, waiting for transfers between devices, along(): return lax.ppermute(x, ('lvl', 'col'), pairs)  46.1 us
    ppermute x18, starting transfers between devices, across(): return lax.ppermute(x, ('lvl', 'col'), pairs)  31.2 us
    pallas_call x15, Pallas kernels, call(): pl.pallas_call(kernel, out_shape=[jax.ShapeDtypeStruct(shape, dtype) for...  14.1 us
    ppermute x18, waiting for transfers between devices, across(): return lax.ppermute(x, ('lvl', 'col'), pairs)  9.18 us
    ppermute x10, starting transfers between devices, along(): return lax.ppermute(x, ('lvl', 'col'), pairs)  9.16 us
  transfers between devices with their start and end apart: 28, of which 9 were waited for; matrix products, arithmetic and copies ran while one was open for 1% of the time, Pallas kernels for 5%

profile of v3, /device:TPU:0, one launch (start us, length us, event | category | flops | bytes accessed | tf_op | source)
XLA Modules:
  0.0 114.1 jit_solution(5760646362517491306)
XLA Ops:
  0.6 0.0 copy-start
  0.6 1.1 copy-done
  1.7 0.9 copy-done.2
  2.6 0.6 shard_map.59
  3.2 0.0 copy-start.3
  3.2 2.4 %collective-permute-start = (bf16[64,1536]{1,0:T(8,128)(2,1)S(1)}, bf16[64,1536]{1,0:T(8,128)(2,1)S(1)}, u32[]{:S(2)}, u32[]{:S(2)}) collective-permute-start(bf16[64,1536]{1,0:T(8,128)(2,1)S(1)} %get-tuple-element.32), channel_id=1, source_target_pairs={{0,1},{1,0},{2,3},{3,2},{4,5},{5,4},{6,7},{7,6},{16,17},{17,16},{1... | collective-permute-start | bytes 589832 | tf_op jit(solution)/shard_map/ppermute | solution.py:123
  5.6 1.3 %slice_bitcast_fusion = (bf16[192,1536]{1,0:T(8,128)(2,1)S(1)}, bf16[192,1536]{1,0:T(8,128)(2,1)S(1)}) fusion(bf16[1,2,192,1536]{3,2,1,0:T(8,128)(2,1)} %param.5), kind=kLoop, calls=%fused_computation | loop fusion | bytes 2359296 | tf_op jit(solution)/shard_map/squeeze | solution.py:213
  6.9 1.3 %shard_map.60.refs_4_.refs_3_.refs_1_.refs_2_.refs_5_ = bf16[192,3328]{1,0:T(8,128)(2,1)S(1)} custom-call(f32[192,128]{1,0:T(8,128)S(1)} %bitcast.12, s32[1,2,12,12]{3,2,1,0:T(8,128)S(1)} %copy.6.refs_1_, bf16[192,1536]{1,0:T(8,128)(2,1)S(1)} %bitcast.9, bf16[192,1536]{1,0:T(8,128)(2,1)S(1)} %get-tuple-element.61.refs_3_, ...), custom_call_target="tpu_custom_call" | custom-call | flops 268435456 | bytes 1868928 | tf_op jit(solution)/shard_map/pallas_call | solution.py:81
  8.2 0.0 collective-permute-done
  8.2 0.1 collective-permute-start.4
  8.3 0.7 collective-permute-start.9
  9.1 5.8 %collective-permute-start.3 = (bf16[64,1536]{1,0:T(8,128)(2,1)S(1)}, bf16[64,1536]{1,0:T(8,128)(2,1)S(1)}, u32[]{:S(2)}, u32[]{:S(2)}) collective-permute-start(bf16[64,1536]{1,0:T(8,128)(2,1)S(1)} %add_convert_fusion.refs_0_), channel_id=1, source_target_pairs={{0,6},{1,7},{2,4},{3,5},{4,2},{5,3},{6,0},{7,1},{16,22},{17,23},{1... | collective-permute-start | bytes 589832 | tf_op jit(solution)/shard_map/ppermute | solution.py:123
  15.0 2.4 %collective-permute-start.2 = (bf16[64,1536]{1,0:T(8,128)(2,1)S(1)}, bf16[64,1536]{1,0:T(8,128)(2,1)S(1)}, u32[]{:S(2)}, u32[]{:S(2)}) collective-permute-start(bf16[64,1536]{1,0:T(8,128)(2,1)S(1)} %add_convert_fusion.refs_0_), channel_id=1, source_target_pairs={{0,4},{1,5},{2,6},{3,7},{4,0},{5,1},{6,2},{7,3},{16,20},{17,21},{1... | collective-permute-start | bytes 589832 | tf_op jit(solution)/shard_map/ppermute | solution.py:123
  17.4 2.0 %collective-permute-start.1 = (bf16[64,1536]{1,0:T(8,128)(2,1)S(1)}, bf16[64,1536]{1,0:T(8,128)(2,1)S(1)}, u32[]{:S(2)}, u32[]{:S(2)}) collective-permute-start(bf16[64,1536]{1,0:T(8,128)(2,1)S(1)} %add_convert_fusion.refs_0_), channel_id=1, source_target_pairs={{0,2},{1,3},{2,0},{3,1},{4,6},{5,7},{6,4},{7,5},{16,18},{17,19},{1... | collective-permute-start | bytes 589832 | tf_op jit(solution)/shard_map/ppermute | solution.py:123
  19.4 0.8 collective-permute-done.3.refs_3_
  20.1 4.1 %collective-permute-done.2.refs_2_ = bf16[64,1536]{1,0:T(8,128)(2,1)S(1)} collective-permute-done((bf16[64,1536]{1,0:T(8,128)(2,1)S(1)}, bf16[64,1536]{1,0:T(8,128)(2,1)S(1)}, u32[]{:S(2)}, u32[]{:S(2)}) %collective-permute-start.2) | collective-permute-done | bytes 196640 | tf_op jit(solution)/shard_map/ppermute | solution.py:123
  24.2 1.3 %collective-permute-done.1.refs_1_ = bf16[64,1536]{1,0:T(8,128)(2,1)S(1)} collective-permute-done((bf16[64,1536]{1,0:T(8,128)(2,1)S(1)}, bf16[64,1536]{1,0:T(8,128)(2,1)S(1)}, u32[]{:S(2)}, u32[]{:S(2)}) %collective-permute-start.1) | collective-permute-done | bytes 196640 | tf_op jit(solution)/shard_map/ppermute | solution.py:123
  25.5 1.2 %shard_map.61 = (bf16[64,1536]{1,0:T(8,128)(2,1)S(1)}, bf16[2,2,32,192]{3,2,1,0:T(8,128)(2,1)S(1)}, bf16[2,2,32,192]{3,2,1,0:T(8,128)(2,1)S(1)}) custom-call(bf16[64,1536]{1,0:T(8,128)(2,1)S(1)} %add_convert_fusion.refs_0_, bf16[64,1536]{1,0:T(8,128)(2,1)S(1)} %collective-permute-done.1.refs_1_, bf16[64,1536]{1,0:T(8,128)(2,1)S(1)} %collective-permute-done.2.refs_2_, ...), custom_call_target="tpu_custom_call" | custom-call | flops 268435456 | bytes 3342336 | tf_op jit(solution)/shard_map/pallas_call | solution.py:81
  26.8 0.7 collective-permute-start.6
  27.4 1.3 %collective-permute-start.5 = (bf16[2,2,32,192]{3,2,1,0:T(8,128)(2,1)S(1)}, bf16[2,2,32,192]{3,2,1,0:T(8,128)(2,1)S(1)}, u32[]{:S(2)}, u32[]{:S(2)}) collective-permute-start(bf16[2,2,32,192]{3,2,1,0:T(8,128)(2,1)S(1)} %get-tuple-element.35), channel_id=1, source_target_pairs={{0,8},{1,9},{2,10},{3,11},{4,12},{5,13},{6,14},{7,15}} | collective-permute-start | bytes 147464 | tf_op jit(solution)/shard_map/ppermute | solution.py:127
  28.7 0.7 collective-permute-start.8
  29.4 1.3 %collective-permute-start.7 = (bf16[2,2,32,192]{3,2,1,0:T(8,128)(2,1)S(1)}, bf16[2,2,32,192]{3,2,1,0:T(8,128)(2,1)S(1)}, u32[]{:S(2)}, u32[]{:S(2)}) collective-permute-start(bf16[2,2,32,192]{3,2,1,0:T(8,128)(2,1)S(1)} %get-tuple-element.36), channel_id=1, source_target_pairs={{0,10},{1,11},{2,8},{3,9},{4,14},{5,15},{6,12},{7,13}} | collective-permute-start | bytes 147464 | tf_op jit(solution)/shard_map/ppermute | solution.py:127
  30.7 0.0 collective-permute-done.6.refs_1_
  30.7 0.3 collective-permute-done.5.refs_0_
  31.0 0.0 collective-permute-done.8.refs_3_
  31.0 1.6 %collective-permute-done.7.refs_2_ = bf16[2,2,32,192]{3,2,1,0:T(8,128)(2,1)S(1)} collective-permute-done((bf16[2,2,32,192]{3,2,1,0:T(8,128)(2,1)S(1)}, bf16[2,2,32,192]{3,2,1,0:T(8,128)(2,1)S(1)}, u32[]{:S(2)}, u32[]{:S(2)}) %collective-permute-start.7) | collective-permute-done | bytes 49184 | tf_op jit(solution)/shard_map/ppermute | solution.py:127
  32.6 0.7 collective-permute-start.10
  33.3 0.0 collective-permute-done.10.refs_7_.refs_6_.refs_4_.refs_5_.refs_8_
  33.3 1.5 %shard_map.62 = (bf16[32,1536]{1,0:T(8,128)(2,1)S(1)}, f32[1,4,32,192]{3,2,1,0:T(8,128)S(1)}) custom-call(bf16[2,2,32,192]{3,2,1,0:T(8,128)(2,1)S(1)} %collective-permute-done.5.refs_0_, bf16[2,2,32,192]{3,2,1,0:T(8,128)(2,1)S(1)} %collective-permute-done.6.refs_1_, bf16[2,2,32,192]{3,2,1,0:T(8,128)(2,1)S(1)} %collective-permute-done.7.refs_2_, ...), custom_call_target="tpu_custom_call" | custom-call | flops 268435456 | bytes 5308416 | tf_op jit(solution)/shard_map/pallas_call | solution.py:81
  34.9 0.7 collective-permute-start.11
  35.6 1.2 %shard_map.63 = (f32[32,1536]{1,0:T(8,128)S(1)}, bf16[1,4,32,192]{3,2,1,0:T(8,128)(2,1)S(1)}) custom-call(bf16[32,1536]{1,0:T(8,128)(2,1)S(1)} %get-tuple-element.38.refs_0_, bf16[32,1536]{1,0:T(8,128)(2,1)S(1)} %collective-permute-done.11.refs_1_, f32[1,4,32,192]{3,2,1,0:T(8,128)S(1)} %get-tuple-element.39.refs_2_, ...), custom_call_target="tpu_custom_call" | custom-call | flops 268435456 | bytes 5406720 | tf_op jit(solution)/shard_map/pallas_call | solution.py:81
  36.8 0.7 collective-permute-start.12
  37.4 0.0 collective-permute-done.12.refs_0_
  37.4 1.5 %shard_map.64.refs_0_ = bf16[32,1536]{1,0:T(8,128)(2,1)S(1)} custom-call(bf16[1,4,32,192]{3,2,1,0:T(8,128)(2,1)S(1)} %collective-permute-done.12.refs_0_, bf16[192,3328]{1,0:T(8,128)(2,1)S(1)} %shard_map.60.refs_4_.refs_3_.refs_1_.refs_2_.refs_5_, bf16[192,3328]{1,0:T(8,128)(2,1)S(1)} %collective-permute-done.4.refs_5_.refs_4_.refs_2_.refs_3_.refs_6_, ...), custom_call_target="tpu_custom_call" | custom-call | flops 268435456 | bytes 5160960 | tf_op jit(solution)/shard_map/pallas_call | solution.py:81
  39.0 0.7 collective-permute-start.13
  39.7 1.2 %shard_map.65 = (f32[32,1536]{1,0:T(8,128)S(1)}, f32[4,32,192]{2,1,0:T(8,128)S(1)}, bf16[1,4,32,192]{3,2,1,0:T(8,128)(2,1)S(1)}) custom-call(bf16[32,1536]{1,0:T(8,128)(2,1)S(1)} %shard_map.64.refs_0_, bf16[32,1536]{1,0:T(8,128)(2,1)S(1)} %collective-permute-done.13.refs_1_, bf16[192,3328]{1,0:T(8,128)(2,1)S(1)} %shard_map.60.refs_4_.refs_3_.refs_1_.refs_2_.refs_5_, ...), custom_call_target="tpu_custom_call" | custom-call | flops 268435456 | bytes 5308416 | tf_op jit(solution)/shard_map/pallas_call | solution.py:81
  40.9 0.7 collective-permute-start.14
  41.6 0.9 shard_map.66.refs_0_
  42.4 0.7 collective-permute-start.15
  43.1 1.9 %collective-permute-start.23 = (bf16[64,1536]{1,0:T(8,128)(2,1)S(1)}, bf16[64,1536]{1,0:T(8,128)(2,1)S(1)}, u32[]{:S(2)}, u32[]{:S(2)}) collective-permute-start(bf16[64,1536]{1,0:T(8,128)(2,1)S(1)} %get-tuple-element.56.refs_0_.refs_4_), channel_id=1, source_target_pairs={{0,1},{1,0},{2,3},{3,2},{4,5},{5,4},{6,7},{7,6},{16,17},{17,16},{1... | collective-permute-start | bytes 589832 | tf_op jit(solution)/shard_map/ppermute | solution.py:123
  45.1 0.9 shard_map.67.refs_9_
  45.9 0.0 collective-permute-done.15.refs_1_
  46.0 1.2 %shard_map.68 = (bf16[2,2,32,192]{3,2,1,0:T(8,128)(2,1)S(1)}, bf16[2,2,32,192]{3,2,1,0:T(8,128)(2,1)S(1)}, f32[2,32,192]{2,1,0:T(8,128)S(1)}, f32[2,32,192]{2,1,...) custom-call(bf16[32,1536]{1,0:T(8,128)(2,1)S(1)} %shard_map.66.refs_0_, ...), custom_call_target="tpu_custom_call" | custom-call | flops 268435456 | bytes 5750784 | tf_op jit(solution)/shard_map/pallas_call | solution.py:81
  47.2 0.7 collective-permute-start.17
  47.8 1.3 %collective-permute-start.16 = (bf16[2,2,32,192]{3,2,1,0:T(8,128)(2,1)S(1)}, bf16[2,2,32,192]{3,2,1,0:T(8,128)(2,1)S(1)}, u32[]{:S(2)}, u32[]{:S(2)}) collective-permute-start(bf16[2,2,32,192]{3,2,1,0:T(8,128)(2,1)S(1)} %get-tuple-element.47), channel_id=1, source_target_pairs={{8,0},{9,1},{10,2},{11,3},{12,4},{13,5},{14,6},{15,7}} | collective-permute-start | bytes 147464 | tf_op jit(solution)/shard_map/ppermute | solution.py:127
  49.1 0.7 collective-permute-start.19
  49.8 1.3 %collective-permute-start.18 = (bf16[2,2,32,192]{3,2,1,0:T(8,128)(2,1)S(1)}, bf16[2,2,32,192]{3,2,1,0:T(8,128)(2,1)S(1)}, u32[]{:S(2)}, u32[]{:S(2)}) collective-permute-start(bf16[2,2,32,192]{3,2,1,0:T(8,128)(2,1)S(1)} %get-tuple-element.48), channel_id=1, source_target_pairs={{8,2},{9,3},{10,0},{11,1},{12,6},{13,7},{14,4},{15,5}} | collective-permute-start | bytes 147464 | tf_op jit(solution)/shard_map/ppermute | solution.py:127
  51.1 40.7 %collective-permute-done.16.refs_0_ = bf16[2,2,32,192]{3,2,1,0:T(8,128)(2,1)S(1)} collective-permute-done((bf16[2,2,32,192]{3,2,1,0:T(8,128)(2,1)S(1)}, bf16[2,2,32,192]{3,2,1,0:T(8,128)(2,1)S(1)}, u32[]{:S(2)}, u32[]{:S(2)}) %collective-permute-start.16) | collective-permute-done | bytes 49184 | tf_op jit(solution)/shard_map/ppermute | solution.py:127
  91.8 3.5 %collective-permute-done.18.refs_2_ = bf16[2,2,32,192]{3,2,1,0:T(8,128)(2,1)S(1)} collective-permute-done((bf16[2,2,32,192]{3,2,1,0:T(8,128)(2,1)S(1)}, bf16[2,2,32,192]{3,2,1,0:T(8,128)(2,1)S(1)}, u32[]{:S(2)}, u32[]{:S(2)}) %collective-permute-start.18) | collective-permute-done | bytes 49184 | tf_op jit(solution)/shard_map/ppermute | solution.py:127
  95.3 0.8 shard_map.69.refs_0_
  96.1 3.4 %collective-permute-start.26 = (bf16[64,1536]{1,0:T(8,128)(2,1)S(1)}, bf16[64,1536]{1,0:T(8,128)(2,1)S(1)}, u32[]{:S(2)}, u32[]{:S(2)}) collective-permute-start(bf16[64,1536]{1,0:T(8,128)(2,1)S(1)} %shard_map.69.refs_0_), channel_id=1, source_target_pairs={{0,6},{1,7},{2,4},{3,5},{4,2},{5,3},{6,0},{7,1},{16,22},{17,23},{1... | collective-permute-start | bytes 589832 | tf_op jit(solution)/shard_map/ppermute | solution.py:123
  99.5 2.4 %collective-permute-start.25 = (bf16[64,1536]{1,0:T(8,128)(2,1)S(1)}, bf16[64,1536]{1,0:T(8,128)(2,1)S(1)}, u32[]{:S(2)}, u32[]{:S(2)}) collective-permute-start(bf16[64,1536]{1,0:T(8,128)(2,1)S(1)} %shard_map.69.refs_0_), channel_id=1, source_target_pairs={{0,4},{1,5},{2,6},{3,7},{4,0},{5,1},{6,2},{7,3},{16,20},{17,21},{1... | collective-permute-start | bytes 589832 | tf_op jit(solution)/shard_map/ppermute | solution.py:123
  101.9 3.4 %collective-permute-start.24 = (bf16[64,1536]{1,0:T(8,128)(2,1)S(1)}, bf16[64,1536]{1,0:T(8,128)(2,1)S(1)}, u32[]{:S(2)}, u32[]{:S(2)}) collective-permute-start(bf16[64,1536]{1,0:T(8,128)(2,1)S(1)} %shard_map.69.refs_0_), channel_id=1, source_target_pairs={{0,2},{1,3},{2,0},{3,1},{4,6},{5,7},{6,4},{7,5},{16,18},{17,19},{1... | collective-permute-start | bytes 589832 | tf_op jit(solution)/shard_map/ppermute | solution.py:123
  105.3 0.7 collective-permute-start.20
  106.0 0.7 collective-permute-start.21
  106.7 0.7 collective-permute-start.22
  107.4 0.4 shard_map.71.refs_2_
  107.7 0.0 copy-start.1
  107.8 0.2 shard_map.70
  107.9 1.5 %collective-permute-done.24.refs_1_ = bf16[64,1536]{1,0:T(8,128)(2,1)S(1)} collective-permute-done((bf16[64,1536]{1,0:T(8,128)(2,1)S(1)}, bf16[64,1536]{1,0:T(8,128)(2,1)S(1)}, u32[]{:S(2)}, u32[]{:S(2)}) %collective-permute-start.24) | collective-permute-done | bytes 196640 | tf_op jit(solution)/shard_map/ppermute | solution.py:123
  109.5 0.1 shard_map.72.refs_0_
  109.6 1.9 %collective-permute-start.27 = (bf16[64,1536]{1,0:T(8,128)(2,1)S(1)}, bf16[64,1536]{1,0:T(8,128)(2,1)S(1)}, u32[]{:S(2)}, u32[]{:S(2)}) collective-permute-start(bf16[64,1536]{1,0:T(8,128)(2,1)S(1)} %shard_map.72.refs_0_), channel_id=1, source_target_pairs={{0,1},{1,0},{2,3},{3,2},{4,5},{5,4},{6,7},{7,6},{16,17},{17,16},{1... | collective-permute-start | bytes 589832 | tf_op jit(solution)/shard_map/ppermute | solution.py:123
  111.5 1.4 %collective-permute-done.27.refs_1_ = bf16[64,1536]{1,0:T(8,128)(2,1)S(1)} collective-permute-done((bf16[64,1536]{1,0:T(8,128)(2,1)S(1)}, bf16[64,1536]{1,0:T(8,128)(2,1)S(1)}, u32[]{:S(2)}, u32[]{:S(2)}) %collective-permute-start.27) | collective-permute-done | bytes 196640 | tf_op jit(solution)/shard_map/ppermute | solution.py:123
  113.0 1.1 %shard_map.73 = (f32[192,128]{1,0:T(8,128)}, f32[192,128]{1,0:T(8,128)}) custom-call(bf16[64,1536]{1,0:T(8,128)(2,1)S(1)} %shard_map.72.refs_0_, bf16[64,1536]{1,0:T(8,128)(2,1)S(1)} %collective-permute-done.27.refs_1_, f32[192,128]{1,0:T(8,128)S(1)} %shard_map.71.refs_2_, f32[192,128]{1,0:T(8,128)S(1)} %get-tuple-element.53.refs_3_, ...), custom_call_target="tpu_custom_call" | custom-call | flops 268435456 | bytes 1277952 | tf_op jit(solution)/shard_map/pallas_call | solution.py:81
  (18 shorter events, 0.1 us)
Async XLA Ops:
  0.6 1.1 copy-start
  1.7 0.9 copy-start.2
  3.2 3.7 %copy-start.3 = (s32[1,2,12,12]{3,1,2,0:T(2,128)S(1)}, s32[1,2,12,12]{3,1,2,0:T(2,128)}, u32[]{:S(2)}) copy-start(s32[1,2,12,12]{3,1,2,0:T(2,128)} %param.7) | copy-start | bytes 3460
  3.2 5.0 %collective-permute-start = (bf16[64,1536]{1,0:T(8,128)(2,1)S(1)}, bf16[64,1536]{1,0:T(8,128)(2,1)S(1)}, u32[]{:S(2)}, u32[]{:S(2)}) collective-permute-start(bf16[64,1536]{1,0:T(8,128)(2,1)S(1)} %get-tuple-element.32), channel_id=1, source_target_pairs={{0,1},{1,0},{2,3},{3,2},{4,5},{5,4},{6,7},{7,6},{16,17},{17,16},{1... | collective-permute-start | bytes 589832 | tf_op jit(solution)/shard_map/ppermute | solution.py:123
  8.2 17.3 %collective-permute-start.4 = (bf16[192,3328]{1,0:T(8,128)(2,1)S(1)}, bf16[192,3328]{1,0:T(8,128)(2,1)S(1)}, u32[]{:S(2)}, u32[]{:S(2)}) collective-permute-start(bf16[192,3328]{1,0:T(8,128)(2,1)S(1)} %shard_map.60.refs_4_.refs_3_.refs_1_.refs_2_.refs_5_), channel_id=1, source_target_pairs={{0,1},{1,0},{2,3},{3,2},{4,5},{5,4},{6,7},{7,6},{8,9},{9,8},{10,11... | collective-permute-start | bytes 3833864 | tf_op jit(solution)/shard_map/ppermute | solution.py:123
  8.3 22.4 %collective-permute-start.9 = (bf16[192,3328]{1,0:T(8,128)(2,1)S(1)}, bf16[192,3328]{1,0:T(8,128)(2,1)S(1)}, u32[]{:S(2)}, u32[]{:S(2)}) collective-permute-start(bf16[192,3328]{1,0:T(8,128)(2,1)S(1)} %shard_map.60.refs_4_.refs_3_.refs_1_.refs_2_.refs_5_), channel_id=1, source_target_pairs={{8,10},{9,11},{10,8},{11,9},{12,14},{13,15},{14,12},{15,13},{24,26... | collective-permute-start | bytes 3833864 | tf_op jit(solution)/shard_map/ppermute | solution.py:123
  9.1 11.0 %collective-permute-start.3 = (bf16[64,1536]{1,0:T(8,128)(2,1)S(1)}, bf16[64,1536]{1,0:T(8,128)(2,1)S(1)}, u32[]{:S(2)}, u32[]{:S(2)}) collective-permute-start(bf16[64,1536]{1,0:T(8,128)(2,1)S(1)} %add_convert_fusion.refs_0_), channel_id=1, source_target_pairs={{0,6},{1,7},{2,4},{3,5},{4,2},{5,3},{6,0},{7,1},{16,22},{17,23},{1... | collective-permute-start | bytes 589832 | tf_op jit(solution)/shard_map/ppermute | solution.py:123
  15.0 9.3 %collective-permute-start.2 = (bf16[64,1536]{1,0:T(8,128)(2,1)S(1)}, bf16[64,1536]{1,0:T(8,128)(2,1)S(1)}, u32[]{:S(2)}, u32[]{:S(2)}) collective-permute-start(bf16[64,1536]{1,0:T(8,128)(2,1)S(1)} %add_convert_fusion.refs_0_), channel_id=1, source_target_pairs={{0,4},{1,5},{2,6},{3,7},{4,0},{5,1},{6,2},{7,3},{16,20},{17,21},{1... | collective-permute-start | bytes 589832 | tf_op jit(solution)/shard_map/ppermute | solution.py:123
  17.4 8.2 %collective-permute-start.1 = (bf16[64,1536]{1,0:T(8,128)(2,1)S(1)}, bf16[64,1536]{1,0:T(8,128)(2,1)S(1)}, u32[]{:S(2)}, u32[]{:S(2)}) collective-permute-start(bf16[64,1536]{1,0:T(8,128)(2,1)S(1)} %add_convert_fusion.refs_0_), channel_id=1, source_target_pairs={{0,2},{1,3},{2,0},{3,1},{4,6},{5,7},{6,4},{7,5},{16,18},{17,19},{1... | collective-permute-start | bytes 589832 | tf_op jit(solution)/shard_map/ppermute | solution.py:123
  26.8 4.0 %collective-permute-start.6 = (bf16[2,2,32,192]{3,2,1,0:T(8,128)(2,1)S(1)}, bf16[2,2,32,192]{3,2,1,0:T(8,128)(2,1)S(1)}, u32[]{:S(2)}, u32[]{:S(2)}) collective-permute-start(bf16[2,2,32,192]{3,2,1,0:T(8,128)(2,1)S(1)} %get-tuple-element.35), channel_id=1, source_target_pairs={{16,8},{17,9},{18,10},{19,11},{20,12},{21,13},{22,14},{23,15}} | collective-permute-start | bytes 147464 | tf_op jit(solution)/shard_map/ppermute | solution.py:127
  27.4 3.6 %collective-permute-start.5 = (bf16[2,2,32,192]{3,2,1,0:T(8,128)(2,1)S(1)}, bf16[2,2,32,192]{3,2,1,0:T(8,128)(2,1)S(1)}, u32[]{:S(2)}, u32[]{:S(2)}) collective-permute-start(bf16[2,2,32,192]{3,2,1,0:T(8,128)(2,1)S(1)} %get-tuple-element.35), channel_id=1, source_target_pairs={{0,8},{1,9},{2,10},{3,11},{4,12},{5,13},{6,14},{7,15}} | collective-permute-start | bytes 147464 | tf_op jit(solution)/shard_map/ppermute | solution.py:127
  28.7 2.3 %collective-permute-start.8 = (bf16[2,2,32,192]{3,2,1,0:T(8,128)(2,1)S(1)}, bf16[2,2,32,192]{3,2,1,0:T(8,128)(2,1)S(1)}, u32[]{:S(2)}, u32[]{:S(2)}) collective-permute-start(bf16[2,2,32,192]{3,2,1,0:T(8,128)(2,1)S(1)} %get-tuple-element.36), channel_id=1, source_target_pairs={{16,10},{17,11},{18,8},{19,9},{20,14},{21,15},{22,12},{23,13}} | collective-permute-start | bytes 147464 | tf_op jit(solution)/shard_map/ppermute | solution.py:127
  29.4 3.2 %collective-permute-start.7 = (bf16[2,2,32,192]{3,2,1,0:T(8,128)(2,1)S(1)}, bf16[2,2,32,192]{3,2,1,0:T(8,128)(2,1)S(1)}, u32[]{:S(2)}, u32[]{:S(2)}) collective-permute-start(bf16[2,2,32,192]{3,2,1,0:T(8,128)(2,1)S(1)} %get-tuple-element.36), channel_id=1, source_target_pairs={{0,10},{1,11},{2,8},{3,9},{4,14},{5,15},{6,12},{7,13}} | collective-permute-start | bytes 147464 | tf_op jit(solution)/shard_map/ppermute | solution.py:127
  32.6 0.7 collective-permute-start.10
  34.9 0.7 collective-permute-start.11
  36.8 0.7 collective-permute-start.12
  39.0 0.7 collective-permute-start.13
  40.9 0.7 collective-permute-start.14
  42.4 3.5 %collective-permute-start.15 = (bf16[32,1536]{1,0:T(8,128)(2,1)S(1)}, bf16[32,1536]{1,0:T(8,128)(2,1)S(1)}, u32[]{:S(2)}, u32[]{:S(2)}) collective-permute-start(bf16[32,1536]{1,0:T(8,128)(2,1)S(1)} %shard_map.66.refs_0_), channel_id=1, source_target_pairs={{8,12},{9,13},{10,14},{11,15},{12,8},{13,9},{14,10},{15,11}} | collective-permute-start | bytes 294920 | tf_op jit(solution)/shard_map/ppermute | solution.py:123
  43.1 62.9 %collective-permute-start.23 = (bf16[64,1536]{1,0:T(8,128)(2,1)S(1)}, bf16[64,1536]{1,0:T(8,128)(2,1)S(1)}, u32[]{:S(2)}, u32[]{:S(2)}) collective-permute-start(bf16[64,1536]{1,0:T(8,128)(2,1)S(1)} %get-tuple-element.56.refs_0_.refs_4_), channel_id=1, source_target_pairs={{0,1},{1,0},{2,3},{3,2},{4,5},{5,4},{6,7},{7,6},{16,17},{17,16},{1... | collective-permute-start | bytes 589832 | tf_op jit(solution)/shard_map/ppermute | solution.py:123
  47.2 3.9 %collective-permute-start.17 = (bf16[2,2,32,192]{3,2,1,0:T(8,128)(2,1)S(1)}, bf16[2,2,32,192]{3,2,1,0:T(8,128)(2,1)S(1)}, u32[]{:S(2)}, u32[]{:S(2)}) collective-permute-start(bf16[2,2,32,192]{3,2,1,0:T(8,128)(2,1)S(1)} %get-tuple-element.47), channel_id=1, source_target_pairs={{8,16},{9,17},{10,18},{11,19},{12,20},{13,21},{14,22},{15,23}} | collective-permute-start | bytes 147464 | tf_op jit(solution)/shard_map/ppermute | solution.py:127
  47.8 43.9 %collective-permute-start.16 = (bf16[2,2,32,192]{3,2,1,0:T(8,128)(2,1)S(1)}, bf16[2,2,32,192]{3,2,1,0:T(8,128)(2,1)S(1)}, u32[]{:S(2)}, u32[]{:S(2)}) collective-permute-start(bf16[2,2,32,192]{3,2,1,0:T(8,128)(2,1)S(1)} %get-tuple-element.47), channel_id=1, source_target_pairs={{8,0},{9,1},{10,2},{11,3},{12,4},{13,5},{14,6},{15,7}} | collective-permute-start | bytes 147464 | tf_op jit(solution)/shard_map/ppermute | solution.py:127
  49.1 42.6 %collective-permute-start.19 = (bf16[2,2,32,192]{3,2,1,0:T(8,128)(2,1)S(1)}, bf16[2,2,32,192]{3,2,1,0:T(8,128)(2,1)S(1)}, u32[]{:S(2)}, u32[]{:S(2)}) collective-permute-start(bf16[2,2,32,192]{3,2,1,0:T(8,128)(2,1)S(1)} %get-tuple-element.48), channel_id=1, source_target_pairs={{8,18},{9,19},{10,16},{11,17},{12,22},{13,23},{14,20},{15,21}} | collective-permute-start | bytes 147464 | tf_op jit(solution)/shard_map/ppermute | solution.py:127
  49.8 45.5 %collective-permute-start.18 = (bf16[2,2,32,192]{3,2,1,0:T(8,128)(2,1)S(1)}, bf16[2,2,32,192]{3,2,1,0:T(8,128)(2,1)S(1)}, u32[]{:S(2)}, u32[]{:S(2)}) collective-permute-start(bf16[2,2,32,192]{3,2,1,0:T(8,128)(2,1)S(1)} %get-tuple-element.48), channel_id=1, source_target_pairs={{8,2},{9,3},{10,0},{11,1},{12,6},{13,7},{14,4},{15,5}} | collective-permute-start | bytes 147464 | tf_op jit(solution)/shard_map/ppermute | solution.py:127
  96.1 11.8 %collective-permute-start.26 = (bf16[64,1536]{1,0:T(8,128)(2,1)S(1)}, bf16[64,1536]{1,0:T(8,128)(2,1)S(1)}, u32[]{:S(2)}, u32[]{:S(2)}) collective-permute-start(bf16[64,1536]{1,0:T(8,128)(2,1)S(1)} %shard_map.69.refs_0_), channel_id=1, source_target_pairs={{0,6},{1,7},{2,4},{3,5},{4,2},{5,3},{6,0},{7,1},{16,22},{17,23},{1... | collective-permute-start | bytes 589832 | tf_op jit(solution)/shard_map/ppermute | solution.py:123
  99.5 8.4 %collective-permute-start.25 = (bf16[64,1536]{1,0:T(8,128)(2,1)S(1)}, bf16[64,1536]{1,0:T(8,128)(2,1)S(1)}, u32[]{:S(2)}, u32[]{:S(2)}) collective-permute-start(bf16[64,1536]{1,0:T(8,128)(2,1)S(1)} %shard_map.69.refs_0_), channel_id=1, source_target_pairs={{0,4},{1,5},{2,6},{3,7},{4,0},{5,1},{6,2},{7,3},{16,20},{17,21},{1... | collective-permute-start | bytes 589832 | tf_op jit(solution)/shard_map/ppermute | solution.py:123
  101.9 7.6 %collective-permute-start.24 = (bf16[64,1536]{1,0:T(8,128)(2,1)S(1)}, bf16[64,1536]{1,0:T(8,128)(2,1)S(1)}, u32[]{:S(2)}, u32[]{:S(2)}) collective-permute-start(bf16[64,1536]{1,0:T(8,128)(2,1)S(1)} %shard_map.69.refs_0_), channel_id=1, source_target_pairs={{0,2},{1,3},{2,0},{3,1},{4,6},{5,7},{6,4},{7,5},{16,18},{17,19},{1... | collective-permute-start | bytes 589832 | tf_op jit(solution)/shard_map/ppermute | solution.py:123
  105.3 1.4 %collective-permute-start.20 = (f32[2,32,192]{2,1,0:T(8,128)S(1)}, f32[2,32,192]{2,1,0:T(8,128)S(1)}, u32[]{:S(2)}, u32[]{:S(2)}) collective-permute-start(f32[2,32,192]{2,1,0:T(8,128)S(1)} %get-tuple-element.50), channel_id=1, source_target_pairs={{8,9},{9,8},{10,11},{11,10},{12,13},{13,12},{14,15},{15,14},{24,25... | collective-permute-start | bytes 147464 | tf_op jit(solution)/shard_map/ppermute | solution.py:123
  106.0 1.7 %collective-permute-start.21 = (f32[2,32,192]{2,1,0:T(8,128)S(1)}, f32[2,32,192]{2,1,0:T(8,128)S(1)}, u32[]{:S(2)}, u32[]{:S(2)}) collective-permute-start(f32[2,32,192]{2,1,0:T(8,128)S(1)} %get-tuple-element.51), channel_id=1, source_target_pairs={{8,10},{9,11},{10,8},{11,9},{12,14},{13,15},{14,12},{15,13},{24,26... | collective-permute-start | bytes 147464 | tf_op jit(solution)/shard_map/ppermute | solution.py:123
  106.7 1.1 collective-permute-start.22
  107.7 5.2 %copy-start.1 = (bf16[1,192,1536]{2,1,0:T(8,128)(2,1)S(1)}, bf16[1,192,1536]{2,1,0:T(8,128)(2,1)}, u32[]{:S(2)}) copy-start(bf16[1,192,1536]{2,1,0:T(8,128)(2,1)} %param.6) | copy-start | bytes 1769476
  109.6 3.3 %collective-permute-start.27 = (bf16[64,1536]{1,0:T(8,128)(2,1)S(1)}, bf16[64,1536]{1,0:T(8,128)(2,1)S(1)}, u32[]{:S(2)}, u32[]{:S(2)}) collective-permute-start(bf16[64,1536]{1,0:T(8,128)(2,1)S(1)} %shard_map.72.refs_0_), channel_id=1, source_target_pairs={{0,1},{1,0},{2,3},{3,2},{4,5},{5,4},{6,7},{7,6},{16,17},{17,16},{1... | collective-permute-start | bytes 589832 | tf_op jit(solution)/shard_map/ppermute | solution.py:123

commit v4 on v3

v4 whole, which is shorter than its diff:
```python
import jax
import jax.numpy as jnp
from jax import lax
from jax.experimental import pallas as pl
from jax.experimental.pallas import tpu as pltpu
from jax.sharding import PartitionSpec as P

F32 = jnp.float32
BF16 = jnp.bfloat16


def trailing_ones(node):
    ones = 0
    while node % 2 == 1:
        ones += 1
        node //= 2
    return ones


def child_links(section, members):
    reach = 2 ** (section - 1)
    parents = [node for node in range(members) if trailing_ones(node) == section]
    links = [[(node - reach, node) for node in parents], [(node + reach, node) for node in parents]]
    return [[(a, b) for a, b in side if a < members] for side in links if any(a < members for a, b in side)]


def mm(a, b):
    return jnp.dot(a, b, preferred_element_type=F32)


def mmt(a, b):
    return lax.dot_general(a, b, (((1,), (1,)), ((), ())), preferred_element_type=F32)


def call(body, outs, args, scratch=()):
    single = isinstance(outs, tuple)
    shapes = [outs] if single else outs

    def kernel(*refs):
        middle = len(args) + len(shapes)
        body(refs[: len(args)], refs[len(args) : middle], *refs[middle:])

    moved = sum(a.size * a.dtype.itemsize for a in args)
    result = pl.pallas_call(
        kernel,
        out_shape=[jax.ShapeDtypeStruct(shape, dtype) for shape, dtype in shapes],
        in_specs=[pl.BlockSpec(memory_space=pltpu.VMEM) for _ in args],
        out_specs=[pl.BlockSpec(memory_space=pltpu.VMEM) for _ in shapes],
        scratch_shapes=list(scratch),
        compiler_params=pltpu.CompilerParams(vmem_limit_bytes=24 << 20),
        cost_estimate=pl.CostEstimate(flops=1 << 28, bytes_accessed=moved, transcendentals=0),
    )(*args)
    return result[0] if single else result


def on_device(rhs, panel, inverse_t, pattern):
    members = lax.axis_size("lvl")
    cols = lax.axis_size("col")
    levels = members.bit_length() - 1
    last = levels - 1
    chips = cols // 2
    lanes = 1 << ((chips.bit_length() - 1) // 2)
    row_count, rhs_count = rhs.shape[1:]
    width = inverse_t.shape[2]
    blocks = 2 * lanes
    group = rhs_count // blocks
    half = rhs_count // 2
    levels_of = [trailing_ones(node) for node in range(members)]
    nodes_at = [[node for node in range(members) if levels_of[node] == s] for s in range(levels + 1)]
    leaves = nodes_at[0]
    inner = [node for node in range(members) if levels_of[node] > 0]

    def place():
        at = lax.axis_index("col")
        core, lane = at % 2, at // 2 % lanes
        return at // blocks, lane, core, core * lanes + lane

    def height():
        at, rank = lax.axis_index("lvl"), 0
        for s in range(1, levels + 1):
            rank = rank + ((at + 1) % 2**s == 0).astype(jnp.int32)
        return rank

    def across(x, offset, planes):
        pairs = [(p * cols + c, p * cols + (c ^ offset)) for p in planes for c in range(cols)]
        return lax.ppermute(x, ("lvl", "col"), pairs)

    def along(x, links, offset=0):
        pairs = [(a * cols + c, b * cols + (c ^ offset)) for a, b in links for c in range(cols)]
        return lax.ppermute(x, ("lvl", "col"), pairs)

    def down(links):
        return [(b, a) for a, b in links]

    def after(x, *earlier):
        return lax.optimization_barrier((x, *earlier))[0]

    def over_chips(mine):
        return [mine] + [across(mine, 2 * chip, leaves) for chip in range(1, chips)]

    def over_rows(mine, planes):
        return [mine] + [across(mine, offset, planes) for offset in range(2 * lanes, cols, 2 * lanes)]

    def chip_total(refs):
        parts = []
        for i in range(lanes):
            total = refs[0][i * group : (i + 1) * group, :].astype(F32)
            for chip in range(1, chips):
                k = i ^ (chip % lanes)
                total = total + refs[chip][k * group : (k + 1) * group, :].astype(F32)
            parts.append(total)
        return jnp.concatenate(parts, axis=0)

    def row_total(refs):
        total = refs[0][...].astype(F32)
        for ref in refs[1:]:
            total = total + ref[...].astype(F32)
        return total

    def total_of(parts):
        total = parts[0]
        for part in parts[1:]:
            total = total + part
        return total

    def groups(b):
        return pl.ds(pl.multiple_of((b ^ place()[3]) * group, group), group)

    inverse_own, rhs_own = inverse_t[0], rhs[0]
    chip_rows = len(range(0, cols, 2 * lanes))

    def leaf_first(ins, outs, turned, ordered):
        turned[...] = ins[0][...].T
        for b in range(blocks):
            ordered[b * group : (b + 1) * group, :] = turned[groups(b), :]
        terms = ordered[...].astype(BF16)
        outs[0][...] = mm(terms[:half], ins[1][...]).astype(BF16)
        outs[1][...] = mm(terms[half:], ins[1][...]).astype(BF16)

    keep, give = call(
        leaf_first,
        [((half, width), BF16)] * 2,
        [rhs_own, inverse_own],
        [pltpu.VMEM((rhs_count, row_count), F32)] * 2,
    )
    got = across(give, 1, leaves)

    tiles = pattern.shape[-1]
    tile = width // tiles

    def build(ins, outs):
        pattern_ref, _, rhs_ref, inv_ref, panel_ref = ins
        first_row = lax.axis_index("col") * row_count
        row_ids = lax.broadcasted_iota(jnp.int32, (row_count, tiles), 0) + first_row
        row_tile = lax.broadcasted_iota(jnp.int32, (row_count, tiles), 1)
        row_pick = ((row_ids >= row_tile * tile) & (row_ids < (row_tile + 1) * tile)).astype(F32).astype(BF16)
        col_ids = lax.broadcasted_iota(jnp.int32, (tiles, width), 1)
        col_tile = lax.broadcasted_iota(jnp.int32, (tiles, width), 0)
        col_pick = ((col_ids >= col_tile * tile) & (col_ids < (col_tile + 1) * tile)).astype(F32).astype(BF16)
        masks = []
        for k in range(levels):
            kept = mm(row_pick, pattern_ref[0, k].astype(F32).astype(BF16)).astype(BF16)
            masks.append(mm(kept, col_pick).astype(BF16))
        high = rhs_ref[...].astype(BF16)
        low = (rhs_ref[...] - high.astype(F32)).astype(BF16)
        outs[0][:, levels * width : levels * width + rhs_count] = high
        outs[0][:, levels * width + rhs_count :] = low
        for k in range(levels):
            block = panel_ref[0, k] * masks[k]
            if k == last:
                block = jnp.where(height() == 0, block, inv_ref[...])
            outs[0][:, k * width : (k + 1) * width] = block

    full = levels * width + 2 * rhs_count
    rows_own = call(build, ((row_count, full), BF16), [pattern, give, rhs_own, inverse_own, panel])
    rows_own = after(rows_own, got)
    rows_far = across(rows_own, 1, range(members))
    rows_lanes = [across(rows_own, 2 * i, inner) for i in range(1, lanes)]
    chip_part = (keep.astype(F32) + got.astype(F32)).astype(BF16)
    terms = over_chips(chip_part)

    def factor_of(ref, k):
        return ref[:, k * width : (k + 1) * width]

    def inverse_of(ref):
        return factor_of(ref, last)

    def leaf_push(ins, outs):
        solved = chip_total(ins[:chips]).astype(BF16)
        outs[0][...] = solved
        for k in range(levels):
            for j in range(2):
                product = mmt(solved, factor_of(ins[chips + j], k)).astype(BF16)
                outs[1][k, j] = product

    vector = ((blocks, group, row_count), F32)
    term = ((group, width), BF16)
    leaf_half, pushed = call(
        leaf_push,
        [((half, width), BF16), ((levels, 2, half, row_count), BF16)],
        [*terms, rows_own, rows_far],
    )
    sides = child_links(1, members)
    early = [along(pushed, links) for links in sides]

    samples = {}
    arrived = []
    for section in range(1, levels + 1):
        remain = levels - section
        nodes = nodes_at[section]

        def inner_first(ins, outs):
            came, pair = ins[:-2], ins[-2:]
            own = lax.broadcasted_iota(jnp.int32, (half, rhs_count), 0)
            at = lax.broadcasted_iota(jnp.int32, (half, rhs_count), 1)
            parts = []
            for j in range(2):
                pick = jnp.zeros((half, rhs_count), BF16)
                for i in range(lanes):
                    mine = (own >= i * group) & (own < (i + 1) * group)
                    spot = own - i * group + (i ^ place()[3]) * group
                    pick = jnp.where(mine & (at == spot), 1.0, pick.astype(F32)).astype(BF16)
                rhs_pair = pair[j][:, levels * width :]
                side = mmt(pick, rhs_pair[:, :rhs_count]) + mmt(pick, rhs_pair[:, rhs_count:])
                less = total_of([ref[0, j].astype(F32) for ref in came])
                parts.append(mm((side - less).astype(BF16), inverse_of(pair[j])))
                for k in range(remain):
                    total = total_of([ref[k + 1, j].astype(F32) for ref in came])
                    outs[1][k, j] = total.astype(BF16)
            outs[0][...] = total_of(parts).astype(BF16)

        outs = [((half, width), BF16)] + ([((remain, 2, half, row_count), BF16)] if remain else [])
        own_term, *more = call(inner_first, outs, [*early, rows_own, rows_far])

        def by_lane(ins, outs):
            total = row_total(ins).astype(BF16)
            for i in range(lanes):
                outs[i][...] = total[i * group : (i + 1) * group]

        parts = over_rows(own_term, nodes)
        if remain:
            early = [along(more[0], links) for links in child_links(section + 1, members)]
            parts[0] = after(parts[0], *early)
        own_term, *others = call(by_lane, [term] * lanes, parts)
        terms = [own_term] + [across(others[i - 1], 2 * i, nodes) for i in range(1, lanes)]
        if arrived:

            def inner_second(ins, outs):
                came, rows_of = ins[:-blocks], ins[-blocks:]
                parts = []
                for b in range(blocks):
                    less = total_of([ref[0, b].astype(F32) for ref in came])
                    parts.append(mm(less.astype(BF16), inverse_of(rows_of[b])))
                outs[0][...] = (-total_of(parts)).astype(BF16)

            terms += over_rows(call(inner_second, term, [*arrived, *inner_rows]), nodes)
        count = len(terms)
        if section == 1:
            inner_rows = [rows_own, rows_far]
            for near in rows_lanes:
                inner_rows += [near, across(after(near, own_term), 1, inner)]
            leaf_far = across(after(leaf_half, own_term), 1, leaves)
        if remain:

            def inner_push(ins, outs):
                solved = row_total(ins[:count])
                came, rows_of = ins[count:-blocks], ins[-blocks:]
                outs[0][...] = solved
                short = solved.astype(BF16)
                for k in range(remain):
                    for b in range(blocks):
                        product = mmt(short, factor_of(rows_of[b], k))
                        if came:
                            product = product + total_of([ref[k + 1, b].astype(F32) for ref in came])
                        outs[1][k, b] = product.astype(BF16)

            samples[section], sent = call(
                inner_push,
                [((group, width), F32), ((remain, blocks, group, row_count), BF16)],
                [*terms, *arrived, *inner_rows],
            )
            arrived = [along(sent, links) for links in child_links(section + 1, members)]

    def root_back(ins, outs):
        solved = row_total(ins[:-blocks])
        outs[0][...] = solved
        short = solved.astype(BF16)
        for b in range(blocks):
            answer = mmt(short, inverse_of(ins[b - blocks]))
            outs[1][b] = answer
            outs[2][0, b] = answer.astype(BF16)

    samples[levels], answer, sent = call(
        root_back,
        [((group, width), F32), vector, ((1, blocks, group, row_count), BF16)],
        [*terms, *inner_rows],
    )

    def split_rows(ins, outs):
        rank = height()
        solved = ins[0][...]
        for s in range(2, levels + 1):
            solved = jnp.where(rank == s, ins[s - 1][...], solved)
        high = solved.astype(BF16)
        stacked = jnp.concatenate([high, (solved - high.astype(F32)).astype(BF16)], axis=0)
        row, lane, core, _ = place()
        for b in range(blocks):
            start = (row * blocks + (b ^ (lane * 2 + core))) * row_count
            at = lax.broadcasted_iota(jnp.int32, (row_count, width), 0) + start
            pick = (lax.broadcasted_iota(jnp.int32, (row_count, width), 1) == at).astype(F32).astype(BF16)
            both = mmt(stacked, pick)
            outs[0][b] = both[:group] + both[group:]

    for section in range(levels - 1, 0, -1):
        remain = levels - section
        ancestry = total_of([along(sent, down(links)) for links in child_links(section + 1, members)])

        def adjoint_first(ins, outs):
            parts = []
            for b in range(blocks):
                for k in range(remain):
                    parts.append(mm(ins[0][k, b], factor_of(ins[1 + b], k)))
            outs[0][...] = total_of(parts).astype(BF16)

        own_term = call(adjoint_first, term, [ancestry, *inner_rows])
        terms = over_rows(own_term, nodes_at[section])
        if section == 1:
            order = [after(samples[s], own_term) for s in range(1, levels + 1)]
            sample_rows = call(split_rows, vector, order)

        def inner_back(ins, outs):
            came, ins = ins[:chip_rows], ins[chip_rows:]
            (solved, anc, higher), rows_of = ins[:3], ins[3 : 3 + blocks]
            back = (solved[...] - row_total(came)).astype(BF16)
            rank = height()
            for b in range(blocks):
                mine = mmt(back, inverse_of(rows_of[b]))
                if section > 1:
                    outs[0][b] = jnp.where(rank == section, mine, higher[b])
                    outs[1][0, b] = mine.astype(BF16)
                    for k in range(remain):
                        outs[1][k + 1, b] = anc[k, b]
                else:
                    outs[b // 2][0, b % 2] = mine.astype(BF16)
                    for k in range(remain):
                        outs[b // 2][k + 1, b % 2] = anc[k, b]
                    outs[lanes + b][0] = ins[-1][b]
                    outs[lanes + b][1] = jnp.where(rank == 1, mine, higher[b])

        args = [*terms, samples[section], ancestry, answer, *inner_rows]
        if section > 1:
            answer, sent = call(
                inner_back, [vector, ((remain + 1, blocks, group, row_count), BF16)], args
            )
        else:
            message = ((levels, 2, group, row_count), BF16)
            outs = [message] * lanes + [((2, group, row_count), F32)] * blocks
            results = call(inner_back, outs, [*args, sample_rows])
            sent, results = results[:lanes], results[lanes:]

    arrived = [along(sent[i], down(links), 2 * i) for i in range(lanes) for links in sides]

    def leaf_adjoint(ins, outs):
        came, pair = ins[:-2], ins[-2:]
        parts = []
        for k in range(levels):
            for j in range(2):
                anc = [came[2 * i][k, j] + came[2 * i + 1][k, j] for i in range(lanes)]
                parts.append(mm(jnp.concatenate(anc, axis=0), factor_of(pair[j], k)))
        outs[0][...] = total_of(parts).astype(BF16)

    own_term = call(leaf_adjoint, ((half, width), BF16), [*arrived, rows_own, rows_far])
    terms = over_chips(own_term)

    def in_order(near, far, whole):
        for b in range(blocks):
            source = near if b < lanes else far
            whole[groups(b), :] = source[b % lanes * group : (b % lanes + 1) * group, :]

    def leaf_rows(ins, outs, whole):
        in_order(ins[0], ins[1], whole)
        at = lax.broadcasted_iota(jnp.int32, (row_count, width), 0) + lax.axis_index("col") * row_count
        pick = (lax.broadcasted_iota(jnp.int32, (row_count, width), 1) == at).astype(F32).astype(BF16)
        outs[0][...] = mmt(pick, whole[...])

    whole_half = [pltpu.VMEM((rhs_count, width), BF16)]
    leaf_sample = call(leaf_rows, ((row_count, rhs_count), F32), [leaf_half, leaf_far], whole_half)

    parts = [results[0]] + [across(results[b], b, inner) for b in range(1, blocks)]

    def join_groups(ins, outs, whole):
        for n in range(2):
            for b in range(blocks):
                whole[groups(b % 2 * lanes + b // 2), :] = ins[b][n]
            outs[n][...] = whole[...].T

    shape = ((row_count, rhs_count), F32)
    inner_sample, inner_answer = call(
        join_groups, [shape] * 2, parts, [pltpu.VMEM((rhs_count, row_count), F32)]
    )

    def leaf_back(ins, outs):
        outs[0][...] = (ins[chips][...].astype(F32) - chip_total(ins[:chips])).astype(BF16)

    terms[0] = after(terms[0], inner_sample, inner_answer, leaf_sample)
    back = call(leaf_back, ((half, width), BF16), [*terms, leaf_half])
    back_far = across(back, 1, leaves)

    def leaf_last(ins, outs, whole):
        in_order(ins[0], ins[1], whole)
        is_leaf = height() == 0
        outs[0][...] = jnp.where(is_leaf, ins[2][...], ins[3][...])
        outs[1][...] = jnp.where(is_leaf, mmt(ins[5][...], whole[...]), ins[4][...])

    sample, answer = call(
        leaf_last,
        [shape] * 2,
        [back, back_far, leaf_sample, inner_sample, inner_answer, inverse_own],
        whole_half,
    )
    return (sample[None], answer[None])


def solution(mesh):
    in_specs = (
        P("lvl", "col", None),
        P("lvl", None, "col", None),
        P("lvl", "col", None),
        P("lvl", None, None, None),
    )
    out_specs = (P("lvl", "col", None), P("lvl", "col", None))
    return jax.shard_map(
        on_device, mesh=mesh, in_specs=in_specs, out_specs=out_specs, check_vma=False
    )
```

time: 115 us -> 106 us (0.922)
  waiting for transfers between devices: 55.2 us -> 49.7 us
  Pallas kernels: 14.1 us -> 9.67 us
    ppermute x10 -> x9, waiting for transfers between devices: 46.1 us -> 40.3 us  [along(): return lax.ppermute(x, ('lvl', 'col'), pairs)]
    pallas_call x15 -> x18, Pallas kernels: 14.1 us -> 9.67 us  [call(): pl.pallas_call(kernel, out_shape=[jax.ShapeDtypeStruct(shape, dtype) for...]
    ppermute x18 -> x21, starting transfers between devices: 31.2 us -> 33.2 us  [across(): return lax.ppermute(x, ('lvl', 'col'), pairs)]
    unnamed x9, local copies, waits for them, and re-layouts: 1.97 us -> 3.94 us
    squeeze x1 -> x0, local copies, waits for them, and re-layouts: 1.32 us -> none  [on_device(): slots = [Columns(panel[0, k], 0, width) for k in range(levels)]]
    ppermute x10 -> x9, starting transfers between devices: 9.16 us -> 7.91 us  [along(): return lax.ppermute(x, ('lvl', 'col'), pairs)]
    ppermute x18 -> x21, waiting for transfers between devices: 9.18 us -> 9.39 us  [across(): return lax.ppermute(x, ('lvl', 'col'), pairs)]
  transfers between devices with their start and end apart: 28 -> 30, of which waited for: 9 -> 9; matrix products, arithmetic and copies ran while one was open for 1% -> 1% of each run, Pallas kernels for 5% -> 6%
where the time goes in v4:
time: 106 us
  waiting for transfers between devices  49.7 us (47%)
  starting transfers between devices  41.1 us (39%)
  Pallas kernels  9.67 us (9%)
  local copies, waits for them, and re-layouts  3.94 us (4%)
  between operations  1.12 us (1%)
    ppermute x9, waiting for transfers between devices, along(): return lax.ppermute(x, ('lvl', 'col'), pairs)  40.3 us
    ppermute x21, starting transfers between devices, across(): return lax.ppermute(x, ('lvl', 'col'), pairs)  33.2 us
    pallas_call x18, Pallas kernels, call(): pl.pallas_call(kernel, out_shape=[jax.ShapeDtypeStruct(shape, dtype) for...  9.67 us
    ppermute x21, waiting for transfers between devices, across(): return lax.ppermute(x, ('lvl', 'col'), pairs)  9.39 us
    ppermute x9, starting transfers between devices, along(): return lax.ppermute(x, ('lvl', 'col'), pairs)  7.91 us
    unnamed x9, local copies, waits for them, and re-layouts  3.94 us
  transfers between devices with their start and end apart: 30, of which 9 were waited for; matrix products, arithmetic and copies ran while one was open for 1% of the time, Pallas kernels for 6%

profile of v4, /device:TPU:0, one launch (start us, length us, event | category | flops | bytes accessed | tf_op | source)
XLA Modules:
  0.0 105.6 jit_solution(15873542260578726579)
XLA Ops:
  0.6 0.0 copy-start
  0.6 1.1 copy-done
  1.7 0.9 copy-done.3
  2.6 0.4 shard_map.59
  3.0 2.4 %collective-permute-start = (bf16[64,1536]{1,0:T(8,128)(2,1)S(1)}, bf16[64,1536]{1,0:T(8,128)(2,1)S(1)}, u32[]{:S(2)}, u32[]{:S(2)}) collective-permute-start(bf16[64,1536]{1,0:T(8,128)(2,1)S(1)} %get-tuple-element.35.refs_1_), channel_id=1, source_target_pairs={{0,1},{1,0},{2,3},{3,2},{4,5},{5,4},{6,7},{7,6},{16,17},{17,16},{1... | collective-permute-start | bytes 589832 | tf_op jit(solution)/shard_map/ppermute | solution.py:86
  5.4 0.7 copy.6.refs_0_
  6.1 1.3 %copy-done.2 = bf16[1,2,192,1536]{3,2,1,0:T(8,128)(2,1)S(1)} copy-done((bf16[1,2,192,1536]{3,2,1,0:T(8,128)(2,1)S(1)}, bf16[1,2,192,1536]{3,2,1,0:T(8,128)(2,1)}, u32[]{:S(2)}) %copy-start.2) | copy-done | bytes 1179672
  7.4 0.7 shard_map.60.refs_4_.refs_2_.refs_1_.refs_5_
  8.1 0.1 collective-permute-start.4
  8.2 0.7 collective-permute-start.12
  9.0 5.8 %collective-permute-start.3 = (bf16[64,1536]{1,0:T(8,128)(2,1)S(1)}, bf16[64,1536]{1,0:T(8,128)(2,1)S(1)}, u32[]{:S(2)}, u32[]{:S(2)}) collective-permute-start(bf16[64,1536]{1,0:T(8,128)(2,1)S(1)} %add_convert_fusion.refs_0_), channel_id=1, source_target_pairs={{0,6},{1,7},{2,4},{3,5},{4,2},{5,3},{6,0},{7,1},{16,22},{17,23},{1... | collective-permute-start | bytes 589832 | tf_op jit(solution)/shard_map/ppermute | solution.py:86
  14.8 2.4 %collective-permute-start.2 = (bf16[64,1536]{1,0:T(8,128)(2,1)S(1)}, bf16[64,1536]{1,0:T(8,128)(2,1)S(1)}, u32[]{:S(2)}, u32[]{:S(2)}) collective-permute-start(bf16[64,1536]{1,0:T(8,128)(2,1)S(1)} %add_convert_fusion.refs_0_), channel_id=1, source_target_pairs={{0,4},{1,5},{2,6},{3,7},{4,0},{5,1},{6,2},{7,3},{16,20},{17,21},{1... | collective-permute-start | bytes 589832 | tf_op jit(solution)/shard_map/ppermute | solution.py:86
  17.2 2.0 %collective-permute-start.1 = (bf16[64,1536]{1,0:T(8,128)(2,1)S(1)}, bf16[64,1536]{1,0:T(8,128)(2,1)S(1)}, u32[]{:S(2)}, u32[]{:S(2)}) collective-permute-start(bf16[64,1536]{1,0:T(8,128)(2,1)S(1)} %add_convert_fusion.refs_0_), channel_id=1, source_target_pairs={{0,2},{1,3},{2,0},{3,1},{4,6},{5,7},{6,4},{7,5},{16,18},{17,19},{1... | collective-permute-start | bytes 589832 | tf_op jit(solution)/shard_map/ppermute | solution.py:86
  19.2 0.8 collective-permute-done.3.refs_3_
  20.0 4.1 %collective-permute-done.2.refs_2_ = bf16[64,1536]{1,0:T(8,128)(2,1)S(1)} collective-permute-done((bf16[64,1536]{1,0:T(8,128)(2,1)S(1)}, bf16[64,1536]{1,0:T(8,128)(2,1)S(1)}, u32[]{:S(2)}, u32[]{:S(2)}) %collective-permute-start.2) | collective-permute-done | bytes 196640 | tf_op jit(solution)/shard_map/ppermute | solution.py:86
  24.1 1.3 %collective-permute-done.1.refs_1_ = bf16[64,1536]{1,0:T(8,128)(2,1)S(1)} collective-permute-done((bf16[64,1536]{1,0:T(8,128)(2,1)S(1)}, bf16[64,1536]{1,0:T(8,128)(2,1)S(1)}, u32[]{:S(2)}, u32[]{:S(2)}) %collective-permute-start.1) | collective-permute-done | bytes 196640 | tf_op jit(solution)/shard_map/ppermute | solution.py:86
  25.4 0.0 collective-permute-done.4.refs_5_.refs_3_.refs_2_.refs_6_
  25.4 0.9 shard_map.61
  26.3 0.7 collective-permute-start.6
  26.9 1.3 %collective-permute-start.5 = (bf16[2,2,64,192]{3,2,1,0:T(8,128)(2,1)S(1)}, bf16[2,2,64,192]{3,2,1,0:T(8,128)(2,1)S(1)}, u32[]{:S(2)}, u32[]{:S(2)}) collective-permute-start(bf16[2,2,64,192]{3,2,1,0:T(8,128)(2,1)S(1)} %get-tuple-element.37), channel_id=1, source_target_pairs={{0,8},{1,9},{2,10},{3,11},{4,12},{5,13},{6,14},{7,15}} | collective-permute-start | bytes 294920 | tf_op jit(solution)/shard_map/ppermute | solution.py:90
  28.2 0.0 collective-permute-done.6.refs_1_
  28.2 2.5 %collective-permute-done.5.refs_0_ = bf16[2,2,64,192]{3,2,1,0:T(8,128)(2,1)S(1)} collective-permute-done((bf16[2,2,64,192]{3,2,1,0:T(8,128)(2,1)S(1)}, bf16[2,2,64,192]{3,2,1,0:T(8,128)(2,1)S(1)}, u32[]{:S(2)}, u32[]{:S(2)}) %collective-permute-start.5) | collective-permute-done | bytes 98336 | tf_op jit(solution)/shard_map/ppermute | solution.py:90
  30.7 0.5 shard_map.62
  31.3 0.7 collective-permute-start.10
  31.9 0.7 collective-permute-start.7
  32.7 0.7 collective-permute-start.13
  33.5 0.5 shard_map.63.refs_0_
  34.0 0.7 collective-permute-start.8
  34.7 0.7 collective-permute-start.11
  35.4 0.8 shard_map.66
  36.2 0.7 collective-permute-start.14
  36.9 0.7 collective-permute-start.9
  37.6 0.5 shard_map.67.refs_2_
  38.2 0.7 collective-permute-start.15
  38.9 0.8 shard_map.68
  39.7 0.7 collective-permute-start.16
  40.4 0.5 shard_map.69.refs_0_
  40.9 0.7 collective-permute-start.17
  41.6 1.9 %collective-permute-start.25 = (bf16[64,1536]{1,0:T(8,128)(2,1)S(1)}, bf16[64,1536]{1,0:T(8,128)(2,1)S(1)}, u32[]{:S(2)}, u32[]{:S(2)}) collective-permute-start(bf16[64,1536]{1,0:T(8,128)(2,1)S(1)} %get-tuple-element.62.refs_0_.refs_4_), channel_id=1, source_target_pairs={{0,1},{1,0},{2,3},{3,2},{4,5},{5,4},{6,7},{7,6},{16,17},{17,16},{1... | collective-permute-start | bytes 589832 | tf_op jit(solution)/shard_map/ppermute | solution.py:86
  43.5 0.9 shard_map.70.refs_9_
  44.4 0.0 collective-permute-done.17.refs_1_
  44.4 0.8 shard_map.71
  45.2 0.7 collective-permute-start.19
  45.9 1.3 %collective-permute-start.18 = (bf16[2,2,32,192]{3,2,1,0:T(8,128)(2,1)S(1)}, bf16[2,2,32,192]{3,2,1,0:T(8,128)(2,1)S(1)}, u32[]{:S(2)}, u32[]{:S(2)}) collective-permute-start(bf16[2,2,32,192]{3,2,1,0:T(8,128)(2,1)S(1)} %get-tuple-element.53), channel_id=1, source_target_pairs={{8,0},{9,1},{10,2},{11,3},{12,4},{13,5},{14,6},{15,7}} | collective-permute-start | bytes 147464 | tf_op jit(solution)/shard_map/ppermute | solution.py:90
  47.2 0.7 collective-permute-start.21
  47.9 1.3 %collective-permute-start.20 = (bf16[2,2,32,192]{3,2,1,0:T(8,128)(2,1)S(1)}, bf16[2,2,32,192]{3,2,1,0:T(8,128)(2,1)S(1)}, u32[]{:S(2)}, u32[]{:S(2)}) collective-permute-start(bf16[2,2,32,192]{3,2,1,0:T(8,128)(2,1)S(1)} %get-tuple-element.54), channel_id=1, source_target_pairs={{8,2},{9,3},{10,0},{11,1},{12,6},{13,7},{14,4},{15,5}} | collective-permute-start | bytes 147464 | tf_op jit(solution)/shard_map/ppermute | solution.py:90
  49.2 34.4 %collective-permute-done.18.refs_0_ = bf16[2,2,32,192]{3,2,1,0:T(8,128)(2,1)S(1)} collective-permute-done((bf16[2,2,32,192]{3,2,1,0:T(8,128)(2,1)S(1)}, bf16[2,2,32,192]{3,2,1,0:T(8,128)(2,1)S(1)}, u32[]{:S(2)}, u32[]{:S(2)}) %collective-permute-start.18) | collective-permute-done | bytes 49184 | tf_op jit(solution)/shard_map/ppermute | solution.py:90
  83.6 3.3 %collective-permute-done.20.refs_2_ = bf16[2,2,32,192]{3,2,1,0:T(8,128)(2,1)S(1)} collective-permute-done((bf16[2,2,32,192]{3,2,1,0:T(8,128)(2,1)S(1)}, bf16[2,2,32,192]{3,2,1,0:T(8,128)(2,1)S(1)}, u32[]{:S(2)}, u32[]{:S(2)}) %collective-permute-start.20) | collective-permute-done | bytes 49184 | tf_op jit(solution)/shard_map/ppermute | solution.py:90
  86.9 0.5 shard_map.72.refs_0_
  87.5 3.6 %collective-permute-start.28 = (bf16[64,1536]{1,0:T(8,128)(2,1)S(1)}, bf16[64,1536]{1,0:T(8,128)(2,1)S(1)}, u32[]{:S(2)}, u32[]{:S(2)}) collective-permute-start(bf16[64,1536]{1,0:T(8,128)(2,1)S(1)} %shard_map.72.refs_0_), channel_id=1, source_target_pairs={{0,6},{1,7},{2,4},{3,5},{4,2},{5,3},{6,0},{7,1},{16,22},{17,23},{1... | collective-permute-start | bytes 589832 | tf_op jit(solution)/shard_map/ppermute | solution.py:86
  91.1 2.4 %collective-permute-start.27 = (bf16[64,1536]{1,0:T(8,128)(2,1)S(1)}, bf16[64,1536]{1,0:T(8,128)(2,1)S(1)}, u32[]{:S(2)}, u32[]{:S(2)}) collective-permute-start(bf16[64,1536]{1,0:T(8,128)(2,1)S(1)} %shard_map.72.refs_0_), channel_id=1, source_target_pairs={{0,4},{1,5},{2,6},{3,7},{4,0},{5,1},{6,2},{7,3},{16,20},{17,21},{1... | collective-permute-start | bytes 589832 | tf_op jit(solution)/shard_map/ppermute | solution.py:86
  93.5 3.2 %collective-permute-start.26 = (bf16[64,1536]{1,0:T(8,128)(2,1)S(1)}, bf16[64,1536]{1,0:T(8,128)(2,1)S(1)}, u32[]{:S(2)}, u32[]{:S(2)}) collective-permute-start(bf16[64,1536]{1,0:T(8,128)(2,1)S(1)} %shard_map.72.refs_0_), channel_id=1, source_target_pairs={{0,2},{1,3},{2,0},{3,1},{4,6},{5,7},{6,4},{7,5},{16,18},{17,19},{1... | collective-permute-start | bytes 589832 | tf_op jit(solution)/shard_map/ppermute | solution.py:86
  96.7 0.7 collective-permute-start.22
  97.4 0.7 collective-permute-start.23
  98.1 0.7 collective-permute-start.24
  98.8 0.4 shard_map.74.refs_2_
  99.1 0.0 copy-start.1
  99.2 0.2 shard_map.73
  99.3 0.1 collective-permute-done.27.refs_2_
  99.4 1.7 %collective-permute-done.26.refs_1_ = bf16[64,1536]{1,0:T(8,128)(2,1)S(1)} collective-permute-done((bf16[64,1536]{1,0:T(8,128)(2,1)S(1)}, bf16[64,1536]{1,0:T(8,128)(2,1)S(1)}, u32[]{:S(2)}, u32[]{:S(2)}) %collective-permute-start.26) | collective-permute-done | bytes 196640 | tf_op jit(solution)/shard_map/ppermute | solution.py:86
  101.1 0.1 shard_map.75.refs_0_
  101.2 1.9 %collective-permute-start.29 = (bf16[64,1536]{1,0:T(8,128)(2,1)S(1)}, bf16[64,1536]{1,0:T(8,128)(2,1)S(1)}, u32[]{:S(2)}, u32[]{:S(2)}) collective-permute-start(bf16[64,1536]{1,0:T(8,128)(2,1)S(1)} %shard_map.75.refs_0_), channel_id=1, source_target_pairs={{0,1},{1,0},{2,3},{3,2},{4,5},{5,4},{6,7},{7,6},{16,17},{17,16},{1... | collective-permute-start | bytes 589832 | tf_op jit(solution)/shard_map/ppermute | solution.py:86
  103.2 1.4 %collective-permute-done.29.refs_1_ = bf16[64,1536]{1,0:T(8,128)(2,1)S(1)} collective-permute-done((bf16[64,1536]{1,0:T(8,128)(2,1)S(1)}, bf16[64,1536]{1,0:T(8,128)(2,1)S(1)}, u32[]{:S(2)}, u32[]{:S(2)}) %collective-permute-start.29) | collective-permute-done | bytes 196640 | tf_op jit(solution)/shard_map/ppermute | solution.py:86
  104.6 1.0 shard_map.76
  (24 shorter events, 0.2 us)
Async XLA Ops:
  0.6 1.1 %copy-start = (bf16[1,192,1536]{2,1,0:T(8,128)(2,1)S(1)}, bf16[1,192,1536]{2,1,0:T(8,128)(2,1)}, u32[]{:S(2)}) copy-start(bf16[1,192,1536]{2,1,0:T(8,128)(2,1)} %param.6) | copy-start | bytes 1769476
  1.7 0.9 copy-start.3
  3.0 5.0 %collective-permute-start = (bf16[64,1536]{1,0:T(8,128)(2,1)S(1)}, bf16[64,1536]{1,0:T(8,128)(2,1)S(1)}, u32[]{:S(2)}, u32[]{:S(2)}) collective-permute-start(bf16[64,1536]{1,0:T(8,128)(2,1)S(1)} %get-tuple-element.35.refs_1_), channel_id=1, source_target_pairs={{0,1},{1,0},{2,3},{3,2},{4,5},{5,4},{6,7},{7,6},{16,17},{17,16},{1... | collective-permute-start | bytes 589832 | tf_op jit(solution)/shard_map/ppermute | solution.py:86
  6.1 1.3 %copy-start.2 = (bf16[1,2,192,1536]{3,2,1,0:T(8,128)(2,1)S(1)}, bf16[1,2,192,1536]{3,2,1,0:T(8,128)(2,1)}, u32[]{:S(2)}) copy-start(bf16[1,2,192,1536]{3,2,1,0:T(8,128)(2,1)} %refs_4_.1) | copy-start | bytes 3538948
  8.1 17.3 %collective-permute-start.4 = (bf16[192,3328]{1,0:T(8,128)(2,1)S(1)}, bf16[192,3328]{1,0:T(8,128)(2,1)S(1)}, u32[]{:S(2)}, u32[]{:S(2)}) collective-permute-start(bf16[192,3328]{1,0:T(8,128)(2,1)S(1)} %shard_map.60.refs_4_.refs_2_.refs_1_.refs_5_), channel_id=1, source_target_pairs={{0,1},{1,0},{2,3},{3,2},{4,5},{5,4},{6,7},{7,6},{8,9},{9,8},{10,11... | collective-permute-start | bytes 3833864 | tf_op jit(solution)/shard_map/ppermute | solution.py:86
  8.2 24.5 %collective-permute-start.12 = (bf16[192,3328]{1,0:T(8,128)(2,1)S(1)}, bf16[192,3328]{1,0:T(8,128)(2,1)S(1)}, u32[]{:S(2)}, u32[]{:S(2)}) collective-permute-start(bf16[192,3328]{1,0:T(8,128)(2,1)S(1)} %shard_map.60.refs_4_.refs_2_.refs_1_.refs_5_), channel_id=1, source_target_pairs={{8,10},{9,11},{10,8},{11,9},{12,14},{13,15},{14,12},{15,13},{24,26... | collective-permute-start | bytes 3833864 | tf_op jit(solution)/shard_map/ppermute | solution.py:86
  9.0 11.0 %collective-permute-start.3 = (bf16[64,1536]{1,0:T(8,128)(2,1)S(1)}, bf16[64,1536]{1,0:T(8,128)(2,1)S(1)}, u32[]{:S(2)}, u32[]{:S(2)}) collective-permute-start(bf16[64,1536]{1,0:T(8,128)(2,1)S(1)} %add_convert_fusion.refs_0_), channel_id=1, source_target_pairs={{0,6},{1,7},{2,4},{3,5},{4,2},{5,3},{6,0},{7,1},{16,22},{17,23},{1... | collective-permute-start | bytes 589832 | tf_op jit(solution)/shard_map/ppermute | solution.py:86
  14.8 9.3 %collective-permute-start.2 = (bf16[64,1536]{1,0:T(8,128)(2,1)S(1)}, bf16[64,1536]{1,0:T(8,128)(2,1)S(1)}, u32[]{:S(2)}, u32[]{:S(2)}) collective-permute-start(bf16[64,1536]{1,0:T(8,128)(2,1)S(1)} %add_convert_fusion.refs_0_), channel_id=1, source_target_pairs={{0,4},{1,5},{2,6},{3,7},{4,0},{5,1},{6,2},{7,3},{16,20},{17,21},{1... | collective-permute-start | bytes 589832 | tf_op jit(solution)/shard_map/ppermute | solution.py:86
  17.2 8.2 %collective-permute-start.1 = (bf16[64,1536]{1,0:T(8,128)(2,1)S(1)}, bf16[64,1536]{1,0:T(8,128)(2,1)S(1)}, u32[]{:S(2)}, u32[]{:S(2)}) collective-permute-start(bf16[64,1536]{1,0:T(8,128)(2,1)S(1)} %add_convert_fusion.refs_0_), channel_id=1, source_target_pairs={{0,2},{1,3},{2,0},{3,1},{4,6},{5,7},{6,4},{7,5},{16,18},{17,19},{1... | collective-permute-start | bytes 589832 | tf_op jit(solution)/shard_map/ppermute | solution.py:86
  26.3 2.0 %collective-permute-start.6 = (bf16[2,2,64,192]{3,2,1,0:T(8,128)(2,1)S(1)}, bf16[2,2,64,192]{3,2,1,0:T(8,128)(2,1)S(1)}, u32[]{:S(2)}, u32[]{:S(2)}) collective-permute-start(bf16[2,2,64,192]{3,2,1,0:T(8,128)(2,1)S(1)} %get-tuple-element.37), channel_id=1, source_target_pairs={{16,8},{17,9},{18,10},{19,11},{20,12},{21,13},{22,14},{23,15}} | collective-permute-start | bytes 294920 | tf_op jit(solution)/shard_map/ppermute | solution.py:90
  26.9 3.8 %collective-permute-start.5 = (bf16[2,2,64,192]{3,2,1,0:T(8,128)(2,1)S(1)}, bf16[2,2,64,192]{3,2,1,0:T(8,128)(2,1)S(1)}, u32[]{:S(2)}, u32[]{:S(2)}) collective-permute-start(bf16[2,2,64,192]{3,2,1,0:T(8,128)(2,1)S(1)} %get-tuple-element.37), channel_id=1, source_target_pairs={{0,8},{1,9},{2,10},{3,11},{4,12},{5,13},{6,14},{7,15}} | collective-permute-start | bytes 294920 | tf_op jit(solution)/shard_map/ppermute | solution.py:90
  31.3 1.4 %collective-permute-start.10 = (bf16[64,1536]{1,0:T(8,128)(2,1)S(1)}, bf16[64,1536]{1,0:T(8,128)(2,1)S(1)}, u32[]{:S(2)}, u32[]{:S(2)}) collective-permute-start(bf16[64,1536]{1,0:T(8,128)(2,1)S(1)} %get-tuple-element.42.refs_0_), channel_id=1, source_target_pairs={{8,12},{9,13},{10,14},{11,15},{12,8},{13,9},{14,10},{15,11}} | collective-permute-start | bytes 589832 | tf_op jit(solution)/shard_map/ppermute | solution.py:86
  31.9 0.7 collective-permute-start.7
  32.7 2.7 %collective-permute-start.13 = (bf16[192,3328]{1,0:T(8,128)(2,1)S(1)}, bf16[192,3328]{1,0:T(8,128)(2,1)S(1)}, u32[]{:S(2)}, u32[]{:S(2)}) collective-permute-start(bf16[192,3328]{1,0:T(8,128)(2,1)S(1)} %collective-permute-done.12.refs_4_.refs_3_.refs_6_.refs_7_), channel_id=1, source_target_pairs={{8,9},{9,8},{10,11},{11,10},{12,13},{13,12},{14,15},{15,14},{24,25... | collective-permute-start | bytes 3833864 | tf_op jit(solution)/shard_map/ppermute | solution.py:86
  34.0 2.9 %collective-permute-start.8 = (bf16[64,1536]{1,0:T(8,128)(2,1)S(1)}, bf16[64,1536]{1,0:T(8,128)(2,1)S(1)}, u32[]{:S(2)}, u32[]{:S(2)}) collective-permute-start(bf16[64,1536]{1,0:T(8,128)(2,1)S(1)} %shard_map.63.refs_0_), channel_id=1, source_target_pairs={{24,28},{25,29},{26,30},{27,31},{28,24},{29,25},{30,26},{31,27}} | collective-permute-start | bytes 589832 | tf_op jit(solution)/shard_map/ppermute | solution.py:86
  34.7 0.7 collective-permute-start.11
  36.2 1.4 %collective-permute-start.14 = (bf16[1,4,32,192]{3,2,1,0:T(8,128)(2,1)S(1)}, bf16[1,4,32,192]{3,2,1,0:T(8,128)(2,1)S(1)}, u32[]{:S(2)}, u32[]{:S(2)}) collective-permute-start(bf16[1,4,32,192]{3,2,1,0:T(8,128)(2,1)S(1)} %get-tuple-element.46), channel_id=1, source_target_pairs={{8,24},{9,25},{10,26},{11,27},{12,28},{13,29},{14,30},{15,31}} | collective-permute-start | bytes 147464 | tf_op jit(solution)/shard_map/ppermute | solution.py:90
  36.9 1.9 %collective-permute-start.9 = (bf16[32,1536]{1,0:T(8,128)(2,1)S(1)}, bf16[32,1536]{1,0:T(8,128)(2,1)S(1)}, u32[]{:S(2)}, u32[]{:S(2)}) collective-permute-start(bf16[32,1536]{1,0:T(8,128)(2,1)S(1)} %get-tuple-element.40), channel_id=1, source_target_pairs={{24,26},{25,27},{26,24},{27,25},{28,30},{29,31},{30,28},{31,29}} | collective-permute-start | bytes 294920 | tf_op jit(solution)/shard_map/ppermute | solution.py:86
  38.2 0.7 collective-permute-start.15
  39.7 0.7 collective-permute-start.16
  40.9 3.5 %collective-permute-start.17 = (bf16[32,1536]{1,0:T(8,128)(2,1)S(1)}, bf16[32,1536]{1,0:T(8,128)(2,1)S(1)}, u32[]{:S(2)}, u32[]{:S(2)}) collective-permute-start(bf16[32,1536]{1,0:T(8,128)(2,1)S(1)} %shard_map.69.refs_0_), channel_id=1, source_target_pairs={{8,12},{9,13},{10,14},{11,15},{12,8},{13,9},{14,10},{15,11}} | collective-permute-start | bytes 294920 | tf_op jit(solution)/shard_map/ppermute | solution.py:86
  41.6 55.8 %collective-permute-start.25 = (bf16[64,1536]{1,0:T(8,128)(2,1)S(1)}, bf16[64,1536]{1,0:T(8,128)(2,1)S(1)}, u32[]{:S(2)}, u32[]{:S(2)}) collective-permute-start(bf16[64,1536]{1,0:T(8,128)(2,1)S(1)} %get-tuple-element.62.refs_0_.refs_4_), channel_id=1, source_target_pairs={{0,1},{1,0},{2,3},{3,2},{4,5},{5,4},{6,7},{7,6},{16,17},{17,16},{1... | collective-permute-start | bytes 589832 | tf_op jit(solution)/shard_map/ppermute | solution.py:86
  45.2 4.0 %collective-permute-start.19 = (bf16[2,2,32,192]{3,2,1,0:T(8,128)(2,1)S(1)}, bf16[2,2,32,192]{3,2,1,0:T(8,128)(2,1)S(1)}, u32[]{:S(2)}, u32[]{:S(2)}) collective-permute-start(bf16[2,2,32,192]{3,2,1,0:T(8,128)(2,1)S(1)} %get-tuple-element.53), channel_id=1, source_target_pairs={{8,16},{9,17},{10,18},{11,19},{12,20},{13,21},{14,22},{15,23}} | collective-permute-start | bytes 147464 | tf_op jit(solution)/shard_map/ppermute | solution.py:90
  45.9 37.7 %collective-permute-start.18 = (bf16[2,2,32,192]{3,2,1,0:T(8,128)(2,1)S(1)}, bf16[2,2,32,192]{3,2,1,0:T(8,128)(2,1)S(1)}, u32[]{:S(2)}, u32[]{:S(2)}) collective-permute-start(bf16[2,2,32,192]{3,2,1,0:T(8,128)(2,1)S(1)} %get-tuple-element.53), channel_id=1, source_target_pairs={{8,0},{9,1},{10,2},{11,3},{12,4},{13,5},{14,6},{15,7}} | collective-permute-start | bytes 147464 | tf_op jit(solution)/shard_map/ppermute | solution.py:90
  47.2 36.4 %collective-permute-start.21 = (bf16[2,2,32,192]{3,2,1,0:T(8,128)(2,1)S(1)}, bf16[2,2,32,192]{3,2,1,0:T(8,128)(2,1)S(1)}, u32[]{:S(2)}, u32[]{:S(2)}) collective-permute-start(bf16[2,2,32,192]{3,2,1,0:T(8,128)(2,1)S(1)} %get-tuple-element.54), channel_id=1, source_target_pairs={{8,18},{9,19},{10,16},{11,17},{12,22},{13,23},{14,20},{15,21}} | collective-permute-start | bytes 147464 | tf_op jit(solution)/shard_map/ppermute | solution.py:90
  47.9 39.1 %collective-permute-start.20 = (bf16[2,2,32,192]{3,2,1,0:T(8,128)(2,1)S(1)}, bf16[2,2,32,192]{3,2,1,0:T(8,128)(2,1)S(1)}, u32[]{:S(2)}, u32[]{:S(2)}) collective-permute-start(bf16[2,2,32,192]{3,2,1,0:T(8,128)(2,1)S(1)} %get-tuple-element.54), channel_id=1, source_target_pairs={{8,2},{9,3},{10,0},{11,1},{12,6},{13,7},{14,4},{15,5}} | collective-permute-start | bytes 147464 | tf_op jit(solution)/shard_map/ppermute | solution.py:90
  87.5 11.8 %collective-permute-start.28 = (bf16[64,1536]{1,0:T(8,128)(2,1)S(1)}, bf16[64,1536]{1,0:T(8,128)(2,1)S(1)}, u32[]{:S(2)}, u32[]{:S(2)}) collective-permute-start(bf16[64,1536]{1,0:T(8,128)(2,1)S(1)} %shard_map.72.refs_0_), channel_id=1, source_target_pairs={{0,6},{1,7},{2,4},{3,5},{4,2},{5,3},{6,0},{7,1},{16,22},{17,23},{1... | collective-permute-start | bytes 589832 | tf_op jit(solution)/shard_map/ppermute | solution.py:86
  91.1 8.3 %collective-permute-start.27 = (bf16[64,1536]{1,0:T(8,128)(2,1)S(1)}, bf16[64,1536]{1,0:T(8,128)(2,1)S(1)}, u32[]{:S(2)}, u32[]{:S(2)}) collective-permute-start(bf16[64,1536]{1,0:T(8,128)(2,1)S(1)} %shard_map.72.refs_0_), channel_id=1, source_target_pairs={{0,4},{1,5},{2,6},{3,7},{4,0},{5,1},{6,2},{7,3},{16,20},{17,21},{1... | collective-permute-start | bytes 589832 | tf_op jit(solution)/shard_map/ppermute | solution.py:86
  93.5 7.6 %collective-permute-start.26 = (bf16[64,1536]{1,0:T(8,128)(2,1)S(1)}, bf16[64,1536]{1,0:T(8,128)(2,1)S(1)}, u32[]{:S(2)}, u32[]{:S(2)}) collective-permute-start(bf16[64,1536]{1,0:T(8,128)(2,1)S(1)} %shard_map.72.refs_0_), channel_id=1, source_target_pairs={{0,2},{1,3},{2,0},{3,1},{4,6},{5,7},{6,4},{7,5},{16,18},{17,19},{1... | collective-permute-start | bytes 589832 | tf_op jit(solution)/shard_map/ppermute | solution.py:86
  96.7 1.4 %collective-permute-start.22 = (f32[2,32,192]{2,1,0:T(8,128)S(1)}, f32[2,32,192]{2,1,0:T(8,128)S(1)}, u32[]{:S(2)}, u32[]{:S(2)}) collective-permute-start(f32[2,32,192]{2,1,0:T(8,128)S(1)} %get-tuple-element.56), channel_id=1, source_target_pairs={{8,9},{9,8},{10,11},{11,10},{12,13},{13,12},{14,15},{15,14},{24,25... | collective-permute-start | bytes 147464 | tf_op jit(solution)/shard_map/ppermute | solution.py:86
  97.4 1.7 %collective-permute-start.23 = (f32[2,32,192]{2,1,0:T(8,128)S(1)}, f32[2,32,192]{2,1,0:T(8,128)S(1)}, u32[]{:S(2)}, u32[]{:S(2)}) collective-permute-start(f32[2,32,192]{2,1,0:T(8,128)S(1)} %get-tuple-element.57), channel_id=1, source_target_pairs={{8,10},{9,11},{10,8},{11,9},{12,14},{13,15},{14,12},{15,13},{24,26... | collective-permute-start | bytes 147464 | tf_op jit(solution)/shard_map/ppermute | solution.py:86
  98.1 1.1 %collective-permute-start.24 = (f32[2,32,192]{2,1,0:T(8,128)S(1)}, f32[2,32,192]{2,1,0:T(8,128)S(1)}, u32[]{:S(2)}, u32[]{:S(2)}) collective-permute-start(f32[2,32,192]{2,1,0:T(8,128)S(1)} %get-tuple-element.58), channel_id=1, source_target_pairs={{8,11},{9,10},{10,9},{11,8},{12,15},{13,14},{14,13},{15,12},{24,27... | collective-permute-start | bytes 147464 | tf_op jit(solution)/shard_map/ppermute | solution.py:86
  99.1 5.4 %copy-start.1 = (bf16[1,192,1536]{2,1,0:T(8,128)(2,1)S(1)}, bf16[1,192,1536]{2,1,0:T(8,128)(2,1)}, u32[]{:S(2)}) copy-start(bf16[1,192,1536]{2,1,0:T(8,128)(2,1)} %param.6) | copy-start | bytes 1769476
  101.2 3.3 %collective-permute-start.29 = (bf16[64,1536]{1,0:T(8,128)(2,1)S(1)}, bf16[64,1536]{1,0:T(8,128)(2,1)S(1)}, u32[]{:S(2)}, u32[]{:S(2)}) collective-permute-start(bf16[64,1536]{1,0:T(8,128)(2,1)S(1)} %shard_map.75.refs_0_), channel_id=1, source_target_pairs={{0,1},{1,0},{2,3},{3,2},{4,5},{5,4},{6,7},{7,6},{16,17},{17,16},{1... | collective-permute-start | bytes 589832 | tf_op jit(solution)/shard_map/ppermute | solution.py:86

commit v5 on v4

--- a/solution.py
+++ b/solution.py
@@ -22,6 +22,24 @@
     parents = [node for node in range(members) if trailing_ones(node) == section]
     links = [[(node - reach, node) for node in parents], [(node + reach, node) for node in parents]]
     return [[(a, b) for a, b in side if a < members] for side in links if any(a < members for a, b in side)]
+
+
+def leaf_rounds(members):
+    rounds = []
+    for leaf in range(0, members, 2):
+        node, slot = leaf, 0
+        while node != members - 1:
+            reach = 2 ** trailing_ones(node)
+            node += reach if node // (2 * reach) % 2 == 0 else -reach
+            for sends in rounds:
+                if all(leaf != a and node != b for a, _, b in sends):
+                    break
+            else:
+                sends = []
+                rounds.append(sends)
+            sends.append((leaf, slot, node))
+            slot += 1
+    return rounds
 
 
 def mm(a, b):
@@ -170,12 +188,17 @@
             if k == last:
                 block = jnp.where(height() == 0, block, inv_ref[...])
             outs[0][:, k * width : (k + 1) * width] = block
+            outs[1][:, k * width : (k + 1) * width] = block
 
     full = levels * width + 2 * rhs_count
-    rows_own = call(build, ((row_count, full), BF16), [pattern, give, rhs_own, inverse_own, panel])
-    rows_own = after(rows_own, got)
+    rows_own, rows_sent = call(
+        build,
+        [((row_count, full), BF16), ((row_count, levels * width), BF16)],
+        [pattern, give, rhs_own, inverse_own, panel],
+    )
+    rows_own, rows_sent = after((rows_own, rows_sent), got)
     rows_far = across(rows_own, 1, range(members))
-    rows_lanes = [across(rows_own, 2 * i, inner) for i in range(1, lanes)]
+    rows_lanes = [across(rows_sent, 2 * i, inner) for i in range(1, lanes)]
     chip_part = (keep.astype(F32) + got.astype(F32)).astype(BF16)
     terms = over_chips(chip_part)
 
@@ -184,65 +207,64 @@
 
     def inverse_of(ref):
         return factor_of(ref, last)
+
+    rounds = leaf_rounds(members)
 
     def leaf_push(ins, outs):
         solved = chip_total(ins[:chips]).astype(BF16)
         outs[0][...] = solved
-        for k in range(levels):
+        for n, sends in enumerate(rounds):
+            slot = total_of([jnp.where(lax.axis_index("lvl") == leaf, k, 0) for leaf, k, _ in sends])
+            columns = pl.ds(pl.multiple_of(slot * width, width), width)
             for j in range(2):
-                product = mmt(solved, factor_of(ins[chips + j], k)).astype(BF16)
-                outs[1][k, j] = product
+                outs[1 + n][j] = mmt(solved, ins[chips + j][:, columns]).astype(BF16)
 
     vector = ((blocks, group, row_count), F32)
     term = ((group, width), BF16)
-    leaf_half, pushed = call(
+    leaf_half, *pushed = call(
         leaf_push,
-        [((half, width), BF16), ((levels, 2, half, row_count), BF16)],
+        [((half, width), BF16)] + [((2, half, row_count), BF16)] * len(rounds),
         [*terms, rows_own, rows_far],
     )
-    sides = child_links(1, members)
-    early = [along(pushed, links) for links in sides]
+    early = [along(sent, [(a, b) for a, _, b in sends]) for sent, sends in zip(pushed, rounds)]
+
+    def inner_first(ins, outs):
+        came, pair = ins[:-2], ins[-2:]
+        own = lax.broadcasted_iota(jnp.int32, (half, rhs_count), 0)
+        at = lax.broadcasted_iota(jnp.int32, (half, rhs_count), 1)
+        pick = jnp.zeros((half, rhs_count), F32)
+        for i in range(lanes):
+            mine = (own >= i * group) & (own < (i + 1) * group)
+            spot = own - i * group + (i ^ place()[3]) * group
+            pick = jnp.where(mine & (at == spot), 1.0, pick)
+        pick = pick.astype(BF16)
+        parts = []
+        for j in range(2):
+            rhs_pair = pair[j][:, levels * width :]
+            side = mmt(pick, rhs_pair[:, :rhs_count]) + mmt(pick, rhs_pair[:, rhs_count:])
+            less = total_of([ref[j].astype(F32) for ref in came])
+            parts.append(mm((side - less).astype(BF16), inverse_of(pair[j])))
+        outs[0][...] = total_of(parts).astype(BF16)
+
+    def by_lane(ins, outs):
+        total = row_total(ins).astype(BF16)
+        for i in range(lanes):
+            outs[i][...] = total[i * group : (i + 1) * group]
+
+    own_term = call(inner_first, ((half, width), BF16), [*early, rows_own, rows_far])
+    first_term, *others = call(by_lane, [term] * lanes, over_rows(own_term, inner))
+    first_terms = [first_term] + [across(others[i - 1], 2 * i, inner) for i in range(1, lanes)]
+    inner_rows = [rows_own, rows_far]
+    for near in rows_lanes:
+        inner_rows += [near, across(after(near, first_term), 1, inner)]
+    leaf_far = across(after(leaf_half, first_term), 1, leaves)
 
     samples = {}
     arrived = []
     for section in range(1, levels + 1):
         remain = levels - section
         nodes = nodes_at[section]
-
-        def inner_first(ins, outs):
-            came, pair = ins[:-2], ins[-2:]
-            own = lax.broadcasted_iota(jnp.int32, (half, rhs_count), 0)
-            at = lax.broadcasted_iota(jnp.int32, (half, rhs_count), 1)
-            parts = []
-            for j in range(2):
-                pick = jnp.zeros((half, rhs_count), BF16)
-                for i in range(lanes):
-                    mine = (own >= i * group) & (own < (i + 1) * group)
-                    spot = own - i * group + (i ^ place()[3]) * group
-                    pick = jnp.where(mine & (at == spot), 1.0, pick.astype(F32)).astype(BF16)
-                rhs_pair = pair[j][:, levels * width :]
-                side = mmt(pick, rhs_pair[:, :rhs_count]) + mmt(pick, rhs_pair[:, rhs_count:])
-                less = total_of([ref[0, j].astype(F32) for ref in came])
-                parts.append(mm((side - less).astype(BF16), inverse_of(pair[j])))
-                for k in range(remain):
-                    total = total_of([ref[k + 1, j].astype(F32) for ref in came])
-                    outs[1][k, j] = total.astype(BF16)
-            outs[0][...] = total_of(parts).astype(BF16)
-
-        outs = [((half, width), BF16)] + ([((remain, 2, half, row_count), BF16)] if remain else [])
-        own_term, *more = call(inner_first, outs, [*early, rows_own, rows_far])
-
-        def by_lane(ins, outs):
-            total = row_total(ins).astype(BF16)
-            for i in range(lanes):
-                outs[i][...] = total[i * group : (i + 1) * group]
-
-        parts = over_rows(own_term, nodes)
-        if remain:
-            early = [along(more[0], links) for links in child_links(section + 1, members)]
-            parts[0] = after(parts[0], *early)
-        own_term, *others = call(by_lane, [term] * lanes, parts)
-        terms = [own_term] + [across(others[i - 1], 2 * i, nodes) for i in range(1, lanes)]
+        terms = list(first_terms)
         if arrived:
 
             def inner_second(ins, outs):
@@ -255,11 +277,6 @@
 
             terms += over_rows(call(inner_second, term, [*arrived, *inner_rows]), nodes)
         count = len(terms)
-        if section == 1:
-            inner_rows = [rows_own, rows_far]
-            for near in rows_lanes:
-                inner_rows += [near, across(after(near, own_term), 1, inner)]
-            leaf_far = across(after(leaf_half, own_term), 1, leaves)
         if remain:
 
             def inner_push(ins, outs):
@@ -296,6 +313,9 @@
         [*terms, *inner_rows],
     )
 
+    leaf_rows_of = [rows_own, rows_far]
+    leaf_lanes = [across(after(rows_sent, sent), 2 * i, leaves) for i in range(1, lanes)]
+
     def split_rows(ins, outs):
         rank = height()
         solved = ins[0][...]
@@ -325,6 +345,8 @@
         own_term = call(adjoint_first, term, [ancestry, *inner_rows])
         terms = over_rows(own_term, nodes_at[section])
         if section == 1:
+            for near in leaf_lanes:
+                leaf_rows_of += [near, across(after(near, own_term), 1, leaves)]
             order = [after(samples[s], own_term) for s in range(1, levels + 1)]
             sample_rows = call(split_rows, vector, order)
 
@@ -335,42 +357,37 @@
             rank = height()
             for b in range(blocks):
                 mine = mmt(back, inverse_of(rows_of[b]))
-                if section > 1:
-                    outs[0][b] = jnp.where(rank == section, mine, higher[b])
-                    outs[1][0, b] = mine.astype(BF16)
-                    for k in range(remain):
-                        outs[1][k + 1, b] = anc[k, b]
+                outs[0][0, b] = mine.astype(BF16)
+                for k in range(remain):
+                    outs[0][k + 1, b] = anc[k, b]
+                chosen = jnp.where(rank == section, mine, higher[b])
+                if section == 1:
+                    outs[1 + b][0] = ins[-1][b]
+                    outs[1 + b][1] = chosen
                 else:
-                    outs[b // 2][0, b % 2] = mine.astype(BF16)
-                    for k in range(remain):
-                        outs[b // 2][k + 1, b % 2] = anc[k, b]
-                    outs[lanes + b][0] = ins[-1][b]
-                    outs[lanes + b][1] = jnp.where(rank == 1, mine, higher[b])
+                    outs[1][b] = chosen
 
         args = [*terms, samples[section], ancestry, answer, *inner_rows]
-        if section > 1:
-            answer, sent = call(
-                inner_back, [vector, ((remain + 1, blocks, group, row_count), BF16)], args
-            )
+        outs = [((remain + 1, blocks, group, row_count), BF16)]
+        if section == 1:
+            args, outs = [*args, sample_rows], outs + [((2, group, row_count), F32)] * blocks
         else:
-            message = ((levels, 2, group, row_count), BF16)
-            outs = [message] * lanes + [((2, group, row_count), F32)] * blocks
-            results = call(inner_back, outs, [*args, sample_rows])
-            sent, results = results[:lanes], results[lanes:]
-
-    arrived = [along(sent[i], down(links), 2 * i) for i in range(lanes) for links in sides]
+            outs = [*outs, vector]
+        sent, *results = call(inner_back, outs, args)
+        answer = results[0]
+
+    ancestry = [along(sent, down(links)) for links in child_links(1, members)]
 
     def leaf_adjoint(ins, outs):
-        came, pair = ins[:-2], ins[-2:]
+        came, rows_of = ins[:-blocks], ins[-blocks:]
         parts = []
-        for k in range(levels):
-            for j in range(2):
-                anc = [came[2 * i][k, j] + came[2 * i + 1][k, j] for i in range(lanes)]
-                parts.append(mm(jnp.concatenate(anc, axis=0), factor_of(pair[j], k)))
+        for b in range(blocks):
+            for k in range(levels):
+                parts.append(mm(total_of([ref[k, b] for ref in came]), factor_of(rows_of[b], k)))
         outs[0][...] = total_of(parts).astype(BF16)
 
-    own_term = call(leaf_adjoint, ((half, width), BF16), [*arrived, rows_own, rows_far])
-    terms = over_chips(own_term)
+    own_term = call(leaf_adjoint, term, [*ancestry, *leaf_rows_of])
+    terms = over_rows(own_term, leaves)
 
     def in_order(near, far, whole):
         for b in range(blocks):
@@ -400,22 +417,25 @@
     )
 
     def leaf_back(ins, outs):
-        outs[0][...] = (ins[chips][...].astype(F32) - chip_total(ins[:chips])).astype(BF16)
+        mine = ins[0][:group, :].astype(F32)
+        outs[0][...] = (mine - row_total(ins[1:])).astype(BF16)
 
     terms[0] = after(terms[0], inner_sample, inner_answer, leaf_sample)
-    back = call(leaf_back, ((half, width), BF16), [*terms, leaf_half])
-    back_far = across(back, 1, leaves)
+    back = call(leaf_back, term, [leaf_half, *terms])
+    backs = [back] + [across(back, b, leaves) for b in range(1, blocks)]
 
     def leaf_last(ins, outs, whole):
-        in_order(ins[0], ins[1], whole)
+        leaf_ref, inner_ref, answer_ref, inv_ref = ins[blocks:]
+        for b in range(blocks):
+            whole[groups(b % 2 * lanes + b // 2), :] = ins[b][...]
         is_leaf = height() == 0
-        outs[0][...] = jnp.where(is_leaf, ins[2][...], ins[3][...])
-        outs[1][...] = jnp.where(is_leaf, mmt(ins[5][...], whole[...]), ins[4][...])
+        outs[0][...] = jnp.where(is_leaf, leaf_ref[...], inner_ref[...])
+        outs[1][...] = jnp.where(is_leaf, mmt(inv_ref[...], whole[...]), answer_ref[...])
 
     sample, answer = call(
         leaf_last,
         [shape] * 2,
-        [back, back_far, leaf_sample, inner_sample, inner_answer, inverse_own],
+        [*backs, leaf_sample, inner_sample, inner_answer, inverse_own],
         whole_half,
     )
     return (sample[None], answer[None])

time: 106 us -> 105 us (level)
  waiting for transfers between devices: 49.7 us -> 47.6 us
  starting transfers between devices: 41.1 us -> 42.4 us
    ppermute x9 -> x6, waiting for transfers between devices: 40.3 us -> 15 us  [along(): return lax.ppermute(x, ('lvl', 'col'), pairs)]
    ppermute x21, waiting for transfers between devices: 9.39 us -> 32.5 us  [across(): return lax.ppermute(x, ('lvl', 'col'), pairs)]
    ppermute x21, starting transfers between devices: 33.2 us -> 36.5 us  [across(): return lax.ppermute(x, ('lvl', 'col'), pairs)]
    ppermute x9 -> x6, starting transfers between devices: 7.91 us -> 5.9 us  [along(): return lax.ppermute(x, ('lvl', 'col'), pairs)]
    pallas_call x18 -> x16, Pallas kernels: 9.67 us -> 9.47 us  [call(): pl.pallas_call(kernel, out_shape=[jax.ShapeDtypeStruct(shape, dtype) for...]
  transfers between devices with their start and end apart: 30 -> 27, of which waited for: 9 -> 9; matrix products, arithmetic and copies ran while one was open for 1% -> 1% of each run, Pallas kernels for 6% -> 6%
where the time goes in v5:
time: 105 us
  waiting for transfers between devices  47.6 us (45%)
  starting transfers between devices  42.4 us (40%)
  Pallas kernels  9.47 us (9%)
  local copies, waits for them, and re-layouts  3.94 us (4%)
    ppermute x21, starting transfers between devices, across(): return lax.ppermute(x, ('lvl', 'col'), pairs)  36.5 us
    ppermute x21, waiting for transfers between devices, across(): return lax.ppermute(x, ('lvl', 'col'), pairs)  32.5 us
    ppermute x6, waiting for transfers between devices, along(): return lax.ppermute(x, ('lvl', 'col'), pairs)  15 us
    pallas_call x16, Pallas kernels, call(): pl.pallas_call(kernel, out_shape=[jax.ShapeDtypeStruct(shape, dtype) for...  9.47 us
    ppermute x6, starting transfers between devices, along(): return lax.ppermute(x, ('lvl', 'col'), pairs)  5.9 us
    unnamed x9, local copies, waits for them, and re-layouts  3.94 us
  transfers between devices with their start and end apart: 27, of which 9 were waited for; matrix products, arithmetic and copies ran while one was open for 1% of the time, Pallas kernels for 6%

profile of v5, /device:TPU:0, one launch (start us, length us, event | category | flops | bytes accessed | tf_op | source)
XLA Modules:
  0.0 104.5 jit_solution(10080222719669266575)
XLA Ops:
  0.6 0.0 copy-start
  0.6 1.1 %copy-done = bf16[1,192,1536]{2,1,0:T(8,128)(2,1)S(1)} copy-done((bf16[1,192,1536]{2,1,0:T(8,128)(2,1)S(1)}, bf16[1,192,1536]{2,1,0:T(8,128)(2,1)}, u32[]{:S(2)}) %copy-start) | copy-done | bytes 589848
  1.7 0.9 copy-done.3
  2.6 0.4 shard_map.59
  3.0 2.4 %collective-permute-start = (bf16[64,1536]{1,0:T(8,128)(2,1)S(1)}, bf16[64,1536]{1,0:T(8,128)(2,1)S(1)}, u32[]{:S(2)}, u32[]{:S(2)}) collective-permute-start(bf16[64,1536]{1,0:T(8,128)(2,1)S(1)} %get-tuple-element.35.refs_1_), channel_id=1, source_target_pairs={{0,1},{1,0},{2,3},{3,2},{4,5},{5,4},{6,7},{7,6},{16,17},{17,16},{1... | collective-permute-start | bytes 589832 | tf_op jit(solution)/shard_map/ppermute | solution.py:104
  5.4 0.7 copy.6.refs_0_
  6.1 1.3 %copy-done.2 = bf16[1,2,192,1536]{3,2,1,0:T(8,128)(2,1)S(1)} copy-done((bf16[1,2,192,1536]{3,2,1,0:T(8,128)(2,1)S(1)}, bf16[1,2,192,1536]{3,2,1,0:T(8,128)(2,1)}, u32[]{:S(2)}) %copy-start.2) | copy-done | bytes 1179672
  7.4 0.7 shard_map.60
  8.1 0.0 collective-permute-done
  8.1 0.1 collective-permute-start.4
  8.2 0.7 collective-permute-start.9
  9.0 5.8 %collective-permute-start.3 = (bf16[64,1536]{1,0:T(8,128)(2,1)S(1)}, bf16[64,1536]{1,0:T(8,128)(2,1)S(1)}, u32[]{:S(2)}, u32[]{:S(2)}) collective-permute-start(bf16[64,1536]{1,0:T(8,128)(2,1)S(1)} %add_convert_fusion.refs_0_), channel_id=1, source_target_pairs={{0,6},{1,7},{2,4},{3,5},{4,2},{5,3},{6,0},{7,1},{16,22},{17,23},{1... | collective-permute-start | bytes 589832 | tf_op jit(solution)/shard_map/ppermute | solution.py:104
  14.8 2.4 %collective-permute-start.2 = (bf16[64,1536]{1,0:T(8,128)(2,1)S(1)}, bf16[64,1536]{1,0:T(8,128)(2,1)S(1)}, u32[]{:S(2)}, u32[]{:S(2)}) collective-permute-start(bf16[64,1536]{1,0:T(8,128)(2,1)S(1)} %add_convert_fusion.refs_0_), channel_id=1, source_target_pairs={{0,4},{1,5},{2,6},{3,7},{4,0},{5,1},{6,2},{7,3},{16,20},{17,21},{1... | collective-permute-start | bytes 589832 | tf_op jit(solution)/shard_map/ppermute | solution.py:104
  17.2 2.0 %collective-permute-start.1 = (bf16[64,1536]{1,0:T(8,128)(2,1)S(1)}, bf16[64,1536]{1,0:T(8,128)(2,1)S(1)}, u32[]{:S(2)}, u32[]{:S(2)}) collective-permute-start(bf16[64,1536]{1,0:T(8,128)(2,1)S(1)} %add_convert_fusion.refs_0_), channel_id=1, source_target_pairs={{0,2},{1,3},{2,0},{3,1},{4,6},{5,7},{6,4},{7,5},{16,18},{17,19},{1... | collective-permute-start | bytes 589832 | tf_op jit(solution)/shard_map/ppermute | solution.py:104
  19.2 0.8 collective-permute-done.3.refs_3_
  20.0 4.1 %collective-permute-done.2.refs_2_ = bf16[64,1536]{1,0:T(8,128)(2,1)S(1)} collective-permute-done((bf16[64,1536]{1,0:T(8,128)(2,1)S(1)}, bf16[64,1536]{1,0:T(8,128)(2,1)S(1)}, u32[]{:S(2)}, u32[]{:S(2)}) %collective-permute-start.2) | collective-permute-done | bytes 196640 | tf_op jit(solution)/shard_map/ppermute | solution.py:104
  24.1 1.3 %collective-permute-done.1.refs_1_ = bf16[64,1536]{1,0:T(8,128)(2,1)S(1)} collective-permute-done((bf16[64,1536]{1,0:T(8,128)(2,1)S(1)}, bf16[64,1536]{1,0:T(8,128)(2,1)S(1)}, u32[]{:S(2)}, u32[]{:S(2)}) %collective-permute-start.1) | collective-permute-done | bytes 196640 | tf_op jit(solution)/shard_map/ppermute | solution.py:104
  25.4 0.9 shard_map.61
  26.3 1.3 %collective-permute-start.5 = (bf16[2,64,192]{2,1,0:T(8,128)(2,1)S(1)}, bf16[2,64,192]{2,1,0:T(8,128)(2,1)S(1)}, u32[]{:S(2)}, u32[]{:S(2)}) collective-permute-start(bf16[2,64,192]{2,1,0:T(8,128)(2,1)S(1)} %get-tuple-element.40), channel_id=1, source_target_pairs={{0,8},{1,9},{2,10},{3,11},{4,12},{5,13},{6,14},{7,15},{16,24},{17,... | collective-permute-start | bytes 147464 | tf_op jit(solution)/shard_map/ppermute | solution.py:108
  27.6 1.3 %collective-permute-start.6 = (bf16[2,64,192]{2,1,0:T(8,128)(2,1)S(1)}, bf16[2,64,192]{2,1,0:T(8,128)(2,1)S(1)}, u32[]{:S(2)}, u32[]{:S(2)}) collective-permute-start(bf16[2,64,192]{2,1,0:T(8,128)(2,1)S(1)} %get-tuple-element.41), channel_id=1, source_target_pairs={{0,24},{1,25},{2,26},{3,27},{4,28},{5,29},{6,30},{7,31},{16,8},{17... | collective-permute-start | bytes 147464 | tf_op jit(solution)/shard_map/ppermute | solution.py:108
  28.9 0.6 collective-permute-done.5.refs_0_
  29.4 1.3 %collective-permute-done.6.refs_1_ = bf16[2,64,192]{2,1,0:T(8,128)(2,1)S(1)} collective-permute-done((bf16[2,64,192]{2,1,0:T(8,128)(2,1)S(1)}, bf16[2,64,192]{2,1,0:T(8,128)(2,1)S(1)}, u32[]{:S(2)}, u32[]{:S(2)}) %collective-permute-start.6) | collective-permute-done | bytes 49184 | tf_op jit(solution)/shard_map/ppermute | solution.py:108
  30.7 0.5 shard_map.62.refs_0_
  31.3 0.7 collective-permute-start.7
  32.0 0.7 collective-permute-start.10
  32.8 0.7 collective-permute-start.8
  33.5 0.0 collective-permute-done.8.refs_1_
  33.5 0.8 shard_map.64
  34.3 0.7 collective-permute-start.11
  35.0 0.0 collective-permute-done.11.refs_0_
  35.0 0.5 shard_map.65.refs_2_
  35.5 0.7 collective-permute-start.12
  36.2 0.0 collective-permute-done.12.refs_3_
  36.2 0.8 shard_map.66
  37.0 2.4 %collective-permute-start.17 = (bf16[192,3072]{1,0:T(8,128)(2,1)S(1)}, bf16[192,3072]{1,0:T(8,128)(2,1)S(1)}, u32[]{:S(2)}, u32[]{:S(2)}) collective-permute-start(bf16[192,3072]{1,0:T(8,128)(2,1)S(1)} %get-tuple-element.54), channel_id=1, source_target_pairs={{0,2},{1,3},{2,0},{3,1},{4,6},{5,7},{6,4},{7,5},{16,18},{17,19},{1... | collective-permute-start | bytes 3538952 | tf_op jit(solution)/shard_map/ppermute | solution.py:104
  39.4 0.7 collective-permute-start.13
  40.1 0.0 collective-permute-done.13.refs_0_.refs_3_
  40.1 0.5 shard_map.67.refs_0_
  40.6 24.3 %collective-permute-done.17.refs_4_ = bf16[192,3072]{1,0:T(8,128)(2,1)S(1)} collective-permute-done((bf16[192,3072]{1,0:T(8,128)(2,1)S(1)}, bf16[192,3072]{1,0:T(8,128)(2,1)S(1)}, u32[]{:S(2)}, u32[]{:S(2)}) %collective-permute-start.17) | collective-permute-done | bytes 1179680 | tf_op jit(solution)/shard_map/ppermute | solution.py:104
  64.9 1.9 %collective-permute-start.18 = (bf16[192,3072]{1,0:T(8,128)(2,1)S(1)}, bf16[192,3072]{1,0:T(8,128)(2,1)S(1)}, u32[]{:S(2)}, u32[]{:S(2)}) collective-permute-start(bf16[192,3072]{1,0:T(8,128)(2,1)S(1)} %collective-permute-done.17.refs_4_), channel_id=1, source_target_pairs={{0,1},{1,0},{2,3},{3,2},{4,5},{5,4},{6,7},{7,6},{16,17},{17,16},{1... | collective-permute-start | bytes 3538952 | tf_op jit(solution)/shard_map/ppermute | solution.py:104
  66.9 0.7 collective-permute-start.14
  67.5 2.4 %collective-permute-start.22 = (bf16[64,1536]{1,0:T(8,128)(2,1)S(1)}, bf16[64,1536]{1,0:T(8,128)(2,1)S(1)}, u32[]{:S(2)}, u32[]{:S(2)}) collective-permute-start(bf16[64,1536]{1,0:T(8,128)(2,1)S(1)} %get-tuple-element.62.refs_0_), channel_id=1, source_target_pairs={{0,1},{1,0},{2,3},{3,2},{4,5},{5,4},{6,7},{7,6},{16,17},{17,16},{1... | collective-permute-start | bytes 589832 | tf_op jit(solution)/shard_map/ppermute | solution.py:104
  69.9 0.9 shard_map.68.refs_9_
  70.8 0.0 collective-permute-done.14.refs_1_
  70.8 0.8 shard_map.69
  71.7 0.7 collective-permute-start.16
  72.4 1.3 %collective-permute-start.15 = (bf16[2,4,32,192]{3,2,1,0:T(8,128)(2,1)S(1)}, bf16[2,4,32,192]{3,2,1,0:T(8,128)(2,1)S(1)}, u32[]{:S(2)}, u32[]{:S(2)}) collective-permute-start(bf16[2,4,32,192]{3,2,1,0:T(8,128)(2,1)S(1)} %get-tuple-element.53), channel_id=1, source_target_pairs={{8,0},{9,1},{10,2},{11,3},{12,4},{13,5},{14,6},{15,7}} | collective-permute-start | bytes 294920 | tf_op jit(solution)/shard_map/ppermute | solution.py:108
  73.7 13.1 %collective-permute-done.15.refs_0_ = bf16[2,4,32,192]{3,2,1,0:T(8,128)(2,1)S(1)} collective-permute-done((bf16[2,4,32,192]{3,2,1,0:T(8,128)(2,1)S(1)}, bf16[2,4,32,192]{3,2,1,0:T(8,128)(2,1)S(1)}, u32[]{:S(2)}, u32[]{:S(2)}) %collective-permute-start.15) | collective-permute-done | bytes 98336 | tf_op jit(solution)/shard_map/ppermute | solution.py:108
  86.8 1.0 shard_map.70.refs_1_
  87.8 3.4 %collective-permute-start.23 = (bf16[32,1536]{1,0:T(8,128)(2,1)S(1)}, bf16[32,1536]{1,0:T(8,128)(2,1)S(1)}, u32[]{:S(2)}, u32[]{:S(2)}) collective-permute-start(bf16[32,1536]{1,0:T(8,128)(2,1)S(1)} %shard_map.70.refs_1_), channel_id=1, source_target_pairs={{0,4},{1,5},{2,6},{3,7},{4,0},{5,1},{6,2},{7,3},{16,20},{17,21},{1... | collective-permute-start | bytes 294920 | tf_op jit(solution)/shard_map/ppermute | solution.py:104
  91.2 0.7 collective-permute-start.19
  91.9 0.7 collective-permute-start.20
  92.6 0.7 collective-permute-start.21
  93.2 0.0 collective-permute-done.22.refs_1_
  93.3 0.4 shard_map.72.refs_4_
  93.6 0.0 copy-start.1
  93.6 0.0 collective-permute-done.20.refs_2_
  93.7 0.2 shard_map.71
  93.8 0.5 collective-permute-done.23.refs_2_
  94.3 1.9 %collective-permute-start.26 = (bf16[32,1536]{1,0:T(8,128)(2,1)S(1)}, bf16[32,1536]{1,0:T(8,128)(2,1)S(1)}, u32[]{:S(2)}, u32[]{:S(2)}) collective-permute-start(bf16[32,1536]{1,0:T(8,128)(2,1)S(1)} %shard_map.73.refs_0_), channel_id=1, source_target_pairs={{0,3},{1,2},{2,1},{3,0},{4,7},{5,6},{6,5},{7,4},{16,19},{17,18},{1... | collective-permute-start | bytes 294920 | tf_op jit(solution)/shard_map/ppermute | solution.py:104
  96.3 3.2 %collective-permute-start.25 = (bf16[32,1536]{1,0:T(8,128)(2,1)S(1)}, bf16[32,1536]{1,0:T(8,128)(2,1)S(1)}, u32[]{:S(2)}, u32[]{:S(2)}) collective-permute-start(bf16[32,1536]{1,0:T(8,128)(2,1)S(1)} %shard_map.73.refs_0_), channel_id=1, source_target_pairs={{0,2},{1,3},{2,0},{3,1},{4,6},{5,7},{6,4},{7,5},{16,18},{17,19},{1... | collective-permute-start | bytes 294920 | tf_op jit(solution)/shard_map/ppermute | solution.py:104
  99.5 2.5 %collective-permute-start.24 = (bf16[32,1536]{1,0:T(8,128)(2,1)S(1)}, bf16[32,1536]{1,0:T(8,128)(2,1)S(1)}, u32[]{:S(2)}, u32[]{:S(2)}) collective-permute-start(bf16[32,1536]{1,0:T(8,128)(2,1)S(1)} %shard_map.73.refs_0_), channel_id=1, source_target_pairs={{0,1},{1,0},{2,3},{3,2},{4,5},{5,4},{6,7},{7,6},{16,17},{17,16},{1... | collective-permute-start | bytes 294920 | tf_op jit(solution)/shard_map/ppermute | solution.py:104
  102.0 1.5 %collective-permute-done.25.refs_2_ = bf16[32,1536]{1,0:T(8,128)(2,1)S(1)} collective-permute-done((bf16[32,1536]{1,0:T(8,128)(2,1)S(1)}, bf16[32,1536]{1,0:T(8,128)(2,1)S(1)}, u32[]{:S(2)}, u32[]{:S(2)}) %collective-permute-start.25) | collective-permute-done | bytes 98336 | tf_op jit(solution)/shard_map/ppermute | solution.py:104
  103.5 1.0 shard_map.74
  (16 shorter events, 0.2 us)
Async XLA Ops:
  0.6 1.1 %copy-start = (bf16[1,192,1536]{2,1,0:T(8,128)(2,1)S(1)}, bf16[1,192,1536]{2,1,0:T(8,128)(2,1)}, u32[]{:S(2)}) copy-start(bf16[1,192,1536]{2,1,0:T(8,128)(2,1)} %param.6) | copy-start | bytes 1769476
  1.7 0.9 copy-start.3
  3.0 5.0 %collective-permute-start = (bf16[64,1536]{1,0:T(8,128)(2,1)S(1)}, bf16[64,1536]{1,0:T(8,128)(2,1)S(1)}, u32[]{:S(2)}, u32[]{:S(2)}) collective-permute-start(bf16[64,1536]{1,0:T(8,128)(2,1)S(1)} %get-tuple-element.35.refs_1_), channel_id=1, source_target_pairs={{0,1},{1,0},{2,3},{3,2},{4,5},{5,4},{6,7},{7,6},{16,17},{17,16},{1... | collective-permute-start | bytes 589832 | tf_op jit(solution)/shard_map/ppermute | solution.py:104
  6.1 1.3 %copy-start.2 = (bf16[1,2,192,1536]{3,2,1,0:T(8,128)(2,1)S(1)}, bf16[1,2,192,1536]{3,2,1,0:T(8,128)(2,1)}, u32[]{:S(2)}) copy-start(bf16[1,2,192,1536]{3,2,1,0:T(8,128)(2,1)} %refs_4_.1) | copy-start | bytes 3538948
  8.1 17.3 %collective-permute-start.4 = (bf16[192,3328]{1,0:T(8,128)(2,1)S(1)}, bf16[192,3328]{1,0:T(8,128)(2,1)S(1)}, u32[]{:S(2)}, u32[]{:S(2)}) collective-permute-start(bf16[192,3328]{1,0:T(8,128)(2,1)S(1)} %get-tuple-element.38.refs_4_.refs_2_.refs_1_.refs_5_), channel_id=1, source_target_pairs={{0,1},{1,0},{2,3},{3,2},{4,5},{5,4},{6,7},{7,6},{8,9},{9,8},{10,11... | collective-permute-start | bytes 3833864 | tf_op jit(solution)/shard_map/ppermute | solution.py:104
  8.2 23.8 %collective-permute-start.9 = (bf16[192,3072]{1,0:T(8,128)(2,1)S(1)}, bf16[192,3072]{1,0:T(8,128)(2,1)S(1)}, u32[]{:S(2)}, u32[]{:S(2)}) collective-permute-start(bf16[192,3072]{1,0:T(8,128)(2,1)S(1)} %get-tuple-element.54), channel_id=1, source_target_pairs={{8,10},{9,11},{10,8},{11,9},{12,14},{13,15},{14,12},{15,13},{24,26... | collective-permute-start | bytes 3538952 | tf_op jit(solution)/shard_map/ppermute | solution.py:104
  9.0 11.0 %collective-permute-start.3 = (bf16[64,1536]{1,0:T(8,128)(2,1)S(1)}, bf16[64,1536]{1,0:T(8,128)(2,1)S(1)}, u32[]{:S(2)}, u32[]{:S(2)}) collective-permute-start(bf16[64,1536]{1,0:T(8,128)(2,1)S(1)} %add_convert_fusion.refs_0_), channel_id=1, source_target_pairs={{0,6},{1,7},{2,4},{3,5},{4,2},{5,3},{6,0},{7,1},{16,22},{17,23},{1... | collective-permute-start | bytes 589832 | tf_op jit(solution)/shard_map/ppermute | solution.py:104
  14.8 9.3 %collective-permute-start.2 = (bf16[64,1536]{1,0:T(8,128)(2,1)S(1)}, bf16[64,1536]{1,0:T(8,128)(2,1)S(1)}, u32[]{:S(2)}, u32[]{:S(2)}) collective-permute-start(bf16[64,1536]{1,0:T(8,128)(2,1)S(1)} %add_convert_fusion.refs_0_), channel_id=1, source_target_pairs={{0,4},{1,5},{2,6},{3,7},{4,0},{5,1},{6,2},{7,3},{16,20},{17,21},{1... | collective-permute-start | bytes 589832 | tf_op jit(solution)/shard_map/ppermute | solution.py:104
  17.2 8.2 %collective-permute-start.1 = (bf16[64,1536]{1,0:T(8,128)(2,1)S(1)}, bf16[64,1536]{1,0:T(8,128)(2,1)S(1)}, u32[]{:S(2)}, u32[]{:S(2)}) collective-permute-start(bf16[64,1536]{1,0:T(8,128)(2,1)S(1)} %add_convert_fusion.refs_0_), channel_id=1, source_target_pairs={{0,2},{1,3},{2,0},{3,1},{4,6},{5,7},{6,4},{7,5},{16,18},{17,19},{1... | collective-permute-start | bytes 589832 | tf_op jit(solution)/shard_map/ppermute | solution.py:104
  26.3 3.2 %collective-permute-start.5 = (bf16[2,64,192]{2,1,0:T(8,128)(2,1)S(1)}, bf16[2,64,192]{2,1,0:T(8,128)(2,1)S(1)}, u32[]{:S(2)}, u32[]{:S(2)}) collective-permute-start(bf16[2,64,192]{2,1,0:T(8,128)(2,1)S(1)} %get-tuple-element.40), channel_id=1, source_target_pairs={{0,8},{1,9},{2,10},{3,11},{4,12},{5,13},{6,14},{7,15},{16,24},{17,... | collective-permute-start | bytes 147464 | tf_op jit(solution)/shard_map/ppermute | solution.py:108
  27.6 3.2 %collective-permute-start.6 = (bf16[2,64,192]{2,1,0:T(8,128)(2,1)S(1)}, bf16[2,64,192]{2,1,0:T(8,128)(2,1)S(1)}, u32[]{:S(2)}, u32[]{:S(2)}) collective-permute-start(bf16[2,64,192]{2,1,0:T(8,128)(2,1)S(1)} %get-tuple-element.41), channel_id=1, source_target_pairs={{0,24},{1,25},{2,26},{3,27},{4,28},{5,29},{6,30},{7,31},{16,8},{17... | collective-permute-start | bytes 147464 | tf_op jit(solution)/shard_map/ppermute | solution.py:108
  31.3 0.7 collective-permute-start.7
  32.0 1.4 %collective-permute-start.10 = (bf16[192,3072]{1,0:T(8,128)(2,1)S(1)}, bf16[192,3072]{1,0:T(8,128)(2,1)S(1)}, u32[]{:S(2)}, u32[]{:S(2)}) collective-permute-start(bf16[192,3072]{1,0:T(8,128)(2,1)S(1)} %collective-permute-done.9.refs_4_.refs_3_.refs_6_.refs_7_), channel_id=1, source_target_pairs={{8,9},{9,8},{10,11},{11,10},{12,13},{13,12},{14,15},{15,14},{24,25... | collective-permute-start | bytes 3538952 | tf_op jit(solution)/shard_map/ppermute | solution.py:104
  32.8 0.7 collective-permute-start.8
  34.3 0.7 collective-permute-start.11
  35.5 0.7 collective-permute-start.12
  37.0 27.9 %collective-permute-start.17 = (bf16[192,3072]{1,0:T(8,128)(2,1)S(1)}, bf16[192,3072]{1,0:T(8,128)(2,1)S(1)}, u32[]{:S(2)}, u32[]{:S(2)}) collective-permute-start(bf16[192,3072]{1,0:T(8,128)(2,1)S(1)} %get-tuple-element.54), channel_id=1, source_target_pairs={{0,2},{1,3},{2,0},{3,1},{4,6},{5,7},{6,4},{7,5},{16,18},{17,19},{1... | collective-permute-start | bytes 3538952 | tf_op jit(solution)/shard_map/ppermute | solution.py:104
  39.4 0.7 collective-permute-start.13
  64.9 21.9 %collective-permute-start.18 = (bf16[192,3072]{1,0:T(8,128)(2,1)S(1)}, bf16[192,3072]{1,0:T(8,128)(2,1)S(1)}, u32[]{:S(2)}, u32[]{:S(2)}) collective-permute-start(bf16[192,3072]{1,0:T(8,128)(2,1)S(1)} %collective-permute-done.17.refs_4_), channel_id=1, source_target_pairs={{0,1},{1,0},{2,3},{3,2},{4,5},{5,4},{6,7},{7,6},{16,17},{17,16},{1... | collective-permute-start | bytes 3538952 | tf_op jit(solution)/shard_map/ppermute | solution.py:104
  66.9 4.0 %collective-permute-start.14 = (bf16[32,1536]{1,0:T(8,128)(2,1)S(1)}, bf16[32,1536]{1,0:T(8,128)(2,1)S(1)}, u32[]{:S(2)}, u32[]{:S(2)}) collective-permute-start(bf16[32,1536]{1,0:T(8,128)(2,1)S(1)} %shard_map.67.refs_0_), channel_id=1, source_target_pairs={{8,12},{9,13},{10,14},{11,15},{12,8},{13,9},{14,10},{15,11}} | collective-permute-start | bytes 294920 | tf_op jit(solution)/shard_map/ppermute | solution.py:104
  67.5 25.7 %collective-permute-start.22 = (bf16[64,1536]{1,0:T(8,128)(2,1)S(1)}, bf16[64,1536]{1,0:T(8,128)(2,1)S(1)}, u32[]{:S(2)}, u32[]{:S(2)}) collective-permute-start(bf16[64,1536]{1,0:T(8,128)(2,1)S(1)} %get-tuple-element.62.refs_0_), channel_id=1, source_target_pairs={{0,1},{1,0},{2,3},{3,2},{4,5},{5,4},{6,7},{7,6},{16,17},{17,16},{1... | collective-permute-start | bytes 589832 | tf_op jit(solution)/shard_map/ppermute | solution.py:104
  71.7 2.0 %collective-permute-start.16 = (bf16[2,4,32,192]{3,2,1,0:T(8,128)(2,1)S(1)}, bf16[2,4,32,192]{3,2,1,0:T(8,128)(2,1)S(1)}, u32[]{:S(2)}, u32[]{:S(2)}) collective-permute-start(bf16[2,4,32,192]{3,2,1,0:T(8,128)(2,1)S(1)} %get-tuple-element.53), channel_id=1, source_target_pairs={{8,16},{9,17},{10,18},{11,19},{12,20},{13,21},{14,22},{15,23}} | collective-permute-start | bytes 294920 | tf_op jit(solution)/shard_map/ppermute | solution.py:108
  72.4 14.5 %collective-permute-start.15 = (bf16[2,4,32,192]{3,2,1,0:T(8,128)(2,1)S(1)}, bf16[2,4,32,192]{3,2,1,0:T(8,128)(2,1)S(1)}, u32[]{:S(2)}, u32[]{:S(2)}) collective-permute-start(bf16[2,4,32,192]{3,2,1,0:T(8,128)(2,1)S(1)} %get-tuple-element.53), channel_id=1, source_target_pairs={{8,0},{9,1},{10,2},{11,3},{12,4},{13,5},{14,6},{15,7}} | collective-permute-start | bytes 294920 | tf_op jit(solution)/shard_map/ppermute | solution.py:108
  87.8 6.5 %collective-permute-start.23 = (bf16[32,1536]{1,0:T(8,128)(2,1)S(1)}, bf16[32,1536]{1,0:T(8,128)(2,1)S(1)}, u32[]{:S(2)}, u32[]{:S(2)}) collective-permute-start(bf16[32,1536]{1,0:T(8,128)(2,1)S(1)} %shard_map.70.refs_1_), channel_id=1, source_target_pairs={{0,4},{1,5},{2,6},{3,7},{4,0},{5,1},{6,2},{7,3},{16,20},{17,21},{1... | collective-permute-start | bytes 294920 | tf_op jit(solution)/shard_map/ppermute | solution.py:104
  91.2 2.4 %collective-permute-start.19 = (f32[2,32,192]{2,1,0:T(8,128)S(1)}, f32[2,32,192]{2,1,0:T(8,128)S(1)}, u32[]{:S(2)}, u32[]{:S(2)}) collective-permute-start(f32[2,32,192]{2,1,0:T(8,128)S(1)} %get-tuple-element.57), channel_id=1, source_target_pairs={{8,9},{9,8},{10,11},{11,10},{12,13},{13,12},{14,15},{15,14},{24,25... | collective-permute-start | bytes 147464 | tf_op jit(solution)/shard_map/ppermute | solution.py:104
  91.9 1.7 %collective-permute-start.20 = (f32[2,32,192]{2,1,0:T(8,128)S(1)}, f32[2,32,192]{2,1,0:T(8,128)S(1)}, u32[]{:S(2)}, u32[]{:S(2)}) collective-permute-start(f32[2,32,192]{2,1,0:T(8,128)S(1)} %get-tuple-element.58), channel_id=1, source_target_pairs={{8,10},{9,11},{10,8},{11,9},{12,14},{13,15},{14,12},{15,13},{24,26... | collective-permute-start | bytes 147464 | tf_op jit(solution)/shard_map/ppermute | solution.py:104
  92.6 1.1 %collective-permute-start.21 = (f32[2,32,192]{2,1,0:T(8,128)S(1)}, f32[2,32,192]{2,1,0:T(8,128)S(1)}, u32[]{:S(2)}, u32[]{:S(2)}) collective-permute-start(f32[2,32,192]{2,1,0:T(8,128)S(1)} %get-tuple-element.59), channel_id=1, source_target_pairs={{8,11},{9,10},{10,9},{11,8},{12,15},{13,14},{14,13},{15,12},{24,27... | collective-permute-start | bytes 147464 | tf_op jit(solution)/shard_map/ppermute | solution.py:104
  93.6 9.9 %copy-start.1 = (bf16[1,192,1536]{2,1,0:T(8,128)(2,1)S(1)}, bf16[1,192,1536]{2,1,0:T(8,128)(2,1)}, u32[]{:S(2)}) copy-start(bf16[1,192,1536]{2,1,0:T(8,128)(2,1)} %param.6) | copy-start | bytes 1769476
  94.3 7.6 %collective-permute-start.26 = (bf16[32,1536]{1,0:T(8,128)(2,1)S(1)}, bf16[32,1536]{1,0:T(8,128)(2,1)S(1)}, u32[]{:S(2)}, u32[]{:S(2)}) collective-permute-start(bf16[32,1536]{1,0:T(8,128)(2,1)S(1)} %shard_map.73.refs_0_), channel_id=1, source_target_pairs={{0,3},{1,2},{2,1},{3,0},{4,7},{5,6},{6,5},{7,4},{16,19},{17,18},{1... | collective-permute-start | bytes 294920 | tf_op jit(solution)/shard_map/ppermute | solution.py:104
  96.3 7.2 %collective-permute-start.25 = (bf16[32,1536]{1,0:T(8,128)(2,1)S(1)}, bf16[32,1536]{1,0:T(8,128)(2,1)S(1)}, u32[]{:S(2)}, u32[]{:S(2)}) collective-permute-start(bf16[32,1536]{1,0:T(8,128)(2,1)S(1)} %shard_map.73.refs_0_), channel_id=1, source_target_pairs={{0,2},{1,3},{2,0},{3,1},{4,6},{5,7},{6,4},{7,5},{16,18},{17,19},{1... | collective-permute-start | bytes 294920 | tf_op jit(solution)/shard_map/ppermute | solution.py:104
  99.5 4.0 %collective-permute-start.24 = (bf16[32,1536]{1,0:T(8,128)(2,1)S(1)}, bf16[32,1536]{1,0:T(8,128)(2,1)S(1)}, u32[]{:S(2)}, u32[]{:S(2)}) collective-permute-start(bf16[32,1536]{1,0:T(8,128)(2,1)S(1)} %shard_map.73.refs_0_), channel_id=1, source_target_pairs={{0,1},{1,0},{2,3},{3,2},{4,5},{5,4},{6,7},{7,6},{16,17},{17,16},{1... | collective-permute-start | bytes 294920 | tf_op jit(solution)/shard_map/ppermute | solution.py:104

commit v6 on v5

--- a/solution.py
+++ b/solution.py
@@ -99,13 +99,24 @@
             rank = rank + ((at + 1) % 2**s == 0).astype(jnp.int32)
         return rank
 
+    def permute(x, moves):
+        pairs = []
+        for plane in range(members):
+            target, offset = moves.get(plane, (plane, 1))
+            pairs += [(plane * cols + c, target * cols + (c ^ offset)) for c in range(cols)]
+        return lax.ppermute(x, ("lvl", "col"), pairs)
+
     def across(x, offset, planes):
-        pairs = [(p * cols + c, p * cols + (c ^ offset)) for p in planes for c in range(cols)]
-        return lax.ppermute(x, ("lvl", "col"), pairs)
+        return permute(x, {plane: (plane, offset) for plane in planes})
 
     def along(x, links, offset=0):
-        pairs = [(a * cols + c, b * cols + (c ^ offset)) for a, b in links for c in range(cols)]
-        return lax.ppermute(x, ("lvl", "col"), pairs)
+        moves = {}
+        for a, b in links:
+            moves[a], moves[b] = (b, offset), (a, offset)
+        return permute(x, moves)
+
+    def from_parent(left, right, section):
+        return jnp.where(lax.axis_index("lvl") // 2**section % 2 == 0, left, right)
 
     def down(links):
         return [(b, a) for a, b in links]
@@ -140,6 +151,9 @@
         for part in parts[1:]:
             total = total + part
         return total
+
+    def span(b):
+        return slice(b * row_count, (b + 1) * row_count)
 
     def groups(b):
         return pl.ds(pl.multiple_of((b ^ place()[3]) * group, group), group)
@@ -217,16 +231,23 @@
             slot = total_of([jnp.where(lax.axis_index("lvl") == leaf, k, 0) for leaf, k, _ in sends])
             columns = pl.ds(pl.multiple_of(slot * width, width), width)
             for j in range(2):
-                outs[1 + n][j] = mmt(solved, ins[chips + j][:, columns]).astype(BF16)
+                outs[1 + n][:, span(j)] = mmt(solved, ins[chips + j][:, columns]).astype(BF16)
 
     vector = ((blocks, group, row_count), F32)
     term = ((group, width), BF16)
     leaf_half, *pushed = call(
         leaf_push,
-        [((half, width), BF16)] + [((2, half, row_count), BF16)] * len(rounds),
+        [((half, width), BF16)] + [((half, 2 * row_count), BF16)] * len(rounds),
         [*terms, rows_own, rows_far],
     )
     early = [along(sent, [(a, b) for a, _, b in sends]) for sent, sends in zip(pushed, rounds)]
+
+    def heard(n, part):
+        targets = [b for _, _, b in rounds[n]]
+        if len(targets) == len(inner):
+            return part
+        here = total_of([(lax.axis_index("lvl") == b).astype(jnp.int32) for b in targets]) > 0
+        return jnp.where(here, part, 0.0)
 
     def inner_first(ins, outs):
         came, pair = ins[:-2], ins[-2:]
@@ -242,7 +263,7 @@
         for j in range(2):
             rhs_pair = pair[j][:, levels * width :]
             side = mmt(pick, rhs_pair[:, :rhs_count]) + mmt(pick, rhs_pair[:, rhs_count:])
-            less = total_of([ref[j].astype(F32) for ref in came])
+            less = total_of([heard(n, ref[:, span(j)].astype(F32)) for n, ref in enumerate(came)])
             parts.append(mm((side - less).astype(BF16), inverse_of(pair[j])))
         outs[0][...] = total_of(parts).astype(BF16)
 
@@ -271,7 +292,7 @@
                 came, rows_of = ins[:-blocks], ins[-blocks:]
                 parts = []
                 for b in range(blocks):
-                    less = total_of([ref[0, b].astype(F32) for ref in came])
+                    less = total_of([ref[0, :, span(b)].astype(F32) for ref in came])
                     parts.append(mm(less.astype(BF16), inverse_of(rows_of[b])))
                 outs[0][...] = (-total_of(parts)).astype(BF16)
 
@@ -288,12 +309,12 @@
                     for b in range(blocks):
                         product = mmt(short, factor_of(rows_of[b], k))
                         if came:
-                            product = product + total_of([ref[k + 1, b].astype(F32) for ref in came])
-                        outs[1][k, b] = product.astype(BF16)
+                            product = product + total_of([ref[k + 1, :, span(b)].astype(F32) for ref in came])
+                        outs[1][k, :, span(b)] = product.astype(BF16)
 
             samples[section], sent = call(
                 inner_push,
-                [((group, width), F32), ((remain, blocks, group, row_count), BF16)],
+                [((group, width), F32), ((remain, group, blocks * row_count), BF16)],
                 [*terms, *arrived, *inner_rows],
             )
             arrived = [along(sent, links) for links in child_links(section + 1, members)]
@@ -305,11 +326,11 @@
         for b in range(blocks):
             answer = mmt(short, inverse_of(ins[b - blocks]))
             outs[1][b] = answer
-            outs[2][0, b] = answer.astype(BF16)
+            outs[2][0, :, span(b)] = answer.astype(BF16)
 
     samples[levels], answer, sent = call(
         root_back,
-        [((group, width), F32), vector, ((1, blocks, group, row_count), BF16)],
+        [((group, width), F32), vector, ((1, group, blocks * row_count), BF16)],
         [*terms, *inner_rows],
     )
 
@@ -333,13 +354,14 @@
 
     for section in range(levels - 1, 0, -1):
         remain = levels - section
-        ancestry = total_of([along(sent, down(links)) for links in child_links(section + 1, members)])
+        ancestry = [along(sent, down(links)) for links in child_links(section + 1, members)]
+        ancestry = ancestry[0] if len(ancestry) == 1 else from_parent(*ancestry, section + 1)
 
         def adjoint_first(ins, outs):
             parts = []
             for b in range(blocks):
                 for k in range(remain):
-                    parts.append(mm(ins[0][k, b], factor_of(ins[1 + b], k)))
+                    parts.append(mm(ins[0][k, :, span(b)], factor_of(ins[1 + b], k)))
             outs[0][...] = total_of(parts).astype(BF16)
 
         own_term = call(adjoint_first, term, [ancestry, *inner_rows])
@@ -355,11 +377,10 @@
             (solved, anc, higher), rows_of = ins[:3], ins[3 : 3 + blocks]
             back = (solved[...] - row_total(came)).astype(BF16)
             rank = height()
+            outs[0][1:] = anc[...]
             for b in range(blocks):
                 mine = mmt(back, inverse_of(rows_of[b]))
-                outs[0][0, b] = mine.astype(BF16)
-                for k in range(remain):
-                    outs[0][k + 1, b] = anc[k, b]
+                outs[0][0, :, span(b)] = mine.astype(BF16)
                 chosen = jnp.where(rank == section, mine, higher[b])
                 if section == 1:
                     outs[1 + b][0] = ins[-1][b]
@@ -368,7 +389,7 @@
                     outs[1][b] = chosen
 
         args = [*terms, samples[section], ancestry, answer, *inner_rows]
-        outs = [((remain + 1, blocks, group, row_count), BF16)]
+        outs = [((remain + 1, group, blocks * row_count), BF16)]
         if section == 1:
             args, outs = [*args, sample_rows], outs + [((2, group, row_count), F32)] * blocks
         else:
@@ -383,7 +404,7 @@
         parts = []
         for b in range(blocks):
             for k in range(levels):
-                parts.append(mm(total_of([ref[k, b] for ref in came]), factor_of(rows_of[b], k)))
+                parts.append(mm(from_parent(*[ref[k, :, span(b)] for ref in came], 1), factor_of(rows_of[b], k)))
         outs[0][...] = total_of(parts).astype(BF16)
 
     own_term = call(leaf_adjoint, term, [*ancestry, *leaf_rows_of])

time: 105 us -> 89.7 us (0.85)
  starting transfers between devices: 42.4 us -> 17.2 us
  waiting for transfers between devices: 47.6 us -> 57.7 us
    ppermute x27, starting transfers between devices: 42.4 us -> 17.2 us  [permute(): return lax.ppermute(x, ('lvl', 'col'), pairs)]
    ppermute x27, waiting for transfers between devices: 47.6 us -> 57.7 us  [permute(): return lax.ppermute(x, ('lvl', 'col'), pairs)]
  transfers between devices with their start and end apart: 27 -> 27, of which waited for: 9 -> 19; matrix products, arithmetic and copies ran while one was open for 1% -> 1% of each run, Pallas kernels for 6% -> 7%
where the time goes in v6:
time: 89.7 us; the launch traced here: 89.4 us
  waiting for transfers between devices  57.7 us (64%)
  starting transfers between devices  17.2 us (19%)
  Pallas kernels  9.78 us (11%)
  local copies, waits for them, and re-layouts  3.94 us (4%)
    ppermute x27, waiting for transfers between devices, permute(): return lax.ppermute(x, ('lvl', 'col'), pairs)  57.7 us
    ppermute x27, starting transfers between devices, permute(): return lax.ppermute(x, ('lvl', 'col'), pairs)  17.2 us
    pallas_call x16, Pallas kernels, call(): pl.pallas_call(kernel, out_shape=[jax.ShapeDtypeStruct(shape, dtype) for...  9.78 us
    unnamed x9, local copies, waits for them, and re-layouts  3.94 us
  transfers between devices with their start and end apart: 27, of which 19 were waited for; matrix products, arithmetic and copies ran while one was open for 1% of the time, Pallas kernels for 7%

profile of v6, /device:TPU:0, one launch (start us, length us, event | category | flops | bytes accessed | tf_op | source)
XLA Modules:
  0.0 89.4 jit_solution(3761574811157516127)
XLA Ops:
  0.6 0.0 copy-start
  0.6 1.1 %copy-done = bf16[1,192,1536]{2,1,0:T(8,128)(2,1)S(1)} copy-done((bf16[1,192,1536]{2,1,0:T(8,128)(2,1)S(1)}, bf16[1,192,1536]{2,1,0:T(8,128)(2,1)}, u32[]{:S(2)}) %copy-start) | copy-done | bytes 589848
  1.7 0.9 copy-done.3
  2.6 0.4 shard_map.59
  3.0 0.5 collective-permute-start
  3.5 0.7 copy.6.refs_0_
  4.2 1.3 %copy-done.2 = bf16[1,2,192,1536]{3,2,1,0:T(8,128)(2,1)S(1)} copy-done((bf16[1,2,192,1536]{3,2,1,0:T(8,128)(2,1)S(1)}, bf16[1,2,192,1536]{3,2,1,0:T(8,128)(2,1)}, u32[]{:S(2)}) %copy-start.2) | copy-done | bytes 1179672
  5.5 0.7 shard_map.60
  6.2 0.1 collective-permute-start.4
  6.3 0.5 collective-permute-start.9
  6.8 3.6 %collective-permute-start.3 = (bf16[64,1536]{1,0:T(8,128)(2,1)S(1)}, bf16[64,1536]{1,0:T(8,128)(2,1)S(1)}, u32[]{:S(2)}, u32[]{:S(2)}) collective-permute-start(bf16[64,1536]{1,0:T(8,128)(2,1)S(1)} %add_convert_fusion.refs_0_), channel_id=1, source_target_pairs={{0,6},{1,7},{2,4},{3,5},{4,2},{5,3},{6,0},{7,1},{8,9},{9,8},{10,11... | collective-permute-start | bytes 589832 | tf_op jit(solution)/shard_map/ppermute | solution.py:107
  10.4 0.5 collective-permute-start.2
  10.9 0.1 collective-permute-start.1
  11.1 5.2 %collective-permute-done.3.refs_3_ = bf16[64,1536]{1,0:T(8,128)(2,1)S(1)} collective-permute-done((bf16[64,1536]{1,0:T(8,128)(2,1)S(1)}, bf16[64,1536]{1,0:T(8,128)(2,1)S(1)}, u32[]{:S(2)}, u32[]{:S(2)}) %collective-permute-start.3) | collective-permute-done | bytes 196640 | tf_op jit(solution)/shard_map/ppermute | solution.py:107
  16.2 3.9 %collective-permute-done.2.refs_2_ = bf16[64,1536]{1,0:T(8,128)(2,1)S(1)} collective-permute-done((bf16[64,1536]{1,0:T(8,128)(2,1)S(1)}, bf16[64,1536]{1,0:T(8,128)(2,1)S(1)}, u32[]{:S(2)}, u32[]{:S(2)}) %collective-permute-start.2) | collective-permute-done | bytes 196640 | tf_op jit(solution)/shard_map/ppermute | solution.py:107
  20.1 0.3 collective-permute-done.1.refs_1_
  20.4 0.9 %shard_map.61 = (bf16[64,1536]{1,0:T(8,128)(2,1)S(1)}, bf16[64,384]{1,0:T(8,128)(2,1)S(1)}, bf16[64,384]{1,0:T(8,128)(2,1)S(1)}) custom-call(bf16[64,1536]{1,0:T(8,128)(2,1)S(1)} %add_convert_fusion.refs_0_, bf16[64,1536]{1,0:T(8,128)(2,1)S(1)} %collective-permute-done.1.refs_1_, bf16[64,1536]{1,0:T(8,128)(2,1)S(1)} %collective-permute-done.2.refs_2_, ...), custom_call_target="tpu_custom_call" | custom-call | flops 268435456 | bytes 3342336 | tf_op jit(solution)/shard_map/pallas_call | solution.py:62
  21.4 0.1 collective-permute-start.5
  21.5 4.1 %collective-permute-start.6 = (bf16[64,384]{1,0:T(8,128)(2,1)S(1)}, bf16[64,384]{1,0:T(8,128)(2,1)S(1)}, u32[]{:S(2)}, u32[]{:S(2)}) collective-permute-start(bf16[64,384]{1,0:T(8,128)(2,1)S(1)} %get-tuple-element.41), channel_id=1, source_target_pairs={{0,24},{1,25},{2,26},{3,27},{4,28},{5,29},{6,30},{7,31},{8,16},{9,... | collective-permute-start | bytes 147464 | tf_op jit(solution)/shard_map/ppermute | solution.py:107
  25.5 0.0 collective-permute-done.5.refs_0_
  25.5 2.6 %collective-permute-done.6.refs_1_ = bf16[64,384]{1,0:T(8,128)(2,1)S(1)} collective-permute-done((bf16[64,384]{1,0:T(8,128)(2,1)S(1)}, bf16[64,384]{1,0:T(8,128)(2,1)S(1)}, u32[]{:S(2)}, u32[]{:S(2)}) %collective-permute-start.6) | collective-permute-done | bytes 49184 | tf_op jit(solution)/shard_map/ppermute | solution.py:107
  28.1 0.5 shard_map.62.refs_0_
  28.7 0.1 collective-permute-start.7
  28.7 1.4 %collective-permute-done.7.refs_1_ = bf16[64,1536]{1,0:T(8,128)(2,1)S(1)} collective-permute-done((bf16[64,1536]{1,0:T(8,128)(2,1)S(1)}, bf16[64,1536]{1,0:T(8,128)(2,1)S(1)}, u32[]{:S(2)}, u32[]{:S(2)}) %collective-permute-start.7) | collective-permute-done | bytes 196640 | tf_op jit(solution)/shard_map/ppermute | solution.py:107
  30.2 0.2 collective-permute-start.10
  30.4 0.4 collective-permute-start.8
  30.8 2.5 %collective-permute-done.8.refs_1_ = bf16[32,1536]{1,0:T(8,128)(2,1)S(1)} collective-permute-done((bf16[32,1536]{1,0:T(8,128)(2,1)S(1)}, bf16[32,1536]{1,0:T(8,128)(2,1)S(1)}, u32[]{:S(2)}, u32[]{:S(2)}) %collective-permute-start.8) | collective-permute-done | bytes 98336 | tf_op jit(solution)/shard_map/ppermute | solution.py:107
  33.3 0.0 collective-permute-done.10.refs_5_.refs_4_.refs_7_.refs_8_
  33.3 0.9 shard_map.64
  34.2 0.2 collective-permute-start.11
  34.3 1.1 %collective-permute-done.11.refs_0_ = bf16[1,32,768]{2,1,0:T(8,128)(2,1)S(1)} collective-permute-done((bf16[1,32,768]{2,1,0:T(8,128)(2,1)S(1)}, bf16[1,32,768]{2,1,0:T(8,128)(2,1)S(1)}, u32[]{:S(2)}, u32[]{:S(2)}) %collective-permute-start.11) | collective-permute-done | bytes 49184 | tf_op jit(solution)/shard_map/ppermute | solution.py:107
  35.4 0.6 shard_map.65.refs_2_
  36.0 0.2 collective-permute-start.12
  36.2 1.1 %collective-permute-done.12.refs_3_ = bf16[32,1536]{1,0:T(8,128)(2,1)S(1)} collective-permute-done((bf16[32,1536]{1,0:T(8,128)(2,1)S(1)}, bf16[32,1536]{1,0:T(8,128)(2,1)S(1)}, u32[]{:S(2)}, u32[]{:S(2)}) %collective-permute-start.12) | collective-permute-done | bytes 98336 | tf_op jit(solution)/shard_map/ppermute | solution.py:107
  37.4 0.9 shard_map.66
  38.3 1.5 %collective-permute-start.17 = (bf16[192,3072]{1,0:T(8,128)(2,1)S(1)}, bf16[192,3072]{1,0:T(8,128)(2,1)S(1)}, u32[]{:S(2)}, u32[]{:S(2)}) collective-permute-start(bf16[192,3072]{1,0:T(8,128)(2,1)S(1)} %get-tuple-element.54), channel_id=1, source_target_pairs={{0,2},{1,3},{2,0},{3,1},{4,6},{5,7},{6,4},{7,5},{8,9},{9,8},{10,11... | collective-permute-start | bytes 3538952 | tf_op jit(solution)/shard_map/ppermute | solution.py:107
  39.8 1.2 %collective-permute-done.13.refs_0_.refs_3_ = bf16[1,32,768]{2,1,0:T(8,128)(2,1)S(1)} collective-permute-done((bf16[1,32,768]{2,1,0:T(8,128)(2,1)S(1)}, bf16[1,32,768]{2,1,0:T(8,128)(2,1)S(1)}, u32[]{:S(2)}, u32[]{:S(2)}) %collective-permute-start.13) | collective-permute-done | bytes 49184 | tf_op jit(solution)/shard_map/ppermute | solution.py:107
  41.0 0.6 shard_map.67.refs_0_
  41.6 24.7 %collective-permute-done.17.refs_4_ = bf16[192,3072]{1,0:T(8,128)(2,1)S(1)} collective-permute-done((bf16[192,3072]{1,0:T(8,128)(2,1)S(1)}, bf16[192,3072]{1,0:T(8,128)(2,1)S(1)}, u32[]{:S(2)}, u32[]{:S(2)}) %collective-permute-start.17) | collective-permute-done | bytes 1179680 | tf_op jit(solution)/shard_map/ppermute | solution.py:107
  66.3 0.5 collective-permute-start.14
  66.8 0.0 collective-permute-start.22
  66.8 0.9 shard_map.68.refs_9_
  67.7 1.6 %collective-permute-done.14.refs_1_ = bf16[32,1536]{1,0:T(8,128)(2,1)S(1)} collective-permute-done((bf16[32,1536]{1,0:T(8,128)(2,1)S(1)}, bf16[32,1536]{1,0:T(8,128)(2,1)S(1)}, u32[]{:S(2)}, u32[]{:S(2)}) %collective-permute-start.14) | collective-permute-done | bytes 98336 | tf_op jit(solution)/shard_map/ppermute | solution.py:107
  69.3 0.9 shard_map.69
  70.2 0.2 collective-permute-start.16
  70.4 0.5 collective-permute-start.15
  70.9 0.6 collective-permute-done.16.refs_1_
  71.5 3.9 %collective-permute-done.15.refs_0_ = bf16[2,32,768]{2,1,0:T(8,128)(2,1)S(1)} collective-permute-done((bf16[2,32,768]{2,1,0:T(8,128)(2,1)S(1)}, bf16[2,32,768]{2,1,0:T(8,128)(2,1)S(1)}, u32[]{:S(2)}, u32[]{:S(2)}) %collective-permute-start.15) | collective-permute-done | bytes 98336 | tf_op jit(solution)/shard_map/ppermute | solution.py:107
  75.4 1.0 %shard_map.70.refs_1_ = bf16[32,1536]{1,0:T(8,128)(2,1)S(1)} custom-call(bf16[2,32,768]{2,1,0:T(8,128)(2,1)S(1)} %collective-permute-done.15.refs_0_, bf16[2,32,768]{2,1,0:T(8,128)(2,1)S(1)} %collective-permute-done.16.refs_1_, bf16[192,3328]{1,0:T(8,128)(2,1)S(1)} %get-tuple-element.38.refs_4_.refs_2_.refs_1_.refs_5_, ...), custom_call_target="tpu_custom_call" | custom-call | flops 268435456 | bytes 5111808 | tf_op jit(solution)/shard_map/pallas_call | solution.py:62
  76.4 1.6 %collective-permute-start.23 = (bf16[32,1536]{1,0:T(8,128)(2,1)S(1)}, bf16[32,1536]{1,0:T(8,128)(2,1)S(1)}, u32[]{:S(2)}, u32[]{:S(2)}) collective-permute-start(bf16[32,1536]{1,0:T(8,128)(2,1)S(1)} %shard_map.70.refs_1_), channel_id=1, source_target_pairs={{0,4},{1,5},{2,6},{3,7},{4,0},{5,1},{6,2},{7,3},{8,9},{9,8},{10,11... | collective-permute-start | bytes 294920 | tf_op jit(solution)/shard_map/ppermute | solution.py:107
  78.0 0.5 collective-permute-start.20
  78.5 0.4 shard_map.72.refs_4_
  78.9 0.0 copy-start.1
  78.9 0.4 collective-permute-done.19.refs_1_
  79.3 0.2 collective-permute-done.20.refs_2_
  79.4 0.4 collective-permute-done.21.refs_3_
  79.8 0.1 shard_map.71
  79.9 1.2 %collective-permute-done.23.refs_2_ = bf16[32,1536]{1,0:T(8,128)(2,1)S(1)} collective-permute-done((bf16[32,1536]{1,0:T(8,128)(2,1)S(1)}, bf16[32,1536]{1,0:T(8,128)(2,1)S(1)}, u32[]{:S(2)}, u32[]{:S(2)}) %collective-permute-start.23) | collective-permute-done | bytes 98336 | tf_op jit(solution)/shard_map/ppermute | solution.py:107
  81.1 0.1 collective-permute-start.26
  81.2 1.6 %collective-permute-start.25 = (bf16[32,1536]{1,0:T(8,128)(2,1)S(1)}, bf16[32,1536]{1,0:T(8,128)(2,1)S(1)}, u32[]{:S(2)}, u32[]{:S(2)}) collective-permute-start(bf16[32,1536]{1,0:T(8,128)(2,1)S(1)} %shard_map.73.refs_0_), channel_id=1, source_target_pairs={{0,2},{1,3},{2,0},{3,1},{4,6},{5,7},{6,4},{7,5},{8,9},{9,8},{10,11... | collective-permute-start | bytes 294920 | tf_op jit(solution)/shard_map/ppermute | solution.py:107
  82.8 0.3 collective-permute-start.24
  83.1 3.2 %collective-permute-done.26.refs_3_ = bf16[32,1536]{1,0:T(8,128)(2,1)S(1)} collective-permute-done((bf16[32,1536]{1,0:T(8,128)(2,1)S(1)}, bf16[32,1536]{1,0:T(8,128)(2,1)S(1)}, u32[]{:S(2)}, u32[]{:S(2)}) %collective-permute-start.26) | collective-permute-done | bytes 98336 | tf_op jit(solution)/shard_map/ppermute | solution.py:107
  86.3 2.1 %collective-permute-done.25.refs_2_ = bf16[32,1536]{1,0:T(8,128)(2,1)S(1)} collective-permute-done((bf16[32,1536]{1,0:T(8,128)(2,1)S(1)}, bf16[32,1536]{1,0:T(8,128)(2,1)S(1)}, u32[]{:S(2)}, u32[]{:S(2)}) %collective-permute-start.25) | collective-permute-done | bytes 98336 | tf_op jit(solution)/shard_map/ppermute | solution.py:107
  88.4 1.0 %shard_map.74 = (f32[192,128]{1,0:T(8,128)}, f32[192,128]{1,0:T(8,128)}) custom-call(bf16[32,1536]{1,0:T(8,128)(2,1)S(1)} %shard_map.73.refs_0_, bf16[32,1536]{1,0:T(8,128)(2,1)S(1)} %collective-permute-done.24.refs_1_, bf16[32,1536]{1,0:T(8,128)(2,1)S(1)} %collective-permute-done.25.refs_2_, bf16[32,1536]{1,0:T(8,128)(2,1)S(1)} %collective-permute-done.26.refs_3_, ...), custom_call_target="tpu_custom_call" | custom-call | flops 268435456 | bytes 1277952 | tf_op jit(solution)/shard_map/pallas_call | solution.py:62
  (16 shorter events, 0.2 us)
Async XLA Ops:
  0.6 1.1 %copy-start = (bf16[1,192,1536]{2,1,0:T(8,128)(2,1)S(1)}, bf16[1,192,1536]{2,1,0:T(8,128)(2,1)}, u32[]{:S(2)}) copy-start(bf16[1,192,1536]{2,1,0:T(8,128)(2,1)} %param.6) | copy-start | bytes 1769476
  1.7 0.9 copy-start.3
  3.0 3.2 %collective-permute-start = (bf16[64,1536]{1,0:T(8,128)(2,1)S(1)}, bf16[64,1536]{1,0:T(8,128)(2,1)S(1)}, u32[]{:S(2)}, u32[]{:S(2)}) collective-permute-start(bf16[64,1536]{1,0:T(8,128)(2,1)S(1)} %get-tuple-element.35.refs_1_), channel_id=1, source_target_pairs={{0,1},{1,0},{2,3},{3,2},{4,5},{5,4},{6,7},{7,6},{8,9},{9,8},{10,11... | collective-permute-start | bytes 589832 | tf_op jit(solution)/shard_map/ppermute | solution.py:107
  4.2 1.3 %copy-start.2 = (bf16[1,2,192,1536]{3,2,1,0:T(8,128)(2,1)S(1)}, bf16[1,2,192,1536]{3,2,1,0:T(8,128)(2,1)}, u32[]{:S(2)}) copy-start(bf16[1,2,192,1536]{3,2,1,0:T(8,128)(2,1)} %refs_4_.1) | copy-start | bytes 3538948
  6.2 14.2 %collective-permute-start.4 = (bf16[192,3328]{1,0:T(8,128)(2,1)S(1)}, bf16[192,3328]{1,0:T(8,128)(2,1)S(1)}, u32[]{:S(2)}, u32[]{:S(2)}) collective-permute-start(bf16[192,3328]{1,0:T(8,128)(2,1)S(1)} %get-tuple-element.38.refs_4_.refs_2_.refs_1_.refs_5_), channel_id=1, source_target_pairs={{0,1},{1,0},{2,3},{3,2},{4,5},{5,4},{6,7},{7,6},{8,9},{9,8},{10,11... | collective-permute-start | bytes 3833864 | tf_op jit(solution)/shard_map/ppermute | solution.py:107
  6.3 23.9 %collective-permute-start.9 = (bf16[192,3072]{1,0:T(8,128)(2,1)S(1)}, bf16[192,3072]{1,0:T(8,128)(2,1)S(1)}, u32[]{:S(2)}, u32[]{:S(2)}) collective-permute-start(bf16[192,3072]{1,0:T(8,128)(2,1)S(1)} %get-tuple-element.54), channel_id=1, source_target_pairs={{0,1},{1,0},{2,3},{3,2},{4,5},{5,4},{6,7},{7,6},{8,10},{9,11},{10,... | collective-permute-start | bytes 3538952 | tf_op jit(solution)/shard_map/ppermute | solution.py:107
  6.8 9.4 %collective-permute-start.3 = (bf16[64,1536]{1,0:T(8,128)(2,1)S(1)}, bf16[64,1536]{1,0:T(8,128)(2,1)S(1)}, u32[]{:S(2)}, u32[]{:S(2)}) collective-permute-start(bf16[64,1536]{1,0:T(8,128)(2,1)S(1)} %add_convert_fusion.refs_0_), channel_id=1, source_target_pairs={{0,6},{1,7},{2,4},{3,5},{4,2},{5,3},{6,0},{7,1},{8,9},{9,8},{10,11... | collective-permute-start | bytes 589832 | tf_op jit(solution)/shard_map/ppermute | solution.py:107
  10.4 9.7 %collective-permute-start.2 = (bf16[64,1536]{1,0:T(8,128)(2,1)S(1)}, bf16[64,1536]{1,0:T(8,128)(2,1)S(1)}, u32[]{:S(2)}, u32[]{:S(2)}) collective-permute-start(bf16[64,1536]{1,0:T(8,128)(2,1)S(1)} %add_convert_fusion.refs_0_), channel_id=1, source_target_pairs={{0,4},{1,5},{2,6},{3,7},{4,0},{5,1},{6,2},{7,3},{8,9},{9,8},{10,11... | collective-permute-start | bytes 589832 | tf_op jit(solution)/shard_map/ppermute | solution.py:107
  10.9 9.5 %collective-permute-start.1 = (bf16[64,1536]{1,0:T(8,128)(2,1)S(1)}, bf16[64,1536]{1,0:T(8,128)(2,1)S(1)}, u32[]{:S(2)}, u32[]{:S(2)}) collective-permute-start(bf16[64,1536]{1,0:T(8,128)(2,1)S(1)} %add_convert_fusion.refs_0_), channel_id=1, source_target_pairs={{0,2},{1,3},{2,0},{3,1},{4,6},{5,7},{6,4},{7,5},{8,9},{9,8},{10,11... | collective-permute-start | bytes 589832 | tf_op jit(solution)/shard_map/ppermute | solution.py:107
  21.4 4.2 %collective-permute-start.5 = (bf16[64,384]{1,0:T(8,128)(2,1)S(1)}, bf16[64,384]{1,0:T(8,128)(2,1)S(1)}, u32[]{:S(2)}, u32[]{:S(2)}) collective-permute-start(bf16[64,384]{1,0:T(8,128)(2,1)S(1)} %get-tuple-element.40), channel_id=1, source_target_pairs={{0,8},{1,9},{2,10},{3,11},{4,12},{5,13},{6,14},{7,15},{8,0},{9,1},... | collective-permute-start | bytes 147464 | tf_op jit(solution)/shard_map/ppermute | solution.py:107
  21.5 6.7 %collective-permute-start.6 = (bf16[64,384]{1,0:T(8,128)(2,1)S(1)}, bf16[64,384]{1,0:T(8,128)(2,1)S(1)}, u32[]{:S(2)}, u32[]{:S(2)}) collective-permute-start(bf16[64,384]{1,0:T(8,128)(2,1)S(1)} %get-tuple-element.41), channel_id=1, source_target_pairs={{0,24},{1,25},{2,26},{3,27},{4,28},{5,29},{6,30},{7,31},{8,16},{9,... | collective-permute-start | bytes 147464 | tf_op jit(solution)/shard_map/ppermute | solution.py:107
  28.7 1.5 %collective-permute-start.7 = (bf16[64,1536]{1,0:T(8,128)(2,1)S(1)}, bf16[64,1536]{1,0:T(8,128)(2,1)S(1)}, u32[]{:S(2)}, u32[]{:S(2)}) collective-permute-start(bf16[64,1536]{1,0:T(8,128)(2,1)S(1)} %shard_map.62.refs_0_), channel_id=1, source_target_pairs={{0,1},{1,0},{2,3},{3,2},{4,5},{5,4},{6,7},{7,6},{8,12},{9,13},{10,... | collective-permute-start | bytes 589832 | tf_op jit(solution)/shard_map/ppermute | solution.py:107
  30.2 3.1 %collective-permute-start.10 = (bf16[192,3072]{1,0:T(8,128)(2,1)S(1)}, bf16[192,3072]{1,0:T(8,128)(2,1)S(1)}, u32[]{:S(2)}, u32[]{:S(2)}) collective-permute-start(bf16[192,3072]{1,0:T(8,128)(2,1)S(1)} %collective-permute-done.9.refs_4_.refs_3_.refs_6_.refs_7_), channel_id=1, source_target_pairs={{0,1},{1,0},{2,3},{3,2},{4,5},{5,4},{6,7},{7,6},{8,9},{9,8},{10,11... | collective-permute-start | bytes 3538952 | tf_op jit(solution)/shard_map/ppermute | solution.py:107
  30.4 2.8 %collective-permute-start.8 = (bf16[32,1536]{1,0:T(8,128)(2,1)S(1)}, bf16[32,1536]{1,0:T(8,128)(2,1)S(1)}, u32[]{:S(2)}, u32[]{:S(2)}) collective-permute-start(bf16[32,1536]{1,0:T(8,128)(2,1)S(1)} %get-tuple-element.43), channel_id=1, source_target_pairs={{0,1},{1,0},{2,3},{3,2},{4,5},{5,4},{6,7},{7,6},{8,10},{9,11},{10,... | collective-permute-start | bytes 294920 | tf_op jit(solution)/shard_map/ppermute | solution.py:107
  34.2 1.3 %collective-permute-start.11 = (bf16[1,32,768]{2,1,0:T(8,128)(2,1)S(1)}, bf16[1,32,768]{2,1,0:T(8,128)(2,1)S(1)}, u32[]{:S(2)}, u32[]{:S(2)}) collective-permute-start(bf16[1,32,768]{2,1,0:T(8,128)(2,1)S(1)} %get-tuple-element.46), channel_id=1, source_target_pairs={{0,1},{1,0},{2,3},{3,2},{4,5},{5,4},{6,7},{7,6},{8,24},{9,25},{10,... | collective-permute-start | bytes 147464 | tf_op jit(solution)/shard_map/ppermute | solution.py:107
  36.0 1.4 %collective-permute-start.12 = (bf16[32,1536]{1,0:T(8,128)(2,1)S(1)}, bf16[32,1536]{1,0:T(8,128)(2,1)S(1)}, u32[]{:S(2)}, u32[]{:S(2)}) collective-permute-start(bf16[32,1536]{1,0:T(8,128)(2,1)S(1)} %shard_map.65.refs_2_), channel_id=1, source_target_pairs={{0,1},{1,0},{2,3},{3,2},{4,5},{5,4},{6,7},{7,6},{8,9},{9,8},{10,11... | collective-permute-start | bytes 294920 | tf_op jit(solution)/shard_map/ppermute | solution.py:107
  38.3 28.1 %collective-permute-start.17 = (bf16[192,3072]{1,0:T(8,128)(2,1)S(1)}, bf16[192,3072]{1,0:T(8,128)(2,1)S(1)}, u32[]{:S(2)}, u32[]{:S(2)}) collective-permute-start(bf16[192,3072]{1,0:T(8,128)(2,1)S(1)} %get-tuple-element.54), channel_id=1, source_target_pairs={{0,2},{1,3},{2,0},{3,1},{4,6},{5,7},{6,4},{7,5},{8,9},{9,8},{10,11... | collective-permute-start | bytes 3538952 | tf_op jit(solution)/shard_map/ppermute | solution.py:107
  39.8 1.2 %collective-permute-start.13 = (bf16[1,32,768]{2,1,0:T(8,128)(2,1)S(1)}, bf16[1,32,768]{2,1,0:T(8,128)(2,1)S(1)}, u32[]{:S(2)}, u32[]{:S(2)}) collective-permute-start(bf16[1,32,768]{2,1,0:T(8,128)(2,1)S(1)} %get-tuple-element.47), channel_id=1, source_target_pairs={{0,1},{1,0},{2,3},{3,2},{4,5},{5,4},{6,7},{7,6},{8,24},{9,25},{10,... | collective-permute-start | bytes 147464 | tf_op jit(solution)/shard_map/ppermute | solution.py:107
  66.3 9.1 %collective-permute-start.18 = (bf16[192,3072]{1,0:T(8,128)(2,1)S(1)}, bf16[192,3072]{1,0:T(8,128)(2,1)S(1)}, u32[]{:S(2)}, u32[]{:S(2)}) collective-permute-start(bf16[192,3072]{1,0:T(8,128)(2,1)S(1)} %collective-permute-done.17.refs_4_), channel_id=1, source_target_pairs={{0,1},{1,0},{2,3},{3,2},{4,5},{5,4},{6,7},{7,6},{8,9},{9,8},{10,11... | collective-permute-start | bytes 3538952 | tf_op jit(solution)/shard_map/ppermute | solution.py:107
  66.3 3.0 %collective-permute-start.14 = (bf16[32,1536]{1,0:T(8,128)(2,1)S(1)}, bf16[32,1536]{1,0:T(8,128)(2,1)S(1)}, u32[]{:S(2)}, u32[]{:S(2)}) collective-permute-start(bf16[32,1536]{1,0:T(8,128)(2,1)S(1)} %shard_map.67.refs_0_), channel_id=1, source_target_pairs={{0,1},{1,0},{2,3},{3,2},{4,5},{5,4},{6,7},{7,6},{8,12},{9,13},{10,... | collective-permute-start | bytes 294920 | tf_op jit(solution)/shard_map/ppermute | solution.py:107
  66.8 11.7 %collective-permute-start.22 = (bf16[64,1536]{1,0:T(8,128)(2,1)S(1)}, bf16[64,1536]{1,0:T(8,128)(2,1)S(1)}, u32[]{:S(2)}, u32[]{:S(2)}) collective-permute-start(bf16[64,1536]{1,0:T(8,128)(2,1)S(1)} %get-tuple-element.62.refs_0_), channel_id=1, source_target_pairs={{0,1},{1,0},{2,3},{3,2},{4,5},{5,4},{6,7},{7,6},{8,9},{9,8},{10,11... | collective-permute-start | bytes 589832 | tf_op jit(solution)/shard_map/ppermute | solution.py:107
  70.2 1.3 %collective-permute-start.16 = (bf16[2,32,768]{2,1,0:T(8,128)(2,1)S(1)}, bf16[2,32,768]{2,1,0:T(8,128)(2,1)S(1)}, u32[]{:S(2)}, u32[]{:S(2)}) collective-permute-start(bf16[2,32,768]{2,1,0:T(8,128)(2,1)S(1)} %get-tuple-element.53), channel_id=1, source_target_pairs={{0,1},{1,0},{2,3},{3,2},{4,5},{5,4},{6,7},{7,6},{8,16},{9,17},{10,... | collective-permute-start | bytes 294920 | tf_op jit(solution)/shard_map/ppermute | solution.py:107
  70.4 5.1 %collective-permute-start.15 = (bf16[2,32,768]{2,1,0:T(8,128)(2,1)S(1)}, bf16[2,32,768]{2,1,0:T(8,128)(2,1)S(1)}, u32[]{:S(2)}, u32[]{:S(2)}) collective-permute-start(bf16[2,32,768]{2,1,0:T(8,128)(2,1)S(1)} %get-tuple-element.53), channel_id=1, source_target_pairs={{0,8},{1,9},{2,10},{3,11},{4,12},{5,13},{6,14},{7,15},{8,0},{9,1},... | collective-permute-start | bytes 294920 | tf_op jit(solution)/shard_map/ppermute | solution.py:107
  76.4 4.7 %collective-permute-start.23 = (bf16[32,1536]{1,0:T(8,128)(2,1)S(1)}, bf16[32,1536]{1,0:T(8,128)(2,1)S(1)}, u32[]{:S(2)}, u32[]{:S(2)}) collective-permute-start(bf16[32,1536]{1,0:T(8,128)(2,1)S(1)} %shard_map.70.refs_1_), channel_id=1, source_target_pairs={{0,4},{1,5},{2,6},{3,7},{4,0},{5,1},{6,2},{7,3},{8,9},{9,8},{10,11... | collective-permute-start | bytes 294920 | tf_op jit(solution)/shard_map/ppermute | solution.py:107
  78.0 1.3 %collective-permute-start.19 = (f32[2,32,192]{2,1,0:T(8,128)S(1)}, f32[2,32,192]{2,1,0:T(8,128)S(1)}, u32[]{:S(2)}, u32[]{:S(2)}) collective-permute-start(f32[2,32,192]{2,1,0:T(8,128)S(1)} %get-tuple-element.57), channel_id=1, source_target_pairs={{0,1},{1,0},{2,3},{3,2},{4,5},{5,4},{6,7},{7,6},{8,9},{9,8},{10,11... | collective-permute-start | bytes 147464 | tf_op jit(solution)/shard_map/ppermute | solution.py:107
  78.0 1.4 %collective-permute-start.20 = (f32[2,32,192]{2,1,0:T(8,128)S(1)}, f32[2,32,192]{2,1,0:T(8,128)S(1)}, u32[]{:S(2)}, u32[]{:S(2)}) collective-permute-start(f32[2,32,192]{2,1,0:T(8,128)S(1)} %get-tuple-element.58), channel_id=1, source_target_pairs={{0,1},{1,0},{2,3},{3,2},{4,5},{5,4},{6,7},{7,6},{8,10},{9,11},{10,... | collective-permute-start | bytes 147464 | tf_op jit(solution)/shard_map/ppermute | solution.py:107
  78.5 1.3 %collective-permute-start.21 = (f32[2,32,192]{2,1,0:T(8,128)S(1)}, f32[2,32,192]{2,1,0:T(8,128)S(1)}, u32[]{:S(2)}, u32[]{:S(2)}) collective-permute-start(f32[2,32,192]{2,1,0:T(8,128)S(1)} %get-tuple-element.59), channel_id=1, source_target_pairs={{0,1},{1,0},{2,3},{3,2},{4,5},{5,4},{6,7},{7,6},{8,11},{9,10},{10,... | collective-permute-start | bytes 147464 | tf_op jit(solution)/shard_map/ppermute | solution.py:107
  78.9 9.5 %copy-start.1 = (bf16[1,192,1536]{2,1,0:T(8,128)(2,1)S(1)}, bf16[1,192,1536]{2,1,0:T(8,128)(2,1)}, u32[]{:S(2)}) copy-start(bf16[1,192,1536]{2,1,0:T(8,128)(2,1)} %param.6) | copy-start | bytes 1769476
  81.1 5.1 %collective-permute-start.26 = (bf16[32,1536]{1,0:T(8,128)(2,1)S(1)}, bf16[32,1536]{1,0:T(8,128)(2,1)S(1)}, u32[]{:S(2)}, u32[]{:S(2)}) collective-permute-start(bf16[32,1536]{1,0:T(8,128)(2,1)S(1)} %shard_map.73.refs_0_), channel_id=1, source_target_pairs={{0,3},{1,2},{2,1},{3,0},{4,7},{5,6},{6,5},{7,4},{8,9},{9,8},{10,11... | collective-permute-start | bytes 294920 | tf_op jit(solution)/shard_map/ppermute | solution.py:107
  81.2 7.2 %collective-permute-start.25 = (bf16[32,1536]{1,0:T(8,128)(2,1)S(1)}, bf16[32,1536]{1,0:T(8,128)(2,1)S(1)}, u32[]{:S(2)}, u32[]{:S(2)}) collective-permute-start(bf16[32,1536]{1,0:T(8,128)(2,1)S(1)} %shard_map.73.refs_0_), channel_id=1, source_target_pairs={{0,2},{1,3},{2,0},{3,1},{4,6},{5,7},{6,4},{7,5},{8,9},{9,8},{10,11... | collective-permute-start | bytes 294920 | tf_op jit(solution)/shard_map/ppermute | solution.py:107
  82.8 5.6 %collective-permute-start.24 = (bf16[32,1536]{1,0:T(8,128)(2,1)S(1)}, bf16[32,1536]{1,0:T(8,128)(2,1)S(1)}, u32[]{:S(2)}, u32[]{:S(2)}) collective-permute-start(bf16[32,1536]{1,0:T(8,128)(2,1)S(1)} %shard_map.73.refs_0_), channel_id=1, source_target_pairs={{0,1},{1,0},{2,3},{3,2},{4,5},{5,4},{6,7},{7,6},{8,9},{9,8},{10,11... | collective-permute-start | bytes 294920 | tf_op jit(solution)/shard_map/ppermute | solution.py:107

commit v7 on v6

--- a/solution.py
+++ b/solution.py
@@ -202,12 +202,13 @@
             if k == last:
                 block = jnp.where(height() == 0, block, inv_ref[...])
             outs[0][:, k * width : (k + 1) * width] = block
-            outs[1][:, k * width : (k + 1) * width] = block
+            if k < last:
+                outs[1][:, k * width : (k + 1) * width] = jnp.where(height() == 1, block, inv_ref[...])
 
     full = levels * width + 2 * rhs_count
     rows_own, rows_sent = call(
         build,
-        [((row_count, full), BF16), ((row_count, levels * width), BF16)],
+        [((row_count, full), BF16), ((row_count, last * width), BF16)],
         [pattern, give, rhs_own, inverse_own, panel],
     )
     rows_own, rows_sent = after((rows_own, rows_sent), got)
@@ -220,7 +221,7 @@
         return ref[:, k * width : (k + 1) * width]
 
     def inverse_of(ref):
-        return factor_of(ref, last)
+        return factor_of(ref, last) if ref.shape[1] == full else ref[:, :width]
 
     rounds = leaf_rounds(members)
 
@@ -265,20 +266,32 @@
             side = mmt(pick, rhs_pair[:, :rhs_count]) + mmt(pick, rhs_pair[:, rhs_count:])
             less = total_of([heard(n, ref[:, span(j)].astype(F32)) for n, ref in enumerate(came)])
             parts.append(mm((side - less).astype(BF16), inverse_of(pair[j])))
-        outs[0][...] = total_of(parts).astype(BF16)
+        product = total_of(parts).astype(BF16)
+        for i in range(lanes):
+            outs[i][...] = product[i * group : (i + 1) * group]
 
     def by_lane(ins, outs):
         total = row_total(ins).astype(BF16)
-        for i in range(lanes):
-            outs[i][...] = total[i * group : (i + 1) * group]
-
-    own_term = call(inner_first, ((half, width), BF16), [*early, rows_own, rows_far])
-    first_term, *others = call(by_lane, [term] * lanes, over_rows(own_term, inner))
-    first_terms = [first_term] + [across(others[i - 1], 2 * i, inner) for i in range(1, lanes)]
-    inner_rows = [rows_own, rows_far]
+        outs[0][...] = total
+
+    leaf_lanes = [across(after(rows_own, leaf_half), 2 * i, leaves) for i in range(1, lanes)]
+    first_rows = [rows_own, rows_far]
     for near in rows_lanes:
-        inner_rows += [near, across(after(near, first_term), 1, inner)]
-    leaf_far = across(after(leaf_half, first_term), 1, leaves)
+        first_rows += [near, across(after(near, *early), 1, inner)]
+    early[0] = after(early[0], *rows_lanes)
+    own_term, *others = call(inner_first, [term] * lanes, [*early, rows_own, rows_far])
+    leaf_rows_of = [rows_own, rows_far]
+    own_term = call(by_lane, term, [own_term] + [across(others[i - 1], 2 * i, inner) for i in range(1, lanes)])
+    first_terms = over_rows(own_term, inner)
+    first_terms[0] = after(first_terms[0], *leaf_lanes)
+    leaf_far = across(after(leaf_half, own_term), 1, leaves)
+
+    def spread(matrix, planes, wait, wait_far):
+        parts = [rows_own, rows_far]
+        for i in range(1, lanes):
+            near = across(after(matrix, wait), 2 * i, planes)
+            parts += [near, across(after(near, wait_far), 1, planes)]
+        return parts
 
     samples = {}
     arrived = []
@@ -296,7 +309,7 @@
                     parts.append(mm(less.astype(BF16), inverse_of(rows_of[b])))
                 outs[0][...] = (-total_of(parts)).astype(BF16)
 
-            terms += over_rows(call(inner_second, term, [*arrived, *inner_rows]), nodes)
+            terms += over_rows(call(inner_second, term, [*arrived, *first_rows]), nodes)
         count = len(terms)
         if remain:
 
@@ -315,9 +328,16 @@
             samples[section], sent = call(
                 inner_push,
                 [((group, width), F32), ((remain, group, blocks * row_count), BF16)],
-                [*terms, *arrived, *inner_rows],
+                [*terms, *arrived, *(first_rows if section == 1 else higher_rows)],
             )
             arrived = [along(sent, links) for links in child_links(section + 1, members)]
+            if section == 1:
+                second_rows = spread(inverse_own, nodes_at[1], own_term, arrived[0])
+                for near in leaf_lanes:
+                    leaf_rows_of += [near, across(after(near, arrived[0]), 1, leaves)]
+                arrived[0] = after(arrived[0], *second_rows[2::2])
+                higher = [node for node in inner if 1 < levels_of[node] < levels]
+                higher_rows = spread(rows_own[:, : last * width], higher, sent, sent) if higher else []
 
     def root_back(ins, outs):
         solved = row_total(ins[:-blocks])
@@ -331,11 +351,9 @@
     samples[levels], answer, sent = call(
         root_back,
         [((group, width), F32), vector, ((1, group, blocks * row_count), BF16)],
-        [*terms, *inner_rows],
-    )
-
-    leaf_rows_of = [rows_own, rows_far]
-    leaf_lanes = [across(after(rows_sent, sent), 2 * i, leaves) for i in range(1, lanes)]
+        [*terms, *first_rows],
+    )
+
 
     def split_rows(ins, outs):
         rank = height()
@@ -356,6 +374,8 @@
         remain = levels - section
         ancestry = [along(sent, down(links)) for links in child_links(section + 1, members)]
         ancestry = ancestry[0] if len(ancestry) == 1 else from_parent(*ancestry, section + 1)
+        if section == 1:
+            ancestry = after(ancestry, *second_rows)
 
         def adjoint_first(ins, outs):
             parts = []
@@ -364,11 +384,9 @@
                     parts.append(mm(ins[0][k, :, span(b)], factor_of(ins[1 + b], k)))
             outs[0][...] = total_of(parts).astype(BF16)
 
-        own_term = call(adjoint_first, term, [ancestry, *inner_rows])
+        own_term = call(adjoint_first, term, [ancestry, *(first_rows if section == 1 else higher_rows)])
         terms = over_rows(own_term, nodes_at[section])
         if section == 1:
-            for near in leaf_lanes:
-                leaf_rows_of += [near, across(after(near, own_term), 1, leaves)]
             order = [after(samples[s], own_term) for s in range(1, levels + 1)]
             sample_rows = call(split_rows, vector, order)
 
@@ -388,7 +406,7 @@
                 else:
                     outs[1][b] = chosen
 
-        args = [*terms, samples[section], ancestry, answer, *inner_rows]
+        args = [*terms, samples[section], ancestry, answer, *(second_rows if section == 1 else first_rows)]
         outs = [((remain + 1, group, blocks * row_count), BF16)]
         if section == 1:
             args, outs = [*args, sample_rows], outs + [((2, group, row_count), F32)] * blocks

time: 89.7 us -> 82.8 us (0.923)
  waiting for transfers between devices: 57.7 us -> 46.8 us
  starting transfers between devices: 17.2 us -> 21.2 us
    ppermute x27 -> x29, waiting for transfers between devices: 57.7 us -> 46.8 us  [permute(): return lax.ppermute(x, ('lvl', 'col'), pairs)]
    ppermute x27 -> x29, starting transfers between devices: 17.2 us -> 21.2 us  [permute(): return lax.ppermute(x, ('lvl', 'col'), pairs)]
  transfers between devices with their start and end apart: 27 -> 29, of which waited for: 19 -> 17; matrix products, arithmetic and copies ran while one was open for 1% -> 1% of each run, Pallas kernels for 7% -> 9%
where the time goes in v7:
time: 82.8 us; the launch traced here: 82.5 us
  waiting for transfers between devices  46.8 us (57%)
  starting transfers between devices  21.2 us (26%)
  Pallas kernels  9.76 us (12%)
  local copies, waits for them, and re-layouts  3.93 us (5%)
    ppermute x29, waiting for transfers between devices, permute(): return lax.ppermute(x, ('lvl', 'col'), pairs)  46.8 us
    ppermute x29, starting transfers between devices, permute(): return lax.ppermute(x, ('lvl', 'col'), pairs)  21.2 us
    pallas_call x16, Pallas kernels, call(): pl.pallas_call(kernel, out_shape=[jax.ShapeDtypeStruct(shape, dtype) for...  9.76 us
    unnamed x9, local copies, waits for them, and re-layouts  3.93 us
  transfers between devices with their start and end apart: 29, of which 17 were waited for; matrix products, arithmetic and copies ran while one was open for 1% of the time, Pallas kernels for 9%

profile of v7, /device:TPU:0, one launch (start us, length us, event | category | flops | bytes accessed | tf_op | source)
XLA Modules:
  0.0 82.5 jit_solution(5805117896948147074)
XLA Ops:
  0.6 0.0 copy-start
  0.6 1.1 %copy-done = bf16[1,192,1536]{2,1,0:T(8,128)(2,1)S(1)} copy-done((bf16[1,192,1536]{2,1,0:T(8,128)(2,1)S(1)}, bf16[1,192,1536]{2,1,0:T(8,128)(2,1)}, u32[]{:S(2)}) %copy-start) | copy-done | bytes 589848
  1.7 0.9 %copy-done.3 = f32[1,192,128]{2,1,0:T(8,128)S(1)} copy-done((f32[1,192,128]{2,1,0:T(8,128)S(1)}, f32[1,192,128]{2,1,0:T(8,128)}, u32[]{:S(2)}) %copy-start.3) | copy-done | bytes 98328
  2.6 0.4 shard_map.59
  3.0 0.5 collective-permute-start
  3.5 0.7 copy.6.refs_0_
  4.2 1.3 %copy-done.2 = bf16[1,2,192,1536]{3,2,1,0:T(8,128)(2,1)S(1)} copy-done((bf16[1,2,192,1536]{3,2,1,0:T(8,128)(2,1)S(1)}, bf16[1,2,192,1536]{3,2,1,0:T(8,128)(2,1)}, u32[]{:S(2)}) %copy-start.2) | copy-done | bytes 1179672
  5.5 0.7 shard_map.60
  6.2 0.0 collective-permute-done
  6.2 0.1 collective-permute-start.4
  6.4 4.0 %collective-permute-start.3 = (bf16[64,1536]{1,0:T(8,128)(2,1)S(1)}, bf16[64,1536]{1,0:T(8,128)(2,1)S(1)}, u32[]{:S(2)}, u32[]{:S(2)}) collective-permute-start(bf16[64,1536]{1,0:T(8,128)(2,1)S(1)} %add_convert_fusion.refs_0_), channel_id=1, source_target_pairs={{0,6},{1,7},{2,4},{3,5},{4,2},{5,3},{6,0},{7,1},{8,9},{9,8},{10,11... | collective-permute-start | bytes 589832 | tf_op jit(solution)/shard_map/ppermute | solution.py:107
  10.3 0.5 collective-permute-start.2
  10.8 0.1 collective-permute-start.1
  11.0 5.1 %collective-permute-done.3.refs_3_ = bf16[64,1536]{1,0:T(8,128)(2,1)S(1)} collective-permute-done((bf16[64,1536]{1,0:T(8,128)(2,1)S(1)}, bf16[64,1536]{1,0:T(8,128)(2,1)S(1)}, u32[]{:S(2)}, u32[]{:S(2)}) %collective-permute-start.3) | collective-permute-done | bytes 196640 | tf_op jit(solution)/shard_map/ppermute | solution.py:107
  16.1 3.5 %collective-permute-done.2.refs_2_ = bf16[64,1536]{1,0:T(8,128)(2,1)S(1)} collective-permute-done((bf16[64,1536]{1,0:T(8,128)(2,1)S(1)}, bf16[64,1536]{1,0:T(8,128)(2,1)S(1)}, u32[]{:S(2)}, u32[]{:S(2)}) %collective-permute-start.2) | collective-permute-done | bytes 196640 | tf_op jit(solution)/shard_map/ppermute | solution.py:107
  19.6 0.3 collective-permute-done.1.refs_1_
  19.9 0.0 collective-permute-done.4.refs_5_.refs_3_.refs_2_.refs_6_
  19.9 0.9 %shard_map.61 = (bf16[64,1536]{1,0:T(8,128)(2,1)S(1)}, bf16[64,384]{1,0:T(8,128)(2,1)S(1)}, bf16[64,384]{1,0:T(8,128)(2,1)S(1)}) custom-call(bf16[64,1536]{1,0:T(8,128)(2,1)S(1)} %add_convert_fusion.refs_0_, bf16[64,1536]{1,0:T(8,128)(2,1)S(1)} %collective-permute-done.1.refs_1_, bf16[64,1536]{1,0:T(8,128)(2,1)S(1)} %collective-permute-done.2.refs_2_, ...), custom_call_target="tpu_custom_call" | custom-call | flops 268435456 | bytes 3342336 | tf_op jit(solution)/shard_map/pallas_call | solution.py:62
  20.9 1.6 %collective-permute-start.9 = (bf16[192,3328]{1,0:T(8,128)(2,1)S(1)}, bf16[192,3328]{1,0:T(8,128)(2,1)S(1)}, u32[]{:S(2)}, u32[]{:S(2)}) collective-permute-start(bf16[192,3328]{1,0:T(8,128)(2,1)S(1)} %get-tuple-element.52.refs_4_.refs_2_.refs_1_.refs_5_), channel_id=1, source_target_pairs={{0,2},{1,3},{2,0},{3,1},{4,6},{5,7},{6,4},{7,5},{8,9},{9,8},{10,11... | collective-permute-start | bytes 3833864 | tf_op jit(solution)/shard_map/ppermute | solution.py:107
  22.4 0.0 collective-permute-start.6
  22.5 4.1 %collective-permute-start.7 = (bf16[64,384]{1,0:T(8,128)(2,1)S(1)}, bf16[64,384]{1,0:T(8,128)(2,1)S(1)}, u32[]{:S(2)}, u32[]{:S(2)}) collective-permute-start(bf16[64,384]{1,0:T(8,128)(2,1)S(1)} %get-tuple-element.49), channel_id=1, source_target_pairs={{0,24},{1,25},{2,26},{3,27},{4,28},{5,29},{6,30},{7,31},{8,16},{9,... | collective-permute-start | bytes 147464 | tf_op jit(solution)/shard_map/ppermute | solution.py:107
  26.5 0.1 collective-permute-done.5.refs_0_
  26.6 3.1 %collective-permute-done.7.refs_1_ = bf16[64,384]{1,0:T(8,128)(2,1)S(1)} collective-permute-done((bf16[64,384]{1,0:T(8,128)(2,1)S(1)}, bf16[64,384]{1,0:T(8,128)(2,1)S(1)}, u32[]{:S(2)}, u32[]{:S(2)}) %collective-permute-start.7) | collective-permute-done | bytes 49184 | tf_op jit(solution)/shard_map/ppermute | solution.py:107
  29.7 0.5 shard_map.62
  30.2 0.6 collective-permute-start.8
  30.8 1.0 %collective-permute-done.8.refs_1_ = bf16[32,1536]{1,0:T(8,128)(2,1)S(1)} collective-permute-done((bf16[32,1536]{1,0:T(8,128)(2,1)S(1)}, bf16[32,1536]{1,0:T(8,128)(2,1)S(1)}, u32[]{:S(2)}, u32[]{:S(2)}) %collective-permute-start.8) | collective-permute-done | bytes 98336 | tf_op jit(solution)/shard_map/ppermute | solution.py:107
  31.9 0.3 collective-permute-start.10
  32.2 0.2 collective-permute-start.13
  32.4 18.2 %collective-permute-done.9.refs_4_ = bf16[192,3328]{1,0:T(8,128)(2,1)S(1)} collective-permute-done((bf16[192,3328]{1,0:T(8,128)(2,1)S(1)}, bf16[192,3328]{1,0:T(8,128)(2,1)S(1)}, u32[]{:S(2)}, u32[]{:S(2)}) %collective-permute-start.9) | collective-permute-done | bytes 1277984 | tf_op jit(solution)/shard_map/ppermute | solution.py:107
  50.7 0.9 %shard_map.64 = (f32[32,1536]{1,0:T(8,128)S(1)}, bf16[1,32,768]{2,1,0:T(8,128)(2,1)S(1)}) custom-call(bf16[32,1536]{1,0:T(8,128)(2,1)S(1)} %shard_map.63.refs_0_, bf16[32,1536]{1,0:T(8,128)(2,1)S(1)} %collective-permute-done.10.refs_1_, bf16[192,3328]{1,0:T(8,128)(2,1)S(1)} %get-tuple-element.52.refs_4_.refs_2_.refs_1_.refs_5_, ...), custom_call_target="tpu_custom_call" | custom-call | flops 268435456 | bytes 3932160 | tf_op jit(solution)/shard_map/pallas_call | solution.py:62
  51.5 0.0 collective-permute-start.12
  51.6 1.2 %collective-permute-done.12.refs_0_ = bf16[1,32,768]{2,1,0:T(8,128)(2,1)S(1)} collective-permute-done((bf16[1,32,768]{2,1,0:T(8,128)(2,1)S(1)}, bf16[1,32,768]{2,1,0:T(8,128)(2,1)S(1)}, u32[]{:S(2)}, u32[]{:S(2)}) %collective-permute-start.12) | collective-permute-done | bytes 49184 | tf_op jit(solution)/shard_map/ppermute | solution.py:107
  52.8 0.2 collective-permute-start.20
  53.0 0.3 collective-permute-start.16
  53.3 0.6 shard_map.65.refs_2_
  53.9 0.2 collective-permute-start.14
  54.1 2.6 %collective-permute-done.14.refs_3_ = bf16[32,1536]{1,0:T(8,128)(2,1)S(1)} collective-permute-done((bf16[32,1536]{1,0:T(8,128)(2,1)S(1)}, bf16[32,1536]{1,0:T(8,128)(2,1)S(1)}, u32[]{:S(2)}, u32[]{:S(2)}) %collective-permute-start.14) | collective-permute-done | bytes 98336 | tf_op jit(solution)/shard_map/ppermute | solution.py:107
  56.8 0.9 %shard_map.66 = (f32[32,1536]{1,0:T(8,128)S(1)}, f32[4,32,192]{2,1,0:T(8,128)S(1)}, bf16[1,32,768]{2,1,0:T(8,128)(2,1)S(1)}) custom-call(bf16[32,1536]{1,0:T(8,128)(2,1)S(1)} %shard_map.63.refs_0_, bf16[32,1536]{1,0:T(8,128)(2,1)S(1)} %collective-permute-done.10.refs_1_, bf16[32,1536]{1,0:T(8,128)(2,1)S(1)} %shard_map.65.refs_2_, ...), custom_call_target="tpu_custom_call" | custom-call | flops 268435456 | bytes 4128768 | tf_op jit(solution)/shard_map/pallas_call | solution.py:62
  57.6 0.2 collective-permute-start.15
  57.8 1.1 %collective-permute-done.15.refs_0_.refs_3_ = bf16[1,32,768]{2,1,0:T(8,128)(2,1)S(1)} collective-permute-done((bf16[1,32,768]{2,1,0:T(8,128)(2,1)S(1)}, bf16[1,32,768]{2,1,0:T(8,128)(2,1)S(1)}, u32[]{:S(2)}, u32[]{:S(2)}) %collective-permute-start.15) | collective-permute-done | bytes 49184 | tf_op jit(solution)/shard_map/ppermute | solution.py:107
  58.9 0.6 shard_map.67.refs_0_
  59.5 0.2 collective-permute-start.17
  59.7 0.3 collective-permute-start.24
  60.1 0.9 %shard_map.68.refs_9_ = f32[4,32,192]{2,1,0:T(8,128)S(1)} custom-call(f32[32,1536]{1,0:T(8,128)S(1)} %get-tuple-element.63.refs_0_.refs_2_, f32[32,1536]{1,0:T(8,128)S(1)} %get-tuple-element.65.refs_1_), custom_call_target="tpu_custom_call" | custom-call | flops 268435456 | bytes 393216 | tf_op jit(solution)/shard_map/pallas_call | solution.py:62
  60.9 0.0 collective-permute-done.17.refs_1_
  60.9 0.9 %shard_map.69 = (bf16[2,32,768]{2,1,0:T(8,128)(2,1)S(1)}, f32[2,32,192]{2,1,0:T(8,128)S(1)}, f32[2,32,192]{2,1,0:T(8,128)S(1)}, f32[2,32,192]{2,1,0:T(8,128)S(1)}, f32[2,32,192]{2,1,0:T(8,128)S(1)}) custom-call(bf16[32,1536]{1,0:T(8,128)(2,1)S(1)} %shard_map.67.refs_0_, bf16[32,1536]{1,0:T(8,128)(2,1)S(1)} %collective-permute-done.17.refs_1_, ...), custom_call_target="tpu_custom_call" | custom-call | flops 268435456 | bytes 4374528 | tf_op jit(solution)/shard_map/pallas_call | solution.py:62
  61.8 0.2 collective-permute-start.19
  62.0 3.9 %collective-permute-start.18 = (bf16[2,32,768]{2,1,0:T(8,128)(2,1)S(1)}, bf16[2,32,768]{2,1,0:T(8,128)(2,1)S(1)}, u32[]{:S(2)}, u32[]{:S(2)}) collective-permute-start(bf16[2,32,768]{2,1,0:T(8,128)(2,1)S(1)} %get-tuple-element.66), channel_id=1, source_target_pairs={{0,8},{1,9},{2,10},{3,11},{4,12},{5,13},{6,14},{7,15},{8,0},{9,1},... | collective-permute-start | bytes 294920 | tf_op jit(solution)/shard_map/ppermute | solution.py:107
  66.0 2.6 %collective-permute-done.18.refs_0_ = bf16[2,32,768]{2,1,0:T(8,128)(2,1)S(1)} collective-permute-done((bf16[2,32,768]{2,1,0:T(8,128)(2,1)S(1)}, bf16[2,32,768]{2,1,0:T(8,128)(2,1)S(1)}, u32[]{:S(2)}, u32[]{:S(2)}) %collective-permute-start.18) | collective-permute-done | bytes 98336 | tf_op jit(solution)/shard_map/ppermute | solution.py:107
  68.6 1.0 %shard_map.70.refs_1_ = bf16[32,1536]{1,0:T(8,128)(2,1)S(1)} custom-call(bf16[2,32,768]{2,1,0:T(8,128)(2,1)S(1)} %collective-permute-done.18.refs_0_, bf16[2,32,768]{2,1,0:T(8,128)(2,1)S(1)} %collective-permute-done.19.refs_1_, bf16[192,3328]{1,0:T(8,128)(2,1)S(1)} %get-tuple-element.52.refs_4_.refs_2_.refs_1_.refs_5_, ...), custom_call_target="tpu_custom_call" | custom-call | flops 268435456 | bytes 5308416 | tf_op jit(solution)/shard_map/pallas_call | solution.py:62
  69.5 1.1 %collective-permute-start.25 = (bf16[32,1536]{1,0:T(8,128)(2,1)S(1)}, bf16[32,1536]{1,0:T(8,128)(2,1)S(1)}, u32[]{:S(2)}, u32[]{:S(2)}) collective-permute-start(bf16[32,1536]{1,0:T(8,128)(2,1)S(1)} %shard_map.70.refs_1_), channel_id=1, source_target_pairs={{0,4},{1,5},{2,6},{3,7},{4,0},{5,1},{6,2},{7,3},{8,9},{9,8},{10,11... | collective-permute-start | bytes 294920 | tf_op jit(solution)/shard_map/ppermute | solution.py:107
  70.6 0.5 collective-permute-start.22
  71.1 0.3 shard_map.72.refs_4_
  71.5 0.4 collective-permute-done.21.refs_1_
  71.9 0.2 collective-permute-done.22.refs_2_
  72.0 0.4 collective-permute-done.23.refs_3_
  72.4 0.1 shard_map.71
  72.5 1.7 %collective-permute-done.25.refs_2_ = bf16[32,1536]{1,0:T(8,128)(2,1)S(1)} collective-permute-done((bf16[32,1536]{1,0:T(8,128)(2,1)S(1)}, bf16[32,1536]{1,0:T(8,128)(2,1)S(1)}, u32[]{:S(2)}, u32[]{:S(2)}) %collective-permute-start.25) | collective-permute-done | bytes 98336 | tf_op jit(solution)/shard_map/ppermute | solution.py:107
  74.3 0.1 collective-permute-start.28
  74.3 1.6 %collective-permute-start.27 = (bf16[32,1536]{1,0:T(8,128)(2,1)S(1)}, bf16[32,1536]{1,0:T(8,128)(2,1)S(1)}, u32[]{:S(2)}, u32[]{:S(2)}) collective-permute-start(bf16[32,1536]{1,0:T(8,128)(2,1)S(1)} %shard_map.73.refs_0_), channel_id=1, source_target_pairs={{0,2},{1,3},{2,0},{3,1},{4,6},{5,7},{6,4},{7,5},{8,9},{9,8},{10,11... | collective-permute-start | bytes 294920 | tf_op jit(solution)/shard_map/ppermute | solution.py:107
  75.9 0.3 collective-permute-start.26
  76.2 3.2 %collective-permute-done.28.refs_3_ = bf16[32,1536]{1,0:T(8,128)(2,1)S(1)} collective-permute-done((bf16[32,1536]{1,0:T(8,128)(2,1)S(1)}, bf16[32,1536]{1,0:T(8,128)(2,1)S(1)}, u32[]{:S(2)}, u32[]{:S(2)}) %collective-permute-start.28) | collective-permute-done | bytes 98336 | tf_op jit(solution)/shard_map/ppermute | solution.py:107
  79.4 2.1 %collective-permute-done.27.refs_2_ = bf16[32,1536]{1,0:T(8,128)(2,1)S(1)} collective-permute-done((bf16[32,1536]{1,0:T(8,128)(2,1)S(1)}, bf16[32,1536]{1,0:T(8,128)(2,1)S(1)}, u32[]{:S(2)}, u32[]{:S(2)}) %collective-permute-start.27) | collective-permute-done | bytes 98336 | tf_op jit(solution)/shard_map/ppermute | solution.py:107
  81.5 1.0 %shard_map.74 = (f32[192,128]{1,0:T(8,128)}, f32[192,128]{1,0:T(8,128)}) custom-call(bf16[32,1536]{1,0:T(8,128)(2,1)S(1)} %shard_map.73.refs_0_, bf16[32,1536]{1,0:T(8,128)(2,1)S(1)} %collective-permute-done.26.refs_1_, bf16[32,1536]{1,0:T(8,128)(2,1)S(1)} %collective-permute-done.27.refs_2_, bf16[32,1536]{1,0:T(8,128)(2,1)S(1)} %collective-permute-done.28.refs_3_, ...), custom_call_target="tpu_custom_call" | custom-call | flops 268435456 | bytes 1277952 | tf_op jit(solution)/shard_map/pallas_call | solution.py:62
  (20 shorter events, 0.2 us)
Async XLA Ops:
  0.6 1.1 %copy-start = (bf16[1,192,1536]{2,1,0:T(8,128)(2,1)S(1)}, bf16[1,192,1536]{2,1,0:T(8,128)(2,1)}, u32[]{:S(2)}) copy-start(bf16[1,192,1536]{2,1,0:T(8,128)(2,1)} %param.6) | copy-start | bytes 1769476
  1.7 0.9 %copy-start.3 = (f32[1,192,128]{2,1,0:T(8,128)S(1)}, f32[1,192,128]{2,1,0:T(8,128)}, u32[]{:S(2)}) copy-start(f32[1,192,128]{2,1,0:T(8,128)} %param.4) | copy-start | bytes 294916
  3.0 3.2 %collective-permute-start = (bf16[64,1536]{1,0:T(8,128)(2,1)S(1)}, bf16[64,1536]{1,0:T(8,128)(2,1)S(1)}, u32[]{:S(2)}, u32[]{:S(2)}) collective-permute-start(bf16[64,1536]{1,0:T(8,128)(2,1)S(1)} %get-tuple-element.41.refs_1_), channel_id=1, source_target_pairs={{0,1},{1,0},{2,3},{3,2},{4,5},{5,4},{6,7},{7,6},{8,9},{9,8},{10,11... | collective-permute-start | bytes 589832 | tf_op jit(solution)/shard_map/ppermute | solution.py:107
  4.2 1.3 %copy-start.2 = (bf16[1,2,192,1536]{3,2,1,0:T(8,128)(2,1)S(1)}, bf16[1,2,192,1536]{3,2,1,0:T(8,128)(2,1)}, u32[]{:S(2)}) copy-start(bf16[1,2,192,1536]{3,2,1,0:T(8,128)(2,1)} %refs_4_.1) | copy-start | bytes 3538948
  6.2 13.7 %collective-permute-start.4 = (bf16[192,3328]{1,0:T(8,128)(2,1)S(1)}, bf16[192,3328]{1,0:T(8,128)(2,1)S(1)}, u32[]{:S(2)}, u32[]{:S(2)}) collective-permute-start(bf16[192,3328]{1,0:T(8,128)(2,1)S(1)} %get-tuple-element.52.refs_4_.refs_2_.refs_1_.refs_5_), channel_id=1, source_target_pairs={{0,1},{1,0},{2,3},{3,2},{4,5},{5,4},{6,7},{7,6},{8,9},{9,8},{10,11... | collective-permute-start | bytes 3833864 | tf_op jit(solution)/shard_map/ppermute | solution.py:107
  6.4 9.7 %collective-permute-start.3 = (bf16[64,1536]{1,0:T(8,128)(2,1)S(1)}, bf16[64,1536]{1,0:T(8,128)(2,1)S(1)}, u32[]{:S(2)}, u32[]{:S(2)}) collective-permute-start(bf16[64,1536]{1,0:T(8,128)(2,1)S(1)} %add_convert_fusion.refs_0_), channel_id=1, source_target_pairs={{0,6},{1,7},{2,4},{3,5},{4,2},{5,3},{6,0},{7,1},{8,9},{9,8},{10,11... | collective-permute-start | bytes 589832 | tf_op jit(solution)/shard_map/ppermute | solution.py:107
  10.3 9.3 %collective-permute-start.2 = (bf16[64,1536]{1,0:T(8,128)(2,1)S(1)}, bf16[64,1536]{1,0:T(8,128)(2,1)S(1)}, u32[]{:S(2)}, u32[]{:S(2)}) collective-permute-start(bf16[64,1536]{1,0:T(8,128)(2,1)S(1)} %add_convert_fusion.refs_0_), channel_id=1, source_target_pairs={{0,4},{1,5},{2,6},{3,7},{4,0},{5,1},{6,2},{7,3},{8,9},{9,8},{10,11... | collective-permute-start | bytes 589832 | tf_op jit(solution)/shard_map/ppermute | solution.py:107
  10.8 9.1 %collective-permute-start.1 = (bf16[64,1536]{1,0:T(8,128)(2,1)S(1)}, bf16[64,1536]{1,0:T(8,128)(2,1)S(1)}, u32[]{:S(2)}, u32[]{:S(2)}) collective-permute-start(bf16[64,1536]{1,0:T(8,128)(2,1)S(1)} %add_convert_fusion.refs_0_), channel_id=1, source_target_pairs={{0,2},{1,3},{2,0},{3,1},{4,6},{5,7},{6,4},{7,5},{8,9},{9,8},{10,11... | collective-permute-start | bytes 589832 | tf_op jit(solution)/shard_map/ppermute | solution.py:107
  20.9 29.8 %collective-permute-start.9 = (bf16[192,3328]{1,0:T(8,128)(2,1)S(1)}, bf16[192,3328]{1,0:T(8,128)(2,1)S(1)}, u32[]{:S(2)}, u32[]{:S(2)}) collective-permute-start(bf16[192,3328]{1,0:T(8,128)(2,1)S(1)} %get-tuple-element.52.refs_4_.refs_2_.refs_1_.refs_5_), channel_id=1, source_target_pairs={{0,2},{1,3},{2,0},{3,1},{4,6},{5,7},{6,4},{7,5},{8,9},{9,8},{10,11... | collective-permute-start | bytes 3833864 | tf_op jit(solution)/shard_map/ppermute | solution.py:107
  22.4 4.1 %collective-permute-start.6 = (bf16[192,1536]{1,0:T(8,128)(2,1)S(1)}, bf16[192,1536]{1,0:T(8,128)(2,1)S(1)}, u32[]{:S(2)}, u32[]{:S(2)}) collective-permute-start(bf16[192,1536]{1,0:T(8,128)(2,1)S(1)} %get-tuple-element.47), channel_id=1, source_target_pairs={{0,1},{1,0},{2,3},{3,2},{4,5},{5,4},{6,7},{7,6},{8,10},{9,11},{10,... | collective-permute-start | bytes 1769480 | tf_op jit(solution)/shard_map/ppermute | solution.py:107
  22.4 4.2 %collective-permute-start.5 = (bf16[64,384]{1,0:T(8,128)(2,1)S(1)}, bf16[64,384]{1,0:T(8,128)(2,1)S(1)}, u32[]{:S(2)}, u32[]{:S(2)}) collective-permute-start(bf16[64,384]{1,0:T(8,128)(2,1)S(1)} %get-tuple-element.46), channel_id=1, source_target_pairs={{0,8},{1,9},{2,10},{3,11},{4,12},{5,13},{6,14},{7,15},{8,0},{9,1},... | collective-permute-start | bytes 147464 | tf_op jit(solution)/shard_map/ppermute | solution.py:107
  22.5 9.8 %copy-start.1 = (bf16[1,192,1536]{2,1,0:T(8,128)(2,1)S(1)}, bf16[1,192,1536]{2,1,0:T(8,128)(2,1)}, u32[]{:S(2)}) copy-start(bf16[1,192,1536]{2,1,0:T(8,128)(2,1)} %param.6) | copy-start | bytes 1769476
  22.5 7.2 %collective-permute-start.7 = (bf16[64,384]{1,0:T(8,128)(2,1)S(1)}, bf16[64,384]{1,0:T(8,128)(2,1)S(1)}, u32[]{:S(2)}, u32[]{:S(2)}) collective-permute-start(bf16[64,384]{1,0:T(8,128)(2,1)S(1)} %get-tuple-element.49), channel_id=1, source_target_pairs={{0,24},{1,25},{2,26},{3,27},{4,28},{5,29},{6,30},{7,31},{8,16},{9,... | collective-permute-start | bytes 147464 | tf_op jit(solution)/shard_map/ppermute | solution.py:107
  29.7 21.0 %collective-permute-start.11 = (bf16[192,1536]{1,0:T(8,128)(2,1)S(1)}, bf16[192,1536]{1,0:T(8,128)(2,1)S(1)}, u32[]{:S(2)}, u32[]{:S(2)}) collective-permute-start(bf16[192,1536]{1,0:T(8,128)(2,1)S(1)} %collective-permute-done.6.refs_4_.refs_3_.refs_6_), channel_id=1, source_target_pairs={{0,1},{1,0},{2,3},{3,2},{4,5},{5,4},{6,7},{7,6},{8,9},{9,8},{10,11... | collective-permute-start | bytes 1769480 | tf_op jit(solution)/shard_map/ppermute | solution.py:107
  30.2 1.6 %collective-permute-start.8 = (bf16[32,1536]{1,0:T(8,128)(2,1)S(1)}, bf16[32,1536]{1,0:T(8,128)(2,1)S(1)}, u32[]{:S(2)}, u32[]{:S(2)}) collective-permute-start(bf16[32,1536]{1,0:T(8,128)(2,1)S(1)} %get-tuple-element.51), channel_id=1, source_target_pairs={{0,1},{1,0},{2,3},{3,2},{4,5},{5,4},{6,7},{7,6},{8,10},{9,11},{10,... | collective-permute-start | bytes 294920 | tf_op jit(solution)/shard_map/ppermute | solution.py:107
  31.9 18.8 %collective-permute-start.10 = (bf16[32,1536]{1,0:T(8,128)(2,1)S(1)}, bf16[32,1536]{1,0:T(8,128)(2,1)S(1)}, u32[]{:S(2)}, u32[]{:S(2)}) collective-permute-start(bf16[32,1536]{1,0:T(8,128)(2,1)S(1)} %shard_map.63.refs_0_), channel_id=1, source_target_pairs={{0,1},{1,0},{2,3},{3,2},{4,5},{5,4},{6,7},{7,6},{8,12},{9,13},{10,... | collective-permute-start | bytes 294920 | tf_op jit(solution)/shard_map/ppermute | solution.py:107
  32.2 20.8 %collective-permute-start.13 = (bf16[192,1536]{1,0:T(8,128)(2,1)S(1)}, bf16[192,1536]{1,0:T(8,128)(2,1)S(1)}, u32[]{:S(2)}, u32[]{:S(2)}) collective-permute-start(bf16[192,1536]{1,0:T(8,128)(2,1)S(1)} %bitcast.6), channel_id=1, source_target_pairs={{0,1},{1,0},{2,3},{3,2},{4,5},{5,4},{6,7},{7,6},{8,10},{9,11},{10,... | collective-permute-start | bytes 1769480 | tf_op jit(solution)/shard_map/ppermute | solution.py:107
  51.5 1.3 %collective-permute-start.12 = (bf16[1,32,768]{2,1,0:T(8,128)(2,1)S(1)}, bf16[1,32,768]{2,1,0:T(8,128)(2,1)S(1)}, u32[]{:S(2)}, u32[]{:S(2)}) collective-permute-start(bf16[1,32,768]{2,1,0:T(8,128)(2,1)S(1)} %get-tuple-element.55), channel_id=1, source_target_pairs={{0,1},{1,0},{2,3},{3,2},{4,5},{5,4},{6,7},{7,6},{8,24},{9,25},{10,... | collective-permute-start | bytes 147464 | tf_op jit(solution)/shard_map/ppermute | solution.py:107
  52.8 15.8 %collective-permute-start.20 = (bf16[192,3328]{1,0:T(8,128)(2,1)S(1)}, bf16[192,3328]{1,0:T(8,128)(2,1)S(1)}, u32[]{:S(2)}, u32[]{:S(2)}) collective-permute-start(bf16[192,3328]{1,0:T(8,128)(2,1)S(1)} %collective-permute-done.9.refs_4_), channel_id=1, source_target_pairs={{0,1},{1,0},{2,3},{3,2},{4,5},{5,4},{6,7},{7,6},{8,9},{9,8},{10,11... | collective-permute-start | bytes 3833864 | tf_op jit(solution)/shard_map/ppermute | solution.py:107
  53.0 5.9 %collective-permute-start.16 = (bf16[192,1536]{1,0:T(8,128)(2,1)S(1)}, bf16[192,1536]{1,0:T(8,128)(2,1)S(1)}, u32[]{:S(2)}, u32[]{:S(2)}) collective-permute-start(bf16[192,1536]{1,0:T(8,128)(2,1)S(1)} %collective-permute-done.13.refs_7_), channel_id=1, source_target_pairs={{0,1},{1,0},{2,3},{3,2},{4,5},{5,4},{6,7},{7,6},{8,9},{9,8},{10,11... | collective-permute-start | bytes 1769480 | tf_op jit(solution)/shard_map/ppermute | solution.py:107
  53.9 2.9 %collective-permute-start.14 = (bf16[32,1536]{1,0:T(8,128)(2,1)S(1)}, bf16[32,1536]{1,0:T(8,128)(2,1)S(1)}, u32[]{:S(2)}, u32[]{:S(2)}) collective-permute-start(bf16[32,1536]{1,0:T(8,128)(2,1)S(1)} %shard_map.65.refs_2_), channel_id=1, source_target_pairs={{0,1},{1,0},{2,3},{3,2},{4,5},{5,4},{6,7},{7,6},{8,9},{9,8},{10,11... | collective-permute-start | bytes 294920 | tf_op jit(solution)/shard_map/ppermute | solution.py:107
  57.6 1.3 %collective-permute-start.15 = (bf16[1,32,768]{2,1,0:T(8,128)(2,1)S(1)}, bf16[1,32,768]{2,1,0:T(8,128)(2,1)S(1)}, u32[]{:S(2)}, u32[]{:S(2)}) collective-permute-start(bf16[1,32,768]{2,1,0:T(8,128)(2,1)S(1)} %get-tuple-element.58), channel_id=1, source_target_pairs={{0,1},{1,0},{2,3},{3,2},{4,5},{5,4},{6,7},{7,6},{8,24},{9,25},{10,... | collective-permute-start | bytes 147464 | tf_op jit(solution)/shard_map/ppermute | solution.py:107
  59.5 1.4 %collective-permute-start.17 = (bf16[32,1536]{1,0:T(8,128)(2,1)S(1)}, bf16[32,1536]{1,0:T(8,128)(2,1)S(1)}, u32[]{:S(2)}, u32[]{:S(2)}) collective-permute-start(bf16[32,1536]{1,0:T(8,128)(2,1)S(1)} %shard_map.67.refs_0_), channel_id=1, source_target_pairs={{0,1},{1,0},{2,3},{3,2},{4,5},{5,4},{6,7},{7,6},{8,12},{9,13},{10,... | collective-permute-start | bytes 294920 | tf_op jit(solution)/shard_map/ppermute | solution.py:107
  59.7 11.4 %collective-permute-start.24 = (bf16[64,1536]{1,0:T(8,128)(2,1)S(1)}, bf16[64,1536]{1,0:T(8,128)(2,1)S(1)}, u32[]{:S(2)}, u32[]{:S(2)}) collective-permute-start(bf16[64,1536]{1,0:T(8,128)(2,1)S(1)} %get-tuple-element.74.refs_0_), channel_id=1, source_target_pairs={{0,1},{1,0},{2,3},{3,2},{4,5},{5,4},{6,7},{7,6},{8,9},{9,8},{10,11... | collective-permute-start | bytes 589832 | tf_op jit(solution)/shard_map/ppermute | solution.py:107
  61.8 4.1 %collective-permute-start.19 = (bf16[2,32,768]{2,1,0:T(8,128)(2,1)S(1)}, bf16[2,32,768]{2,1,0:T(8,128)(2,1)S(1)}, u32[]{:S(2)}, u32[]{:S(2)}) collective-permute-start(bf16[2,32,768]{2,1,0:T(8,128)(2,1)S(1)} %get-tuple-element.66), channel_id=1, source_target_pairs={{0,1},{1,0},{2,3},{3,2},{4,5},{5,4},{6,7},{7,6},{8,16},{9,17},{10,... | collective-permute-start | bytes 294920 | tf_op jit(solution)/shard_map/ppermute | solution.py:107
  62.0 6.5 %collective-permute-start.18 = (bf16[2,32,768]{2,1,0:T(8,128)(2,1)S(1)}, bf16[2,32,768]{2,1,0:T(8,128)(2,1)S(1)}, u32[]{:S(2)}, u32[]{:S(2)}) collective-permute-start(bf16[2,32,768]{2,1,0:T(8,128)(2,1)S(1)} %get-tuple-element.66), channel_id=1, source_target_pairs={{0,8},{1,9},{2,10},{3,11},{4,12},{5,13},{6,14},{7,15},{8,0},{9,1},... | collective-permute-start | bytes 294920 | tf_op jit(solution)/shard_map/ppermute | solution.py:107
  69.5 4.7 %collective-permute-start.25 = (bf16[32,1536]{1,0:T(8,128)(2,1)S(1)}, bf16[32,1536]{1,0:T(8,128)(2,1)S(1)}, u32[]{:S(2)}, u32[]{:S(2)}) collective-permute-start(bf16[32,1536]{1,0:T(8,128)(2,1)S(1)} %shard_map.70.refs_1_), channel_id=1, source_target_pairs={{0,4},{1,5},{2,6},{3,7},{4,0},{5,1},{6,2},{7,3},{8,9},{9,8},{10,11... | collective-permute-start | bytes 294920 | tf_op jit(solution)/shard_map/ppermute | solution.py:107
  70.6 1.3 %collective-permute-start.21 = (f32[2,32,192]{2,1,0:T(8,128)S(1)}, f32[2,32,192]{2,1,0:T(8,128)S(1)}, u32[]{:S(2)}, u32[]{:S(2)}) collective-permute-start(f32[2,32,192]{2,1,0:T(8,128)S(1)} %get-tuple-element.69), channel_id=1, source_target_pairs={{0,1},{1,0},{2,3},{3,2},{4,5},{5,4},{6,7},{7,6},{8,9},{9,8},{10,11... | collective-permute-start | bytes 147464 | tf_op jit(solution)/shard_map/ppermute | solution.py:107
  70.6 1.4 %collective-permute-start.22 = (f32[2,32,192]{2,1,0:T(8,128)S(1)}, f32[2,32,192]{2,1,0:T(8,128)S(1)}, u32[]{:S(2)}, u32[]{:S(2)}) collective-permute-start(f32[2,32,192]{2,1,0:T(8,128)S(1)} %get-tuple-element.70), channel_id=1, source_target_pairs={{0,1},{1,0},{2,3},{3,2},{4,5},{5,4},{6,7},{7,6},{8,10},{9,11},{10,... | collective-permute-start | bytes 147464 | tf_op jit(solution)/shard_map/ppermute | solution.py:107
  71.1 1.3 %collective-permute-start.23 = (f32[2,32,192]{2,1,0:T(8,128)S(1)}, f32[2,32,192]{2,1,0:T(8,128)S(1)}, u32[]{:S(2)}, u32[]{:S(2)}) collective-permute-start(f32[2,32,192]{2,1,0:T(8,128)S(1)} %get-tuple-element.71), channel_id=1, source_target_pairs={{0,1},{1,0},{2,3},{3,2},{4,5},{5,4},{6,7},{7,6},{8,11},{9,10},{10,... | collective-permute-start | bytes 147464 | tf_op jit(solution)/shard_map/ppermute | solution.py:107
  74.3 5.1 %collective-permute-start.28 = (bf16[32,1536]{1,0:T(8,128)(2,1)S(1)}, bf16[32,1536]{1,0:T(8,128)(2,1)S(1)}, u32[]{:S(2)}, u32[]{:S(2)}) collective-permute-start(bf16[32,1536]{1,0:T(8,128)(2,1)S(1)} %shard_map.73.refs_0_), channel_id=1, source_target_pairs={{0,3},{1,2},{2,1},{3,0},{4,7},{5,6},{6,5},{7,4},{8,9},{9,8},{10,11... | collective-permute-start | bytes 294920 | tf_op jit(solution)/shard_map/ppermute | solution.py:107
  74.3 7.2 %collective-permute-start.27 = (bf16[32,1536]{1,0:T(8,128)(2,1)S(1)}, bf16[32,1536]{1,0:T(8,128)(2,1)S(1)}, u32[]{:S(2)}, u32[]{:S(2)}) collective-permute-start(bf16[32,1536]{1,0:T(8,128)(2,1)S(1)} %shard_map.73.refs_0_), channel_id=1, source_target_pairs={{0,2},{1,3},{2,0},{3,1},{4,6},{5,7},{6,4},{7,5},{8,9},{9,8},{10,11... | collective-permute-start | bytes 294920 | tf_op jit(solution)/shard_map/ppermute | solution.py:107
  75.9 5.6 %collective-permute-start.26 = (bf16[32,1536]{1,0:T(8,128)(2,1)S(1)}, bf16[32,1536]{1,0:T(8,128)(2,1)S(1)}, u32[]{:S(2)}, u32[]{:S(2)}) collective-permute-start(bf16[32,1536]{1,0:T(8,128)(2,1)S(1)} %shard_map.73.refs_0_), channel_id=1, source_target_pairs={{0,1},{1,0},{2,3},{3,2},{4,5},{5,4},{6,7},{7,6},{8,9},{9,8},{10,11... | collective-permute-start | bytes 294920 | tf_op jit(solution)/shard_map/ppermute | solution.py:107

commit v8 on v7

--- a/solution.py
+++ b/solution.py
@@ -275,15 +275,13 @@
         outs[0][...] = total
 
     leaf_lanes = [across(after(rows_own, leaf_half), 2 * i, leaves) for i in range(1, lanes)]
+    own_term, *others = call(inner_first, [term] * lanes, [*early, rows_own, rows_far])
     first_rows = [rows_own, rows_far]
     for near in rows_lanes:
-        first_rows += [near, across(after(near, *early), 1, inner)]
-    early[0] = after(early[0], *rows_lanes)
-    own_term, *others = call(inner_first, [term] * lanes, [*early, rows_own, rows_far])
+        first_rows += [near, across(after(near, own_term), 1, inner)]
     leaf_rows_of = [rows_own, rows_far]
     own_term = call(by_lane, term, [own_term] + [across(others[i - 1], 2 * i, inner) for i in range(1, lanes)])
     first_terms = over_rows(own_term, inner)
-    first_terms[0] = after(first_terms[0], *leaf_lanes)
     leaf_far = across(after(leaf_half, own_term), 1, leaves)
 
     def spread(matrix, planes, wait, wait_far):
@@ -335,7 +333,7 @@
                 second_rows = spread(inverse_own, nodes_at[1], own_term, arrived[0])
                 for near in leaf_lanes:
                     leaf_rows_of += [near, across(after(near, arrived[0]), 1, leaves)]
-                arrived[0] = after(arrived[0], *second_rows[2::2])
+                arrived[0] = after(arrived[0], *second_rows[2::2], *leaf_lanes)
                 higher = [node for node in inner if 1 < levels_of[node] < levels]
                 higher_rows = spread(rows_own[:, : last * width], higher, sent, sent) if higher else []
 
@@ -461,12 +459,13 @@
 
     terms[0] = after(terms[0], inner_sample, inner_answer, leaf_sample)
     back = call(leaf_back, term, [leaf_half, *terms])
-    backs = [back] + [across(back, b, leaves) for b in range(1, blocks)]
+    near = [back] + [across(back, 2 * i, leaves) for i in range(1, lanes)]
+    near = jnp.concatenate(near, axis=0)
+    far = across(near, 1, leaves)
 
     def leaf_last(ins, outs, whole):
-        leaf_ref, inner_ref, answer_ref, inv_ref = ins[blocks:]
-        for b in range(blocks):
-            whole[groups(b % 2 * lanes + b // 2), :] = ins[b][...]
+        near_ref, far_ref, leaf_ref, inner_ref, answer_ref, inv_ref = ins
+        in_order(near_ref, far_ref, whole)
         is_leaf = height() == 0
         outs[0][...] = jnp.where(is_leaf, leaf_ref[...], inner_ref[...])
         outs[1][...] = jnp.where(is_leaf, mmt(inv_ref[...], whole[...]), answer_ref[...])
@@ -474,7 +473,7 @@
     sample, answer = call(
         leaf_last,
         [shape] * 2,
-        [*backs, leaf_sample, inner_sample, inner_answer, inverse_own],
+        [near, far, leaf_sample, inner_sample, inner_answer, inverse_own],
         whole_half,
     )
     return (sample[None], answer[None])

time: 82.8 us -> 81.1 us (0.979)
  waiting for transfers between devices: 46.8 us -> 44.2 us
  starting transfers between devices: 21.2 us -> 22.1 us
    ppermute x29 -> x28, waiting for transfers between devices: 46.8 us -> 44.2 us  [permute(): return lax.ppermute(x, ('lvl', 'col'), pairs)]
    ppermute x29 -> x28, starting transfers between devices: 21.2 us -> 22.1 us  [permute(): return lax.ppermute(x, ('lvl', 'col'), pairs)]
  transfers between devices with their start and end apart: 29 -> 28, of which waited for: 17 -> 17; matrix products, arithmetic and copies ran while one was open for 1% -> 1% of each run, Pallas kernels for 9% -> 9%
where the time goes in v8:
time: 81.1 us; the launch traced here: 80.8 us
  waiting for transfers between devices  44.2 us (55%)
  starting transfers between devices  22.1 us (27%)
  Pallas kernels  9.76 us (12%)
  local copies, waits for them, and re-layouts  3.93 us (5%)
    ppermute x28, waiting for transfers between devices, permute(): return lax.ppermute(x, ('lvl', 'col'), pairs)  44.2 us
    ppermute x28, starting transfers between devices, permute(): return lax.ppermute(x, ('lvl', 'col'), pairs)  22.1 us
    pallas_call x16, Pallas kernels, call(): pl.pallas_call(kernel, out_shape=[jax.ShapeDtypeStruct(shape, dtype) for...  9.76 us
    unnamed x9, local copies, waits for them, and re-layouts  3.93 us
  transfers between devices with their start and end apart: 28, of which 17 were waited for; matrix products, arithmetic and copies ran while one was open for 1% of the time, Pallas kernels for 9%

profile of v8, /device:TPU:0, one launch (start us, length us, event | category | flops | bytes accessed | tf_op | source)
XLA Modules:
  0.0 80.8 jit_solution(11047272242413236341)
XLA Ops:
  0.6 0.0 copy-start
  0.6 1.1 %copy-done = bf16[1,192,1536]{2,1,0:T(8,128)(2,1)S(1)} copy-done((bf16[1,192,1536]{2,1,0:T(8,128)(2,1)S(1)}, bf16[1,192,1536]{2,1,0:T(8,128)(2,1)}, u32[]{:S(2)}) %copy-start) | copy-done | bytes 589848
  1.7 0.9 %copy-done.3 = f32[1,192,128]{2,1,0:T(8,128)S(1)} copy-done((f32[1,192,128]{2,1,0:T(8,128)S(1)}, f32[1,192,128]{2,1,0:T(8,128)}, u32[]{:S(2)}) %copy-start.3) | copy-done | bytes 98328
  2.6 0.4 shard_map.59
  3.0 0.5 collective-permute-start
  3.5 0.7 copy.6.refs_0_
  4.2 1.3 %copy-done.2 = bf16[1,2,192,1536]{3,2,1,0:T(8,128)(2,1)S(1)} copy-done((bf16[1,2,192,1536]{3,2,1,0:T(8,128)(2,1)S(1)}, bf16[1,2,192,1536]{3,2,1,0:T(8,128)(2,1)}, u32[]{:S(2)}) %copy-start.2) | copy-done | bytes 1179672
  5.5 0.7 shard_map.60
  6.2 0.1 collective-permute-start.4
  6.4 3.0 %collective-permute-start.1 = (bf16[64,1536]{1,0:T(8,128)(2,1)S(1)}, bf16[64,1536]{1,0:T(8,128)(2,1)S(1)}, u32[]{:S(2)}, u32[]{:S(2)}) collective-permute-start(bf16[64,1536]{1,0:T(8,128)(2,1)S(1)} %add_convert_fusion.refs_0_), channel_id=1, source_target_pairs={{0,2},{1,3},{2,0},{3,1},{4,6},{5,7},{6,4},{7,5},{8,9},{9,8},{10,11... | collective-permute-start | bytes 589832 | tf_op jit(solution)/shard_map/ppermute | solution.py:107
  9.4 1.5 %collective-permute-start.2 = (bf16[64,1536]{1,0:T(8,128)(2,1)S(1)}, bf16[64,1536]{1,0:T(8,128)(2,1)S(1)}, u32[]{:S(2)}, u32[]{:S(2)}) collective-permute-start(bf16[64,1536]{1,0:T(8,128)(2,1)S(1)} %add_convert_fusion.refs_0_), channel_id=1, source_target_pairs={{0,4},{1,5},{2,6},{3,7},{4,0},{5,1},{6,2},{7,3},{8,9},{9,8},{10,11... | collective-permute-start | bytes 589832 | tf_op jit(solution)/shard_map/ppermute | solution.py:107
  10.9 0.0 collective-permute-start.3
  10.9 4.2 %collective-permute-done.1.refs_1_ = bf16[64,1536]{1,0:T(8,128)(2,1)S(1)} collective-permute-done((bf16[64,1536]{1,0:T(8,128)(2,1)S(1)}, bf16[64,1536]{1,0:T(8,128)(2,1)S(1)}, u32[]{:S(2)}, u32[]{:S(2)}) %collective-permute-start.1) | collective-permute-done | bytes 196640 | tf_op jit(solution)/shard_map/ppermute | solution.py:107
  15.1 5.1 %collective-permute-done.2.refs_2_ = bf16[64,1536]{1,0:T(8,128)(2,1)S(1)} collective-permute-done((bf16[64,1536]{1,0:T(8,128)(2,1)S(1)}, bf16[64,1536]{1,0:T(8,128)(2,1)S(1)}, u32[]{:S(2)}, u32[]{:S(2)}) %collective-permute-start.2) | collective-permute-done | bytes 196640 | tf_op jit(solution)/shard_map/ppermute | solution.py:107
  20.2 0.9 %shard_map.61 = (bf16[64,1536]{1,0:T(8,128)(2,1)S(1)}, bf16[64,384]{1,0:T(8,128)(2,1)S(1)}, bf16[64,384]{1,0:T(8,128)(2,1)S(1)}) custom-call(bf16[64,1536]{1,0:T(8,128)(2,1)S(1)} %add_convert_fusion.refs_0_, bf16[64,1536]{1,0:T(8,128)(2,1)S(1)} %collective-permute-done.1.refs_1_, bf16[64,1536]{1,0:T(8,128)(2,1)S(1)} %collective-permute-done.2.refs_2_, ...), custom_call_target="tpu_custom_call" | custom-call | flops 268435456 | bytes 3342336 | tf_op jit(solution)/shard_map/pallas_call | solution.py:62
  21.1 1.3 %collective-permute-start.13 = (bf16[192,3328]{1,0:T(8,128)(2,1)S(1)}, bf16[192,3328]{1,0:T(8,128)(2,1)S(1)}, u32[]{:S(2)}, u32[]{:S(2)}) collective-permute-start(bf16[192,3328]{1,0:T(8,128)(2,1)S(1)} %get-tuple-element.52.refs_4_.refs_2_.refs_1_.refs_5_), channel_id=1, source_target_pairs={{0,2},{1,3},{2,0},{3,1},{4,6},{5,7},{6,4},{7,5},{8,9},{9,8},{10,11... | collective-permute-start | bytes 3833864 | tf_op jit(solution)/shard_map/ppermute | solution.py:107
  22.4 0.0 collective-permute-start.9
  22.4 0.0 collective-permute-start.5
  22.4 4.1 %collective-permute-start.6 = (bf16[64,384]{1,0:T(8,128)(2,1)S(1)}, bf16[64,384]{1,0:T(8,128)(2,1)S(1)}, u32[]{:S(2)}, u32[]{:S(2)}) collective-permute-start(bf16[64,384]{1,0:T(8,128)(2,1)S(1)} %get-tuple-element.45), channel_id=1, source_target_pairs={{0,24},{1,25},{2,26},{3,27},{4,28},{5,29},{6,30},{7,31},{8,16},{9,... | collective-permute-start | bytes 147464 | tf_op jit(solution)/shard_map/ppermute | solution.py:107
  26.5 0.1 collective-permute-done.5.refs_0_
  26.6 3.1 %collective-permute-done.6.refs_1_ = bf16[64,384]{1,0:T(8,128)(2,1)S(1)} collective-permute-done((bf16[64,384]{1,0:T(8,128)(2,1)S(1)}, bf16[64,384]{1,0:T(8,128)(2,1)S(1)}, u32[]{:S(2)}, u32[]{:S(2)}) %collective-permute-start.6) | collective-permute-done | bytes 49184 | tf_op jit(solution)/shard_map/ppermute | solution.py:107
  29.6 0.5 shard_map.62
  30.2 0.0 collective-permute-done.9.refs_4_.refs_3_.refs_6_
  30.2 0.1 collective-permute-start.10
  30.3 0.5 collective-permute-start.7
  30.8 1.6 %collective-permute-done.7.refs_1_ = bf16[32,1536]{1,0:T(8,128)(2,1)S(1)} collective-permute-done((bf16[32,1536]{1,0:T(8,128)(2,1)S(1)}, bf16[32,1536]{1,0:T(8,128)(2,1)S(1)}, u32[]{:S(2)}, u32[]{:S(2)}) %collective-permute-start.7) | collective-permute-done | bytes 98336 | tf_op jit(solution)/shard_map/ppermute | solution.py:107
  32.4 0.2 collective-permute-start.8
  32.6 0.4 collective-permute-start.12
  33.0 0.8 collective-permute-done.8.refs_1_
  33.8 0.0 collective-permute-done.10.refs_5_.refs_4_.refs_7_
  33.8 0.9 %shard_map.64 = (f32[32,1536]{1,0:T(8,128)S(1)}, bf16[1,32,768]{2,1,0:T(8,128)(2,1)S(1)}) custom-call(bf16[32,1536]{1,0:T(8,128)(2,1)S(1)} %shard_map.63.refs_0_, bf16[32,1536]{1,0:T(8,128)(2,1)S(1)} %collective-permute-done.8.refs_1_, bf16[192,3328]{1,0:T(8,128)(2,1)S(1)} %get-tuple-element.52.refs_4_.refs_2_.refs_1_.refs_5_, ...), custom_call_target="tpu_custom_call" | custom-call | flops 268435456 | bytes 3932160 | tf_op jit(solution)/shard_map/pallas_call | solution.py:62
  34.7 0.2 collective-permute-start.11
  34.9 1.1 %collective-permute-done.11.refs_0_ = bf16[1,32,768]{2,1,0:T(8,128)(2,1)S(1)} collective-permute-done((bf16[1,32,768]{2,1,0:T(8,128)(2,1)S(1)}, bf16[1,32,768]{2,1,0:T(8,128)(2,1)S(1)}, u32[]{:S(2)}, u32[]{:S(2)}) %collective-permute-start.11) | collective-permute-done | bytes 49184 | tf_op jit(solution)/shard_map/ppermute | solution.py:107
  35.9 14.2 %collective-permute-done.13.refs_4_ = bf16[192,3328]{1,0:T(8,128)(2,1)S(1)} collective-permute-done((bf16[192,3328]{1,0:T(8,128)(2,1)S(1)}, bf16[192,3328]{1,0:T(8,128)(2,1)S(1)}, u32[]{:S(2)}, u32[]{:S(2)}) %collective-permute-start.13) | collective-permute-done | bytes 1277984 | tf_op jit(solution)/shard_map/ppermute | solution.py:107
  50.1 0.0 collective-permute-start.20
  50.1 0.5 collective-permute-start.16
  50.6 0.6 shard_map.65.refs_2_
  51.2 0.1 collective-permute-start.14
  51.3 2.8 %collective-permute-done.14.refs_3_ = bf16[32,1536]{1,0:T(8,128)(2,1)S(1)} collective-permute-done((bf16[32,1536]{1,0:T(8,128)(2,1)S(1)}, bf16[32,1536]{1,0:T(8,128)(2,1)S(1)}, u32[]{:S(2)}, u32[]{:S(2)}) %collective-permute-start.14) | collective-permute-done | bytes 98336 | tf_op jit(solution)/shard_map/ppermute | solution.py:107
  54.1 0.9 %shard_map.66 = (f32[32,1536]{1,0:T(8,128)S(1)}, f32[4,32,192]{2,1,0:T(8,128)S(1)}, bf16[1,32,768]{2,1,0:T(8,128)(2,1)S(1)}) custom-call(bf16[32,1536]{1,0:T(8,128)(2,1)S(1)} %shard_map.63.refs_0_, bf16[32,1536]{1,0:T(8,128)(2,1)S(1)} %collective-permute-done.8.refs_1_, bf16[32,1536]{1,0:T(8,128)(2,1)S(1)} %shard_map.65.refs_2_, ...), custom_call_target="tpu_custom_call" | custom-call | flops 268435456 | bytes 4128768 | tf_op jit(solution)/shard_map/pallas_call | solution.py:62
  54.9 0.2 collective-permute-start.15
  55.1 1.1 %collective-permute-done.15.refs_0_.refs_3_ = bf16[1,32,768]{2,1,0:T(8,128)(2,1)S(1)} collective-permute-done((bf16[1,32,768]{2,1,0:T(8,128)(2,1)S(1)}, bf16[1,32,768]{2,1,0:T(8,128)(2,1)S(1)}, u32[]{:S(2)}, u32[]{:S(2)}) %collective-permute-start.15) | collective-permute-done | bytes 49184 | tf_op jit(solution)/shard_map/ppermute | solution.py:107
  56.2 0.6 shard_map.67.refs_0_
  56.8 0.2 collective-permute-start.17
  57.0 0.3 collective-permute-start.24
  57.4 0.9 %shard_map.68.refs_9_ = f32[4,32,192]{2,1,0:T(8,128)S(1)} custom-call(f32[32,1536]{1,0:T(8,128)S(1)} %get-tuple-element.59.refs_0_.refs_2_, f32[32,1536]{1,0:T(8,128)S(1)} %get-tuple-element.61.refs_1_), custom_call_target="tpu_custom_call" | custom-call | flops 268435456 | bytes 393216 | tf_op jit(solution)/shard_map/pallas_call | solution.py:62
  58.2 0.0 collective-permute-done.17.refs_1_
  58.2 0.9 %shard_map.69 = (bf16[2,32,768]{2,1,0:T(8,128)(2,1)S(1)}, f32[2,32,192]{2,1,0:T(8,128)S(1)}, f32[2,32,192]{2,1,0:T(8,128)S(1)}, f32[2,32,192]{2,1,0:T(8,128)S(1)}, f32[2,32,192]{2,1,0:T(8,128)S(1)}) custom-call(bf16[32,1536]{1,0:T(8,128)(2,1)S(1)} %shard_map.67.refs_0_, bf16[32,1536]{1,0:T(8,128)(2,1)S(1)} %collective-permute-done.17.refs_1_, ...), custom_call_target="tpu_custom_call" | custom-call | flops 268435456 | bytes 4374528 | tf_op jit(solution)/shard_map/pallas_call | solution.py:62
  59.1 6.1 %collective-permute-start.18 = (bf16[2,32,768]{2,1,0:T(8,128)(2,1)S(1)}, bf16[2,32,768]{2,1,0:T(8,128)(2,1)S(1)}, u32[]{:S(2)}, u32[]{:S(2)}) collective-permute-start(bf16[2,32,768]{2,1,0:T(8,128)(2,1)S(1)} %get-tuple-element.62), channel_id=1, source_target_pairs={{0,8},{1,9},{2,10},{3,11},{4,12},{5,13},{6,14},{7,15},{8,0},{9,1},... | collective-permute-start | bytes 294920 | tf_op jit(solution)/shard_map/ppermute | solution.py:107
  65.3 2.6 %collective-permute-done.18.refs_0_ = bf16[2,32,768]{2,1,0:T(8,128)(2,1)S(1)} collective-permute-done((bf16[2,32,768]{2,1,0:T(8,128)(2,1)S(1)}, bf16[2,32,768]{2,1,0:T(8,128)(2,1)S(1)}, u32[]{:S(2)}, u32[]{:S(2)}) %collective-permute-start.18) | collective-permute-done | bytes 98336 | tf_op jit(solution)/shard_map/ppermute | solution.py:107
  67.9 1.0 %shard_map.70.refs_1_ = bf16[32,1536]{1,0:T(8,128)(2,1)S(1)} custom-call(bf16[2,32,768]{2,1,0:T(8,128)(2,1)S(1)} %collective-permute-done.18.refs_0_, bf16[2,32,768]{2,1,0:T(8,128)(2,1)S(1)} %collective-permute-done.19.refs_1_, bf16[192,3328]{1,0:T(8,128)(2,1)S(1)} %get-tuple-element.52.refs_4_.refs_2_.refs_1_.refs_5_, ...), custom_call_target="tpu_custom_call" | custom-call | flops 268435456 | bytes 5308416 | tf_op jit(solution)/shard_map/pallas_call | solution.py:62
  68.8 0.6 collective-permute-start.25
  69.4 0.5 collective-permute-start.22
  69.9 0.4 shard_map.72.refs_2_
  70.3 0.4 collective-permute-done.21.refs_1_
  70.7 0.2 collective-permute-done.22.refs_2_
  70.8 0.4 collective-permute-done.23.refs_3_
  71.2 0.1 shard_map.71
  71.3 2.2 %collective-permute-done.25.refs_2_ = bf16[32,1536]{1,0:T(8,128)(2,1)S(1)} collective-permute-done((bf16[32,1536]{1,0:T(8,128)(2,1)S(1)}, bf16[32,1536]{1,0:T(8,128)(2,1)S(1)}, u32[]{:S(2)}, u32[]{:S(2)}) %collective-permute-start.25) | collective-permute-done | bytes 98336 | tf_op jit(solution)/shard_map/ppermute | solution.py:107
  73.6 1.6 %collective-permute-start.26 = (bf16[32,1536]{1,0:T(8,128)(2,1)S(1)}, bf16[32,1536]{1,0:T(8,128)(2,1)S(1)}, u32[]{:S(2)}, u32[]{:S(2)}) collective-permute-start(bf16[32,1536]{1,0:T(8,128)(2,1)S(1)} %shard_map.73), channel_id=1, source_target_pairs={{0,2},{1,3},{2,0},{3,1},{4,6},{5,7},{6,4},{7,5},{8,9},{9,8},{10,11... | collective-permute-start | bytes 294920 | tf_op jit(solution)/shard_map/ppermute | solution.py:107
  75.1 3.1 %collective-permute-done.26 = bf16[32,1536]{1,0:T(8,128)(2,1)S(1)} collective-permute-done((bf16[32,1536]{1,0:T(8,128)(2,1)S(1)}, bf16[32,1536]{1,0:T(8,128)(2,1)S(1)}, u32[]{:S(2)}, u32[]{:S(2)}) %collective-permute-start.26) | collective-permute-done | bytes 98336 | tf_op jit(solution)/shard_map/ppermute | solution.py:107
  78.3 0.1 collective-permute-start.27
  78.3 1.4 %collective-permute-done.27.refs_1_ = bf16[64,1536]{1,0:T(8,128)(2,1)S(1)} collective-permute-done((bf16[64,1536]{1,0:T(8,128)(2,1)S(1)}, bf16[64,1536]{1,0:T(8,128)(2,1)S(1)}, u32[]{:S(2)}, u32[]{:S(2)}) %collective-permute-start.27) | collective-permute-done | bytes 196640 | tf_op jit(solution)/shard_map/ppermute | solution.py:107
  79.8 1.0 %shard_map.74 = (f32[192,128]{1,0:T(8,128)}, f32[192,128]{1,0:T(8,128)}) custom-call(bf16[64,1536]{1,0:T(8,128)(2,1)S(1)} %pad_maximum_fusion.refs_0_, bf16[64,1536]{1,0:T(8,128)(2,1)S(1)} %collective-permute-done.27.refs_1_, f32[192,128]{1,0:T(8,128)S(1)} %shard_map.72.refs_2_, f32[192,128]{1,0:T(8,128)S(1)} %get-tuple-element.68.refs_3_, ...), custom_call_target="tpu_custom_call" | custom-call | flops 268435456 | bytes 1277952 | tf_op jit(solution)/shard_map/pallas_call | solution.py:62
  (19 shorter events, 0.2 us)
Async XLA Ops:
  0.6 1.1 %copy-start = (bf16[1,192,1536]{2,1,0:T(8,128)(2,1)S(1)}, bf16[1,192,1536]{2,1,0:T(8,128)(2,1)}, u32[]{:S(2)}) copy-start(bf16[1,192,1536]{2,1,0:T(8,128)(2,1)} %param.6) | copy-start | bytes 1769476
  1.7 0.9 %copy-start.3 = (f32[1,192,128]{2,1,0:T(8,128)S(1)}, f32[1,192,128]{2,1,0:T(8,128)}, u32[]{:S(2)}) copy-start(f32[1,192,128]{2,1,0:T(8,128)} %param.4) | copy-start | bytes 294916
  3.0 3.2 %collective-permute-start = (bf16[64,1536]{1,0:T(8,128)(2,1)S(1)}, bf16[64,1536]{1,0:T(8,128)(2,1)S(1)}, u32[]{:S(2)}, u32[]{:S(2)}) collective-permute-start(bf16[64,1536]{1,0:T(8,128)(2,1)S(1)} %get-tuple-element.39.refs_1_), channel_id=1, source_target_pairs={{0,1},{1,0},{2,3},{3,2},{4,5},{5,4},{6,7},{7,6},{8,9},{9,8},{10,11... | collective-permute-start | bytes 589832 | tf_op jit(solution)/shard_map/ppermute | solution.py:107
  4.2 1.3 %copy-start.2 = (bf16[1,2,192,1536]{3,2,1,0:T(8,128)(2,1)S(1)}, bf16[1,2,192,1536]{3,2,1,0:T(8,128)(2,1)}, u32[]{:S(2)}) copy-start(bf16[1,2,192,1536]{3,2,1,0:T(8,128)(2,1)} %refs_4_.1) | copy-start | bytes 3538948
  6.2 13.9 %collective-permute-start.4 = (bf16[192,3328]{1,0:T(8,128)(2,1)S(1)}, bf16[192,3328]{1,0:T(8,128)(2,1)S(1)}, u32[]{:S(2)}, u32[]{:S(2)}) collective-permute-start(bf16[192,3328]{1,0:T(8,128)(2,1)S(1)} %get-tuple-element.52.refs_4_.refs_2_.refs_1_.refs_5_), channel_id=1, source_target_pairs={{0,1},{1,0},{2,3},{3,2},{4,5},{5,4},{6,7},{7,6},{8,9},{9,8},{10,11... | collective-permute-start | bytes 3833864 | tf_op jit(solution)/shard_map/ppermute | solution.py:107
  6.4 8.7 %collective-permute-start.1 = (bf16[64,1536]{1,0:T(8,128)(2,1)S(1)}, bf16[64,1536]{1,0:T(8,128)(2,1)S(1)}, u32[]{:S(2)}, u32[]{:S(2)}) collective-permute-start(bf16[64,1536]{1,0:T(8,128)(2,1)S(1)} %add_convert_fusion.refs_0_), channel_id=1, source_target_pairs={{0,2},{1,3},{2,0},{3,1},{4,6},{5,7},{6,4},{7,5},{8,9},{9,8},{10,11... | collective-permute-start | bytes 589832 | tf_op jit(solution)/shard_map/ppermute | solution.py:107
  9.4 10.8 %collective-permute-start.2 = (bf16[64,1536]{1,0:T(8,128)(2,1)S(1)}, bf16[64,1536]{1,0:T(8,128)(2,1)S(1)}, u32[]{:S(2)}, u32[]{:S(2)}) collective-permute-start(bf16[64,1536]{1,0:T(8,128)(2,1)S(1)} %add_convert_fusion.refs_0_), channel_id=1, source_target_pairs={{0,4},{1,5},{2,6},{3,7},{4,0},{5,1},{6,2},{7,3},{8,9},{9,8},{10,11... | collective-permute-start | bytes 589832 | tf_op jit(solution)/shard_map/ppermute | solution.py:107
  10.9 9.2 %collective-permute-start.3 = (bf16[64,1536]{1,0:T(8,128)(2,1)S(1)}, bf16[64,1536]{1,0:T(8,128)(2,1)S(1)}, u32[]{:S(2)}, u32[]{:S(2)}) collective-permute-start(bf16[64,1536]{1,0:T(8,128)(2,1)S(1)} %add_convert_fusion.refs_0_), channel_id=1, source_target_pairs={{0,6},{1,7},{2,4},{3,5},{4,2},{5,3},{6,0},{7,1},{8,9},{9,8},{10,11... | collective-permute-start | bytes 589832 | tf_op jit(solution)/shard_map/ppermute | solution.py:107
  21.1 29.0 %collective-permute-start.13 = (bf16[192,3328]{1,0:T(8,128)(2,1)S(1)}, bf16[192,3328]{1,0:T(8,128)(2,1)S(1)}, u32[]{:S(2)}, u32[]{:S(2)}) collective-permute-start(bf16[192,3328]{1,0:T(8,128)(2,1)S(1)} %get-tuple-element.52.refs_4_.refs_2_.refs_1_.refs_5_), channel_id=1, source_target_pairs={{0,2},{1,3},{2,0},{3,1},{4,6},{5,7},{6,4},{7,5},{8,9},{9,8},{10,11... | collective-permute-start | bytes 3833864 | tf_op jit(solution)/shard_map/ppermute | solution.py:107
  22.4 7.8 %collective-permute-start.9 = (bf16[192,1536]{1,0:T(8,128)(2,1)S(1)}, bf16[192,1536]{1,0:T(8,128)(2,1)S(1)}, u32[]{:S(2)}, u32[]{:S(2)}) collective-permute-start(bf16[192,1536]{1,0:T(8,128)(2,1)S(1)} %get-tuple-element.48), channel_id=1, source_target_pairs={{0,1},{1,0},{2,3},{3,2},{4,5},{5,4},{6,7},{7,6},{8,10},{9,11},{10,... | collective-permute-start | bytes 1769480 | tf_op jit(solution)/shard_map/ppermute | solution.py:107
  22.4 4.2 %collective-permute-start.5 = (bf16[64,384]{1,0:T(8,128)(2,1)S(1)}, bf16[64,384]{1,0:T(8,128)(2,1)S(1)}, u32[]{:S(2)}, u32[]{:S(2)}) collective-permute-start(bf16[64,384]{1,0:T(8,128)(2,1)S(1)} %get-tuple-element.44), channel_id=1, source_target_pairs={{0,8},{1,9},{2,10},{3,11},{4,12},{5,13},{6,14},{7,15},{8,0},{9,1},... | collective-permute-start | bytes 147464 | tf_op jit(solution)/shard_map/ppermute | solution.py:107
  22.4 10.2 %copy-start.1 = (bf16[1,192,1536]{2,1,0:T(8,128)(2,1)S(1)}, bf16[1,192,1536]{2,1,0:T(8,128)(2,1)}, u32[]{:S(2)}) copy-start(bf16[1,192,1536]{2,1,0:T(8,128)(2,1)} %param.6) | copy-start | bytes 1769476
  22.4 7.2 %collective-permute-start.6 = (bf16[64,384]{1,0:T(8,128)(2,1)S(1)}, bf16[64,384]{1,0:T(8,128)(2,1)S(1)}, u32[]{:S(2)}, u32[]{:S(2)}) collective-permute-start(bf16[64,384]{1,0:T(8,128)(2,1)S(1)} %get-tuple-element.45), channel_id=1, source_target_pairs={{0,24},{1,25},{2,26},{3,27},{4,28},{5,29},{6,30},{7,31},{8,16},{9,... | collective-permute-start | bytes 147464 | tf_op jit(solution)/shard_map/ppermute | solution.py:107
  30.2 3.6 %collective-permute-start.10 = (bf16[192,1536]{1,0:T(8,128)(2,1)S(1)}, bf16[192,1536]{1,0:T(8,128)(2,1)S(1)}, u32[]{:S(2)}, u32[]{:S(2)}) collective-permute-start(bf16[192,1536]{1,0:T(8,128)(2,1)S(1)} %collective-permute-done.9.refs_4_.refs_3_.refs_6_), channel_id=1, source_target_pairs={{0,1},{1,0},{2,3},{3,2},{4,5},{5,4},{6,7},{7,6},{8,9},{9,8},{10,11... | collective-permute-start | bytes 1769480 | tf_op jit(solution)/shard_map/ppermute | solution.py:107
  30.3 2.1 %collective-permute-start.7 = (bf16[32,1536]{1,0:T(8,128)(2,1)S(1)}, bf16[32,1536]{1,0:T(8,128)(2,1)S(1)}, u32[]{:S(2)}, u32[]{:S(2)}) collective-permute-start(bf16[32,1536]{1,0:T(8,128)(2,1)S(1)} %get-tuple-element.47), channel_id=1, source_target_pairs={{0,1},{1,0},{2,3},{3,2},{4,5},{5,4},{6,7},{7,6},{8,10},{9,11},{10,... | collective-permute-start | bytes 294920 | tf_op jit(solution)/shard_map/ppermute | solution.py:107
  32.4 1.4 %collective-permute-start.8 = (bf16[32,1536]{1,0:T(8,128)(2,1)S(1)}, bf16[32,1536]{1,0:T(8,128)(2,1)S(1)}, u32[]{:S(2)}, u32[]{:S(2)}) collective-permute-start(bf16[32,1536]{1,0:T(8,128)(2,1)S(1)} %shard_map.63.refs_0_), channel_id=1, source_target_pairs={{0,1},{1,0},{2,3},{3,2},{4,5},{5,4},{6,7},{7,6},{8,12},{9,13},{10,... | collective-permute-start | bytes 294920 | tf_op jit(solution)/shard_map/ppermute | solution.py:107
  32.6 17.5 %collective-permute-start.12 = (bf16[192,1536]{1,0:T(8,128)(2,1)S(1)}, bf16[192,1536]{1,0:T(8,128)(2,1)S(1)}, u32[]{:S(2)}, u32[]{:S(2)}) collective-permute-start(bf16[192,1536]{1,0:T(8,128)(2,1)S(1)} %bitcast.6), channel_id=1, source_target_pairs={{0,1},{1,0},{2,3},{3,2},{4,5},{5,4},{6,7},{7,6},{8,10},{9,11},{10,... | collective-permute-start | bytes 1769480 | tf_op jit(solution)/shard_map/ppermute | solution.py:107
  34.7 1.3 %collective-permute-start.11 = (bf16[1,32,768]{2,1,0:T(8,128)(2,1)S(1)}, bf16[1,32,768]{2,1,0:T(8,128)(2,1)S(1)}, u32[]{:S(2)}, u32[]{:S(2)}) collective-permute-start(bf16[1,32,768]{2,1,0:T(8,128)(2,1)S(1)} %get-tuple-element.50), channel_id=1, source_target_pairs={{0,1},{1,0},{2,3},{3,2},{4,5},{5,4},{6,7},{7,6},{8,24},{9,25},{10,... | collective-permute-start | bytes 147464 | tf_op jit(solution)/shard_map/ppermute | solution.py:107
  50.1 17.8 %collective-permute-start.20 = (bf16[192,3328]{1,0:T(8,128)(2,1)S(1)}, bf16[192,3328]{1,0:T(8,128)(2,1)S(1)}, u32[]{:S(2)}, u32[]{:S(2)}) collective-permute-start(bf16[192,3328]{1,0:T(8,128)(2,1)S(1)} %collective-permute-done.13.refs_4_), channel_id=1, source_target_pairs={{0,1},{1,0},{2,3},{3,2},{4,5},{5,4},{6,7},{7,6},{8,9},{9,8},{10,11... | collective-permute-start | bytes 3833864 | tf_op jit(solution)/shard_map/ppermute | solution.py:107
  50.1 5.0 %collective-permute-start.16 = (bf16[192,1536]{1,0:T(8,128)(2,1)S(1)}, bf16[192,1536]{1,0:T(8,128)(2,1)S(1)}, u32[]{:S(2)}, u32[]{:S(2)}) collective-permute-start(bf16[192,1536]{1,0:T(8,128)(2,1)S(1)} %collective-permute-done.12.refs_7_), channel_id=1, source_target_pairs={{0,1},{1,0},{2,3},{3,2},{4,5},{5,4},{6,7},{7,6},{8,9},{9,8},{10,11... | collective-permute-start | bytes 1769480 | tf_op jit(solution)/shard_map/ppermute | solution.py:107
  51.2 2.9 %collective-permute-start.14 = (bf16[32,1536]{1,0:T(8,128)(2,1)S(1)}, bf16[32,1536]{1,0:T(8,128)(2,1)S(1)}, u32[]{:S(2)}, u32[]{:S(2)}) collective-permute-start(bf16[32,1536]{1,0:T(8,128)(2,1)S(1)} %shard_map.65.refs_2_), channel_id=1, source_target_pairs={{0,1},{1,0},{2,3},{3,2},{4,5},{5,4},{6,7},{7,6},{8,9},{9,8},{10,11... | collective-permute-start | bytes 294920 | tf_op jit(solution)/shard_map/ppermute | solution.py:107
  54.9 1.3 %collective-permute-start.15 = (bf16[1,32,768]{2,1,0:T(8,128)(2,1)S(1)}, bf16[1,32,768]{2,1,0:T(8,128)(2,1)S(1)}, u32[]{:S(2)}, u32[]{:S(2)}) collective-permute-start(bf16[1,32,768]{2,1,0:T(8,128)(2,1)S(1)} %get-tuple-element.54), channel_id=1, source_target_pairs={{0,1},{1,0},{2,3},{3,2},{4,5},{5,4},{6,7},{7,6},{8,24},{9,25},{10,... | collective-permute-start | bytes 147464 | tf_op jit(solution)/shard_map/ppermute | solution.py:107
  56.8 1.4 %collective-permute-start.17 = (bf16[32,1536]{1,0:T(8,128)(2,1)S(1)}, bf16[32,1536]{1,0:T(8,128)(2,1)S(1)}, u32[]{:S(2)}, u32[]{:S(2)}) collective-permute-start(bf16[32,1536]{1,0:T(8,128)(2,1)S(1)} %shard_map.67.refs_0_), channel_id=1, source_target_pairs={{0,1},{1,0},{2,3},{3,2},{4,5},{5,4},{6,7},{7,6},{8,12},{9,13},{10,... | collective-permute-start | bytes 294920 | tf_op jit(solution)/shard_map/ppermute | solution.py:107
  57.0 12.9 %collective-permute-start.24 = (bf16[64,1536]{1,0:T(8,128)(2,1)S(1)}, bf16[64,1536]{1,0:T(8,128)(2,1)S(1)}, u32[]{:S(2)}, u32[]{:S(2)}) collective-permute-start(bf16[64,1536]{1,0:T(8,128)(2,1)S(1)} %get-tuple-element.70.refs_0_), channel_id=1, source_target_pairs={{0,1},{1,0},{2,3},{3,2},{4,5},{5,4},{6,7},{7,6},{8,9},{9,8},{10,11... | collective-permute-start | bytes 589832 | tf_op jit(solution)/shard_map/ppermute | solution.py:107
  59.1 8.7 %collective-permute-start.18 = (bf16[2,32,768]{2,1,0:T(8,128)(2,1)S(1)}, bf16[2,32,768]{2,1,0:T(8,128)(2,1)S(1)}, u32[]{:S(2)}, u32[]{:S(2)}) collective-permute-start(bf16[2,32,768]{2,1,0:T(8,128)(2,1)S(1)} %get-tuple-element.62), channel_id=1, source_target_pairs={{0,8},{1,9},{2,10},{3,11},{4,12},{5,13},{6,14},{7,15},{8,0},{9,1},... | collective-permute-start | bytes 294920 | tf_op jit(solution)/shard_map/ppermute | solution.py:107
  65.3 2.6 %collective-permute-start.19 = (bf16[2,32,768]{2,1,0:T(8,128)(2,1)S(1)}, bf16[2,32,768]{2,1,0:T(8,128)(2,1)S(1)}, u32[]{:S(2)}, u32[]{:S(2)}) collective-permute-start(bf16[2,32,768]{2,1,0:T(8,128)(2,1)S(1)} %get-tuple-element.62), channel_id=1, source_target_pairs={{0,1},{1,0},{2,3},{3,2},{4,5},{5,4},{6,7},{7,6},{8,16},{9,17},{10,... | collective-permute-start | bytes 294920 | tf_op jit(solution)/shard_map/ppermute | solution.py:107
  68.8 4.7 %collective-permute-start.25 = (bf16[32,1536]{1,0:T(8,128)(2,1)S(1)}, bf16[32,1536]{1,0:T(8,128)(2,1)S(1)}, u32[]{:S(2)}, u32[]{:S(2)}) collective-permute-start(bf16[32,1536]{1,0:T(8,128)(2,1)S(1)} %shard_map.70.refs_1_), channel_id=1, source_target_pairs={{0,4},{1,5},{2,6},{3,7},{4,0},{5,1},{6,2},{7,3},{8,9},{9,8},{10,11... | collective-permute-start | bytes 294920 | tf_op jit(solution)/shard_map/ppermute | solution.py:107
  69.4 1.3 %collective-permute-start.21 = (f32[2,32,192]{2,1,0:T(8,128)S(1)}, f32[2,32,192]{2,1,0:T(8,128)S(1)}, u32[]{:S(2)}, u32[]{:S(2)}) collective-permute-start(f32[2,32,192]{2,1,0:T(8,128)S(1)} %get-tuple-element.65), channel_id=1, source_target_pairs={{0,1},{1,0},{2,3},{3,2},{4,5},{5,4},{6,7},{7,6},{8,9},{9,8},{10,11... | collective-permute-start | bytes 147464 | tf_op jit(solution)/shard_map/ppermute | solution.py:107
  69.4 1.4 %collective-permute-start.22 = (f32[2,32,192]{2,1,0:T(8,128)S(1)}, f32[2,32,192]{2,1,0:T(8,128)S(1)}, u32[]{:S(2)}, u32[]{:S(2)}) collective-permute-start(f32[2,32,192]{2,1,0:T(8,128)S(1)} %get-tuple-element.66), channel_id=1, source_target_pairs={{0,1},{1,0},{2,3},{3,2},{4,5},{5,4},{6,7},{7,6},{8,10},{9,11},{10,... | collective-permute-start | bytes 147464 | tf_op jit(solution)/shard_map/ppermute | solution.py:107
  69.9 1.3 %collective-permute-start.23 = (f32[2,32,192]{2,1,0:T(8,128)S(1)}, f32[2,32,192]{2,1,0:T(8,128)S(1)}, u32[]{:S(2)}, u32[]{:S(2)}) collective-permute-start(f32[2,32,192]{2,1,0:T(8,128)S(1)} %get-tuple-element.67), channel_id=1, source_target_pairs={{0,1},{1,0},{2,3},{3,2},{4,5},{5,4},{6,7},{7,6},{8,11},{9,10},{10,... | collective-permute-start | bytes 147464 | tf_op jit(solution)/shard_map/ppermute | solution.py:107
  73.6 4.7 %collective-permute-start.26 = (bf16[32,1536]{1,0:T(8,128)(2,1)S(1)}, bf16[32,1536]{1,0:T(8,128)(2,1)S(1)}, u32[]{:S(2)}, u32[]{:S(2)}) collective-permute-start(bf16[32,1536]{1,0:T(8,128)(2,1)S(1)} %shard_map.73), channel_id=1, source_target_pairs={{0,2},{1,3},{2,0},{3,1},{4,6},{5,7},{6,4},{7,5},{8,9},{9,8},{10,11... | collective-permute-start | bytes 294920 | tf_op jit(solution)/shard_map/ppermute | solution.py:107
  78.3 1.5 %collective-permute-start.27 = (bf16[64,1536]{1,0:T(8,128)(2,1)S(1)}, bf16[64,1536]{1,0:T(8,128)(2,1)S(1)}, u32[]{:S(2)}, u32[]{:S(2)}) collective-permute-start(bf16[64,1536]{1,0:T(8,128)(2,1)S(1)} %pad_maximum_fusion.refs_0_), channel_id=1, source_target_pairs={{0,1},{1,0},{2,3},{3,2},{4,5},{5,4},{6,7},{7,6},{8,9},{9,8},{10,11... | collective-permute-start | bytes 589832 | tf_op jit(solution)/shard_map/ppermute | solution.py:107

commit v9 on v8

--- a/solution.py
+++ b/solution.py
@@ -270,18 +270,14 @@
         for i in range(lanes):
             outs[i][...] = product[i * group : (i + 1) * group]
 
-    def by_lane(ins, outs):
-        total = row_total(ins).astype(BF16)
-        outs[0][...] = total
-
     leaf_lanes = [across(after(rows_own, leaf_half), 2 * i, leaves) for i in range(1, lanes)]
     own_term, *others = call(inner_first, [term] * lanes, [*early, rows_own, rows_far])
     first_rows = [rows_own, rows_far]
     for near in rows_lanes:
         first_rows += [near, across(after(near, own_term), 1, inner)]
     leaf_rows_of = [rows_own, rows_far]
-    own_term = call(by_lane, term, [own_term] + [across(others[i - 1], 2 * i, inner) for i in range(1, lanes)])
-    first_terms = over_rows(own_term, inner)
+    by_lane = [own_term, *others]
+    first_terms = [own_term] + [across(by_lane[chip % lanes], 2 * chip, inner) for chip in range(1, chips)]
     leaf_far = across(after(leaf_half, own_term), 1, leaves)
 
     def spread(matrix, planes, wait, wait_far):
@@ -330,10 +326,12 @@
             )
             arrived = [along(sent, links) for links in child_links(section + 1, members)]
             if section == 1:
-                second_rows = spread(inverse_own, nodes_at[1], own_term, arrived[0])
+                second_lanes = [
+                    across(after(inverse_own, first_terms[-1]), 2 * i, nodes_at[1]) for i in range(1, lanes)
+                ]
                 for near in leaf_lanes:
                     leaf_rows_of += [near, across(after(near, arrived[0]), 1, leaves)]
-                arrived[0] = after(arrived[0], *second_rows[2::2], *leaf_lanes)
+                arrived[0] = after(arrived[0], *leaf_lanes)
                 higher = [node for node in inner if 1 < levels_of[node] < levels]
                 higher_rows = spread(rows_own[:, : last * width], higher, sent, sent) if higher else []
 
@@ -346,12 +344,17 @@
             outs[1][b] = answer
             outs[2][0, :, span(b)] = answer.astype(BF16)
 
+    terms[0] = after(terms[0], *second_lanes)
     samples[levels], answer, sent = call(
         root_back,
         [((group, width), F32), vector, ((1, group, blocks * row_count), BF16)],
         [*terms, *first_rows],
     )
 
+
+    second_rows = [rows_own, rows_far]
+    for near in second_lanes:
+        second_rows += [near, across(after(near, sent), 1, nodes_at[1])]
 
     def split_rows(ins, outs):
         rank = height()
@@ -372,8 +375,6 @@
         remain = levels - section
         ancestry = [along(sent, down(links)) for links in child_links(section + 1, members)]
         ancestry = ancestry[0] if len(ancestry) == 1 else from_parent(*ancestry, section + 1)
-        if section == 1:
-            ancestry = after(ancestry, *second_rows)
 
         def adjoint_first(ins, outs):
             parts = []

time: 81.1 us -> 78.8 us (0.972)
  starting transfers between devices: 22.1 us -> 20.9 us
  waiting for transfers between devices: 44.2 us -> 43.1 us
    ppermute x28 -> x29, starting transfers between devices: 22.1 us -> 20.9 us  [permute(): return lax.ppermute(x, ('lvl', 'col'), pairs)]
    ppermute x28 -> x29, waiting for transfers between devices: 44.2 us -> 43.1 us  [permute(): return lax.ppermute(x, ('lvl', 'col'), pairs)]
    pallas_call x16 -> x15, Pallas kernels: 9.76 us -> 9.72 us  [call(): pl.pallas_call(kernel, out_shape=[jax.ShapeDtypeStruct(shape, dtype) for...]
  transfers between devices with their start and end apart: 28 -> 29, of which waited for: 17 -> 17; matrix products, arithmetic and copies ran while one was open for 1% -> 1% of each run, Pallas kernels for 9% -> 9%
where the time goes in v9:
time: 78.8 us; the launch traced here: 78.5 us
  waiting for transfers between devices  43.1 us (55%)
  starting transfers between devices  20.9 us (27%)
  Pallas kernels  9.72 us (12%)
  local copies, waits for them, and re-layouts  3.93 us (5%)
    ppermute x29, waiting for transfers between devices, permute(): return lax.ppermute(x, ('lvl', 'col'), pairs)  43.1 us
    ppermute x29, starting transfers between devices, permute(): return lax.ppermute(x, ('lvl', 'col'), pairs)  20.9 us
    pallas_call x15, Pallas kernels, call(): pl.pallas_call(kernel, out_shape=[jax.ShapeDtypeStruct(shape, dtype) for...  9.72 us
    unnamed x9, local copies, waits for them, and re-layouts  3.93 us
  transfers between devices with their start and end apart: 29, of which 17 were waited for; matrix products, arithmetic and copies ran while one was open for 1% of the time, Pallas kernels for 9%

profile of v9, /device:TPU:0, one launch (start us, length us, event | category | flops | bytes accessed | tf_op | source)
XLA Modules:
  0.0 78.5 jit_solution(15301389981984691810)
XLA Ops:
  0.6 0.0 copy-start
  0.6 1.1 %copy-done = bf16[1,192,1536]{2,1,0:T(8,128)(2,1)S(1)} copy-done((bf16[1,192,1536]{2,1,0:T(8,128)(2,1)S(1)}, bf16[1,192,1536]{2,1,0:T(8,128)(2,1)}, u32[]{:S(2)}) %copy-start) | copy-done | bytes 589848
  1.7 0.9 %copy-done.3 = f32[1,192,128]{2,1,0:T(8,128)S(1)} copy-done((f32[1,192,128]{2,1,0:T(8,128)S(1)}, f32[1,192,128]{2,1,0:T(8,128)}, u32[]{:S(2)}) %copy-start.3) | copy-done | bytes 98328
  2.6 0.4 shard_map.59
  3.0 0.5 collective-permute-start
  3.5 0.7 copy.6.refs_0_
  4.2 1.3 %copy-done.2 = bf16[1,2,192,1536]{3,2,1,0:T(8,128)(2,1)S(1)} copy-done((bf16[1,2,192,1536]{3,2,1,0:T(8,128)(2,1)S(1)}, bf16[1,2,192,1536]{3,2,1,0:T(8,128)(2,1)}, u32[]{:S(2)}) %copy-start.2) | copy-done | bytes 1179672
  5.5 0.7 shard_map.60
  6.2 0.0 collective-permute-done
  6.2 0.1 collective-permute-start.4
  6.4 3.0 %collective-permute-start.1 = (bf16[64,1536]{1,0:T(8,128)(2,1)S(1)}, bf16[64,1536]{1,0:T(8,128)(2,1)S(1)}, u32[]{:S(2)}, u32[]{:S(2)}) collective-permute-start(bf16[64,1536]{1,0:T(8,128)(2,1)S(1)} %add_convert_fusion.refs_0_), channel_id=1, source_target_pairs={{0,2},{1,3},{2,0},{3,1},{4,6},{5,7},{6,4},{7,5},{8,9},{9,8},{10,11... | collective-permute-start | bytes 589832 | tf_op jit(solution)/shard_map/ppermute | solution.py:107
  9.4 1.5 %collective-permute-start.2 = (bf16[64,1536]{1,0:T(8,128)(2,1)S(1)}, bf16[64,1536]{1,0:T(8,128)(2,1)S(1)}, u32[]{:S(2)}, u32[]{:S(2)}) collective-permute-start(bf16[64,1536]{1,0:T(8,128)(2,1)S(1)} %add_convert_fusion.refs_0_), channel_id=1, source_target_pairs={{0,4},{1,5},{2,6},{3,7},{4,0},{5,1},{6,2},{7,3},{8,9},{9,8},{10,11... | collective-permute-start | bytes 589832 | tf_op jit(solution)/shard_map/ppermute | solution.py:107
  10.9 0.0 collective-permute-start.3
  10.9 4.2 %collective-permute-done.1.refs_1_ = bf16[64,1536]{1,0:T(8,128)(2,1)S(1)} collective-permute-done((bf16[64,1536]{1,0:T(8,128)(2,1)S(1)}, bf16[64,1536]{1,0:T(8,128)(2,1)S(1)}, u32[]{:S(2)}, u32[]{:S(2)}) %collective-permute-start.1) | collective-permute-done | bytes 196640 | tf_op jit(solution)/shard_map/ppermute | solution.py:107
  15.1 5.1 %collective-permute-done.2.refs_2_ = bf16[64,1536]{1,0:T(8,128)(2,1)S(1)} collective-permute-done((bf16[64,1536]{1,0:T(8,128)(2,1)S(1)}, bf16[64,1536]{1,0:T(8,128)(2,1)S(1)}, u32[]{:S(2)}, u32[]{:S(2)}) %collective-permute-start.2) | collective-permute-done | bytes 196640 | tf_op jit(solution)/shard_map/ppermute | solution.py:107
  20.1 0.0 collective-permute-done.4.refs_5_.refs_3_.refs_2_.refs_7_.refs_6_
  20.2 0.9 %shard_map.61 = (bf16[64,1536]{1,0:T(8,128)(2,1)S(1)}, bf16[64,384]{1,0:T(8,128)(2,1)S(1)}, bf16[64,384]{1,0:T(8,128)(2,1)S(1)}) custom-call(bf16[64,1536]{1,0:T(8,128)(2,1)S(1)} %add_convert_fusion.refs_0_, bf16[64,1536]{1,0:T(8,128)(2,1)S(1)} %collective-permute-done.1.refs_1_, bf16[64,1536]{1,0:T(8,128)(2,1)S(1)} %collective-permute-done.2.refs_2_, ...), custom_call_target="tpu_custom_call" | custom-call | flops 268435456 | bytes 3342336 | tf_op jit(solution)/shard_map/pallas_call | solution.py:62
  21.1 1.3 %collective-permute-start.14 = (bf16[192,3328]{1,0:T(8,128)(2,1)S(1)}, bf16[192,3328]{1,0:T(8,128)(2,1)S(1)}, u32[]{:S(2)}, u32[]{:S(2)}) collective-permute-start(bf16[192,3328]{1,0:T(8,128)(2,1)S(1)} %get-tuple-element.53.refs_4_.refs_2_.refs_1_.refs_6_.refs_5_), channel_id=1, source_target_pairs={{0,2},{1,3},{2,0},{3,1},{4,6},{5,7},{6,4},{7,5},{8,9},{9,8},{10,11... | collective-permute-start | bytes 3833864 | tf_op jit(solution)/shard_map/ppermute | solution.py:107
  22.4 0.0 collective-permute-start.11
  22.4 4.1 %collective-permute-start.6 = (bf16[64,384]{1,0:T(8,128)(2,1)S(1)}, bf16[64,384]{1,0:T(8,128)(2,1)S(1)}, u32[]{:S(2)}, u32[]{:S(2)}) collective-permute-start(bf16[64,384]{1,0:T(8,128)(2,1)S(1)} %get-tuple-element.45), channel_id=1, source_target_pairs={{0,24},{1,25},{2,26},{3,27},{4,28},{5,29},{6,30},{7,31},{8,16},{9,... | collective-permute-start | bytes 147464 | tf_op jit(solution)/shard_map/ppermute | solution.py:107
  26.5 0.1 collective-permute-done.5.refs_0_
  26.6 3.1 %collective-permute-done.6.refs_1_ = bf16[64,384]{1,0:T(8,128)(2,1)S(1)} collective-permute-done((bf16[64,384]{1,0:T(8,128)(2,1)S(1)}, bf16[64,384]{1,0:T(8,128)(2,1)S(1)}, u32[]{:S(2)}, u32[]{:S(2)}) %collective-permute-start.6) | collective-permute-done | bytes 49184 | tf_op jit(solution)/shard_map/ppermute | solution.py:107
  29.6 0.5 shard_map.62
  30.2 0.0 collective-permute-done.11.refs_6_.refs_3_.refs_8_
  30.2 0.1 collective-permute-start.12
  30.3 0.5 collective-permute-start.7
  30.8 0.1 collective-permute-start.9
  30.8 0.4 collective-permute-start.10
  31.3 1.1 %collective-permute-done.7.refs_3_ = bf16[32,1536]{1,0:T(8,128)(2,1)S(1)} collective-permute-done((bf16[32,1536]{1,0:T(8,128)(2,1)S(1)}, bf16[32,1536]{1,0:T(8,128)(2,1)S(1)}, u32[]{:S(2)}, u32[]{:S(2)}) %collective-permute-start.7) | collective-permute-done | bytes 98336 | tf_op jit(solution)/shard_map/ppermute | solution.py:107
  32.4 0.1 collective-permute-start.8
  32.5 0.1 collective-permute-done.10.refs_2_
  32.7 0.9 %shard_map.63 = (f32[32,1536]{1,0:T(8,128)S(1)}, bf16[1,32,768]{2,1,0:T(8,128)(2,1)S(1)}) custom-call(bf16[32,1536]{1,0:T(8,128)(2,1)S(1)} %get-tuple-element.49.refs_0_, bf16[32,1536]{1,0:T(8,128)(2,1)S(1)} %collective-permute-done.9.refs_1_, bf16[32,1536]{1,0:T(8,128)(2,1)S(1)} %collective-permute-done.10.refs_2_, ...), custom_call_target="tpu_custom_call" | custom-call | flops 268435456 | bytes 4128768 | tf_op jit(solution)/shard_map/pallas_call | solution.py:62
  33.6 0.3 collective-permute-start.13
  33.8 1.0 %collective-permute-done.13.refs_0_ = bf16[1,32,768]{2,1,0:T(8,128)(2,1)S(1)} collective-permute-done((bf16[1,32,768]{2,1,0:T(8,128)(2,1)S(1)}, bf16[1,32,768]{2,1,0:T(8,128)(2,1)S(1)}, u32[]{:S(2)}, u32[]{:S(2)}) %collective-permute-start.13) | collective-permute-done | bytes 49184 | tf_op jit(solution)/shard_map/ppermute | solution.py:107
  34.8 15.3 %collective-permute-done.14.refs_4_ = bf16[192,3328]{1,0:T(8,128)(2,1)S(1)} collective-permute-done((bf16[192,3328]{1,0:T(8,128)(2,1)S(1)}, bf16[192,3328]{1,0:T(8,128)(2,1)S(1)}, u32[]{:S(2)}, u32[]{:S(2)}) %collective-permute-start.14) | collective-permute-done | bytes 1277984 | tf_op jit(solution)/shard_map/ppermute | solution.py:107
  50.1 0.6 shard_map.64.refs_4_
  50.7 0.6 collective-permute-start.15
  51.3 2.0 %collective-permute-done.15.refs_5_ = bf16[32,1536]{1,0:T(8,128)(2,1)S(1)} collective-permute-done((bf16[32,1536]{1,0:T(8,128)(2,1)S(1)}, bf16[32,1536]{1,0:T(8,128)(2,1)S(1)}, u32[]{:S(2)}, u32[]{:S(2)}) %collective-permute-start.15) | collective-permute-done | bytes 98336 | tf_op jit(solution)/shard_map/ppermute | solution.py:107
  53.2 0.9 %shard_map.65 = (f32[32,1536]{1,0:T(8,128)S(1)}, f32[4,32,192]{2,1,0:T(8,128)S(1)}, bf16[1,32,768]{2,1,0:T(8,128)(2,1)S(1)}) custom-call(bf16[32,1536]{1,0:T(8,128)(2,1)S(1)} %get-tuple-element.49.refs_0_, bf16[32,1536]{1,0:T(8,128)(2,1)S(1)} %collective-permute-done.9.refs_1_, bf16[32,1536]{1,0:T(8,128)(2,1)S(1)} %collective-permute-done.10.refs_2_, ...), custom_call_target="tpu_custom_call" | custom-call | flops 268435456 | bytes 4325376 | tf_op jit(solution)/shard_map/pallas_call | solution.py:62
  54.1 0.2 collective-permute-start.18
  54.3 0.4 collective-permute-start.16
  54.6 1.6 %collective-permute-done.16.refs_0_.refs_3_ = bf16[1,32,768]{2,1,0:T(8,128)(2,1)S(1)} collective-permute-done((bf16[1,32,768]{2,1,0:T(8,128)(2,1)S(1)}, bf16[1,32,768]{2,1,0:T(8,128)(2,1)S(1)}, u32[]{:S(2)}, u32[]{:S(2)}) %collective-permute-start.16) | collective-permute-done | bytes 49184 | tf_op jit(solution)/shard_map/ppermute | solution.py:107
  56.2 0.6 shard_map.66.refs_0_
  56.8 0.2 collective-permute-start.17
  57.0 0.4 collective-permute-start.25
  57.4 0.9 %shard_map.67.refs_9_ = f32[4,32,192]{2,1,0:T(8,128)S(1)} custom-call(f32[32,1536]{1,0:T(8,128)S(1)} %get-tuple-element.59.refs_0_.refs_2_, f32[32,1536]{1,0:T(8,128)S(1)} %get-tuple-element.61.refs_1_), custom_call_target="tpu_custom_call" | custom-call | flops 268435456 | bytes 393216 | tf_op jit(solution)/shard_map/pallas_call | solution.py:62
  58.2 0.0 collective-permute-done.17.refs_1_
  58.2 0.9 %shard_map.68 = (bf16[2,32,768]{2,1,0:T(8,128)(2,1)S(1)}, f32[2,32,192]{2,1,0:T(8,128)S(1)}, f32[2,32,192]{2,1,0:T(8,128)S(1)}, f32[2,32,192]{2,1,0:T(8,128)S(1)}, f32[2,32,192]{2,1,0:T(8,128)S(1)}) custom-call(bf16[32,1536]{1,0:T(8,128)(2,1)S(1)} %shard_map.66.refs_0_, bf16[32,1536]{1,0:T(8,128)(2,1)S(1)} %collective-permute-done.17.refs_1_, ...), custom_call_target="tpu_custom_call" | custom-call | flops 268435456 | bytes 4374528 | tf_op jit(solution)/shard_map/pallas_call | solution.py:62
  59.1 3.9 %collective-permute-start.19 = (bf16[2,32,768]{2,1,0:T(8,128)(2,1)S(1)}, bf16[2,32,768]{2,1,0:T(8,128)(2,1)S(1)}, u32[]{:S(2)}, u32[]{:S(2)}) collective-permute-start(bf16[2,32,768]{2,1,0:T(8,128)(2,1)S(1)} %get-tuple-element.62), channel_id=1, source_target_pairs={{0,8},{1,9},{2,10},{3,11},{4,12},{5,13},{6,14},{7,15},{8,0},{9,1},... | collective-permute-start | bytes 294920 | tf_op jit(solution)/shard_map/ppermute | solution.py:107
  63.0 2.6 %collective-permute-done.19.refs_0_ = bf16[2,32,768]{2,1,0:T(8,128)(2,1)S(1)} collective-permute-done((bf16[2,32,768]{2,1,0:T(8,128)(2,1)S(1)}, bf16[2,32,768]{2,1,0:T(8,128)(2,1)S(1)}, u32[]{:S(2)}, u32[]{:S(2)}) %collective-permute-start.19) | collective-permute-done | bytes 98336 | tf_op jit(solution)/shard_map/ppermute | solution.py:107
  65.6 1.0 %shard_map.69.refs_1_ = bf16[32,1536]{1,0:T(8,128)(2,1)S(1)} custom-call(bf16[2,32,768]{2,1,0:T(8,128)(2,1)S(1)} %collective-permute-done.19.refs_0_, bf16[2,32,768]{2,1,0:T(8,128)(2,1)S(1)} %collective-permute-done.20.refs_1_, bf16[192,3328]{1,0:T(8,128)(2,1)S(1)} %get-tuple-element.53.refs_4_.refs_2_.refs_1_.refs_6_.refs_5_, ...), custom_call_target="tpu_custom_call" | custom-call | flops 268435456 | bytes 5308416 | tf_op jit(solution)/shard_map/pallas_call | solution.py:62
  66.6 1.4 %collective-permute-start.26 = (bf16[32,1536]{1,0:T(8,128)(2,1)S(1)}, bf16[32,1536]{1,0:T(8,128)(2,1)S(1)}, u32[]{:S(2)}, u32[]{:S(2)}) collective-permute-start(bf16[32,1536]{1,0:T(8,128)(2,1)S(1)} %shard_map.69.refs_1_), channel_id=1, source_target_pairs={{0,4},{1,5},{2,6},{3,7},{4,0},{5,1},{6,2},{7,3},{8,9},{9,8},{10,11... | collective-permute-start | bytes 294920 | tf_op jit(solution)/shard_map/ppermute | solution.py:107
  67.9 0.5 collective-permute-start.23
  68.5 0.4 shard_map.71.refs_2_
  68.8 0.4 collective-permute-done.22.refs_1_
  69.2 0.2 collective-permute-done.23.refs_2_
  69.4 0.4 collective-permute-done.24.refs_3_
  69.7 0.1 shard_map.70
  69.9 1.4 %collective-permute-done.26.refs_2_ = bf16[32,1536]{1,0:T(8,128)(2,1)S(1)} collective-permute-done((bf16[32,1536]{1,0:T(8,128)(2,1)S(1)}, bf16[32,1536]{1,0:T(8,128)(2,1)S(1)}, u32[]{:S(2)}, u32[]{:S(2)}) %collective-permute-start.26) | collective-permute-done | bytes 98336 | tf_op jit(solution)/shard_map/ppermute | solution.py:107
  71.3 1.3 %collective-permute-start.27 = (bf16[32,1536]{1,0:T(8,128)(2,1)S(1)}, bf16[32,1536]{1,0:T(8,128)(2,1)S(1)}, u32[]{:S(2)}, u32[]{:S(2)}) collective-permute-start(bf16[32,1536]{1,0:T(8,128)(2,1)S(1)} %shard_map.72), channel_id=1, source_target_pairs={{0,2},{1,3},{2,0},{3,1},{4,6},{5,7},{6,4},{7,5},{8,9},{9,8},{10,11... | collective-permute-start | bytes 294920 | tf_op jit(solution)/shard_map/ppermute | solution.py:107
  72.6 3.3 %collective-permute-done.27 = bf16[32,1536]{1,0:T(8,128)(2,1)S(1)} collective-permute-done((bf16[32,1536]{1,0:T(8,128)(2,1)S(1)}, bf16[32,1536]{1,0:T(8,128)(2,1)S(1)}, u32[]{:S(2)}, u32[]{:S(2)}) %collective-permute-start.27) | collective-permute-done | bytes 98336 | tf_op jit(solution)/shard_map/ppermute | solution.py:107
  76.0 0.1 collective-permute-start.28
  76.1 1.4 %collective-permute-done.28.refs_1_ = bf16[64,1536]{1,0:T(8,128)(2,1)S(1)} collective-permute-done((bf16[64,1536]{1,0:T(8,128)(2,1)S(1)}, bf16[64,1536]{1,0:T(8,128)(2,1)S(1)}, u32[]{:S(2)}, u32[]{:S(2)}) %collective-permute-start.28) | collective-permute-done | bytes 196640 | tf_op jit(solution)/shard_map/ppermute | solution.py:107
  77.5 1.0 %shard_map.73 = (f32[192,128]{1,0:T(8,128)}, f32[192,128]{1,0:T(8,128)}) custom-call(bf16[64,1536]{1,0:T(8,128)(2,1)S(1)} %pad_maximum_fusion.refs_0_, bf16[64,1536]{1,0:T(8,128)(2,1)S(1)} %collective-permute-done.28.refs_1_, f32[192,128]{1,0:T(8,128)S(1)} %shard_map.71.refs_2_, f32[192,128]{1,0:T(8,128)S(1)} %get-tuple-element.68.refs_3_, ...), custom_call_target="tpu_custom_call" | custom-call | flops 268435456 | bytes 1277952 | tf_op jit(solution)/shard_map/pallas_call | solution.py:62
  (20 shorter events, 0.1 us)
Async XLA Ops:
  0.6 1.1 %copy-start = (bf16[1,192,1536]{2,1,0:T(8,128)(2,1)S(1)}, bf16[1,192,1536]{2,1,0:T(8,128)(2,1)}, u32[]{:S(2)}) copy-start(bf16[1,192,1536]{2,1,0:T(8,128)(2,1)} %param.6) | copy-start | bytes 1769476
  1.7 0.9 %copy-start.3 = (f32[1,192,128]{2,1,0:T(8,128)S(1)}, f32[1,192,128]{2,1,0:T(8,128)}, u32[]{:S(2)}) copy-start(f32[1,192,128]{2,1,0:T(8,128)} %param.4) | copy-start | bytes 294916
  3.0 3.2 %collective-permute-start = (bf16[64,1536]{1,0:T(8,128)(2,1)S(1)}, bf16[64,1536]{1,0:T(8,128)(2,1)S(1)}, u32[]{:S(2)}, u32[]{:S(2)}) collective-permute-start(bf16[64,1536]{1,0:T(8,128)(2,1)S(1)} %get-tuple-element.39.refs_1_), channel_id=1, source_target_pairs={{0,1},{1,0},{2,3},{3,2},{4,5},{5,4},{6,7},{7,6},{8,9},{9,8},{10,11... | collective-permute-start | bytes 589832 | tf_op jit(solution)/shard_map/ppermute | solution.py:107
  4.2 1.3 %copy-start.2 = (bf16[1,2,192,1536]{3,2,1,0:T(8,128)(2,1)S(1)}, bf16[1,2,192,1536]{3,2,1,0:T(8,128)(2,1)}, u32[]{:S(2)}) copy-start(bf16[1,2,192,1536]{3,2,1,0:T(8,128)(2,1)} %refs_4_.1) | copy-start | bytes 3538948
  6.2 13.9 %collective-permute-start.4 = (bf16[192,3328]{1,0:T(8,128)(2,1)S(1)}, bf16[192,3328]{1,0:T(8,128)(2,1)S(1)}, u32[]{:S(2)}, u32[]{:S(2)}) collective-permute-start(bf16[192,3328]{1,0:T(8,128)(2,1)S(1)} %get-tuple-element.53.refs_4_.refs_2_.refs_1_.refs_6_.refs_5_), channel_id=1, source_target_pairs={{0,1},{1,0},{2,3},{3,2},{4,5},{5,4},{6,7},{7,6},{8,9},{9,8},{10,11... | collective-permute-start | bytes 3833864 | tf_op jit(solution)/shard_map/ppermute | solution.py:107
  6.4 8.7 %collective-permute-start.1 = (bf16[64,1536]{1,0:T(8,128)(2,1)S(1)}, bf16[64,1536]{1,0:T(8,128)(2,1)S(1)}, u32[]{:S(2)}, u32[]{:S(2)}) collective-permute-start(bf16[64,1536]{1,0:T(8,128)(2,1)S(1)} %add_convert_fusion.refs_0_), channel_id=1, source_target_pairs={{0,2},{1,3},{2,0},{3,1},{4,6},{5,7},{6,4},{7,5},{8,9},{9,8},{10,11... | collective-permute-start | bytes 589832 | tf_op jit(solution)/shard_map/ppermute | solution.py:107
  9.4 10.8 %collective-permute-start.2 = (bf16[64,1536]{1,0:T(8,128)(2,1)S(1)}, bf16[64,1536]{1,0:T(8,128)(2,1)S(1)}, u32[]{:S(2)}, u32[]{:S(2)}) collective-permute-start(bf16[64,1536]{1,0:T(8,128)(2,1)S(1)} %add_convert_fusion.refs_0_), channel_id=1, source_target_pairs={{0,4},{1,5},{2,6},{3,7},{4,0},{5,1},{6,2},{7,3},{8,9},{9,8},{10,11... | collective-permute-start | bytes 589832 | tf_op jit(solution)/shard_map/ppermute | solution.py:107
  10.9 9.2 %collective-permute-start.3 = (bf16[64,1536]{1,0:T(8,128)(2,1)S(1)}, bf16[64,1536]{1,0:T(8,128)(2,1)S(1)}, u32[]{:S(2)}, u32[]{:S(2)}) collective-permute-start(bf16[64,1536]{1,0:T(8,128)(2,1)S(1)} %add_convert_fusion.refs_0_), channel_id=1, source_target_pairs={{0,6},{1,7},{2,4},{3,5},{4,2},{5,3},{6,0},{7,1},{8,9},{9,8},{10,11... | collective-permute-start | bytes 589832 | tf_op jit(solution)/shard_map/ppermute | solution.py:107
  21.1 29.0 %collective-permute-start.14 = (bf16[192,3328]{1,0:T(8,128)(2,1)S(1)}, bf16[192,3328]{1,0:T(8,128)(2,1)S(1)}, u32[]{:S(2)}, u32[]{:S(2)}) collective-permute-start(bf16[192,3328]{1,0:T(8,128)(2,1)S(1)} %get-tuple-element.53.refs_4_.refs_2_.refs_1_.refs_6_.refs_5_), channel_id=1, source_target_pairs={{0,2},{1,3},{2,0},{3,1},{4,6},{5,7},{6,4},{7,5},{8,9},{9,8},{10,11... | collective-permute-start | bytes 3833864 | tf_op jit(solution)/shard_map/ppermute | solution.py:107
  22.4 7.8 %collective-permute-start.11 = (bf16[192,1536]{1,0:T(8,128)(2,1)S(1)}, bf16[192,1536]{1,0:T(8,128)(2,1)S(1)}, u32[]{:S(2)}, u32[]{:S(2)}) collective-permute-start(bf16[192,1536]{1,0:T(8,128)(2,1)S(1)} %get-tuple-element.50), channel_id=1, source_target_pairs={{0,1},{1,0},{2,3},{3,2},{4,5},{5,4},{6,7},{7,6},{8,10},{9,11},{10,... | collective-permute-start | bytes 1769480 | tf_op jit(solution)/shard_map/ppermute | solution.py:107
  22.4 4.2 %collective-permute-start.5 = (bf16[64,384]{1,0:T(8,128)(2,1)S(1)}, bf16[64,384]{1,0:T(8,128)(2,1)S(1)}, u32[]{:S(2)}, u32[]{:S(2)}) collective-permute-start(bf16[64,384]{1,0:T(8,128)(2,1)S(1)} %get-tuple-element.44), channel_id=1, source_target_pairs={{0,8},{1,9},{2,10},{3,11},{4,12},{5,13},{6,14},{7,15},{8,0},{9,1},... | collective-permute-start | bytes 147464 | tf_op jit(solution)/shard_map/ppermute | solution.py:107
  22.4 10.0 %copy-start.1 = (bf16[1,192,1536]{2,1,0:T(8,128)(2,1)S(1)}, bf16[1,192,1536]{2,1,0:T(8,128)(2,1)}, u32[]{:S(2)}) copy-start(bf16[1,192,1536]{2,1,0:T(8,128)(2,1)} %param.6) | copy-start | bytes 1769476
  22.4 7.2 %collective-permute-start.6 = (bf16[64,384]{1,0:T(8,128)(2,1)S(1)}, bf16[64,384]{1,0:T(8,128)(2,1)S(1)}, u32[]{:S(2)}, u32[]{:S(2)}) collective-permute-start(bf16[64,384]{1,0:T(8,128)(2,1)S(1)} %get-tuple-element.45), channel_id=1, source_target_pairs={{0,24},{1,25},{2,26},{3,27},{4,28},{5,29},{6,30},{7,31},{8,16},{9,... | collective-permute-start | bytes 147464 | tf_op jit(solution)/shard_map/ppermute | solution.py:107
  30.2 2.5 %collective-permute-start.12 = (bf16[192,1536]{1,0:T(8,128)(2,1)S(1)}, bf16[192,1536]{1,0:T(8,128)(2,1)S(1)}, u32[]{:S(2)}, u32[]{:S(2)}) collective-permute-start(bf16[192,1536]{1,0:T(8,128)(2,1)S(1)} %collective-permute-done.11.refs_6_.refs_3_.refs_8_), channel_id=1, source_target_pairs={{0,1},{1,0},{2,3},{3,2},{4,5},{5,4},{6,7},{7,6},{8,9},{9,8},{10,11... | collective-permute-start | bytes 1769480 | tf_op jit(solution)/shard_map/ppermute | solution.py:107
  30.3 2.1 %collective-permute-start.7 = (bf16[32,1536]{1,0:T(8,128)(2,1)S(1)}, bf16[32,1536]{1,0:T(8,128)(2,1)S(1)}, u32[]{:S(2)}, u32[]{:S(2)}) collective-permute-start(bf16[32,1536]{1,0:T(8,128)(2,1)S(1)} %get-tuple-element.47), channel_id=1, source_target_pairs={{0,1},{1,0},{2,3},{3,2},{4,5},{5,4},{6,7},{7,6},{8,14},{9,15},{10,... | collective-permute-start | bytes 294920 | tf_op jit(solution)/shard_map/ppermute | solution.py:107
  30.8 1.8 %collective-permute-start.9 = (bf16[32,1536]{1,0:T(8,128)(2,1)S(1)}, bf16[32,1536]{1,0:T(8,128)(2,1)S(1)}, u32[]{:S(2)}, u32[]{:S(2)}) collective-permute-start(bf16[32,1536]{1,0:T(8,128)(2,1)S(1)} %get-tuple-element.47), channel_id=1, source_target_pairs={{0,1},{1,0},{2,3},{3,2},{4,5},{5,4},{6,7},{7,6},{8,10},{9,11},{10,... | collective-permute-start | bytes 294920 | tf_op jit(solution)/shard_map/ppermute | solution.py:107
  30.8 1.8 %collective-permute-start.10 = (bf16[32,1536]{1,0:T(8,128)(2,1)S(1)}, bf16[32,1536]{1,0:T(8,128)(2,1)S(1)}, u32[]{:S(2)}, u32[]{:S(2)}) collective-permute-start(bf16[32,1536]{1,0:T(8,128)(2,1)S(1)} %get-tuple-element.49.refs_0_), channel_id=1, source_target_pairs={{0,1},{1,0},{2,3},{3,2},{4,5},{5,4},{6,7},{7,6},{8,12},{9,13},{10,... | collective-permute-start | bytes 294920 | tf_op jit(solution)/shard_map/ppermute | solution.py:107
  32.4 18.9 %collective-permute-start.8 = (bf16[192,1536]{1,0:T(8,128)(2,1)S(1)}, bf16[192,1536]{1,0:T(8,128)(2,1)S(1)}, u32[]{:S(2)}, u32[]{:S(2)}) collective-permute-start(bf16[192,1536]{1,0:T(8,128)(2,1)S(1)} %bitcast.6), channel_id=1, source_target_pairs={{0,1},{1,0},{2,3},{3,2},{4,5},{5,4},{6,7},{7,6},{8,10},{9,11},{10,... | collective-permute-start | bytes 1769480 | tf_op jit(solution)/shard_map/ppermute | solution.py:107
  33.6 1.3 %collective-permute-start.13 = (bf16[1,32,768]{2,1,0:T(8,128)(2,1)S(1)}, bf16[1,32,768]{2,1,0:T(8,128)(2,1)S(1)}, u32[]{:S(2)}, u32[]{:S(2)}) collective-permute-start(bf16[1,32,768]{2,1,0:T(8,128)(2,1)S(1)} %get-tuple-element.52), channel_id=1, source_target_pairs={{0,1},{1,0},{2,3},{3,2},{4,5},{5,4},{6,7},{7,6},{8,24},{9,25},{10,... | collective-permute-start | bytes 147464 | tf_op jit(solution)/shard_map/ppermute | solution.py:107
  50.1 15.5 %collective-permute-start.21 = (bf16[192,3328]{1,0:T(8,128)(2,1)S(1)}, bf16[192,3328]{1,0:T(8,128)(2,1)S(1)}, u32[]{:S(2)}, u32[]{:S(2)}) collective-permute-start(bf16[192,3328]{1,0:T(8,128)(2,1)S(1)} %collective-permute-done.14.refs_4_), channel_id=1, source_target_pairs={{0,1},{1,0},{2,3},{3,2},{4,5},{5,4},{6,7},{7,6},{8,9},{9,8},{10,11... | collective-permute-start | bytes 3833864 | tf_op jit(solution)/shard_map/ppermute | solution.py:107
  50.7 2.5 %collective-permute-start.15 = (bf16[32,1536]{1,0:T(8,128)(2,1)S(1)}, bf16[32,1536]{1,0:T(8,128)(2,1)S(1)}, u32[]{:S(2)}, u32[]{:S(2)}) collective-permute-start(bf16[32,1536]{1,0:T(8,128)(2,1)S(1)} %shard_map.64.refs_4_), channel_id=1, source_target_pairs={{0,1},{1,0},{2,3},{3,2},{4,5},{5,4},{6,7},{7,6},{8,9},{9,8},{10,11... | collective-permute-start | bytes 294920 | tf_op jit(solution)/shard_map/ppermute | solution.py:107
  54.1 4.1 %collective-permute-start.18 = (bf16[192,1536]{1,0:T(8,128)(2,1)S(1)}, bf16[192,1536]{1,0:T(8,128)(2,1)S(1)}, u32[]{:S(2)}, u32[]{:S(2)}) collective-permute-start(bf16[192,1536]{1,0:T(8,128)(2,1)S(1)} %collective-permute-done.8.refs_7_), channel_id=1, source_target_pairs={{0,1},{1,0},{2,3},{3,2},{4,5},{5,4},{6,7},{7,6},{8,9},{9,8},{10,11... | collective-permute-start | bytes 1769480 | tf_op jit(solution)/shard_map/ppermute | solution.py:107
  54.3 1.9 %collective-permute-start.16 = (bf16[1,32,768]{2,1,0:T(8,128)(2,1)S(1)}, bf16[1,32,768]{2,1,0:T(8,128)(2,1)S(1)}, u32[]{:S(2)}, u32[]{:S(2)}) collective-permute-start(bf16[1,32,768]{2,1,0:T(8,128)(2,1)S(1)} %get-tuple-element.55), channel_id=1, source_target_pairs={{0,1},{1,0},{2,3},{3,2},{4,5},{5,4},{6,7},{7,6},{8,24},{9,25},{10,... | collective-permute-start | bytes 147464 | tf_op jit(solution)/shard_map/ppermute | solution.py:107
  56.8 1.4 %collective-permute-start.17 = (bf16[32,1536]{1,0:T(8,128)(2,1)S(1)}, bf16[32,1536]{1,0:T(8,128)(2,1)S(1)}, u32[]{:S(2)}, u32[]{:S(2)}) collective-permute-start(bf16[32,1536]{1,0:T(8,128)(2,1)S(1)} %shard_map.66.refs_0_), channel_id=1, source_target_pairs={{0,1},{1,0},{2,3},{3,2},{4,5},{5,4},{6,7},{7,6},{8,12},{9,13},{10,... | collective-permute-start | bytes 294920 | tf_op jit(solution)/shard_map/ppermute | solution.py:107
  57.0 11.5 %collective-permute-start.25 = (bf16[64,1536]{1,0:T(8,128)(2,1)S(1)}, bf16[64,1536]{1,0:T(8,128)(2,1)S(1)}, u32[]{:S(2)}, u32[]{:S(2)}) collective-permute-start(bf16[64,1536]{1,0:T(8,128)(2,1)S(1)} %get-tuple-element.70.refs_0_), channel_id=1, source_target_pairs={{0,1},{1,0},{2,3},{3,2},{4,5},{5,4},{6,7},{7,6},{8,9},{9,8},{10,11... | collective-permute-start | bytes 589832 | tf_op jit(solution)/shard_map/ppermute | solution.py:107
  59.1 6.5 %collective-permute-start.19 = (bf16[2,32,768]{2,1,0:T(8,128)(2,1)S(1)}, bf16[2,32,768]{2,1,0:T(8,128)(2,1)S(1)}, u32[]{:S(2)}, u32[]{:S(2)}) collective-permute-start(bf16[2,32,768]{2,1,0:T(8,128)(2,1)S(1)} %get-tuple-element.62), channel_id=1, source_target_pairs={{0,8},{1,9},{2,10},{3,11},{4,12},{5,13},{6,14},{7,15},{8,0},{9,1},... | collective-permute-start | bytes 294920 | tf_op jit(solution)/shard_map/ppermute | solution.py:107
  63.0 2.6 %collective-permute-start.20 = (bf16[2,32,768]{2,1,0:T(8,128)(2,1)S(1)}, bf16[2,32,768]{2,1,0:T(8,128)(2,1)S(1)}, u32[]{:S(2)}, u32[]{:S(2)}) collective-permute-start(bf16[2,32,768]{2,1,0:T(8,128)(2,1)S(1)} %get-tuple-element.62), channel_id=1, source_target_pairs={{0,1},{1,0},{2,3},{3,2},{4,5},{5,4},{6,7},{7,6},{8,16},{9,17},{10,... | collective-permute-start | bytes 294920 | tf_op jit(solution)/shard_map/ppermute | solution.py:107
  66.6 4.7 %collective-permute-start.26 = (bf16[32,1536]{1,0:T(8,128)(2,1)S(1)}, bf16[32,1536]{1,0:T(8,128)(2,1)S(1)}, u32[]{:S(2)}, u32[]{:S(2)}) collective-permute-start(bf16[32,1536]{1,0:T(8,128)(2,1)S(1)} %shard_map.69.refs_1_), channel_id=1, source_target_pairs={{0,4},{1,5},{2,6},{3,7},{4,0},{5,1},{6,2},{7,3},{8,9},{9,8},{10,11... | collective-permute-start | bytes 294920 | tf_op jit(solution)/shard_map/ppermute | solution.py:107
  67.9 1.3 %collective-permute-start.22 = (f32[2,32,192]{2,1,0:T(8,128)S(1)}, f32[2,32,192]{2,1,0:T(8,128)S(1)}, u32[]{:S(2)}, u32[]{:S(2)}) collective-permute-start(f32[2,32,192]{2,1,0:T(8,128)S(1)} %get-tuple-element.65), channel_id=1, source_target_pairs={{0,1},{1,0},{2,3},{3,2},{4,5},{5,4},{6,7},{7,6},{8,9},{9,8},{10,11... | collective-permute-start | bytes 147464 | tf_op jit(solution)/shard_map/ppermute | solution.py:107
  67.9 1.4 %collective-permute-start.23 = (f32[2,32,192]{2,1,0:T(8,128)S(1)}, f32[2,32,192]{2,1,0:T(8,128)S(1)}, u32[]{:S(2)}, u32[]{:S(2)}) collective-permute-start(f32[2,32,192]{2,1,0:T(8,128)S(1)} %get-tuple-element.66), channel_id=1, source_target_pairs={{0,1},{1,0},{2,3},{3,2},{4,5},{5,4},{6,7},{7,6},{8,10},{9,11},{10,... | collective-permute-start | bytes 147464 | tf_op jit(solution)/shard_map/ppermute | solution.py:107
  68.5 1.3 %collective-permute-start.24 = (f32[2,32,192]{2,1,0:T(8,128)S(1)}, f32[2,32,192]{2,1,0:T(8,128)S(1)}, u32[]{:S(2)}, u32[]{:S(2)}) collective-permute-start(f32[2,32,192]{2,1,0:T(8,128)S(1)} %get-tuple-element.67), channel_id=1, source_target_pairs={{0,1},{1,0},{2,3},{3,2},{4,5},{5,4},{6,7},{7,6},{8,11},{9,10},{10,... | collective-permute-start | bytes 147464 | tf_op jit(solution)/shard_map/ppermute | solution.py:107
  71.3 4.7 %collective-permute-start.27 = (bf16[32,1536]{1,0:T(8,128)(2,1)S(1)}, bf16[32,1536]{1,0:T(8,128)(2,1)S(1)}, u32[]{:S(2)}, u32[]{:S(2)}) collective-permute-start(bf16[32,1536]{1,0:T(8,128)(2,1)S(1)} %shard_map.72), channel_id=1, source_target_pairs={{0,2},{1,3},{2,0},{3,1},{4,6},{5,7},{6,4},{7,5},{8,9},{9,8},{10,11... | collective-permute-start | bytes 294920 | tf_op jit(solution)/shard_map/ppermute | solution.py:107
  76.0 1.5 %collective-permute-start.28 = (bf16[64,1536]{1,0:T(8,128)(2,1)S(1)}, bf16[64,1536]{1,0:T(8,128)(2,1)S(1)}, u32[]{:S(2)}, u32[]{:S(2)}) collective-permute-start(bf16[64,1536]{1,0:T(8,128)(2,1)S(1)} %pad_maximum_fusion.refs_0_), channel_id=1, source_target_pairs={{0,1},{1,0},{2,3},{3,2},{4,5},{5,4},{6,7},{7,6},{8,9},{9,8},{10,11... | collective-permute-start | bytes 589832 | tf_op jit(solution)/shard_map/ppermute | solution.py:107
